TPU v7x, 32 devices: a whole 2x2x4 slice. The times are simulated.
32 devices in a mesh: gx: 4 (over z), gy: 8 (over y, x, core).
Axes of the slice: x: 2, y: 2, z: 4, core: 2. Of those that a mesh axis runs over, the one named last changes fastest.
Arguments:
- refl_left: float32 [32, 256, 256], P(('gx', 'gy')), may hold values from -1 to 1, as said below
- refl_right: float32 [32, 256, 256], P(('gx', 'gy')), may hold values from -1 to 1, as said below
- trans: float32 [32, 256, 256], P(('gx', 'gy')), may hold values from -2 to 2
Outputs:
- prefix_left: float32 [32, 256, 256], P(('gx', 'gy'))
- prefix_right: float32 [32, 256, 256], P(('gx', 'gy'))
- prefix_trans: float32 [32, 256, 256], P(('gx', 'gy'))
Inputs may be any that keep to these rules, and one draw needn't show every extreme that they name: `refl_left`: every section's reflection matrix is symmetric. `refl_right`: every section's reflection matrix is symmetric.
All inputs are finite; a program needn't handle non-finite values.
Results may differ from a plain program's by a relative error of at most 0.0003.
Values sent between devices are 32-bit elements; how exact they have to be, the bound alone decides.
No kernel may reach another device: no remote copies, remote signals or barrier semaphores. Data moves between devices by JAX's collectives and lax.ppermute only.
A program may use at most 64 MiB of HBM per device.

v0:
```python
import functools

import jax
import jax.numpy as jnp
from jax import lax
from jax.experimental import pallas as pl
from jax.experimental.pallas import tpu as pltpu
from jax.sharding import PartitionSpec as P

AXES = ("gx", "gy")
NS_STEPS = 5
PAD = 8
F32 = jnp.float32
BF16 = jnp.bfloat16
NN = (((1,), (0,)), ((), ()))
NT = (((1,), (1,)), ((), ()))


def swap(block, distance):
    count = lax.axis_size(AXES)
    return lax.ppermute(block, AXES, [(i, i ^ distance) for i in range(count)])


def split(x):
    high = x.astype(BF16)
    return high, (x - high.astype(F32)).astype(BF16)


def dot1(a, b, dims=NN):
    return lax.dot_general(a, b, dims, preferred_element_type=F32)


def dot3(a, b, dims=NN):
    return dot1(a[0], b[0], dims) + (dot1(a[0], b[1], dims) + dot1(a[1], b[0], dims))


def half(x):
    return x.astype(BF16)


def inverse_less_eye(coupling):
    rest, power = coupling, half(coupling)
    for _ in range(NS_STEPS - 1):
        squared = dot1(power, power)
        power = half(squared)
        rest = rest + squared + dot1(half(rest), power)
    rest = half(rest)
    high, low = split(coupling)
    rest32 = rest.astype(F32)
    residual = (coupling - rest32) + (dot1(high, rest) + dot1(low, rest))
    return rest32 + residual + dot1(rest, half(residual))


def before_trans(own, facing):
    near, away, out = own
    f, o, s = split(facing), split(near), split(out)
    coupling = dot3(f, o)
    inner = split(dot3(f, s, NT))
    rest = split(inverse_less_eye(coupling))
    leading = out + dot3(s, rest)
    mirror = near + dot3(o, rest)
    return leading, mirror, away + dot3(split(leading), inner)


def after_trans(leading, mirror, away, into):
    q = split(into)
    trans = dot3(split(leading), q)
    bounced = split(dot3(split(mirror), q))
    return trans, away + dot3(split(into.T), bounced)


def place():
    return lax.axis_index("gx") * lax.axis_size("gy") + lax.axis_index("gy")


def bit(me, distance):
    return me & distance != 0


def lower_upper(h):
    row = lax.broadcasted_iota(jnp.int32, (h, h), 0)
    col = lax.broadcasted_iota(jnp.int32, (h, h), 1)
    return row > col, row < col


def pack_symmetric(x, core, ref, start):
    h = x.shape[0] // 2
    q = h // 2
    below, above = lower_upper(h)
    a, b, c = x[:h, :h], x[:h, h:], x[h:, h:]
    diagonal = jnp.sum(jnp.where(below | above, 0.0, c), axis=0, keepdims=True)
    both = jnp.concatenate([b, jnp.where(above, c, a)], 1)
    ref[start : start + q, :] = jnp.where(core, both[q:], both[:q])
    diagonal = jnp.concatenate([diagonal, diagonal], 1)
    ref[start + q : start + q + PAD, :] = jnp.broadcast_to(diagonal, (PAD, 2 * h))


def joined(near_ref, far_ref, core, lo, hi):
    near, far = near_ref[lo:hi, :], far_ref[lo:hi, :]
    return jnp.concatenate([jnp.where(core, far, near), jnp.where(core, near, far)], 0)


def unpack_symmetric(near_ref, far_ref, core, start):
    h = near_ref.shape[1] // 2
    q = h // 2
    below, above = lower_upper(h)
    both = joined(near_ref, far_ref, core, start, start + q)
    diagonal = near_ref[start + q : start + q + 1, :h]
    b, w = both[:, :h], both[:, h:]
    turned = w.T
    a = jnp.where(above, turned, w)
    c = jnp.where(above, w, jnp.where(below, turned, diagonal))
    return jnp.concatenate([jnp.concatenate([a, b], 1), jnp.concatenate([b.T, c], 1)], 0)


def unpack_second(near_ref, far_ref, core):
    h = near_ref.shape[1] // 2
    return joined(near_ref, far_ref, core, 0, h), unpack_symmetric(near_ref, far_ref, core, h)


def send_total(own_side, other_side, trans, same, core, own_ref, first_ref, second_ref):
    turned = trans.T
    near = jnp.where(same, other_side, own_side)
    away = jnp.where(same, own_side, other_side)
    h = trans.shape[0] // 2
    back = jnp.where(same, turned, trans)
    own_ref[0] = near
    own_ref[1] = away
    own_ref[2] = jnp.where(same, trans, turned)
    pack_symmetric(near, core, first_ref, 0)
    second_ref[0:h, :] = jnp.where(core, back[h:], back[:h])
    pack_symmetric(away, core, second_ref, h)


def first_kernel(section_ref, got1, got2, got3, own_ref, prefix_ref, first_ref, second_ref):
    me = place()
    upper = bit(me, 1)
    left, right, trans = section_ref[0], section_ref[1], section_ref[2]
    pick = lambda a, b: jnp.where(upper, a, b)
    own = pick(left, right), pick(right, left), pick(trans, trans.T)
    leading, mirror, own_side = before_trans(own, pick(got2[0], got1[0]))
    into = pick(got3[0], got3[0].T)
    through, other_side = after_trans(leading, mirror, pick(got1[0], got2[0]), into)
    send_total(own_side, other_side, through, upper == bit(me, 2), upper, own_ref, first_ref, second_ref)
    prefix_ref[0] = pick(other_side, left)
    prefix_ref[1] = pick(own_side, right)
    prefix_ref[2] = pick(through, trans)


def early_kernel(own_ref, near_ref, far_ref, half_ref):
    core = bit(place(), 1)
    facing = unpack_symmetric(near_ref, far_ref, core, 0)
    for i, x in enumerate(before_trans((own_ref[0], own_ref[1], own_ref[2]), facing)):
        half_ref[i] = x


def late_kernel(distance, half_ref, near_ref, far_ref, own_ref, first_ref, second_ref):
    me = place()
    core = bit(me, 1)
    into, away = unpack_second(near_ref, far_ref, core)
    trans, other_side = after_trans(half_ref[0], half_ref[1], away, into)
    same = bit(me, distance) == bit(me, 2 * distance)
    send_total(half_ref[2], other_side, trans, same, core, own_ref, first_ref, second_ref)


def prefix_kernel(distance, old_ref, near1, far1, near2, far2, new_ref):
    me = place()
    core, upper = bit(me, 1), bit(me, distance)
    facing = unpack_symmetric(near1, far1, core, 0)
    leading, mirror, right = before_trans((old_ref[0], old_ref[1], old_ref[2]), facing)
    into, away = unpack_second(near2, far2, core)
    trans, left = after_trans(leading, mirror, away, into)
    for i, x in enumerate((left, right, trans)):
        new_ref[i] = jnp.where(upper, x, old_ref[i])


def last_kernel(distance, old_ref, half_ref, near_ref, far_ref, left_ref, right_ref, trans_ref):
    me = place()
    core, upper = bit(me, 1), bit(me, distance)
    into, away = unpack_second(near_ref, far_ref, core)
    trans, left = after_trans(half_ref[0], half_ref[1], away, into)
    right_ref[0] = jnp.where(upper, half_ref[2], old_ref[1])
    trans_ref[0] = jnp.where(upper, trans, old_ref[2])
    left_ref[0] = jnp.where(upper, left, old_ref[0])


def call(kernel, products, outs, *args):
    vmem = pl.BlockSpec(memory_space=pltpu.VMEM)
    m = args[0].shape[-1]
    return pl.pallas_call(
        kernel,
        out_shape=[jax.ShapeDtypeStruct(s, F32) for s in outs],
        in_specs=[vmem] * len(args),
        out_specs=[vmem] * len(outs),
        cost_estimate=pl.CostEstimate(flops=2 * products * m**3, bytes_accessed=4 * m**2 * len(args), transcendentals=0),
        compiler_params=pltpu.CompilerParams(vmem_limit_bytes=40 * 2**20),
    )(*args)


def shards(refl_left, refl_right, trans):
    m = trans.shape[1]
    levels = lax.axis_size(AXES).bit_length() - 1
    stack = (3, m, m)
    first, second = (m // 4 + PAD, m), (m // 2 + m // 4 + PAD, m)
    sections = refl_left, refl_right, trans
    got = [swap(x, 1) for x in sections]
    section = jnp.concatenate(sections, 0)
    own, prefix, send1, send2 = call(first_kernel, 36, [stack, stack, first, second], section, *got)
    pending = None
    for level in range(1, levels):
        distance = 1 << level
        bind = lambda kernel: functools.partial(kernel, distance)
        near1, near2 = swap(send1, distance), swap(send2, distance)
        if pending is not None:
            (prefix,) = pending(prefix)
            near1, prefix = lax.optimization_barrier((near1, prefix))
        far1 = swap(near1, 1)
        if level == levels - 1:
            (halfway,) = call(early_kernel, 27, [stack], prefix, near1, far1)
            near2, halfway = lax.optimization_barrier((near2, halfway))
            far2 = swap(near2, 1)
            return tuple(call(bind(last_kernel), 9, [(1, m, m)] * 3, prefix, halfway, near2, far2))
        (halfway,) = call(early_kernel, 27, [stack], own, near1, far1)
        near2, halfway = lax.optimization_barrier((near2, halfway))
        far2 = swap(near2, 1)
        own, send1, send2 = call(bind(late_kernel), 9, [stack, first, second], halfway, near2, far2)
        pending = lambda old, kernel=bind(prefix_kernel), got=(near1, far1, near2, far2): call(kernel, 36, [stack], old, *got)


def solution(mesh):
    spec = P(AXES, None, None)
    return jax.shard_map(
        shards,
        mesh=mesh,
        in_specs=(spec,) * 3,
        out_specs=(spec,) * 3,
        check_vma=False,
    )
```

profile of v0, /device:TPU:0, one launch (start us, length us, event | category | flops | bytes accessed | tf_op | source)
XLA Modules:
  0.0 60.9 jit_solution(1794395961498672663)
XLA Ops:
  0.6 0.5 collective-permute-start
  1.2 0.4 collective-permute-start.2
  1.7 1.2 %pad_maximum_fusion.section_ref = f32[3,256,256]{2,1,0:T(8,128)S(1)} fusion(f32[1,256,256]{2,1,0:T(8,128)} %param.5, f32[1,256,256]{2,1,0:T(8,128)} %param.4, f32[1,256,256]{2,1,0:T(8,128)} %param.3), kind=kLoop, calls=%fused_computation | loop fusion | flops 393216 | bytes 1572864 | tf_op jit(solution)/shard_map/concatenate | solution.py:207
  2.9 0.4 collective-permute-done.2.got3
  3.3 3.0 %shard_map.58 = (f32[3,256,256]{2,1,0:T(8,128)S(1)}, f32[3,256,256]{2,1,0:T(8,128)S(1)}, f32[72,256]{1,0:T(8,128)S(1)}, f32[200,256]{1,0:T(8,128)S(1)}) custom-call(f32[3,256,256]{2,1,0:T(8,128)S(1)} %pad_maximum_fusion.section_ref, f32[1,256,256]{2,1,0:T(8,128)S(1)} %collective-permute-done.got1, f32[1,256,256]{2,1,0:T(8,128)S(1)} %collective-permute-done.1.got2, ...), custom_call_target="tpu_custom_call" | custom-call | flops 1207959552 | bytes 1048576 | tf_op jit(solution)/shard_map/pallas_call | solution.py:190
  6.2 2.9 %collective-permute-start.4 = (f32[72,256]{1,0:T(8,128)S(1)}, f32[72,256]{1,0:T(8,128)S(1)}, u32[]{:S(2)}, u32[]{:S(2)}) collective-permute-start(f32[72,256]{1,0:T(8,128)S(1)} %get-tuple-element.31), channel_id=1, source_target_pairs={{0,2},{1,3},{2,0},{3,1},{4,6},{5,7},{6,4},{7,5},{8,10},{9,11},{10,... | collective-permute-start | bytes 221192 | tf_op jit(solution)/shard_map/ppermute | solution.py:21
  9.2 2.6 %collective-permute-done.4.near_ref.near1 = f32[72,256]{1,0:T(8,128)S(1)} collective-permute-done((f32[72,256]{1,0:T(8,128)S(1)}, f32[72,256]{1,0:T(8,128)S(1)}, u32[]{:S(2)}, u32[]{:S(2)}) %collective-permute-start.4) | collective-permute-done | bytes 73760 | tf_op jit(solution)/shard_map/ppermute | solution.py:21
  11.9 1.3 %collective-permute-done.5.far_ref.far1 = f32[72,256]{1,0:T(8,128)S(1)} collective-permute-done((f32[72,256]{1,0:T(8,128)S(1)}, f32[72,256]{1,0:T(8,128)S(1)}, u32[]{:S(2)}, u32[]{:S(2)}) %collective-permute-start.5) | collective-permute-done | bytes 73760 | tf_op jit(solution)/shard_map/ppermute | solution.py:21
  13.1 2.4 %shard_map.59.half_ref = f32[3,256,256]{2,1,0:T(8,128)S(1)} custom-call(f32[3,256,256]{2,1,0:T(8,128)S(1)} %get-tuple-element.30.own_ref, f32[72,256]{1,0:T(8,128)S(1)} %collective-permute-done.4.near_ref.near1, f32[72,256]{1,0:T(8,128)S(1)} %collective-permute-done.5.far_ref.far1), custom_call_target="tpu_custom_call" | custom-call | flops 905969664 | bytes 786432 | tf_op jit(solution)/shard_map/pallas_call | solution.py:190
  15.6 0.5 collective-permute-done.3.near_ref.near2
  16.1 1.5 %collective-permute-done.6.far_ref.far2 = f32[200,256]{1,0:T(8,128)S(1)} collective-permute-done((f32[200,256]{1,0:T(8,128)S(1)}, f32[200,256]{1,0:T(8,128)S(1)}, u32[]{:S(2)}, u32[]{:S(2)}) %collective-permute-start.6) | collective-permute-done | bytes 204832 | tf_op jit(solution)/shard_map/ppermute | solution.py:21
  17.6 0.8 %shard_map.60 = (f32[3,256,256]{2,1,0:T(8,128)S(1)}, f32[72,256]{1,0:T(8,128)S(1)}, f32[200,256]{1,0:T(8,128)S(1)}) custom-call(f32[3,256,256]{2,1,0:T(8,128)S(1)} %shard_map.59.half_ref, f32[200,256]{1,0:T(8,128)S(1)} %collective-permute-done.3.near_ref.near2, f32[200,256]{1,0:T(8,128)S(1)} %collective-permute-done.6.far_ref.far2), custom_call_target="tpu_custom_call" | custom-call | flops 301989888 | bytes 786432 | tf_op jit(solution)/shard_map/pallas_call | solution.py:190
  18.4 1.9 %collective-permute-start.8 = (f32[72,256]{1,0:T(8,128)S(1)}, f32[72,256]{1,0:T(8,128)S(1)}, u32[]{:S(2)}, u32[]{:S(2)}) collective-permute-start(f32[72,256]{1,0:T(8,128)S(1)} %get-tuple-element.36), channel_id=1, source_target_pairs={{0,4},{1,5},{2,6},{3,7},{4,0},{5,1},{6,2},{7,3},{8,12},{9,13},{10,... | collective-permute-start | bytes 221192 | tf_op jit(solution)/shard_map/ppermute | solution.py:21
  20.5 3.0 %shard_map.61.old_ref = f32[3,256,256]{2,1,0:T(8,128)S(1)} custom-call(f32[3,256,256]{2,1,0:T(8,128)S(1)} %get-tuple-element.37.old_ref, f32[72,256]{1,0:T(8,128)S(1)} %collective-permute-done.4.near_ref.near1, f32[72,256]{1,0:T(8,128)S(1)} %collective-permute-done.5.far_ref.far1, f32[200,256]{1,0:T(8,128)S(1)} %collective-permute-done.3.near_ref.near2, ...), custom_call_target="tpu_custom_call" | custom-call | flops 1207959552 | bytes 1310720 | tf_op jit(solution)/shard_map/pallas_call | solution.py:190
  23.6 1.3 %collective-permute-done.9.far_ref.far1 = f32[72,256]{1,0:T(8,128)S(1)} collective-permute-done((f32[72,256]{1,0:T(8,128)S(1)}, f32[72,256]{1,0:T(8,128)S(1)}, u32[]{:S(2)}, u32[]{:S(2)}) %collective-permute-start.9) | collective-permute-done | bytes 73760 | tf_op jit(solution)/shard_map/ppermute | solution.py:21
  24.8 2.4 %shard_map.62.half_ref = f32[3,256,256]{2,1,0:T(8,128)S(1)} custom-call(f32[3,256,256]{2,1,0:T(8,128)S(1)} %get-tuple-element.35.own_ref, f32[72,256]{1,0:T(8,128)S(1)} %collective-permute-done.8.near_ref.near1, f32[72,256]{1,0:T(8,128)S(1)} %collective-permute-done.9.far_ref.far1), custom_call_target="tpu_custom_call" | custom-call | flops 905969664 | bytes 786432 | tf_op jit(solution)/shard_map/pallas_call | solution.py:190
  27.5 1.3 %collective-permute-done.10.far_ref.far2 = f32[200,256]{1,0:T(8,128)S(1)} collective-permute-done((f32[200,256]{1,0:T(8,128)S(1)}, f32[200,256]{1,0:T(8,128)S(1)}, u32[]{:S(2)}, u32[]{:S(2)}) %collective-permute-start.10) | collective-permute-done | bytes 204832 | tf_op jit(solution)/shard_map/ppermute | solution.py:21
  28.8 0.8 %shard_map.63 = (f32[3,256,256]{2,1,0:T(8,128)S(1)}, f32[72,256]{1,0:T(8,128)S(1)}, f32[200,256]{1,0:T(8,128)S(1)}) custom-call(f32[3,256,256]{2,1,0:T(8,128)S(1)} %shard_map.62.half_ref, f32[200,256]{1,0:T(8,128)S(1)} %collective-permute-done.7.near_ref.near2, f32[200,256]{1,0:T(8,128)S(1)} %collective-permute-done.10.far_ref.far2), custom_call_target="tpu_custom_call" | custom-call | flops 301989888 | bytes 786432 | tf_op jit(solution)/shard_map/pallas_call | solution.py:190
  29.6 1.9 %collective-permute-start.12 = (f32[72,256]{1,0:T(8,128)S(1)}, f32[72,256]{1,0:T(8,128)S(1)}, u32[]{:S(2)}, u32[]{:S(2)}) collective-permute-start(f32[72,256]{1,0:T(8,128)S(1)} %get-tuple-element.43), channel_id=1, source_target_pairs={{0,8},{1,9},{2,10},{3,11},{4,12},{5,13},{6,14},{7,15},{8,0},{9,1},... | collective-permute-start | bytes 221192 | tf_op jit(solution)/shard_map/ppermute | solution.py:21
  31.7 3.0 %shard_map.64.old_ref = f32[3,256,256]{2,1,0:T(8,128)S(1)} custom-call(f32[3,256,256]{2,1,0:T(8,128)S(1)} %shard_map.61.old_ref, f32[72,256]{1,0:T(8,128)S(1)} %collective-permute-done.8.near_ref.near1, f32[72,256]{1,0:T(8,128)S(1)} %collective-permute-done.9.far_ref.far1, f32[200,256]{1,0:T(8,128)S(1)} %collective-permute-done.7.near_ref.near2, ...), custom_call_target="tpu_custom_call" | custom-call | flops 1207959552 | bytes 1310720 | tf_op jit(solution)/shard_map/pallas_call | solution.py:190
  34.8 1.3 %collective-permute-done.13.far_ref.far1 = f32[72,256]{1,0:T(8,128)S(1)} collective-permute-done((f32[72,256]{1,0:T(8,128)S(1)}, f32[72,256]{1,0:T(8,128)S(1)}, u32[]{:S(2)}, u32[]{:S(2)}) %collective-permute-start.13) | collective-permute-done | bytes 73760 | tf_op jit(solution)/shard_map/ppermute | solution.py:21
  36.0 2.4 %shard_map.65.half_ref = f32[3,256,256]{2,1,0:T(8,128)S(1)} custom-call(f32[3,256,256]{2,1,0:T(8,128)S(1)} %get-tuple-element.42.own_ref, f32[72,256]{1,0:T(8,128)S(1)} %collective-permute-done.12.near_ref.near1, f32[72,256]{1,0:T(8,128)S(1)} %collective-permute-done.13.far_ref.far1), custom_call_target="tpu_custom_call" | custom-call | flops 905969664 | bytes 786432 | tf_op jit(solution)/shard_map/pallas_call | solution.py:190
  38.7 1.3 %collective-permute-done.14.far_ref.far2 = f32[200,256]{1,0:T(8,128)S(1)} collective-permute-done((f32[200,256]{1,0:T(8,128)S(1)}, f32[200,256]{1,0:T(8,128)S(1)}, u32[]{:S(2)}, u32[]{:S(2)}) %collective-permute-start.14) | collective-permute-done | bytes 204832 | tf_op jit(solution)/shard_map/ppermute | solution.py:21
  40.0 1.9 %shard_map.66 = (f32[3,256,256]{2,1,0:T(8,128)}, f32[72,256]{1,0:T(8,128)S(1)}, f32[200,256]{1,0:T(8,128)S(1)}) custom-call(f32[3,256,256]{2,1,0:T(8,128)S(1)} %shard_map.65.half_ref, f32[200,256]{1,0:T(8,128)S(1)} %collective-permute-done.11.near_ref.near2, f32[200,256]{1,0:T(8,128)S(1)} %collective-permute-done.14.far_ref.far2), custom_call_target="tpu_custom_call" | custom-call | flops 301989888 | bytes 786432 | tf_op jit(solution)/shard_map/pallas_call | solution.py:190
  41.9 2.9 %collective-permute-start.15 = (f32[72,256]{1,0:T(8,128)S(1)}, f32[72,256]{1,0:T(8,128)S(1)}, u32[]{:S(2)}, u32[]{:S(2)}) collective-permute-start(f32[72,256]{1,0:T(8,128)S(1)} %get-tuple-element.48), channel_id=1, source_target_pairs={{0,16},{1,17},{2,18},{3,19},{4,20},{5,21},{6,22},{7,23},{8,24},{9,... | collective-permute-start | bytes 221192 | tf_op jit(solution)/shard_map/ppermute | solution.py:21
  44.8 3.0 %shard_map.67.own_ref.old_ref = f32[3,256,256]{2,1,0:T(8,128)S(1)} custom-call(f32[3,256,256]{2,1,0:T(8,128)S(1)} %shard_map.64.old_ref, f32[72,256]{1,0:T(8,128)S(1)} %collective-permute-done.12.near_ref.near1, f32[72,256]{1,0:T(8,128)S(1)} %collective-permute-done.13.far_ref.far1, f32[200,256]{1,0:T(8,128)S(1)} %collective-permute-done.11.near_ref.near2, ...), custom_call_target="tpu_custom_call" | custom-call | flops 1207959552 | bytes 1310720 | tf_op jit(solution)/shard_map/pallas_call | solution.py:190
  47.8 1.5 %collective-permute-done.15.near_ref = f32[72,256]{1,0:T(8,128)S(1)} collective-permute-done((f32[72,256]{1,0:T(8,128)S(1)}, f32[72,256]{1,0:T(8,128)S(1)}, u32[]{:S(2)}, u32[]{:S(2)}) %collective-permute-start.15) | collective-permute-done | bytes 73760 | tf_op jit(solution)/shard_map/ppermute | solution.py:21
  49.3 1.3 %collective-permute-done.17.far_ref = f32[72,256]{1,0:T(8,128)S(1)} collective-permute-done((f32[72,256]{1,0:T(8,128)S(1)}, f32[72,256]{1,0:T(8,128)S(1)}, u32[]{:S(2)}, u32[]{:S(2)}) %collective-permute-start.17) | collective-permute-done | bytes 73760 | tf_op jit(solution)/shard_map/ppermute | solution.py:21
  50.5 2.4 %shard_map.68.half_ref = f32[3,256,256]{2,1,0:T(8,128)S(1)} custom-call(f32[3,256,256]{2,1,0:T(8,128)S(1)} %shard_map.67.own_ref.old_ref, f32[72,256]{1,0:T(8,128)S(1)} %collective-permute-done.15.near_ref, f32[72,256]{1,0:T(8,128)S(1)} %collective-permute-done.17.far_ref), custom_call_target="tpu_custom_call" | custom-call | flops 905969664 | bytes 786432 | tf_op jit(solution)/shard_map/pallas_call | solution.py:190
  53.0 4.8 %collective-permute-done.16.near_ref = f32[200,256]{1,0:T(8,128)S(1)} collective-permute-done((f32[200,256]{1,0:T(8,128)S(1)}, f32[200,256]{1,0:T(8,128)S(1)}, u32[]{:S(2)}, u32[]{:S(2)}) %collective-permute-start.16) | collective-permute-done | bytes 204832 | tf_op jit(solution)/shard_map/ppermute | solution.py:21
  57.7 1.5 %collective-permute-done.18.far_ref = f32[200,256]{1,0:T(8,128)S(1)} collective-permute-done((f32[200,256]{1,0:T(8,128)S(1)}, f32[200,256]{1,0:T(8,128)S(1)}, u32[]{:S(2)}, u32[]{:S(2)}) %collective-permute-start.18) | collective-permute-done | bytes 204832 | tf_op jit(solution)/shard_map/ppermute | solution.py:21
  59.2 1.7 %shard_map.69 = (f32[1,256,256]{2,1,0:T(8,128)}, f32[1,256,256]{2,1,0:T(8,128)}, f32[1,256,256]{2,1,0:T(8,128)}) custom-call(f32[3,256,256]{2,1,0:T(8,128)S(1)} %shard_map.67.own_ref.old_ref, f32[3,256,256]{2,1,0:T(8,128)S(1)} %shard_map.68.half_ref, f32[200,256]{1,0:T(8,128)S(1)} %collective-permute-done.16.near_ref, ...), custom_call_target="tpu_custom_call" | custom-call | flops 301989888 | bytes 1048576 | tf_op jit(solution)/shard_map/pallas_call | solution.py:190
  (19 shorter events, 1.2 us)
Async XLA Ops:
  0.6 2.2 %collective-permute-start = (f32[1,256,256]{2,1,0:T(8,128)}, f32[1,256,256]{2,1,0:T(8,128)S(1)}, u32[]{:S(2)}, u32[]{:S(2)}) collective-permute-start(f32[1,256,256]{2,1,0:T(8,128)} %param.3), channel_id=1, source_target_pairs={{0,1},{1,0},{2,3},{3,2},{4,5},{5,4},{6,7},{7,6},{8,9},{9,8},{10,11... | collective-permute-start | bytes 786440 | tf_op jit(solution)/shard_map/ppermute | solution.py:21
  1.1 1.7 %collective-permute-start.1 = (f32[1,256,256]{2,1,0:T(8,128)}, f32[1,256,256]{2,1,0:T(8,128)S(1)}, u32[]{:S(2)}, u32[]{:S(2)}) collective-permute-start(f32[1,256,256]{2,1,0:T(8,128)} %param.4), channel_id=1, source_target_pairs={{0,1},{1,0},{2,3},{3,2},{4,5},{5,4},{6,7},{7,6},{8,9},{9,8},{10,11... | collective-permute-start | bytes 786440 | tf_op jit(solution)/shard_map/ppermute | solution.py:21
  1.2 2.0 %collective-permute-start.2 = (f32[1,256,256]{2,1,0:T(8,128)}, f32[1,256,256]{2,1,0:T(8,128)S(1)}, u32[]{:S(2)}, u32[]{:S(2)}) collective-permute-start(f32[1,256,256]{2,1,0:T(8,128)} %param.5), channel_id=1, source_target_pairs={{0,1},{1,0},{2,3},{3,2},{4,5},{5,4},{6,7},{7,6},{8,9},{9,8},{10,11... | collective-permute-start | bytes 786440 | tf_op jit(solution)/shard_map/ppermute | solution.py:21
  6.2 5.6 %collective-permute-start.4 = (f32[72,256]{1,0:T(8,128)S(1)}, f32[72,256]{1,0:T(8,128)S(1)}, u32[]{:S(2)}, u32[]{:S(2)}) collective-permute-start(f32[72,256]{1,0:T(8,128)S(1)} %get-tuple-element.31), channel_id=1, source_target_pairs={{0,2},{1,3},{2,0},{3,1},{4,6},{5,7},{6,4},{7,5},{8,10},{9,11},{10,... | collective-permute-start | bytes 221192 | tf_op jit(solution)/shard_map/ppermute | solution.py:21
  9.2 7.0 %collective-permute-start.3 = (f32[200,256]{1,0:T(8,128)S(1)}, f32[200,256]{1,0:T(8,128)S(1)}, u32[]{:S(2)}, u32[]{:S(2)}) collective-permute-start(f32[200,256]{1,0:T(8,128)S(1)} %get-tuple-element.29), channel_id=1, source_target_pairs={{0,2},{1,3},{2,0},{3,1},{4,6},{5,7},{6,4},{7,5},{8,10},{9,11},{10,... | collective-permute-start | bytes 614408 | tf_op jit(solution)/shard_map/ppermute | solution.py:21
  11.9 1.3 %collective-permute-start.5 = (f32[72,256]{1,0:T(8,128)S(1)}, f32[72,256]{1,0:T(8,128)S(1)}, u32[]{:S(2)}, u32[]{:S(2)}) collective-permute-start(f32[72,256]{1,0:T(8,128)S(1)} %collective-permute-done.4.near_ref.near1), channel_id=1, source_target_pairs={{0,1},{1,0},{2,3},{3,2},{4,5},{5,4},{6,7},{7,6},{8,9},{9,8},{10,11... | collective-permute-start | bytes 221192 | tf_op jit(solution)/shard_map/ppermute | solution.py:21
  16.1 1.5 %collective-permute-start.6 = (f32[200,256]{1,0:T(8,128)S(1)}, f32[200,256]{1,0:T(8,128)S(1)}, u32[]{:S(2)}, u32[]{:S(2)}) collective-permute-start(f32[200,256]{1,0:T(8,128)S(1)} %collective-permute-done.3.near_ref.near2), channel_id=1, source_target_pairs={{0,1},{1,0},{2,3},{3,2},{4,5},{5,4},{6,7},{7,6},{8,9},{9,8},{10,11... | collective-permute-start | bytes 614408 | tf_op jit(solution)/shard_map/ppermute | solution.py:21
  18.4 5.1 %collective-permute-start.8 = (f32[72,256]{1,0:T(8,128)S(1)}, f32[72,256]{1,0:T(8,128)S(1)}, u32[]{:S(2)}, u32[]{:S(2)}) collective-permute-start(f32[72,256]{1,0:T(8,128)S(1)} %get-tuple-element.36), channel_id=1, source_target_pairs={{0,4},{1,5},{2,6},{3,7},{4,0},{5,1},{6,2},{7,3},{8,12},{9,13},{10,... | collective-permute-start | bytes 221192 | tf_op jit(solution)/shard_map/ppermute | solution.py:21
  20.3 7.0 %collective-permute-start.7 = (f32[200,256]{1,0:T(8,128)S(1)}, f32[200,256]{1,0:T(8,128)S(1)}, u32[]{:S(2)}, u32[]{:S(2)}) collective-permute-start(f32[200,256]{1,0:T(8,128)S(1)} %get-tuple-element.34), channel_id=1, source_target_pairs={{0,4},{1,5},{2,6},{3,7},{4,0},{5,1},{6,2},{7,3},{8,12},{9,13},{10,... | collective-permute-start | bytes 614408 | tf_op jit(solution)/shard_map/ppermute | solution.py:21
  23.5 1.3 %collective-permute-start.9 = (f32[72,256]{1,0:T(8,128)S(1)}, f32[72,256]{1,0:T(8,128)S(1)}, u32[]{:S(2)}, u32[]{:S(2)}) collective-permute-start(f32[72,256]{1,0:T(8,128)S(1)} %collective-permute-done.8.near_ref.near1), channel_id=1, source_target_pairs={{0,1},{1,0},{2,3},{3,2},{4,5},{5,4},{6,7},{7,6},{8,9},{9,8},{10,11... | collective-permute-start | bytes 221192 | tf_op jit(solution)/shard_map/ppermute | solution.py:21
  27.3 1.5 %collective-permute-start.10 = (f32[200,256]{1,0:T(8,128)S(1)}, f32[200,256]{1,0:T(8,128)S(1)}, u32[]{:S(2)}, u32[]{:S(2)}) collective-permute-start(f32[200,256]{1,0:T(8,128)S(1)} %collective-permute-done.7.near_ref.near2), channel_id=1, source_target_pairs={{0,1},{1,0},{2,3},{3,2},{4,5},{5,4},{6,7},{7,6},{8,9},{9,8},{10,11... | collective-permute-start | bytes 614408 | tf_op jit(solution)/shard_map/ppermute | solution.py:21
  29.6 5.1 %collective-permute-start.12 = (f32[72,256]{1,0:T(8,128)S(1)}, f32[72,256]{1,0:T(8,128)S(1)}, u32[]{:S(2)}, u32[]{:S(2)}) collective-permute-start(f32[72,256]{1,0:T(8,128)S(1)} %get-tuple-element.43), channel_id=1, source_target_pairs={{0,8},{1,9},{2,10},{3,11},{4,12},{5,13},{6,14},{7,15},{8,0},{9,1},... | collective-permute-start | bytes 221192 | tf_op jit(solution)/shard_map/ppermute | solution.py:21
  31.6 7.0 %collective-permute-start.11 = (f32[200,256]{1,0:T(8,128)S(1)}, f32[200,256]{1,0:T(8,128)S(1)}, u32[]{:S(2)}, u32[]{:S(2)}) collective-permute-start(f32[200,256]{1,0:T(8,128)S(1)} %get-tuple-element.41), channel_id=1, source_target_pairs={{0,8},{1,9},{2,10},{3,11},{4,12},{5,13},{6,14},{7,15},{8,0},{9,1},... | collective-permute-start | bytes 614408 | tf_op jit(solution)/shard_map/ppermute | solution.py:21
  34.7 1.3 %collective-permute-start.13 = (f32[72,256]{1,0:T(8,128)S(1)}, f32[72,256]{1,0:T(8,128)S(1)}, u32[]{:S(2)}, u32[]{:S(2)}) collective-permute-start(f32[72,256]{1,0:T(8,128)S(1)} %collective-permute-done.12.near_ref.near1), channel_id=1, source_target_pairs={{0,1},{1,0},{2,3},{3,2},{4,5},{5,4},{6,7},{7,6},{8,9},{9,8},{10,11... | collective-permute-start | bytes 221192 | tf_op jit(solution)/shard_map/ppermute | solution.py:21
  38.5 1.5 %collective-permute-start.14 = (f32[200,256]{1,0:T(8,128)S(1)}, f32[200,256]{1,0:T(8,128)S(1)}, u32[]{:S(2)}, u32[]{:S(2)}) collective-permute-start(f32[200,256]{1,0:T(8,128)S(1)} %collective-permute-done.11.near_ref.near2), channel_id=1, source_target_pairs={{0,1},{1,0},{2,3},{3,2},{4,5},{5,4},{6,7},{7,6},{8,9},{9,8},{10,11... | collective-permute-start | bytes 614408 | tf_op jit(solution)/shard_map/ppermute | solution.py:21
  41.9 7.4 %collective-permute-start.15 = (f32[72,256]{1,0:T(8,128)S(1)}, f32[72,256]{1,0:T(8,128)S(1)}, u32[]{:S(2)}, u32[]{:S(2)}) collective-permute-start(f32[72,256]{1,0:T(8,128)S(1)} %get-tuple-element.48), channel_id=1, source_target_pairs={{0,16},{1,17},{2,18},{3,19},{4,20},{5,21},{6,22},{7,23},{8,24},{9,... | collective-permute-start | bytes 221192 | tf_op jit(solution)/shard_map/ppermute | solution.py:21
  44.8 12.9 %collective-permute-start.16 = (f32[200,256]{1,0:T(8,128)S(1)}, f32[200,256]{1,0:T(8,128)S(1)}, u32[]{:S(2)}, u32[]{:S(2)}) collective-permute-start(f32[200,256]{1,0:T(8,128)S(1)} %get-tuple-element.51), channel_id=1, source_target_pairs={{0,16},{1,17},{2,18},{3,19},{4,20},{5,21},{6,22},{7,23},{8,24},{9,... | collective-permute-start | bytes 614408 | tf_op jit(solution)/shard_map/ppermute | solution.py:21
  49.3 1.3 %collective-permute-start.17 = (f32[72,256]{1,0:T(8,128)S(1)}, f32[72,256]{1,0:T(8,128)S(1)}, u32[]{:S(2)}, u32[]{:S(2)}) collective-permute-start(f32[72,256]{1,0:T(8,128)S(1)} %collective-permute-done.15.near_ref), channel_id=1, source_target_pairs={{0,1},{1,0},{2,3},{3,2},{4,5},{5,4},{6,7},{7,6},{8,9},{9,8},{10,11... | collective-permute-start | bytes 221192 | tf_op jit(solution)/shard_map/ppermute | solution.py:21
  57.7 1.5 %collective-permute-start.18 = (f32[200,256]{1,0:T(8,128)S(1)}, f32[200,256]{1,0:T(8,128)S(1)}, u32[]{:S(2)}, u32[]{:S(2)}) collective-permute-start(f32[200,256]{1,0:T(8,128)S(1)} %collective-permute-done.16.near_ref), channel_id=1, source_target_pairs={{0,1},{1,0},{2,3},{3,2},{4,5},{5,4},{6,7},{7,6},{8,9},{9,8},{10,11... | collective-permute-start | bytes 614408 | tf_op jit(solution)/shard_map/ppermute | solution.py:21
where the time goes:
time: 61 us; the launch traced here: 60.9 us
  Pallas kernels  26.8 us (44%)
  waiting for transfers between devices  20.4 us (33%)
  starting transfers between devices  11.7 us (19%)
  other arithmetic  1.16 us (2%)
  between operations  0.77 us (1%)
    pallas_call x12, Pallas kernels, call(): pl.pallas_call(kernel, out_shape=[jax.ShapeDtypeStruct(s, F32) for s in o...  26.8 us
    ppermute x19, waiting for transfers between devices, swap(): return lax.ppermute(block, AXES, [(i, i ^ distance) for i in range(count)])  20.4 us
    ppermute x19, starting transfers between devices, swap(): return lax.ppermute(block, AXES, [(i, i ^ distance) for i in range(count)])  11.7 us
  transfers between devices with their start and end apart: 19, of which 15 were waited for; matrix products, arithmetic and copies ran while one was open for 2% of the time, Pallas kernels for 31%

commit v1 on v0

--- a/solution.py
+++ b/solution.py
@@ -27,7 +27,9 @@
 
 
 def dot1(a, b, dims=NN):
-    return lax.dot_general(a, b, dims, preferred_element_type=F32)
+    h = a.shape[0] // 2
+    parts = [lax.dot_general(x, b, dims, preferred_element_type=F32) for x in (a[:h], a[h:])]
+    return jnp.concatenate(parts, 0)
 
 
 def dot3(a, b, dims=NN):
@@ -38,27 +40,28 @@
     return x.astype(BF16)
 
 
-def inverse_less_eye(coupling):
-    rest, power = coupling, half(coupling)
+def four_steps(power):
+    rest, power = power, half(power)
     for _ in range(NS_STEPS - 1):
         squared = dot1(power, power)
         power = half(squared)
         rest = rest + squared + dot1(half(rest), power)
-    rest = half(rest)
-    high, low = split(coupling)
-    rest32 = rest.astype(F32)
-    residual = (coupling - rest32) + (dot1(high, rest) + dot1(low, rest))
-    return rest32 + residual + dot1(rest, half(residual))
+    return half(rest)
 
 
 def before_trans(own, facing):
     near, away, out = own
     f, o, s = split(facing), split(near), split(out)
-    coupling = dot3(f, o)
+    rough = dot1(f[0], o[0])
+    rest = four_steps(rough)
+    coupling = rough + (dot1(f[0], o[1]) + dot1(f[1], o[0]))
     inner = split(dot3(f, s, NT))
-    rest = split(inverse_less_eye(coupling))
-    leading = out + dot3(s, rest)
-    mirror = near + dot3(o, rest)
+    high, low = split(coupling)
+    error = half((coupling - rest.astype(F32)) + (dot1(high, rest) + dot1(low, rest)))
+    leading = out + (dot1(s[0], rest) + dot1(s[1], rest))
+    mirror = near + (dot1(o[0], rest) + dot1(o[1], rest))
+    leading = leading + dot1(half(leading), error)
+    mirror = mirror + dot1(half(mirror), error)
     return leading, mirror, away + dot3(split(leading), inner)
 
 

time: 61 us -> 59.6 us (0.977)
  Pallas kernels: 26.8 us -> 23.2 us
  waiting for transfers between devices: 20.4 us -> 23 us
    pallas_call x12, Pallas kernels: 26.8 us -> 23.2 us  [call(): pl.pallas_call(kernel, out_shape=[jax.ShapeDtypeStruct(s, F32) for s in o...]
    ppermute x19, waiting for transfers between devices: 20.4 us -> 23 us  [swap(): return lax.ppermute(block, AXES, [(i, i ^ distance) for i in range(count)])]
  transfers between devices with their start and end apart: 19 -> 19, of which waited for: 15 -> 16; matrix products, arithmetic and copies ran while one was open for 2% -> 2% of each run, Pallas kernels for 31% -> 27%
where the time goes in v1:
time: 59.6 us; the launch traced here: 59.5 us
  Pallas kernels  23.2 us (39%)
  waiting for transfers between devices  23 us (39%)
  starting transfers between devices  11.3 us (19%)
  other arithmetic  1.16 us (2%)
  between operations  0.77 us (1%)
    pallas_call x12, Pallas kernels, call(): pl.pallas_call(kernel, out_shape=[jax.ShapeDtypeStruct(s, F32) for s in o...  23.2 us
    ppermute x19, waiting for transfers between devices, swap(): return lax.ppermute(block, AXES, [(i, i ^ distance) for i in range(count)])  23 us
    ppermute x19, starting transfers between devices, swap(): return lax.ppermute(block, AXES, [(i, i ^ distance) for i in range(count)])  11.3 us
  transfers between devices with their start and end apart: 19, of which 16 were waited for; matrix products, arithmetic and copies ran while one was open for 2% of the time, Pallas kernels for 27%

profile of v1, /device:TPU:0, one launch (start us, length us, event | category | flops | bytes accessed | tf_op | source)
XLA Modules:
  0.0 59.5 jit_solution(17375791876356906700)
XLA Ops:
  0.6 0.5 collective-permute-start
  1.7 1.2 %pad_maximum_fusion.section_ref = f32[3,256,256]{2,1,0:T(8,128)S(1)} fusion(f32[1,256,256]{2,1,0:T(8,128)} %param.5, f32[1,256,256]{2,1,0:T(8,128)} %param.4, f32[1,256,256]{2,1,0:T(8,128)} %param.3), kind=kLoop, calls=%fused_computation | loop fusion | flops 393216 | bytes 1572864 | tf_op jit(solution)/shard_map/concatenate | solution.py:210
  3.3 2.6 %shard_map.58 = (f32[3,256,256]{2,1,0:T(8,128)S(1)}, f32[3,256,256]{2,1,0:T(8,128)S(1)}, f32[72,256]{1,0:T(8,128)S(1)}, f32[200,256]{1,0:T(8,128)S(1)}) custom-call(f32[3,256,256]{2,1,0:T(8,128)S(1)} %pad_maximum_fusion.section_ref, f32[1,256,256]{2,1,0:T(8,128)S(1)} %collective-permute-done.got1, f32[1,256,256]{2,1,0:T(8,128)S(1)} %collective-permute-done.1.got2, ...), custom_call_target="tpu_custom_call" | custom-call | flops 1207959552 | bytes 1048576 | tf_op jit(solution)/shard_map/pallas_call | solution.py:193
  5.9 2.9 %collective-permute-start.4 = (f32[72,256]{1,0:T(8,128)S(1)}, f32[72,256]{1,0:T(8,128)S(1)}, u32[]{:S(2)}, u32[]{:S(2)}) collective-permute-start(f32[72,256]{1,0:T(8,128)S(1)} %get-tuple-element.31), channel_id=1, source_target_pairs={{0,2},{1,3},{2,0},{3,1},{4,6},{5,7},{6,4},{7,5},{8,10},{9,11},{10,... | collective-permute-start | bytes 221192 | tf_op jit(solution)/shard_map/ppermute | solution.py:21
  8.9 2.6 %collective-permute-done.4.near_ref.near1 = f32[72,256]{1,0:T(8,128)S(1)} collective-permute-done((f32[72,256]{1,0:T(8,128)S(1)}, f32[72,256]{1,0:T(8,128)S(1)}, u32[]{:S(2)}, u32[]{:S(2)}) %collective-permute-start.4) | collective-permute-done | bytes 73760 | tf_op jit(solution)/shard_map/ppermute | solution.py:21
  11.5 1.3 %collective-permute-done.5.far_ref.far1 = f32[72,256]{1,0:T(8,128)S(1)} collective-permute-done((f32[72,256]{1,0:T(8,128)S(1)}, f32[72,256]{1,0:T(8,128)S(1)}, u32[]{:S(2)}, u32[]{:S(2)}) %collective-permute-start.5) | collective-permute-done | bytes 73760 | tf_op jit(solution)/shard_map/ppermute | solution.py:21
  12.8 2.1 %shard_map.59.half_ref = f32[3,256,256]{2,1,0:T(8,128)S(1)} custom-call(f32[3,256,256]{2,1,0:T(8,128)S(1)} %get-tuple-element.30.own_ref, f32[72,256]{1,0:T(8,128)S(1)} %collective-permute-done.4.near_ref.near1, f32[72,256]{1,0:T(8,128)S(1)} %collective-permute-done.5.far_ref.far1), custom_call_target="tpu_custom_call" | custom-call | flops 905969664 | bytes 786432 | tf_op jit(solution)/shard_map/pallas_call | solution.py:193
  14.9 0.9 %collective-permute-done.3.near_ref.near2 = f32[200,256]{1,0:T(8,128)S(1)} collective-permute-done((f32[200,256]{1,0:T(8,128)S(1)}, f32[200,256]{1,0:T(8,128)S(1)}, u32[]{:S(2)}, u32[]{:S(2)}) %collective-permute-start.3) | collective-permute-done | bytes 204832 | tf_op jit(solution)/shard_map/ppermute | solution.py:21
  15.8 1.5 %collective-permute-done.6.far_ref.far2 = f32[200,256]{1,0:T(8,128)S(1)} collective-permute-done((f32[200,256]{1,0:T(8,128)S(1)}, f32[200,256]{1,0:T(8,128)S(1)}, u32[]{:S(2)}, u32[]{:S(2)}) %collective-permute-start.6) | collective-permute-done | bytes 204832 | tf_op jit(solution)/shard_map/ppermute | solution.py:21
  17.2 0.7 %shard_map.60 = (f32[3,256,256]{2,1,0:T(8,128)S(1)}, f32[72,256]{1,0:T(8,128)S(1)}, f32[200,256]{1,0:T(8,128)S(1)}) custom-call(f32[3,256,256]{2,1,0:T(8,128)S(1)} %shard_map.59.half_ref, f32[200,256]{1,0:T(8,128)S(1)} %collective-permute-done.3.near_ref.near2, f32[200,256]{1,0:T(8,128)S(1)} %collective-permute-done.6.far_ref.far2), custom_call_target="tpu_custom_call" | custom-call | flops 301989888 | bytes 786432 | tf_op jit(solution)/shard_map/pallas_call | solution.py:193
  17.9 1.9 %collective-permute-start.8 = (f32[72,256]{1,0:T(8,128)S(1)}, f32[72,256]{1,0:T(8,128)S(1)}, u32[]{:S(2)}, u32[]{:S(2)}) collective-permute-start(f32[72,256]{1,0:T(8,128)S(1)} %get-tuple-element.36), channel_id=1, source_target_pairs={{0,4},{1,5},{2,6},{3,7},{4,0},{5,1},{6,2},{7,3},{8,12},{9,13},{10,... | collective-permute-start | bytes 221192 | tf_op jit(solution)/shard_map/ppermute | solution.py:21
  20.0 2.6 %shard_map.61.old_ref = f32[3,256,256]{2,1,0:T(8,128)S(1)} custom-call(f32[3,256,256]{2,1,0:T(8,128)S(1)} %get-tuple-element.37.old_ref, f32[72,256]{1,0:T(8,128)S(1)} %collective-permute-done.4.near_ref.near1, f32[72,256]{1,0:T(8,128)S(1)} %collective-permute-done.5.far_ref.far1, f32[200,256]{1,0:T(8,128)S(1)} %collective-permute-done.3.near_ref.near2, ...), custom_call_target="tpu_custom_call" | custom-call | flops 1207959552 | bytes 1310720 | tf_op jit(solution)/shard_map/pallas_call | solution.py:193
  22.7 1.3 %collective-permute-done.9.far_ref.far1 = f32[72,256]{1,0:T(8,128)S(1)} collective-permute-done((f32[72,256]{1,0:T(8,128)S(1)}, f32[72,256]{1,0:T(8,128)S(1)}, u32[]{:S(2)}, u32[]{:S(2)}) %collective-permute-start.9) | collective-permute-done | bytes 73760 | tf_op jit(solution)/shard_map/ppermute | solution.py:21
  24.0 2.1 %shard_map.62.half_ref = f32[3,256,256]{2,1,0:T(8,128)S(1)} custom-call(f32[3,256,256]{2,1,0:T(8,128)S(1)} %get-tuple-element.35.own_ref, f32[72,256]{1,0:T(8,128)S(1)} %collective-permute-done.8.near_ref.near1, f32[72,256]{1,0:T(8,128)S(1)} %collective-permute-done.9.far_ref.far1), custom_call_target="tpu_custom_call" | custom-call | flops 905969664 | bytes 786432 | tf_op jit(solution)/shard_map/pallas_call | solution.py:193
  26.0 0.7 %collective-permute-done.7.near_ref.near2 = f32[200,256]{1,0:T(8,128)S(1)} collective-permute-done((f32[200,256]{1,0:T(8,128)S(1)}, f32[200,256]{1,0:T(8,128)S(1)}, u32[]{:S(2)}, u32[]{:S(2)}) %collective-permute-start.7) | collective-permute-done | bytes 204832 | tf_op jit(solution)/shard_map/ppermute | solution.py:21
  26.8 1.5 %collective-permute-done.10.far_ref.far2 = f32[200,256]{1,0:T(8,128)S(1)} collective-permute-done((f32[200,256]{1,0:T(8,128)S(1)}, f32[200,256]{1,0:T(8,128)S(1)}, u32[]{:S(2)}, u32[]{:S(2)}) %collective-permute-start.10) | collective-permute-done | bytes 204832 | tf_op jit(solution)/shard_map/ppermute | solution.py:21
  28.2 0.7 %shard_map.63 = (f32[3,256,256]{2,1,0:T(8,128)S(1)}, f32[72,256]{1,0:T(8,128)S(1)}, f32[200,256]{1,0:T(8,128)S(1)}) custom-call(f32[3,256,256]{2,1,0:T(8,128)S(1)} %shard_map.62.half_ref, f32[200,256]{1,0:T(8,128)S(1)} %collective-permute-done.7.near_ref.near2, f32[200,256]{1,0:T(8,128)S(1)} %collective-permute-done.10.far_ref.far2), custom_call_target="tpu_custom_call" | custom-call | flops 301989888 | bytes 786432 | tf_op jit(solution)/shard_map/pallas_call | solution.py:193
  28.9 1.9 %collective-permute-start.12 = (f32[72,256]{1,0:T(8,128)S(1)}, f32[72,256]{1,0:T(8,128)S(1)}, u32[]{:S(2)}, u32[]{:S(2)}) collective-permute-start(f32[72,256]{1,0:T(8,128)S(1)} %get-tuple-element.43), channel_id=1, source_target_pairs={{0,8},{1,9},{2,10},{3,11},{4,12},{5,13},{6,14},{7,15},{8,0},{9,1},... | collective-permute-start | bytes 221192 | tf_op jit(solution)/shard_map/ppermute | solution.py:21
  31.0 2.6 %shard_map.64.old_ref = f32[3,256,256]{2,1,0:T(8,128)S(1)} custom-call(f32[3,256,256]{2,1,0:T(8,128)S(1)} %shard_map.61.old_ref, f32[72,256]{1,0:T(8,128)S(1)} %collective-permute-done.8.near_ref.near1, f32[72,256]{1,0:T(8,128)S(1)} %collective-permute-done.9.far_ref.far1, f32[200,256]{1,0:T(8,128)S(1)} %collective-permute-done.7.near_ref.near2, ...), custom_call_target="tpu_custom_call" | custom-call | flops 1207959552 | bytes 1310720 | tf_op jit(solution)/shard_map/pallas_call | solution.py:193
  33.7 1.3 %collective-permute-done.13.far_ref.far1 = f32[72,256]{1,0:T(8,128)S(1)} collective-permute-done((f32[72,256]{1,0:T(8,128)S(1)}, f32[72,256]{1,0:T(8,128)S(1)}, u32[]{:S(2)}, u32[]{:S(2)}) %collective-permute-start.13) | collective-permute-done | bytes 73760 | tf_op jit(solution)/shard_map/ppermute | solution.py:21
  34.9 2.1 %shard_map.65.half_ref = f32[3,256,256]{2,1,0:T(8,128)S(1)} custom-call(f32[3,256,256]{2,1,0:T(8,128)S(1)} %get-tuple-element.42.own_ref, f32[72,256]{1,0:T(8,128)S(1)} %collective-permute-done.12.near_ref.near1, f32[72,256]{1,0:T(8,128)S(1)} %collective-permute-done.13.far_ref.far1), custom_call_target="tpu_custom_call" | custom-call | flops 905969664 | bytes 786432 | tf_op jit(solution)/shard_map/pallas_call | solution.py:193
  37.0 0.8 %collective-permute-done.11.near_ref.near2 = f32[200,256]{1,0:T(8,128)S(1)} collective-permute-done((f32[200,256]{1,0:T(8,128)S(1)}, f32[200,256]{1,0:T(8,128)S(1)}, u32[]{:S(2)}, u32[]{:S(2)}) %collective-permute-start.11) | collective-permute-done | bytes 204832 | tf_op jit(solution)/shard_map/ppermute | solution.py:21
  37.8 1.5 %collective-permute-done.14.far_ref.far2 = f32[200,256]{1,0:T(8,128)S(1)} collective-permute-done((f32[200,256]{1,0:T(8,128)S(1)}, f32[200,256]{1,0:T(8,128)S(1)}, u32[]{:S(2)}, u32[]{:S(2)}) %collective-permute-start.14) | collective-permute-done | bytes 204832 | tf_op jit(solution)/shard_map/ppermute | solution.py:21
  39.3 1.6 %shard_map.66 = (f32[3,256,256]{2,1,0:T(8,128)}, f32[72,256]{1,0:T(8,128)S(1)}, f32[200,256]{1,0:T(8,128)S(1)}) custom-call(f32[3,256,256]{2,1,0:T(8,128)S(1)} %shard_map.65.half_ref, f32[200,256]{1,0:T(8,128)S(1)} %collective-permute-done.11.near_ref.near2, f32[200,256]{1,0:T(8,128)S(1)} %collective-permute-done.14.far_ref.far2), custom_call_target="tpu_custom_call" | custom-call | flops 301989888 | bytes 786432 | tf_op jit(solution)/shard_map/pallas_call | solution.py:193
  40.8 2.8 %collective-permute-start.15 = (f32[72,256]{1,0:T(8,128)S(1)}, f32[72,256]{1,0:T(8,128)S(1)}, u32[]{:S(2)}, u32[]{:S(2)}) collective-permute-start(f32[72,256]{1,0:T(8,128)S(1)} %get-tuple-element.48), channel_id=1, source_target_pairs={{0,16},{1,17},{2,18},{3,19},{4,20},{5,21},{6,22},{7,23},{8,24},{9,... | collective-permute-start | bytes 221192 | tf_op jit(solution)/shard_map/ppermute | solution.py:21
  43.8 2.7 %shard_map.67.own_ref.old_ref = f32[3,256,256]{2,1,0:T(8,128)S(1)} custom-call(f32[3,256,256]{2,1,0:T(8,128)S(1)} %shard_map.64.old_ref, f32[72,256]{1,0:T(8,128)S(1)} %collective-permute-done.12.near_ref.near1, f32[72,256]{1,0:T(8,128)S(1)} %collective-permute-done.13.far_ref.far1, f32[200,256]{1,0:T(8,128)S(1)} %collective-permute-done.11.near_ref.near2, ...), custom_call_target="tpu_custom_call" | custom-call | flops 1207959552 | bytes 1310720 | tf_op jit(solution)/shard_map/pallas_call | solution.py:193
  46.5 6.1 %collective-permute-done.15.near_ref = f32[72,256]{1,0:T(8,128)S(1)} collective-permute-done((f32[72,256]{1,0:T(8,128)S(1)}, f32[72,256]{1,0:T(8,128)S(1)}, u32[]{:S(2)}, u32[]{:S(2)}) %collective-permute-start.15) | collective-permute-done | bytes 73760 | tf_op jit(solution)/shard_map/ppermute | solution.py:21
  52.6 1.3 %collective-permute-done.17.far_ref = f32[72,256]{1,0:T(8,128)S(1)} collective-permute-done((f32[72,256]{1,0:T(8,128)S(1)}, f32[72,256]{1,0:T(8,128)S(1)}, u32[]{:S(2)}, u32[]{:S(2)}) %collective-permute-start.17) | collective-permute-done | bytes 73760 | tf_op jit(solution)/shard_map/ppermute | solution.py:21
  53.9 2.1 %shard_map.68.half_ref = f32[3,256,256]{2,1,0:T(8,128)S(1)} custom-call(f32[3,256,256]{2,1,0:T(8,128)S(1)} %shard_map.67.own_ref.old_ref, f32[72,256]{1,0:T(8,128)S(1)} %collective-permute-done.15.near_ref, f32[72,256]{1,0:T(8,128)S(1)} %collective-permute-done.17.far_ref), custom_call_target="tpu_custom_call" | custom-call | flops 905969664 | bytes 786432 | tf_op jit(solution)/shard_map/pallas_call | solution.py:193
  56.0 0.6 collective-permute-done.16.near_ref
  56.6 1.5 %collective-permute-done.18.far_ref = f32[200,256]{1,0:T(8,128)S(1)} collective-permute-done((f32[200,256]{1,0:T(8,128)S(1)}, f32[200,256]{1,0:T(8,128)S(1)}, u32[]{:S(2)}, u32[]{:S(2)}) %collective-permute-start.18) | collective-permute-done | bytes 204832 | tf_op jit(solution)/shard_map/ppermute | solution.py:21
  58.0 1.4 %shard_map.69 = (f32[1,256,256]{2,1,0:T(8,128)}, f32[1,256,256]{2,1,0:T(8,128)}, f32[1,256,256]{2,1,0:T(8,128)}) custom-call(f32[3,256,256]{2,1,0:T(8,128)S(1)} %shard_map.67.own_ref.old_ref, f32[3,256,256]{2,1,0:T(8,128)S(1)} %shard_map.68.half_ref, f32[200,256]{1,0:T(8,128)S(1)} %collective-permute-done.16.near_ref, ...), custom_call_target="tpu_custom_call" | custom-call | flops 301989888 | bytes 1048576 | tf_op jit(solution)/shard_map/pallas_call | solution.py:193
  (19 shorter events, 1.7 us)
Async XLA Ops:
  0.6 2.2 %collective-permute-start = (f32[1,256,256]{2,1,0:T(8,128)}, f32[1,256,256]{2,1,0:T(8,128)S(1)}, u32[]{:S(2)}, u32[]{:S(2)}) collective-permute-start(f32[1,256,256]{2,1,0:T(8,128)} %param.3), channel_id=1, source_target_pairs={{0,1},{1,0},{2,3},{3,2},{4,5},{5,4},{6,7},{7,6},{8,9},{9,8},{10,11... | collective-permute-start | bytes 786440 | tf_op jit(solution)/shard_map/ppermute | solution.py:21
  1.1 1.7 %collective-permute-start.1 = (f32[1,256,256]{2,1,0:T(8,128)}, f32[1,256,256]{2,1,0:T(8,128)S(1)}, u32[]{:S(2)}, u32[]{:S(2)}) collective-permute-start(f32[1,256,256]{2,1,0:T(8,128)} %param.4), channel_id=1, source_target_pairs={{0,1},{1,0},{2,3},{3,2},{4,5},{5,4},{6,7},{7,6},{8,9},{9,8},{10,11... | collective-permute-start | bytes 786440 | tf_op jit(solution)/shard_map/ppermute | solution.py:21
  1.2 2.0 %collective-permute-start.2 = (f32[1,256,256]{2,1,0:T(8,128)}, f32[1,256,256]{2,1,0:T(8,128)S(1)}, u32[]{:S(2)}, u32[]{:S(2)}) collective-permute-start(f32[1,256,256]{2,1,0:T(8,128)} %param.5), channel_id=1, source_target_pairs={{0,1},{1,0},{2,3},{3,2},{4,5},{5,4},{6,7},{7,6},{8,9},{9,8},{10,11... | collective-permute-start | bytes 786440 | tf_op jit(solution)/shard_map/ppermute | solution.py:21
  5.9 5.6 %collective-permute-start.4 = (f32[72,256]{1,0:T(8,128)S(1)}, f32[72,256]{1,0:T(8,128)S(1)}, u32[]{:S(2)}, u32[]{:S(2)}) collective-permute-start(f32[72,256]{1,0:T(8,128)S(1)} %get-tuple-element.31), channel_id=1, source_target_pairs={{0,2},{1,3},{2,0},{3,1},{4,6},{5,7},{6,4},{7,5},{8,10},{9,11},{10,... | collective-permute-start | bytes 221192 | tf_op jit(solution)/shard_map/ppermute | solution.py:21
  8.8 7.0 %collective-permute-start.3 = (f32[200,256]{1,0:T(8,128)S(1)}, f32[200,256]{1,0:T(8,128)S(1)}, u32[]{:S(2)}, u32[]{:S(2)}) collective-permute-start(f32[200,256]{1,0:T(8,128)S(1)} %get-tuple-element.29), channel_id=1, source_target_pairs={{0,2},{1,3},{2,0},{3,1},{4,6},{5,7},{6,4},{7,5},{8,10},{9,11},{10,... | collective-permute-start | bytes 614408 | tf_op jit(solution)/shard_map/ppermute | solution.py:21
  11.5 1.3 %collective-permute-start.5 = (f32[72,256]{1,0:T(8,128)S(1)}, f32[72,256]{1,0:T(8,128)S(1)}, u32[]{:S(2)}, u32[]{:S(2)}) collective-permute-start(f32[72,256]{1,0:T(8,128)S(1)} %collective-permute-done.4.near_ref.near1), channel_id=1, source_target_pairs={{0,1},{1,0},{2,3},{3,2},{4,5},{5,4},{6,7},{7,6},{8,9},{9,8},{10,11... | collective-permute-start | bytes 221192 | tf_op jit(solution)/shard_map/ppermute | solution.py:21
  15.8 1.5 %collective-permute-start.6 = (f32[200,256]{1,0:T(8,128)S(1)}, f32[200,256]{1,0:T(8,128)S(1)}, u32[]{:S(2)}, u32[]{:S(2)}) collective-permute-start(f32[200,256]{1,0:T(8,128)S(1)} %collective-permute-done.3.near_ref.near2), channel_id=1, source_target_pairs={{0,1},{1,0},{2,3},{3,2},{4,5},{5,4},{6,7},{7,6},{8,9},{9,8},{10,11... | collective-permute-start | bytes 614408 | tf_op jit(solution)/shard_map/ppermute | solution.py:21
  17.9 4.7 %collective-permute-start.8 = (f32[72,256]{1,0:T(8,128)S(1)}, f32[72,256]{1,0:T(8,128)S(1)}, u32[]{:S(2)}, u32[]{:S(2)}) collective-permute-start(f32[72,256]{1,0:T(8,128)S(1)} %get-tuple-element.36), channel_id=1, source_target_pairs={{0,4},{1,5},{2,6},{3,7},{4,0},{5,1},{6,2},{7,3},{8,12},{9,13},{10,... | collective-permute-start | bytes 221192 | tf_op jit(solution)/shard_map/ppermute | solution.py:21
  19.8 7.0 %collective-permute-start.7 = (f32[200,256]{1,0:T(8,128)S(1)}, f32[200,256]{1,0:T(8,128)S(1)}, u32[]{:S(2)}, u32[]{:S(2)}) collective-permute-start(f32[200,256]{1,0:T(8,128)S(1)} %get-tuple-element.34), channel_id=1, source_target_pairs={{0,4},{1,5},{2,6},{3,7},{4,0},{5,1},{6,2},{7,3},{8,12},{9,13},{10,... | collective-permute-start | bytes 614408 | tf_op jit(solution)/shard_map/ppermute | solution.py:21
  22.6 1.3 %collective-permute-start.9 = (f32[72,256]{1,0:T(8,128)S(1)}, f32[72,256]{1,0:T(8,128)S(1)}, u32[]{:S(2)}, u32[]{:S(2)}) collective-permute-start(f32[72,256]{1,0:T(8,128)S(1)} %collective-permute-done.8.near_ref.near1), channel_id=1, source_target_pairs={{0,1},{1,0},{2,3},{3,2},{4,5},{5,4},{6,7},{7,6},{8,9},{9,8},{10,11... | collective-permute-start | bytes 221192 | tf_op jit(solution)/shard_map/ppermute | solution.py:21
  26.8 1.5 %collective-permute-start.10 = (f32[200,256]{1,0:T(8,128)S(1)}, f32[200,256]{1,0:T(8,128)S(1)}, u32[]{:S(2)}, u32[]{:S(2)}) collective-permute-start(f32[200,256]{1,0:T(8,128)S(1)} %collective-permute-done.7.near_ref.near2), channel_id=1, source_target_pairs={{0,1},{1,0},{2,3},{3,2},{4,5},{5,4},{6,7},{7,6},{8,9},{9,8},{10,11... | collective-permute-start | bytes 614408 | tf_op jit(solution)/shard_map/ppermute | solution.py:21
  28.9 4.7 %collective-permute-start.12 = (f32[72,256]{1,0:T(8,128)S(1)}, f32[72,256]{1,0:T(8,128)S(1)}, u32[]{:S(2)}, u32[]{:S(2)}) collective-permute-start(f32[72,256]{1,0:T(8,128)S(1)} %get-tuple-element.43), channel_id=1, source_target_pairs={{0,8},{1,9},{2,10},{3,11},{4,12},{5,13},{6,14},{7,15},{8,0},{9,1},... | collective-permute-start | bytes 221192 | tf_op jit(solution)/shard_map/ppermute | solution.py:21
  30.8 7.0 %collective-permute-start.11 = (f32[200,256]{1,0:T(8,128)S(1)}, f32[200,256]{1,0:T(8,128)S(1)}, u32[]{:S(2)}, u32[]{:S(2)}) collective-permute-start(f32[200,256]{1,0:T(8,128)S(1)} %get-tuple-element.41), channel_id=1, source_target_pairs={{0,8},{1,9},{2,10},{3,11},{4,12},{5,13},{6,14},{7,15},{8,0},{9,1},... | collective-permute-start | bytes 614408 | tf_op jit(solution)/shard_map/ppermute | solution.py:21
  33.6 1.3 %collective-permute-start.13 = (f32[72,256]{1,0:T(8,128)S(1)}, f32[72,256]{1,0:T(8,128)S(1)}, u32[]{:S(2)}, u32[]{:S(2)}) collective-permute-start(f32[72,256]{1,0:T(8,128)S(1)} %collective-permute-done.12.near_ref.near1), channel_id=1, source_target_pairs={{0,1},{1,0},{2,3},{3,2},{4,5},{5,4},{6,7},{7,6},{8,9},{9,8},{10,11... | collective-permute-start | bytes 221192 | tf_op jit(solution)/shard_map/ppermute | solution.py:21
  37.8 1.5 %collective-permute-start.14 = (f32[200,256]{1,0:T(8,128)S(1)}, f32[200,256]{1,0:T(8,128)S(1)}, u32[]{:S(2)}, u32[]{:S(2)}) collective-permute-start(f32[200,256]{1,0:T(8,128)S(1)} %collective-permute-done.11.near_ref.near2), channel_id=1, source_target_pairs={{0,1},{1,0},{2,3},{3,2},{4,5},{5,4},{6,7},{7,6},{8,9},{9,8},{10,11... | collective-permute-start | bytes 614408 | tf_op jit(solution)/shard_map/ppermute | solution.py:21
  40.8 11.8 %collective-permute-start.15 = (f32[72,256]{1,0:T(8,128)S(1)}, f32[72,256]{1,0:T(8,128)S(1)}, u32[]{:S(2)}, u32[]{:S(2)}) collective-permute-start(f32[72,256]{1,0:T(8,128)S(1)} %get-tuple-element.48), channel_id=1, source_target_pairs={{0,16},{1,17},{2,18},{3,19},{4,20},{5,21},{6,22},{7,23},{8,24},{9,... | collective-permute-start | bytes 221192 | tf_op jit(solution)/shard_map/ppermute | solution.py:21
  43.6 12.9 %collective-permute-start.16 = (f32[200,256]{1,0:T(8,128)S(1)}, f32[200,256]{1,0:T(8,128)S(1)}, u32[]{:S(2)}, u32[]{:S(2)}) collective-permute-start(f32[200,256]{1,0:T(8,128)S(1)} %get-tuple-element.51), channel_id=1, source_target_pairs={{0,16},{1,17},{2,18},{3,19},{4,20},{5,21},{6,22},{7,23},{8,24},{9,... | collective-permute-start | bytes 614408 | tf_op jit(solution)/shard_map/ppermute | solution.py:21
  52.6 1.3 %collective-permute-start.17 = (f32[72,256]{1,0:T(8,128)S(1)}, f32[72,256]{1,0:T(8,128)S(1)}, u32[]{:S(2)}, u32[]{:S(2)}) collective-permute-start(f32[72,256]{1,0:T(8,128)S(1)} %collective-permute-done.15.near_ref), channel_id=1, source_target_pairs={{0,1},{1,0},{2,3},{3,2},{4,5},{5,4},{6,7},{7,6},{8,9},{9,8},{10,11... | collective-permute-start | bytes 221192 | tf_op jit(solution)/shard_map/ppermute | solution.py:21
  56.6 1.5 %collective-permute-start.18 = (f32[200,256]{1,0:T(8,128)S(1)}, f32[200,256]{1,0:T(8,128)S(1)}, u32[]{:S(2)}, u32[]{:S(2)}) collective-permute-start(f32[200,256]{1,0:T(8,128)S(1)} %collective-permute-done.16.near_ref), channel_id=1, source_target_pairs={{0,1},{1,0},{2,3},{3,2},{4,5},{5,4},{6,7},{7,6},{8,9},{9,8},{10,11... | collective-permute-start | bytes 614408 | tf_op jit(solution)/shard_map/ppermute | solution.py:21

commit v2 on v1

v2 whole, which is shorter than its diff:
```python
import functools

import jax
import jax.numpy as jnp
from jax import lax
from jax.experimental import pallas as pl
from jax.experimental.pallas import tpu as pltpu
from jax.sharding import PartitionSpec as P

AXES = ("gx", "gy")
NS_STEPS = 5
PAD = 8
F32 = jnp.float32
BF16 = jnp.bfloat16
NN = (((1,), (0,)), ((), ()))
NT = (((1,), (1,)), ((), ()))


def swap(block, distance):
    count = lax.axis_size(AXES)
    return lax.ppermute(block, AXES, [(i, i ^ distance) for i in range(count)])


def pair(block, first, second):
    count = lax.axis_size(AXES)
    quarter = count // 4
    shift = (second - first) * quarter
    step = {first: lambda i: i + shift, second: lambda i: i - shift}
    return lax.ppermute(block, AXES, [(i, step.get(i // quarter, lambda i: i ^ 1)(i)) for i in range(count)])


def shift(block, distance):
    count = lax.axis_size(AXES)
    return lax.ppermute(block, AXES, [(i, i + distance) for i in range(count - distance)])


def after(value, *done):
    return lax.optimization_barrier((value, *done))[0]


def split(x):
    high = x.astype(BF16)
    return high, (x - high.astype(F32)).astype(BF16)


def dot1(a, b, dims=NN):
    h = a.shape[0] // 2
    parts = [lax.dot_general(x, b, dims, preferred_element_type=F32) for x in (a[:h], a[h:])]
    return jnp.concatenate(parts, 0)


def dot3(a, b, dims=NN):
    return dot1(a[0], b[0], dims) + (dot1(a[0], b[1], dims) + dot1(a[1], b[0], dims))


def half(x):
    return x.astype(BF16)


def four_steps(power):
    rest, power = power, half(power)
    for _ in range(NS_STEPS - 1):
        squared = dot1(power, power)
        power = half(squared)
        rest = rest + squared + dot1(half(rest), power)
    return half(rest)


def before_trans(own, facing):
    near, away, out = own
    f, o, s = split(facing), split(near), split(out)
    rough = dot1(f[0], o[0])
    rest = four_steps(rough)
    coupling = rough + (dot1(f[0], o[1]) + dot1(f[1], o[0]))
    inner = split(dot3(f, s, NT))
    high, low = split(coupling)
    error = half((coupling - rest.astype(F32)) + (dot1(high, rest) + dot1(low, rest)))
    leading = out + (dot1(s[0], rest) + dot1(s[1], rest))
    mirror = near + (dot1(o[0], rest) + dot1(o[1], rest))
    leading = leading + dot1(half(leading), error)
    mirror = mirror + dot1(half(mirror), error)
    return leading, mirror, away + dot3(split(leading), inner)


def after_trans(leading, mirror, away, into):
    q = split(into)
    trans = dot3(split(leading), q)
    bounced = split(dot3(split(mirror), q))
    return trans, away + dot3(split(into.T), bounced)


def place():
    return lax.axis_index("gx") * lax.axis_size("gy") + lax.axis_index("gy")


def bit(me, distance):
    return me & distance != 0


def lower_upper(h):
    row = lax.broadcasted_iota(jnp.int32, (h, h), 0)
    col = lax.broadcasted_iota(jnp.int32, (h, h), 1)
    return row > col, row < col


def pack_symmetric(x):
    h = x.shape[0] // 2
    below, above = lower_upper(h)
    a, b, c = x[:h, :h], x[:h, h:], x[h:, h:]
    diagonal = jnp.sum(jnp.where(below | above, 0.0, c), axis=0, keepdims=True)
    diagonal = jnp.broadcast_to(jnp.concatenate([diagonal, diagonal], 1), (PAD, 2 * h))
    return jnp.concatenate([b, jnp.where(above, c, a)], 1), diagonal


def unpack_symmetric(rows, diagonal):
    h = rows.shape[0]
    below, above = lower_upper(h)
    b, w = rows[:, :h], rows[:, h:]
    turned = w.T
    a = jnp.where(above, turned, w)
    c = jnp.where(above, w, jnp.where(below, turned, diagonal[:1, :h]))
    return jnp.concatenate([jnp.concatenate([a, b], 1), jnp.concatenate([b.T, c], 1)], 0)


def own_half(x, core):
    h = x.shape[0] // 2
    return jnp.where(core, x[h:], x[:h])


def joined(near, far, core):
    return jnp.concatenate([jnp.where(core, far, near), jnp.where(core, near, far)], 0)


def unpack_first(near, far, core):
    return joined(near[:-PAD], far[:-PAD], core), near[-PAD:]


def unpack_second(near, far, core):
    h = near.shape[1] // 2
    return joined(near[:h], far[:h], core), unpack_symmetric(*unpack_first(near[h:], far[h:], core))


def pack_message(facing, away, into, core, first_ref, second_ref, early_ref=None):
    rows, diagonal = pack_symmetric(facing)
    more, more_diagonal = pack_symmetric(away)
    second = jnp.concatenate([own_half(into, core), own_half(more, core), more_diagonal], 0)
    first_ref[...] = jnp.concatenate([own_half(rows, core), diagonal], 0)
    second_ref[...] = second
    if early_ref is not None:
        early_ref[...] = jnp.concatenate([rows, diagonal, second], 0)


def send_total(own_side, other_side, trans, me, distance, quarter, own_ref, *message_refs):
    core, upper = bit(me, 1), bit(me, distance)
    turned = trans.T
    if 2 * distance == quarter:
        left, right = jnp.where(upper, other_side, own_side), jnp.where(upper, own_side, other_side)
        trans = jnp.where(upper, trans, turned)
        state, message = (left, right, trans), (right, left, trans)
    else:
        same = upper == bit(me, 2 * distance)
        near, away = jnp.where(same, other_side, own_side), jnp.where(same, own_side, other_side)
        state = near, away, jnp.where(same, trans, turned)
        message = near, away, jnp.where(same, turned, trans)
    pack_message(*message, core, *message_refs)
    for i, x in enumerate(state):
        own_ref[i] = x


def first_kernel(quarter, section_ref, got1, got2, got3, prefix_ref, own_ref, *message_refs):
    me = place()
    upper = bit(me, 1)
    left, right, trans = section_ref[0], section_ref[1], section_ref[2]
    choose = lambda a, b: jnp.where(upper, a, b)
    own = choose(left, right), choose(right, left), choose(trans, trans.T)
    leading, mirror, own_side = before_trans(own, choose(got2[0], got1[0]))
    into = choose(got3[0], got3[0].T)
    through, other_side = after_trans(leading, mirror, choose(got1[0], got2[0]), into)
    send_total(own_side, other_side, through, me, 1, quarter, own_ref, *message_refs)
    prefix_ref[0] = choose(other_side, left)
    prefix_ref[1] = choose(own_side, right)
    prefix_ref[2] = choose(through, trans)


def early_kernel(distance, quarter, own_ref, near_ref, far_ref, half_ref):
    me = place()

    def body():
        facing = unpack_symmetric(*unpack_first(near_ref[...], far_ref[...], bit(me, 1)))
        for i, x in enumerate(before_trans((own_ref[0], own_ref[1], own_ref[2]), facing)):
            half_ref[i] = x

    only_group(1, me, distance, quarter, body, half_ref)


def late_kernel(distance, quarter, half_ref, near_ref, far_ref, *out_refs):
    me = place()
    core = bit(me, 1)

    def body():
        into, away = unpack_second(near_ref[...], far_ref[...], core)
        trans, other_side = after_trans(half_ref[0], half_ref[1], away, into)
        if distance == quarter:
            pack_message(half_ref[2], other_side, trans, core, *out_refs)
        else:
            send_total(half_ref[2], other_side, trans, me, distance, quarter, *out_refs)

    only_group(1, me, distance, quarter, body, *out_refs)


def only_group(group, me, distance, quarter, body, *out_refs):
    if distance != quarter:
        body()
        return
    pl.when(me // quarter == group)(body)

    @pl.when(me // quarter != group)
    def _():
        for ref in out_refs:
            ref[...] = jnp.zeros_like(ref)


def prefix_kernel(distance, quarter, old_ref, near1, far1, near2, far2, new_ref):
    me = place()
    core = bit(me, 1)
    grown = me >= quarter if distance == quarter else bit(me, distance)
    old = old_ref[0], old_ref[1], old_ref[2]
    facing = unpack_symmetric(*unpack_first(near1[...], far1[...], core))
    leading, mirror, right = before_trans(old, facing)
    into, away = unpack_second(near2[...], far2[...], core)
    trans, left = after_trans(leading, mirror, away, into)
    for i, x in enumerate((left, right, trans)):
        new_ref[i] = jnp.where(grown, x, old[i])


def last_early_kernel(quarter, own_ref, near_ref, far_ref, near_early, half_ref):
    me = place()
    picked = me // quarter == 2
    rows, diagonal = unpack_first(near_ref[...], far_ref[...], bit(me, 1))
    h = rows.shape[0]
    rows = jnp.where(picked, near_early[:h, :], rows)
    diagonal = jnp.where(picked, near_early[h : h + PAD, :], diagonal)
    for i, x in enumerate(before_trans((own_ref[0], own_ref[1], own_ref[2]), unpack_symmetric(rows, diagonal))):
        half_ref[i] = x


def last_kernel(quarter, old_ref, half_ref, near_ref, far_ref, near_early, far_early, left_ref, right_ref, trans_ref):
    me = place()
    group, cut = me // quarter, near_early.shape[0] - near_ref.shape[0]
    near = jnp.where(group == 2, near_early[cut:, :], near_ref[...])
    far = jnp.where(group == 2, far_early[cut:, :], far_ref[...])
    into, away = unpack_second(near, far, bit(me, 1))
    trans, left = after_trans(half_ref[0], half_ref[1], away, into)
    grown = group >= 2
    right_ref[0] = jnp.where(grown, half_ref[2], old_ref[1])
    trans_ref[0] = jnp.where(grown, trans, old_ref[2])
    left_ref[0] = jnp.where(grown, left, old_ref[0])


def call(kernel, products, outs, *args):
    vmem = pl.BlockSpec(memory_space=pltpu.VMEM)
    m = args[0].shape[-1]
    return pl.pallas_call(
        kernel,
        out_shape=[jax.ShapeDtypeStruct(s, F32) for s in outs],
        in_specs=[vmem] * len(args),
        out_specs=[vmem] * len(outs),
        cost_estimate=pl.CostEstimate(flops=2 * products * m**3, bytes_accessed=4 * m**2 * len(args), transcendentals=0),
        compiler_params=pltpu.CompilerParams(vmem_limit_bytes=40 * 2**20),
    )(*args)


def shards(refl_left, refl_right, trans):
    m = trans.shape[1]
    quarter = lax.axis_size(AXES) // 4
    stack, first, second = (3, m, m), (m // 4 + PAD, m), (m // 2 + m // 4 + PAD, m)
    whole = (m // 2 + PAD + second[0], m)
    sections = refl_left, refl_right, trans
    got = [swap(x, 1) for x in sections]
    section = jnp.concatenate(sections, 0)

    def message(distance):
        return [stack, first, second] + [whole] * (2 * distance == quarter)

    prefix, own, *send = call(functools.partial(first_kernel, quarter), 36, [stack] + message(1), section, *got)
    pending = None
    distance = 2
    while True:
        bind = lambda kernel: functools.partial(kernel, distance, quarter)
        move = shift if distance == quarter else swap
        near1, near2 = move(send[0], distance), move(send[1], distance)
        if distance == quarter:
            early = pair(send[2], 0, 2)
        if pending is not None:
            (prefix,) = pending(prefix)
            near1 = after(near1, prefix)
        far1 = swap(near1, 1)
        (halfway,) = call(bind(early_kernel), 27, [stack], own, near1, far1)
        near2 = after(near2, halfway)
        far2 = swap(near2, 1)
        got = near1, far1, near2, far2
        if distance == quarter:
            break
        own, *send = call(bind(late_kernel), 9, message(distance), halfway, near2, far2)
        pending = lambda old, kernel=bind(prefix_kernel), got=got: call(kernel, 36, [stack], old, *got)
        distance *= 2

    send = call(bind(late_kernel), 9, [first, second], halfway, near2, far2)
    near1, near2 = pair(send[0], 1, 3), pair(send[1], 1, 3)
    (prefix,) = call(bind(prefix_kernel), 36, [stack], after(prefix, early), *got)
    near1 = after(near1, prefix)
    far1 = swap(near1, 1)
    (halfway,) = call(functools.partial(last_early_kernel, quarter), 27, [stack], prefix, near1, far1, early)
    near2 = after(near2, halfway)
    far2 = swap(near2, 1)

    args = prefix, halfway, near2, far2, early, swap(early, 1)
    return tuple(call(functools.partial(last_kernel, quarter), 9, [(1, m, m)] * 3, *args))


def solution(mesh):
    spec = P(AXES, None, None)
    return jax.shard_map(
        shards,
        mesh=mesh,
        in_specs=(spec,) * 3,
        out_specs=(spec,) * 3,
        check_vma=False,
    )
```

time: 59.6 us -> 66.2 us (1.11)
  waiting for transfers between devices: 23 us -> 28.4 us
  starting transfers between devices: 11.3 us -> 16 us
  Pallas kernels: 23.2 us -> 19.7 us
    ppermute x0 -> x5, waiting for transfers between devices: none -> 16 us  [the longest x3 15.7 us: pair(): lax.ppermute(block, AXES, [(i, step.get(i // quarter, lambda i: i ^ 1)(i)...]
    ppermute x19 -> x16, waiting for transfers between devices: 23 us -> 12.3 us  [swap(): return lax.ppermute(block, AXES, [(i, i ^ distance) for i in range(count)])]
    ppermute x0 -> x5, starting transfers between devices: none -> 8.89 us  [the longest x2 7.24 us: shift(): lax.ppermute(block, AXES, [(i, i + distance) for i in range(count - dista...]
    ppermute x19 -> x16, starting transfers between devices: 11.3 us -> 7.07 us  [swap(): return lax.ppermute(block, AXES, [(i, i ^ distance) for i in range(count)])]
    pallas_call x12, Pallas kernels: 23.2 us -> 19.7 us  [call(): pl.pallas_call(kernel, out_shape=[jax.ShapeDtypeStruct(s, F32) for s in o...]
  transfers between devices with their start and end apart: 19 -> 21, of which waited for: 16 -> 14; matrix products, arithmetic and copies ran while one was open for 2% -> 2% of each run, Pallas kernels for 27% -> 21%
where the time goes in v2:
time: 66.2 us; the launch traced here: 66 us
  waiting for transfers between devices  28.4 us (43%)
  Pallas kernels  19.7 us (30%)
  starting transfers between devices  16 us (24%)
  other arithmetic  1.16 us (2%)
  between operations  0.81 us (1%)
    pallas_call x12, Pallas kernels, call(): pl.pallas_call(kernel, out_shape=[jax.ShapeDtypeStruct(s, F32) for s in o...  19.7 us
    ppermute x3, waiting for transfers between devices, pair(): lax.ppermute(block, AXES, [(i, step.get(i // quarter, lambda i: i ^ 1)(i)...  15.7 us
    ppermute x16, waiting for transfers between devices, swap(): return lax.ppermute(block, AXES, [(i, i ^ distance) for i in range(count)])  12.3 us
    ppermute x2, starting transfers between devices, shift(): lax.ppermute(block, AXES, [(i, i + distance) for i in range(count - dista...  7.24 us
    ppermute x16, starting transfers between devices, swap(): return lax.ppermute(block, AXES, [(i, i ^ distance) for i in range(count)])  7.07 us
    ppermute x3, starting transfers between devices, pair(): lax.ppermute(block, AXES, [(i, step.get(i // quarter, lambda i: i ^ 1)(i)...  1.65 us
  transfers between devices with their start and end apart: 21, of which 14 were waited for; matrix products, arithmetic and copies ran while one was open for 2% of the time, Pallas kernels for 21%

profile of v2, /device:TPU:0, one launch (start us, length us, event | category | flops | bytes accessed | tf_op | source)
XLA Modules:
  0.0 66.0 jit_solution(15725306624281603294)
XLA Ops:
  0.6 0.5 collective-permute-start
  1.2 0.4 collective-permute-start.2
  1.7 1.2 %pad_maximum_fusion.section_ref = f32[3,256,256]{2,1,0:T(8,128)S(1)} fusion(f32[1,256,256]{2,1,0:T(8,128)} %param.5, f32[1,256,256]{2,1,0:T(8,128)} %param.4, f32[1,256,256]{2,1,0:T(8,128)} %param.3), kind=kLoop, calls=%fused_computation | loop fusion | flops 393216 | bytes 1572864 | tf_op jit(solution)/shard_map/concatenate | solution.py:280
  2.9 0.4 collective-permute-done.2.got3
  3.3 2.6 %shard_map.58 = (f32[3,256,256]{2,1,0:T(8,128)S(1)}, f32[3,256,256]{2,1,0:T(8,128)S(1)}, f32[72,256]{1,0:T(8,128)S(1)}, f32[200,256]{1,0:T(8,128)S(1)}) custom-call(f32[3,256,256]{2,1,0:T(8,128)S(1)} %pad_maximum_fusion.section_ref, f32[1,256,256]{2,1,0:T(8,128)S(1)} %collective-permute-done.got1, f32[1,256,256]{2,1,0:T(8,128)S(1)} %collective-permute-done.1.got2, ...), custom_call_target="tpu_custom_call" | custom-call | flops 1207959552 | bytes 1048576 | tf_op jit(solution)/shard_map/pallas_call | solution.py:263
  5.9 2.9 %collective-permute-start.3 = (f32[72,256]{1,0:T(8,128)S(1)}, f32[72,256]{1,0:T(8,128)S(1)}, u32[]{:S(2)}, u32[]{:S(2)}) collective-permute-start(f32[72,256]{1,0:T(8,128)S(1)} %get-tuple-element.25), channel_id=1, source_target_pairs={{0,2},{1,3},{2,0},{3,1},{4,6},{5,7},{6,4},{7,5},{8,10},{9,11},{10,... | collective-permute-start | bytes 221192 | tf_op jit(solution)/shard_map/ppermute | solution.py:21
  8.9 2.6 %collective-permute-done.3.near_ref.near1 = f32[72,256]{1,0:T(8,128)S(1)} collective-permute-done((f32[72,256]{1,0:T(8,128)S(1)}, f32[72,256]{1,0:T(8,128)S(1)}, u32[]{:S(2)}, u32[]{:S(2)}) %collective-permute-start.3) | collective-permute-done | bytes 73760 | tf_op jit(solution)/shard_map/ppermute | solution.py:21
  11.5 1.3 %collective-permute-done.4.far_ref.far1 = f32[72,256]{1,0:T(8,128)S(1)} collective-permute-done((f32[72,256]{1,0:T(8,128)S(1)}, f32[72,256]{1,0:T(8,128)S(1)}, u32[]{:S(2)}, u32[]{:S(2)}) %collective-permute-start.4) | collective-permute-done | bytes 73760 | tf_op jit(solution)/shard_map/ppermute | solution.py:21
  12.8 2.1 %shard_map.59.half_ref = f32[3,256,256]{2,1,0:T(8,128)S(1)} custom-call(f32[3,256,256]{2,1,0:T(8,128)S(1)} %get-tuple-element.27.own_ref, f32[72,256]{1,0:T(8,128)S(1)} %collective-permute-done.3.near_ref.near1, f32[72,256]{1,0:T(8,128)S(1)} %collective-permute-done.4.far_ref.far1), custom_call_target="tpu_custom_call" | custom-call | flops 905969664 | bytes 786432 | tf_op jit(solution)/shard_map/pallas_call | solution.py:263
  14.9 0.9 %collective-permute-done.5.near2.near_ref = f32[200,256]{1,0:T(8,128)S(1)} collective-permute-done((f32[200,256]{1,0:T(8,128)S(1)}, f32[200,256]{1,0:T(8,128)S(1)}, u32[]{:S(2)}, u32[]{:S(2)}) %collective-permute-start.5) | collective-permute-done | bytes 204832 | tf_op jit(solution)/shard_map/ppermute | solution.py:21
  15.8 1.5 %collective-permute-done.6.far2.far_ref = f32[200,256]{1,0:T(8,128)S(1)} collective-permute-done((f32[200,256]{1,0:T(8,128)S(1)}, f32[200,256]{1,0:T(8,128)S(1)}, u32[]{:S(2)}, u32[]{:S(2)}) %collective-permute-start.6) | collective-permute-done | bytes 204832 | tf_op jit(solution)/shard_map/ppermute | solution.py:21
  17.2 0.7 %shard_map.61 = (f32[3,256,256]{2,1,0:T(8,128)S(1)}, f32[72,256]{1,0:T(8,128)S(1)}, f32[200,256]{1,0:T(8,128)S(1)}) custom-call(f32[3,256,256]{2,1,0:T(8,128)S(1)} %shard_map.59.half_ref, f32[200,256]{1,0:T(8,128)S(1)} %collective-permute-done.5.near2.near_ref, f32[200,256]{1,0:T(8,128)S(1)} %collective-permute-done.6.far2.far_ref), custom_call_target="tpu_custom_call" | custom-call | flops 301989888 | bytes 786432 | tf_op jit(solution)/shard_map/pallas_call | solution.py:263
  17.9 1.9 %collective-permute-start.7 = (f32[72,256]{1,0:T(8,128)S(1)}, f32[72,256]{1,0:T(8,128)S(1)}, u32[]{:S(2)}, u32[]{:S(2)}) collective-permute-start(f32[72,256]{1,0:T(8,128)S(1)} %get-tuple-element.29), channel_id=1, source_target_pairs={{0,4},{1,5},{2,6},{3,7},{4,0},{5,1},{6,2},{7,3},{8,12},{9,13},{10,... | collective-permute-start | bytes 221192 | tf_op jit(solution)/shard_map/ppermute | solution.py:21
  20.0 2.6 %shard_map.60.old_ref = f32[3,256,256]{2,1,0:T(8,128)S(1)} custom-call(f32[3,256,256]{2,1,0:T(8,128)S(1)} %get-tuple-element.24.old_ref, f32[72,256]{1,0:T(8,128)S(1)} %collective-permute-done.3.near_ref.near1, f32[72,256]{1,0:T(8,128)S(1)} %collective-permute-done.4.far_ref.far1, f32[200,256]{1,0:T(8,128)S(1)} %collective-permute-done.5.near2.near_ref, ...), custom_call_target="tpu_custom_call" | custom-call | flops 1207959552 | bytes 1310720 | tf_op jit(solution)/shard_map/pallas_call | solution.py:263
  22.7 1.3 %collective-permute-done.8.far_ref.far1 = f32[72,256]{1,0:T(8,128)S(1)} collective-permute-done((f32[72,256]{1,0:T(8,128)S(1)}, f32[72,256]{1,0:T(8,128)S(1)}, u32[]{:S(2)}, u32[]{:S(2)}) %collective-permute-start.8) | collective-permute-done | bytes 73760 | tf_op jit(solution)/shard_map/ppermute | solution.py:21
  23.9 2.1 %shard_map.62.half_ref = f32[3,256,256]{2,1,0:T(8,128)S(1)} custom-call(f32[3,256,256]{2,1,0:T(8,128)S(1)} %get-tuple-element.32.own_ref, f32[72,256]{1,0:T(8,128)S(1)} %collective-permute-done.7.near_ref.near1, f32[72,256]{1,0:T(8,128)S(1)} %collective-permute-done.8.far_ref.far1), custom_call_target="tpu_custom_call" | custom-call | flops 905969664 | bytes 786432 | tf_op jit(solution)/shard_map/pallas_call | solution.py:263
  26.0 0.7 %collective-permute-done.9.near2.near_ref = f32[200,256]{1,0:T(8,128)S(1)} collective-permute-done((f32[200,256]{1,0:T(8,128)S(1)}, f32[200,256]{1,0:T(8,128)S(1)}, u32[]{:S(2)}, u32[]{:S(2)}) %collective-permute-start.9) | collective-permute-done | bytes 204832 | tf_op jit(solution)/shard_map/ppermute | solution.py:21
  26.8 1.5 %collective-permute-done.10.far2.far_ref = f32[200,256]{1,0:T(8,128)S(1)} collective-permute-done((f32[200,256]{1,0:T(8,128)S(1)}, f32[200,256]{1,0:T(8,128)S(1)}, u32[]{:S(2)}, u32[]{:S(2)}) %collective-permute-start.10) | collective-permute-done | bytes 204832 | tf_op jit(solution)/shard_map/ppermute | solution.py:21
  28.2 0.7 %shard_map.64 = (f32[3,256,256]{2,1,0:T(8,128)S(1)}, f32[72,256]{1,0:T(8,128)S(1)}, f32[200,256]{1,0:T(8,128)S(1)}, f32[336,256]{1,0:T(8,128)S(1)}) custom-call(f32[3,256,256]{2,1,0:T(8,128)S(1)} %shard_map.62.half_ref, f32[200,256]{1,0:T(8,128)S(1)} %collective-permute-done.9.near2.near_ref, f32[200,256]{1,0:T(8,128)S(1)} %collective-permute-done.10.far2.far_ref), custom_call_target="tpu_custom_call" | custom-call | flops 301989888 | bytes 786432 | tf_op jit(solution)/shard_map/pallas_call | solution.py:263
  29.0 3.7 %collective-permute-start.12 = (f32[72,256]{1,0:T(8,128)S(1)}, f32[72,256]{1,0:T(8,128)S(1)}, u32[]{:S(2)}, u32[]{:S(2)}) collective-permute-start(f32[72,256]{1,0:T(8,128)S(1)} %get-tuple-element.36), channel_id=1, source_target_pairs={{0,8},{1,9},{2,10},{3,11},{4,12},{5,13},{6,14},{7,15},{8,16},{9,17... | collective-permute-start | bytes 221192 | tf_op jit(solution)/shard_map/ppermute | solution.py:34
  32.7 3.5 %collective-permute-start.14 = (f32[200,256]{1,0:T(8,128)S(1)}, f32[200,256]{1,0:T(8,128)S(1)}, u32[]{:S(2)}, u32[]{:S(2)}) collective-permute-start(f32[200,256]{1,0:T(8,128)S(1)} %get-tuple-element.38), channel_id=1, source_target_pairs={{0,8},{1,9},{2,10},{3,11},{4,12},{5,13},{6,14},{7,15},{8,16},{9,17... | collective-permute-start | bytes 614408 | tf_op jit(solution)/shard_map/ppermute | solution.py:34
  36.2 2.6 %shard_map.63.old_ref = f32[3,256,256]{2,1,0:T(8,128)S(1)} custom-call(f32[3,256,256]{2,1,0:T(8,128)S(1)} %shard_map.60.old_ref, f32[72,256]{1,0:T(8,128)S(1)} %collective-permute-done.7.near_ref.near1, f32[72,256]{1,0:T(8,128)S(1)} %collective-permute-done.8.far_ref.far1, f32[200,256]{1,0:T(8,128)S(1)} %collective-permute-done.9.near2.near_ref, ...), custom_call_target="tpu_custom_call" | custom-call | flops 1207959552 | bytes 1310720 | tf_op jit(solution)/shard_map/pallas_call | solution.py:263
  38.9 1.1 %collective-permute-start.11 = (f32[336,256]{1,0:T(8,128)S(1)}, f32[336,256]{1,0:T(8,128)S(1)}, u32[]{:S(2)}, u32[]{:S(2)}) collective-permute-start(f32[336,256]{1,0:T(8,128)S(1)} %get-tuple-element.34), channel_id=1, source_target_pairs={{0,16},{1,17},{2,18},{3,19},{4,20},{5,21},{6,22},{7,23},{8,9},{9,8... | collective-permute-start | bytes 1032200 | tf_op jit(solution)/shard_map/ppermute | solution.py:29
  40.2 0.4 collective-permute-done.14.near2.near_ref
  40.5 15.7 %collective-permute-done.11.near_early = f32[336,256]{1,0:T(8,128)S(1)} collective-permute-done((f32[336,256]{1,0:T(8,128)S(1)}, f32[336,256]{1,0:T(8,128)S(1)}, u32[]{:S(2)}, u32[]{:S(2)}) %collective-permute-start.11) | collective-permute-done | bytes 344096 | tf_op jit(solution)/shard_map/ppermute | solution.py:29
  56.5 0.5 collective-permute-start.18
  57.0 2.6 %shard_map.66.own_ref.old_ref = f32[3,256,256]{2,1,0:T(8,128)S(1)} custom-call(f32[3,256,256]{2,1,0:T(8,128)S(1)} %shard_map.63.old_ref, f32[72,256]{1,0:T(8,128)S(1)} %collective-permute-done.12.near_ref.near1, f32[72,256]{1,0:T(8,128)S(1)} %collective-permute-done.13.far_ref.far1, f32[200,256]{1,0:T(8,128)S(1)} %collective-permute-done.14.near2.near_ref, ...), custom_call_target="tpu_custom_call" | custom-call | flops 1207959552 | bytes 1310720 | tf_op jit(solution)/shard_map/pallas_call | solution.py:263
  59.8 0.4 collective-permute-start.20
  60.2 0.8 %collective-permute-done.17.far_ref = f32[72,256]{1,0:T(8,128)S(1)} collective-permute-done((f32[72,256]{1,0:T(8,128)S(1)}, f32[72,256]{1,0:T(8,128)S(1)}, u32[]{:S(2)}, u32[]{:S(2)}) %collective-permute-start.17) | collective-permute-done | bytes 73760 | tf_op jit(solution)/shard_map/ppermute | solution.py:21
  60.9 2.1 %shard_map.68.half_ref = f32[3,256,256]{2,1,0:T(8,128)S(1)} custom-call(f32[3,256,256]{2,1,0:T(8,128)S(1)} %shard_map.66.own_ref.old_ref, f32[72,256]{1,0:T(8,128)S(1)} %collective-permute-done.16.near_ref, f32[72,256]{1,0:T(8,128)S(1)} %collective-permute-done.17.far_ref, f32[336,256]{1,0:T(8,128)S(1)} %collective-permute-done.11.near_early), custom_call_target="tpu_custom_call" | custom-call | flops 905969664 | bytes 1048576 | tf_op jit(solution)/shard_map/pallas_call | solution.py:263
  63.3 1.3 %collective-permute-done.19.far_ref = f32[200,256]{1,0:T(8,128)S(1)} collective-permute-done((f32[200,256]{1,0:T(8,128)S(1)}, f32[200,256]{1,0:T(8,128)S(1)}, u32[]{:S(2)}, u32[]{:S(2)}) %collective-permute-start.19) | collective-permute-done | bytes 204832 | tf_op jit(solution)/shard_map/ppermute | solution.py:21
  64.6 1.4 %shard_map.69 = (f32[1,256,256]{2,1,0:T(8,128)}, f32[1,256,256]{2,1,0:T(8,128)}, f32[1,256,256]{2,1,0:T(8,128)}) custom-call(f32[3,256,256]{2,1,0:T(8,128)S(1)} %shard_map.66.own_ref.old_ref, f32[3,256,256]{2,1,0:T(8,128)S(1)} %shard_map.68.half_ref, f32[200,256]{1,0:T(8,128)S(1)} %collective-permute-done.18.near_ref, ...), custom_call_target="tpu_custom_call" | custom-call | flops 301989888 | bytes 1572864 | tf_op jit(solution)/shard_map/pallas_call | solution.py:263
  (23 shorter events, 1.5 us)
Async XLA Ops:
  0.6 2.2 %collective-permute-start = (f32[1,256,256]{2,1,0:T(8,128)}, f32[1,256,256]{2,1,0:T(8,128)S(1)}, u32[]{:S(2)}, u32[]{:S(2)}) collective-permute-start(f32[1,256,256]{2,1,0:T(8,128)} %param.3), channel_id=1, source_target_pairs={{0,1},{1,0},{2,3},{3,2},{4,5},{5,4},{6,7},{7,6},{8,9},{9,8},{10,11... | collective-permute-start | bytes 786440 | tf_op jit(solution)/shard_map/ppermute | solution.py:21
  1.1 1.7 %collective-permute-start.1 = (f32[1,256,256]{2,1,0:T(8,128)}, f32[1,256,256]{2,1,0:T(8,128)S(1)}, u32[]{:S(2)}, u32[]{:S(2)}) collective-permute-start(f32[1,256,256]{2,1,0:T(8,128)} %param.4), channel_id=1, source_target_pairs={{0,1},{1,0},{2,3},{3,2},{4,5},{5,4},{6,7},{7,6},{8,9},{9,8},{10,11... | collective-permute-start | bytes 786440 | tf_op jit(solution)/shard_map/ppermute | solution.py:21
  1.2 2.0 %collective-permute-start.2 = (f32[1,256,256]{2,1,0:T(8,128)}, f32[1,256,256]{2,1,0:T(8,128)S(1)}, u32[]{:S(2)}, u32[]{:S(2)}) collective-permute-start(f32[1,256,256]{2,1,0:T(8,128)} %param.5), channel_id=1, source_target_pairs={{0,1},{1,0},{2,3},{3,2},{4,5},{5,4},{6,7},{7,6},{8,9},{9,8},{10,11... | collective-permute-start | bytes 786440 | tf_op jit(solution)/shard_map/ppermute | solution.py:21
  5.9 5.6 %collective-permute-start.3 = (f32[72,256]{1,0:T(8,128)S(1)}, f32[72,256]{1,0:T(8,128)S(1)}, u32[]{:S(2)}, u32[]{:S(2)}) collective-permute-start(f32[72,256]{1,0:T(8,128)S(1)} %get-tuple-element.25), channel_id=1, source_target_pairs={{0,2},{1,3},{2,0},{3,1},{4,6},{5,7},{6,4},{7,5},{8,10},{9,11},{10,... | collective-permute-start | bytes 221192 | tf_op jit(solution)/shard_map/ppermute | solution.py:21
  8.8 7.0 %collective-permute-start.5 = (f32[200,256]{1,0:T(8,128)S(1)}, f32[200,256]{1,0:T(8,128)S(1)}, u32[]{:S(2)}, u32[]{:S(2)}) collective-permute-start(f32[200,256]{1,0:T(8,128)S(1)} %get-tuple-element.26), channel_id=1, source_target_pairs={{0,2},{1,3},{2,0},{3,1},{4,6},{5,7},{6,4},{7,5},{8,10},{9,11},{10,... | collective-permute-start | bytes 614408 | tf_op jit(solution)/shard_map/ppermute | solution.py:21
  11.5 1.3 %collective-permute-start.4 = (f32[72,256]{1,0:T(8,128)S(1)}, f32[72,256]{1,0:T(8,128)S(1)}, u32[]{:S(2)}, u32[]{:S(2)}) collective-permute-start(f32[72,256]{1,0:T(8,128)S(1)} %collective-permute-done.3.near_ref.near1), channel_id=1, source_target_pairs={{0,1},{1,0},{2,3},{3,2},{4,5},{5,4},{6,7},{7,6},{8,9},{9,8},{10,11... | collective-permute-start | bytes 221192 | tf_op jit(solution)/shard_map/ppermute | solution.py:21
  15.8 1.5 %collective-permute-start.6 = (f32[200,256]{1,0:T(8,128)S(1)}, f32[200,256]{1,0:T(8,128)S(1)}, u32[]{:S(2)}, u32[]{:S(2)}) collective-permute-start(f32[200,256]{1,0:T(8,128)S(1)} %collective-permute-done.5.near2.near_ref), channel_id=1, source_target_pairs={{0,1},{1,0},{2,3},{3,2},{4,5},{5,4},{6,7},{7,6},{8,9},{9,8},{10,11... | collective-permute-start | bytes 614408 | tf_op jit(solution)/shard_map/ppermute | solution.py:21
  17.9 4.7 %collective-permute-start.7 = (f32[72,256]{1,0:T(8,128)S(1)}, f32[72,256]{1,0:T(8,128)S(1)}, u32[]{:S(2)}, u32[]{:S(2)}) collective-permute-start(f32[72,256]{1,0:T(8,128)S(1)} %get-tuple-element.29), channel_id=1, source_target_pairs={{0,4},{1,5},{2,6},{3,7},{4,0},{5,1},{6,2},{7,3},{8,12},{9,13},{10,... | collective-permute-start | bytes 221192 | tf_op jit(solution)/shard_map/ppermute | solution.py:21
  19.8 7.0 %collective-permute-start.9 = (f32[200,256]{1,0:T(8,128)S(1)}, f32[200,256]{1,0:T(8,128)S(1)}, u32[]{:S(2)}, u32[]{:S(2)}) collective-permute-start(f32[200,256]{1,0:T(8,128)S(1)} %get-tuple-element.31), channel_id=1, source_target_pairs={{0,4},{1,5},{2,6},{3,7},{4,0},{5,1},{6,2},{7,3},{8,12},{9,13},{10,... | collective-permute-start | bytes 614408 | tf_op jit(solution)/shard_map/ppermute | solution.py:21
  22.6 1.3 %collective-permute-start.8 = (f32[72,256]{1,0:T(8,128)S(1)}, f32[72,256]{1,0:T(8,128)S(1)}, u32[]{:S(2)}, u32[]{:S(2)}) collective-permute-start(f32[72,256]{1,0:T(8,128)S(1)} %collective-permute-done.7.near_ref.near1), channel_id=1, source_target_pairs={{0,1},{1,0},{2,3},{3,2},{4,5},{5,4},{6,7},{7,6},{8,9},{9,8},{10,11... | collective-permute-start | bytes 221192 | tf_op jit(solution)/shard_map/ppermute | solution.py:21
  26.8 1.5 %collective-permute-start.10 = (f32[200,256]{1,0:T(8,128)S(1)}, f32[200,256]{1,0:T(8,128)S(1)}, u32[]{:S(2)}, u32[]{:S(2)}) collective-permute-start(f32[200,256]{1,0:T(8,128)S(1)} %collective-permute-done.9.near2.near_ref), channel_id=1, source_target_pairs={{0,1},{1,0},{2,3},{3,2},{4,5},{5,4},{6,7},{7,6},{8,9},{9,8},{10,11... | collective-permute-start | bytes 614408 | tf_op jit(solution)/shard_map/ppermute | solution.py:21
  29.0 9.8 %collective-permute-start.12 = (f32[72,256]{1,0:T(8,128)S(1)}, f32[72,256]{1,0:T(8,128)S(1)}, u32[]{:S(2)}, u32[]{:S(2)}) collective-permute-start(f32[72,256]{1,0:T(8,128)S(1)} %get-tuple-element.36), channel_id=1, source_target_pairs={{0,8},{1,9},{2,10},{3,11},{4,12},{5,13},{6,14},{7,15},{8,16},{9,17... | collective-permute-start | bytes 221192 | tf_op jit(solution)/shard_map/ppermute | solution.py:34
  32.7 7.8 %collective-permute-start.14 = (f32[200,256]{1,0:T(8,128)S(1)}, f32[200,256]{1,0:T(8,128)S(1)}, u32[]{:S(2)}, u32[]{:S(2)}) collective-permute-start(f32[200,256]{1,0:T(8,128)S(1)} %get-tuple-element.38), channel_id=1, source_target_pairs={{0,8},{1,9},{2,10},{3,11},{4,12},{5,13},{6,14},{7,15},{8,16},{9,17... | collective-permute-start | bytes 614408 | tf_op jit(solution)/shard_map/ppermute | solution.py:34
  38.8 1.3 %collective-permute-start.13 = (f32[72,256]{1,0:T(8,128)S(1)}, f32[72,256]{1,0:T(8,128)S(1)}, u32[]{:S(2)}, u32[]{:S(2)}) collective-permute-start(f32[72,256]{1,0:T(8,128)S(1)} %collective-permute-done.12.near_ref.near1), channel_id=1, source_target_pairs={{0,1},{1,0},{2,3},{3,2},{4,5},{5,4},{6,7},{7,6},{8,9},{9,8},{10,11... | collective-permute-start | bytes 221192 | tf_op jit(solution)/shard_map/ppermute | solution.py:21
  38.9 17.3 %collective-permute-start.11 = (f32[336,256]{1,0:T(8,128)S(1)}, f32[336,256]{1,0:T(8,128)S(1)}, u32[]{:S(2)}, u32[]{:S(2)}) collective-permute-start(f32[336,256]{1,0:T(8,128)S(1)} %get-tuple-element.34), channel_id=1, source_target_pairs={{0,16},{1,17},{2,18},{3,19},{4,20},{5,21},{6,22},{7,23},{8,9},{9,8... | collective-permute-start | bytes 1032200 | tf_op jit(solution)/shard_map/ppermute | solution.py:29
  40.5 15.7 %collective-permute-start.15 = (f32[200,256]{1,0:T(8,128)S(1)}, f32[200,256]{1,0:T(8,128)S(1)}, u32[]{:S(2)}, u32[]{:S(2)}) collective-permute-start(f32[200,256]{1,0:T(8,128)S(1)} %collective-permute-done.14.near2.near_ref), channel_id=1, source_target_pairs={{0,1},{1,0},{2,3},{3,2},{4,5},{5,4},{6,7},{7,6},{8,9},{9,8},{10,11... | collective-permute-start | bytes 614408 | tf_op jit(solution)/shard_map/ppermute | solution.py:21
  56.4 3.2 %collective-permute-start.16 = (f32[72,256]{1,0:T(8,128)S(1)}, f32[72,256]{1,0:T(8,128)S(1)}, u32[]{:S(2)}, u32[]{:S(2)}) collective-permute-start(f32[72,256]{1,0:T(8,128)S(1)} %get-tuple-element.41), channel_id=1, source_target_pairs={{0,1},{1,0},{2,3},{3,2},{4,5},{5,4},{6,7},{7,6},{8,24},{9,25},{10,... | collective-permute-start | bytes 221192 | tf_op jit(solution)/shard_map/ppermute | solution.py:29
  56.5 6.5 %collective-permute-start.18 = (f32[200,256]{1,0:T(8,128)S(1)}, f32[200,256]{1,0:T(8,128)S(1)}, u32[]{:S(2)}, u32[]{:S(2)}) collective-permute-start(f32[200,256]{1,0:T(8,128)S(1)} %get-tuple-element.43), channel_id=1, source_target_pairs={{0,1},{1,0},{2,3},{3,2},{4,5},{5,4},{6,7},{7,6},{8,24},{9,25},{10,... | collective-permute-start | bytes 614408 | tf_op jit(solution)/shard_map/ppermute | solution.py:29
  59.6 1.3 %collective-permute-start.17 = (f32[72,256]{1,0:T(8,128)S(1)}, f32[72,256]{1,0:T(8,128)S(1)}, u32[]{:S(2)}, u32[]{:S(2)}) collective-permute-start(f32[72,256]{1,0:T(8,128)S(1)} %collective-permute-done.16.near_ref), channel_id=1, source_target_pairs={{0,1},{1,0},{2,3},{3,2},{4,5},{5,4},{6,7},{7,6},{8,9},{9,8},{10,11... | collective-permute-start | bytes 221192 | tf_op jit(solution)/shard_map/ppermute | solution.py:21
  59.8 3.5 %collective-permute-start.20 = (f32[336,256]{1,0:T(8,128)S(1)}, f32[336,256]{1,0:T(8,128)S(1)}, u32[]{:S(2)}, u32[]{:S(2)}) collective-permute-start(f32[336,256]{1,0:T(8,128)S(1)} %collective-permute-done.11.near_early), channel_id=1, source_target_pairs={{0,1},{1,0},{2,3},{3,2},{4,5},{5,4},{6,7},{7,6},{8,9},{9,8},{10,11... | collective-permute-start | bytes 1032200 | tf_op jit(solution)/shard_map/ppermute | solution.py:21
  63.0 1.5 %collective-permute-start.19 = (f32[200,256]{1,0:T(8,128)S(1)}, f32[200,256]{1,0:T(8,128)S(1)}, u32[]{:S(2)}, u32[]{:S(2)}) collective-permute-start(f32[200,256]{1,0:T(8,128)S(1)} %collective-permute-done.18.near_ref), channel_id=1, source_target_pairs={{0,1},{1,0},{2,3},{3,2},{4,5},{5,4},{6,7},{7,6},{8,9},{9,8},{10,11... | collective-permute-start | bytes 614408 | tf_op jit(solution)/shard_map/ppermute | solution.py:21

commit v3 on v1

--- a/solution.py
+++ b/solution.py
@@ -19,6 +19,14 @@
 def swap(block, distance):
     count = lax.axis_size(AXES)
     return lax.ppermute(block, AXES, [(i, i ^ distance) for i in range(count)])
+
+
+def pair(block, first, second):
+    count = lax.axis_size(AXES)
+    quarter = count // 4
+    shift = (second - first) * quarter
+    step = {first: lambda i: i + shift, second: lambda i: i - shift}
+    return lax.ppermute(block, AXES, [(i, step.get(i // quarter, lambda i: i ^ 1)(i)) for i in range(count)])
 
 
 def split(x):
@@ -121,21 +129,19 @@
     return joined(near_ref, far_ref, core, 0, h), unpack_symmetric(near_ref, far_ref, core, h)
 
 
-def send_total(own_side, other_side, trans, same, core, own_ref, first_ref, second_ref):
+def send_total(own_side, other_side, trans, same, core, first_ref, second_ref, own_ref):
     turned = trans.T
     near = jnp.where(same, other_side, own_side)
     away = jnp.where(same, own_side, other_side)
-    h = trans.shape[0] // 2
     back = jnp.where(same, turned, trans)
     own_ref[0] = near
     own_ref[1] = away
     own_ref[2] = jnp.where(same, trans, turned)
     pack_symmetric(near, core, first_ref, 0)
-    second_ref[0:h, :] = jnp.where(core, back[h:], back[:h])
-    pack_symmetric(away, core, second_ref, h)
-
-
-def first_kernel(section_ref, got1, got2, got3, own_ref, prefix_ref, first_ref, second_ref):
+    pack_second(back, away, core, second_ref)
+
+
+def first_kernel(section_ref, got1, got2, got3, prefix_ref, *send_refs):
     me = place()
     upper = bit(me, 1)
     left, right, trans = section_ref[0], section_ref[1], section_ref[2]
@@ -144,26 +150,42 @@
     leading, mirror, own_side = before_trans(own, pick(got2[0], got1[0]))
     into = pick(got3[0], got3[0].T)
     through, other_side = after_trans(leading, mirror, pick(got1[0], got2[0]), into)
-    send_total(own_side, other_side, through, upper == bit(me, 2), upper, own_ref, first_ref, second_ref)
+    send_total(own_side, other_side, through, upper == bit(me, 2), upper, *send_refs)
     prefix_ref[0] = pick(other_side, left)
     prefix_ref[1] = pick(own_side, right)
     prefix_ref[2] = pick(through, trans)
 
 
-def early_kernel(own_ref, near_ref, far_ref, half_ref):
+def early_kernel(own_ref, near_ref, far_ref, half_ref, *first_ref):
     core = bit(place(), 1)
     facing = unpack_symmetric(near_ref, far_ref, core, 0)
-    for i, x in enumerate(before_trans((own_ref[0], own_ref[1], own_ref[2]), facing)):
+    half = before_trans((own_ref[0], own_ref[1], own_ref[2]), facing)
+    for ref in first_ref:
+        pack_symmetric(half[2], core, ref, 0)
+    for i, x in enumerate(half):
         half_ref[i] = x
 
 
-def late_kernel(distance, half_ref, near_ref, far_ref, own_ref, first_ref, second_ref):
+def final_kernel(half_ref, near_ref, far_ref, second_ref):
+    core = bit(place(), 1)
+    into, away = unpack_second(near_ref, far_ref, core)
+    trans, other_side = after_trans(half_ref[0], half_ref[1], away, into)
+    pack_second(trans, other_side, core, second_ref)
+
+
+def pack_second(back, away, core, ref):
+    h = back.shape[0] // 2
+    ref[0:h, :] = jnp.where(core, back[h:], back[:h])
+    pack_symmetric(away, core, ref, h)
+
+
+def late_kernel(distance, half_ref, near_ref, far_ref, *send_refs):
     me = place()
     core = bit(me, 1)
     into, away = unpack_second(near_ref, far_ref, core)
     trans, other_side = after_trans(half_ref[0], half_ref[1], away, into)
     same = bit(me, distance) == bit(me, 2 * distance)
-    send_total(half_ref[2], other_side, trans, same, core, own_ref, first_ref, second_ref)
+    send_total(half_ref[2], other_side, trans, same, core, *send_refs)
 
 
 def prefix_kernel(distance, old_ref, near1, far1, near2, far2, new_ref):
@@ -177,10 +199,22 @@
         new_ref[i] = jnp.where(upper, x, old_ref[i])
 
 
-def last_kernel(distance, old_ref, half_ref, near_ref, far_ref, left_ref, right_ref, trans_ref):
-    me = place()
-    core, upper = bit(me, 1), bit(me, distance)
-    into, away = unpack_second(near_ref, far_ref, core)
+def by_third(distance, me, near2, far2, near3, far3):
+    third = bit(me, distance // 2)
+    return jnp.where(third, near3[...], near2[...]), jnp.where(third, far3[...], far2[...])
+
+
+def last_early_kernel(distance, own_ref, near2, far2, near3, far3, half_ref):
+    me = place()
+    facing = unpack_symmetric(*by_third(distance, me, near2, far2, near3, far3), bit(me, 1), 0)
+    for i, x in enumerate(before_trans((own_ref[0], own_ref[1], own_ref[2]), facing)):
+        half_ref[i] = x
+
+
+def last_kernel(distance, old_ref, half_ref, near2, far2, near3, far3, left_ref, right_ref, trans_ref):
+    me = place()
+    upper = bit(me, distance)
+    into, away = unpack_second(*by_third(distance, me, near2, far2, near3, far3), bit(me, 1))
     trans, left = after_trans(half_ref[0], half_ref[1], away, into)
     right_ref[0] = jnp.where(upper, half_ref[2], old_ref[1])
     trans_ref[0] = jnp.where(upper, trans, old_ref[2])
@@ -208,9 +242,9 @@
     sections = refl_left, refl_right, trans
     got = [swap(x, 1) for x in sections]
     section = jnp.concatenate(sections, 0)
-    own, prefix, send1, send2 = call(first_kernel, 36, [stack, stack, first, second], section, *got)
+    prefix, send1, send2, own = call(first_kernel, 36, [stack, first, second, stack], section, *got)
     pending = None
-    for level in range(1, levels):
+    for level in range(1, levels - 1):
         distance = 1 << level
         bind = lambda kernel: functools.partial(kernel, distance)
         near1, near2 = swap(send1, distance), swap(send2, distance)
@@ -218,16 +252,26 @@
             (prefix,) = pending(prefix)
             near1, prefix = lax.optimization_barrier((near1, prefix))
         far1 = swap(near1, 1)
-        if level == levels - 1:
-            (halfway,) = call(early_kernel, 27, [stack], prefix, near1, far1)
-            near2, halfway = lax.optimization_barrier((near2, halfway))
-            far2 = swap(near2, 1)
-            return tuple(call(bind(last_kernel), 9, [(1, m, m)] * 3, prefix, halfway, near2, far2))
-        (halfway,) = call(early_kernel, 27, [stack], own, near1, far1)
+        outs = [stack] + [first] * (level == levels - 2)
+        halfway, *sends = call(early_kernel, 27, outs, own, near1, far1)
         near2, halfway = lax.optimization_barrier((near2, halfway))
         far2 = swap(near2, 1)
-        own, send1, send2 = call(bind(late_kernel), 9, [stack, first, second], halfway, near2, far2)
         pending = lambda old, kernel=bind(prefix_kernel), got=(near1, far1, near2, far2): call(kernel, 36, [stack], old, *got)
+        if level < levels - 2:
+            send1, send2, own = call(bind(late_kernel), 9, [first, second, stack], halfway, near2, far2)
+
+    distance *= 2
+    (send1,) = sends
+    first3, first2 = pair(send1, 1, 3), pair(send1, 1, 2)
+    (send2,) = call(final_kernel, 9, [second], halfway, near2, far2)
+    near3, near2 = pair(send2, 1, 3), pair(send2, 1, 2)
+    first3, first2, prefix = lax.optimization_barrier((first3, first2, prefix))
+    (prefix,) = pending(prefix)
+    args = prefix, first2, swap(first2, 1), first3, swap(first3, 1)
+    (halfway,) = call(functools.partial(last_early_kernel, distance), 27, [stack], *args)
+    near2, near3, halfway = lax.optimization_barrier((near2, near3, halfway))
+    args = prefix, halfway, near2, swap(near2, 1), near3, swap(near3, 1)
+    return tuple(call(functools.partial(last_kernel, distance), 9, [(1, m, m)] * 3, *args))
 
 
 def solution(mesh):

time: 59.6 us -> 56.1 us (0.941)
  the two profiles are of different devices: /device:TPU:0 before, /device:TPU:17 now
where the time goes in v3:
time: 56.1 us; the launch traced here: 55.2 us
  Pallas kernels  22.1 us (39%)
  starting transfers between devices  18.9 us (34%)
  waiting for transfers between devices  12.2 us (22%)
  other arithmetic  1.16 us (2%)
  between operations  0.8 us (1%)
    pallas_call x12, Pallas kernels, call(): pl.pallas_call(kernel, out_shape=[jax.ShapeDtypeStruct(s, F32) for s in o...  22.1 us
    ppermute x19, starting transfers between devices, swap(): return lax.ppermute(block, AXES, [(i, i ^ distance) for i in range(count)])  15.7 us
    ppermute x19, waiting for transfers between devices, swap(): return lax.ppermute(block, AXES, [(i, i ^ distance) for i in range(count)])  9.18 us
    ppermute x4, starting transfers between devices, pair(): lax.ppermute(block, AXES, [(i, step.get(i // quarter, lambda i: i ^ 1)(i)...  3.22 us
    ppermute x4, waiting for transfers between devices, pair(): lax.ppermute(block, AXES, [(i, step.get(i // quarter, lambda i: i ^ 1)(i)...  2.99 us
    concatenate x1, other arithmetic, shards(): section = jnp.concatenate(sections, 0)  1.16 us
  transfers between devices with their start and end apart: 23, of which 12 were waited for; matrix products, arithmetic and copies ran while one was open for 2% of the time, Pallas kernels for 30%

profile of v3, /device:TPU:17, one launch (start us, length us, event | category | flops | bytes accessed | tf_op | source)
XLA Modules:
  0.0 55.2 jit_solution(4609971459559604861)
XLA Ops:
  0.6 0.7 %collective-permute-start = (f32[1,256,256]{2,1,0:T(8,128)}, f32[1,256,256]{2,1,0:T(8,128)S(1)}, u32[]{:S(2)}, u32[]{:S(2)}) collective-permute-start(f32[1,256,256]{2,1,0:T(8,128)} %param.3), channel_id=1, source_target_pairs={{0,1},{1,0},{2,3},{3,2},{4,5},{5,4},{6,7},{7,6},{8,9},{9,8},{10,11... | collective-permute-start | bytes 786440 | tf_op jit(solution)/shard_map/ppermute | solution.py:21
  1.9 1.2 %pad_maximum_fusion.section_ref = f32[3,256,256]{2,1,0:T(8,128)S(1)} fusion(f32[1,256,256]{2,1,0:T(8,128)} %param.5, f32[1,256,256]{2,1,0:T(8,128)} %param.4, f32[1,256,256]{2,1,0:T(8,128)} %param.3), kind=kLoop, calls=%fused_computation | loop fusion | flops 393216 | bytes 1572864 | tf_op jit(solution)/shard_map/concatenate | solution.py:244
  3.5 2.6 %shard_map.58 = (f32[3,256,256]{2,1,0:T(8,128)S(1)}, f32[72,256]{1,0:T(8,128)S(1)}, f32[200,256]{1,0:T(8,128)S(1)}, f32[3,256,256]{2,1,0:T(8,128)S(1)}) custom-call(f32[3,256,256]{2,1,0:T(8,128)S(1)} %pad_maximum_fusion.section_ref, f32[1,256,256]{2,1,0:T(8,128)S(1)} %collective-permute-done.got1, f32[1,256,256]{2,1,0:T(8,128)S(1)} %collective-permute-done.1.got2, ...), custom_call_target="tpu_custom_call" | custom-call | flops 1207959552 | bytes 1048576 | tf_op jit(solution)/shard_map/pallas_call | solution.py:227
  6.1 1.3 %collective-permute-start.4 = (f32[72,256]{1,0:T(8,128)S(1)}, f32[72,256]{1,0:T(8,128)S(1)}, u32[]{:S(2)}, u32[]{:S(2)}) collective-permute-start(f32[72,256]{1,0:T(8,128)S(1)} %get-tuple-element.33), channel_id=1, source_target_pairs={{0,2},{1,3},{2,0},{3,1},{4,6},{5,7},{6,4},{7,5},{8,10},{9,11},{10,... | collective-permute-start | bytes 221192 | tf_op jit(solution)/shard_map/ppermute | solution.py:21
  7.7 1.7 %collective-permute-done.4.near_ref.near1 = f32[72,256]{1,0:T(8,128)S(1)} collective-permute-done((f32[72,256]{1,0:T(8,128)S(1)}, f32[72,256]{1,0:T(8,128)S(1)}, u32[]{:S(2)}, u32[]{:S(2)}) %collective-permute-start.4) | collective-permute-done | bytes 73760 | tf_op jit(solution)/shard_map/ppermute | solution.py:21
  9.4 2.0 %collective-permute-start.5 = (f32[72,256]{1,0:T(8,128)S(1)}, f32[72,256]{1,0:T(8,128)S(1)}, u32[]{:S(2)}, u32[]{:S(2)}) collective-permute-start(f32[72,256]{1,0:T(8,128)S(1)} %collective-permute-done.4.near_ref.near1), channel_id=1, source_target_pairs={{0,1},{1,0},{2,3},{3,2},{4,5},{5,4},{6,7},{7,6},{8,9},{9,8},{10,11... | collective-permute-start | bytes 221192 | tf_op jit(solution)/shard_map/ppermute | solution.py:21
  11.4 0.9 %collective-permute-done.5.far_ref.far1 = f32[72,256]{1,0:T(8,128)S(1)} collective-permute-done((f32[72,256]{1,0:T(8,128)S(1)}, f32[72,256]{1,0:T(8,128)S(1)}, u32[]{:S(2)}, u32[]{:S(2)}) %collective-permute-start.5) | collective-permute-done | bytes 73760 | tf_op jit(solution)/shard_map/ppermute | solution.py:21
  12.3 2.1 %shard_map.59.half_ref = f32[3,256,256]{2,1,0:T(8,128)S(1)} custom-call(f32[3,256,256]{2,1,0:T(8,128)S(1)} %get-tuple-element.32.own_ref, f32[72,256]{1,0:T(8,128)S(1)} %collective-permute-done.4.near_ref.near1, f32[72,256]{1,0:T(8,128)S(1)} %collective-permute-done.5.far_ref.far1), custom_call_target="tpu_custom_call" | custom-call | flops 905969664 | bytes 786432 | tf_op jit(solution)/shard_map/pallas_call | solution.py:227
  14.4 0.9 %collective-permute-start.6 = (f32[200,256]{1,0:T(8,128)S(1)}, f32[200,256]{1,0:T(8,128)S(1)}, u32[]{:S(2)}, u32[]{:S(2)}) collective-permute-start(f32[200,256]{1,0:T(8,128)S(1)} %collective-permute-done.3.near_ref.near2), channel_id=1, source_target_pairs={{0,1},{1,0},{2,3},{3,2},{4,5},{5,4},{6,7},{7,6},{8,9},{9,8},{10,11... | collective-permute-start | bytes 614408 | tf_op jit(solution)/shard_map/ppermute | solution.py:21
  15.3 1.1 %collective-permute-done.6.far_ref.far2 = f32[200,256]{1,0:T(8,128)S(1)} collective-permute-done((f32[200,256]{1,0:T(8,128)S(1)}, f32[200,256]{1,0:T(8,128)S(1)}, u32[]{:S(2)}, u32[]{:S(2)}) %collective-permute-start.6) | collective-permute-done | bytes 204832 | tf_op jit(solution)/shard_map/ppermute | solution.py:21
  16.4 0.7 %shard_map.60 = (f32[72,256]{1,0:T(8,128)S(1)}, f32[200,256]{1,0:T(8,128)S(1)}, f32[3,256,256]{2,1,0:T(8,128)S(1)}) custom-call(f32[3,256,256]{2,1,0:T(8,128)S(1)} %shard_map.59.half_ref, f32[200,256]{1,0:T(8,128)S(1)} %collective-permute-done.3.near_ref.near2, f32[200,256]{1,0:T(8,128)S(1)} %collective-permute-done.6.far_ref.far2), custom_call_target="tpu_custom_call" | custom-call | flops 301989888 | bytes 786432 | tf_op jit(solution)/shard_map/pallas_call | solution.py:227
  17.1 1.3 %collective-permute-start.8 = (f32[72,256]{1,0:T(8,128)S(1)}, f32[72,256]{1,0:T(8,128)S(1)}, u32[]{:S(2)}, u32[]{:S(2)}) collective-permute-start(f32[72,256]{1,0:T(8,128)S(1)} %get-tuple-element.38), channel_id=1, source_target_pairs={{0,4},{1,5},{2,6},{3,7},{4,0},{5,1},{6,2},{7,3},{8,12},{9,13},{10,... | collective-permute-start | bytes 221192 | tf_op jit(solution)/shard_map/ppermute | solution.py:21
  18.6 2.6 %shard_map.61.old_ref = f32[3,256,256]{2,1,0:T(8,128)S(1)} custom-call(f32[3,256,256]{2,1,0:T(8,128)S(1)} %get-tuple-element.39.old_ref, f32[72,256]{1,0:T(8,128)S(1)} %collective-permute-done.4.near_ref.near1, f32[72,256]{1,0:T(8,128)S(1)} %collective-permute-done.5.far_ref.far1, f32[200,256]{1,0:T(8,128)S(1)} %collective-permute-done.3.near_ref.near2, ...), custom_call_target="tpu_custom_call" | custom-call | flops 1207959552 | bytes 1310720 | tf_op jit(solution)/shard_map/pallas_call | solution.py:227
  21.2 1.2 %collective-permute-start.9 = (f32[72,256]{1,0:T(8,128)S(1)}, f32[72,256]{1,0:T(8,128)S(1)}, u32[]{:S(2)}, u32[]{:S(2)}) collective-permute-start(f32[72,256]{1,0:T(8,128)S(1)} %collective-permute-done.8.near_ref.near1), channel_id=1, source_target_pairs={{0,1},{1,0},{2,3},{3,2},{4,5},{5,4},{6,7},{7,6},{8,9},{9,8},{10,11... | collective-permute-start | bytes 221192 | tf_op jit(solution)/shard_map/ppermute | solution.py:21
  22.3 0.9 %collective-permute-done.9.far_ref.far1 = f32[72,256]{1,0:T(8,128)S(1)} collective-permute-done((f32[72,256]{1,0:T(8,128)S(1)}, f32[72,256]{1,0:T(8,128)S(1)}, u32[]{:S(2)}, u32[]{:S(2)}) %collective-permute-start.9) | collective-permute-done | bytes 73760 | tf_op jit(solution)/shard_map/ppermute | solution.py:21
  23.2 2.1 %shard_map.62.half_ref = f32[3,256,256]{2,1,0:T(8,128)S(1)} custom-call(f32[3,256,256]{2,1,0:T(8,128)S(1)} %get-tuple-element.37.own_ref, f32[72,256]{1,0:T(8,128)S(1)} %collective-permute-done.8.near_ref.near1, f32[72,256]{1,0:T(8,128)S(1)} %collective-permute-done.9.far_ref.far1), custom_call_target="tpu_custom_call" | custom-call | flops 905969664 | bytes 786432 | tf_op jit(solution)/shard_map/pallas_call | solution.py:227
  25.3 0.9 %collective-permute-start.10 = (f32[200,256]{1,0:T(8,128)S(1)}, f32[200,256]{1,0:T(8,128)S(1)}, u32[]{:S(2)}, u32[]{:S(2)}) collective-permute-start(f32[200,256]{1,0:T(8,128)S(1)} %collective-permute-done.7.near_ref.near2), channel_id=1, source_target_pairs={{0,1},{1,0},{2,3},{3,2},{4,5},{5,4},{6,7},{7,6},{8,9},{9,8},{10,11... | collective-permute-start | bytes 614408 | tf_op jit(solution)/shard_map/ppermute | solution.py:21
  26.3 1.1 %collective-permute-done.10.far_ref.far2 = f32[200,256]{1,0:T(8,128)S(1)} collective-permute-done((f32[200,256]{1,0:T(8,128)S(1)}, f32[200,256]{1,0:T(8,128)S(1)}, u32[]{:S(2)}, u32[]{:S(2)}) %collective-permute-start.10) | collective-permute-done | bytes 204832 | tf_op jit(solution)/shard_map/ppermute | solution.py:21
  28.1 1.4 %collective-permute-start.11 = (f32[72,256]{1,0:T(8,128)S(1)}, f32[72,256]{1,0:T(8,128)S(1)}, u32[]{:S(2)}, u32[]{:S(2)}) collective-permute-start(f32[72,256]{1,0:T(8,128)S(1)} %get-tuple-element.44), channel_id=1, source_target_pairs={{0,8},{1,9},{2,10},{3,11},{4,12},{5,13},{6,14},{7,15},{8,0},{9,1},... | collective-permute-start | bytes 221192 | tf_op jit(solution)/shard_map/ppermute | solution.py:21
  29.6 2.6 %shard_map.64.old_ref = f32[3,256,256]{2,1,0:T(8,128)S(1)} custom-call(f32[3,256,256]{2,1,0:T(8,128)S(1)} %shard_map.61.old_ref, f32[72,256]{1,0:T(8,128)S(1)} %collective-permute-done.8.near_ref.near1, f32[72,256]{1,0:T(8,128)S(1)} %collective-permute-done.9.far_ref.far1, f32[200,256]{1,0:T(8,128)S(1)} %collective-permute-done.7.near_ref.near2, ...), custom_call_target="tpu_custom_call" | custom-call | flops 1207959552 | bytes 1310720 | tf_op jit(solution)/shard_map/pallas_call | solution.py:227
  32.2 1.1 %collective-permute-start.12 = (f32[72,256]{1,0:T(8,128)S(1)}, f32[72,256]{1,0:T(8,128)S(1)}, u32[]{:S(2)}, u32[]{:S(2)}) collective-permute-start(f32[72,256]{1,0:T(8,128)S(1)} %collective-permute-done.11.near_ref.near1), channel_id=1, source_target_pairs={{0,1},{1,0},{2,3},{3,2},{4,5},{5,4},{6,7},{7,6},{8,9},{9,8},{10,11... | collective-permute-start | bytes 221192 | tf_op jit(solution)/shard_map/ppermute | solution.py:21
  33.2 0.9 %collective-permute-done.12.far_ref.far1 = f32[72,256]{1,0:T(8,128)S(1)} collective-permute-done((f32[72,256]{1,0:T(8,128)S(1)}, f32[72,256]{1,0:T(8,128)S(1)}, u32[]{:S(2)}, u32[]{:S(2)}) %collective-permute-start.12) | collective-permute-done | bytes 73760 | tf_op jit(solution)/shard_map/ppermute | solution.py:21
  34.2 2.1 %shard_map.65 = (f32[3,256,256]{2,1,0:T(8,128)S(1)}, f32[72,256]{1,0:T(8,128)S(1)}) custom-call(f32[3,256,256]{2,1,0:T(8,128)S(1)} %get-tuple-element.43.own_ref, f32[72,256]{1,0:T(8,128)S(1)} %collective-permute-done.11.near_ref.near1, f32[72,256]{1,0:T(8,128)S(1)} %collective-permute-done.12.far_ref.far1), custom_call_target="tpu_custom_call" | custom-call | flops 905969664 | bytes 786432 | tf_op jit(solution)/shard_map/pallas_call | solution.py:227
  36.3 1.0 %collective-permute-start.16 = (f32[200,256]{1,0:T(8,128)S(1)}, f32[200,256]{1,0:T(8,128)S(1)}, u32[]{:S(2)}, u32[]{:S(2)}) collective-permute-start(f32[200,256]{1,0:T(8,128)S(1)} %collective-permute-done.15.near2.near_ref), channel_id=1, source_target_pairs={{0,1},{1,0},{2,3},{3,2},{4,5},{5,4},{6,7},{7,6},{8,9},{9,8},{10,11... | collective-permute-start | bytes 614408 | tf_op jit(solution)/shard_map/ppermute | solution.py:21
  39.4 2.4 %collective-permute-start.17 = (f32[200,256]{1,0:T(8,128)S(1)}, f32[200,256]{1,0:T(8,128)S(1)}, u32[]{:S(2)}, u32[]{:S(2)}) collective-permute-start(f32[200,256]{1,0:T(8,128)S(1)} %shard_map.67), channel_id=1, source_target_pairs={{0,1},{1,0},{2,3},{3,2},{4,5},{5,4},{6,7},{7,6},{8,16},{9,17},{10,... | collective-permute-start | bytes 614408 | tf_op jit(solution)/shard_map/ppermute | solution.py:29
  41.8 1.1 %collective-permute-start.19 = (f32[72,256]{1,0:T(8,128)S(1)}, f32[72,256]{1,0:T(8,128)S(1)}, u32[]{:S(2)}, u32[]{:S(2)}) collective-permute-start(f32[72,256]{1,0:T(8,128)S(1)} %collective-permute-done.14.near2), channel_id=1, source_target_pairs={{0,1},{1,0},{2,3},{3,2},{4,5},{5,4},{6,7},{7,6},{8,9},{9,8},{10,11... | collective-permute-start | bytes 221192 | tf_op jit(solution)/shard_map/ppermute | solution.py:21
  43.2 2.6 %shard_map.66.own_ref.old_ref = f32[3,256,256]{2,1,0:T(8,128)S(1)} custom-call(f32[3,256,256]{2,1,0:T(8,128)S(1)} %shard_map.64.old_ref, f32[72,256]{1,0:T(8,128)S(1)} %collective-permute-done.11.near_ref.near1, f32[72,256]{1,0:T(8,128)S(1)} %collective-permute-done.12.far_ref.far1, f32[200,256]{1,0:T(8,128)S(1)} %collective-permute-done.15.near2.near_ref, ...), custom_call_target="tpu_custom_call" | custom-call | flops 1207959552 | bytes 1310720 | tf_op jit(solution)/shard_map/pallas_call | solution.py:227
  45.8 2.1 %shard_map.68.half_ref = f32[3,256,256]{2,1,0:T(8,128)S(1)} custom-call(f32[3,256,256]{2,1,0:T(8,128)S(1)} %shard_map.66.own_ref.old_ref, f32[72,256]{1,0:T(8,128)S(1)} %collective-permute-done.14.near2, f32[72,256]{1,0:T(8,128)S(1)} %collective-permute-done.19.far2, f32[72,256]{1,0:T(8,128)S(1)} %collective-permute-done.13.near3, ...), custom_call_target="tpu_custom_call" | custom-call | flops 905969664 | bytes 1310720 | tf_op jit(solution)/shard_map/pallas_call | solution.py:227
  47.9 3.0 %collective-permute-done.17.near2 = f32[200,256]{1,0:T(8,128)S(1)} collective-permute-done((f32[200,256]{1,0:T(8,128)S(1)}, f32[200,256]{1,0:T(8,128)S(1)}, u32[]{:S(2)}, u32[]{:S(2)}) %collective-permute-start.17) | collective-permute-done | bytes 204832 | tf_op jit(solution)/shard_map/ppermute | solution.py:29
  50.9 1.4 %collective-permute-start.21 = (f32[200,256]{1,0:T(8,128)S(1)}, f32[200,256]{1,0:T(8,128)S(1)}, u32[]{:S(2)}, u32[]{:S(2)}) collective-permute-start(f32[200,256]{1,0:T(8,128)S(1)} %collective-permute-done.17.near2), channel_id=1, source_target_pairs={{0,1},{1,0},{2,3},{3,2},{4,5},{5,4},{6,7},{7,6},{8,9},{9,8},{10,11... | collective-permute-start | bytes 614408 | tf_op jit(solution)/shard_map/ppermute | solution.py:21
  52.3 1.1 %collective-permute-done.21.far2 = f32[200,256]{1,0:T(8,128)S(1)} collective-permute-done((f32[200,256]{1,0:T(8,128)S(1)}, f32[200,256]{1,0:T(8,128)S(1)}, u32[]{:S(2)}, u32[]{:S(2)}) %collective-permute-start.21) | collective-permute-done | bytes 204832 | tf_op jit(solution)/shard_map/ppermute | solution.py:21
  53.7 1.4 %shard_map.69 = (f32[1,256,256]{2,1,0:T(8,128)}, f32[1,256,256]{2,1,0:T(8,128)}, f32[1,256,256]{2,1,0:T(8,128)}) custom-call(f32[3,256,256]{2,1,0:T(8,128)S(1)} %shard_map.66.own_ref.old_ref, f32[3,256,256]{2,1,0:T(8,128)S(1)} %shard_map.68.half_ref, f32[200,256]{1,0:T(8,128)S(1)} %collective-permute-done.17.near2, ...), custom_call_target="tpu_custom_call" | custom-call | flops 301989888 | bytes 1572864 | tf_op jit(solution)/shard_map/pallas_call | solution.py:227
  (27 shorter events, 5.2 us)
Async XLA Ops:
  0.6 2.4 %collective-permute-start = (f32[1,256,256]{2,1,0:T(8,128)}, f32[1,256,256]{2,1,0:T(8,128)S(1)}, u32[]{:S(2)}, u32[]{:S(2)}) collective-permute-start(f32[1,256,256]{2,1,0:T(8,128)} %param.3), channel_id=1, source_target_pairs={{0,1},{1,0},{2,3},{3,2},{4,5},{5,4},{6,7},{7,6},{8,9},{9,8},{10,11... | collective-permute-start | bytes 786440 | tf_op jit(solution)/shard_map/ppermute | solution.py:21
  1.4 1.7 %collective-permute-start.1 = (f32[1,256,256]{2,1,0:T(8,128)}, f32[1,256,256]{2,1,0:T(8,128)S(1)}, u32[]{:S(2)}, u32[]{:S(2)}) collective-permute-start(f32[1,256,256]{2,1,0:T(8,128)} %param.4), channel_id=1, source_target_pairs={{0,1},{1,0},{2,3},{3,2},{4,5},{5,4},{6,7},{7,6},{8,9},{9,8},{10,11... | collective-permute-start | bytes 786440 | tf_op jit(solution)/shard_map/ppermute | solution.py:21
  1.4 2.0 %collective-permute-start.2 = (f32[1,256,256]{2,1,0:T(8,128)}, f32[1,256,256]{2,1,0:T(8,128)S(1)}, u32[]{:S(2)}, u32[]{:S(2)}) collective-permute-start(f32[1,256,256]{2,1,0:T(8,128)} %param.5), channel_id=1, source_target_pairs={{0,1},{1,0},{2,3},{3,2},{4,5},{5,4},{6,7},{7,6},{8,9},{9,8},{10,11... | collective-permute-start | bytes 786440 | tf_op jit(solution)/shard_map/ppermute | solution.py:21
  6.1 3.3 %collective-permute-start.4 = (f32[72,256]{1,0:T(8,128)S(1)}, f32[72,256]{1,0:T(8,128)S(1)}, u32[]{:S(2)}, u32[]{:S(2)}) collective-permute-start(f32[72,256]{1,0:T(8,128)S(1)} %get-tuple-element.33), channel_id=1, source_target_pairs={{0,2},{1,3},{2,0},{3,1},{4,6},{5,7},{6,4},{7,5},{8,10},{9,11},{10,... | collective-permute-start | bytes 221192 | tf_op jit(solution)/shard_map/ppermute | solution.py:21
  7.4 7.0 %collective-permute-start.3 = (f32[200,256]{1,0:T(8,128)S(1)}, f32[200,256]{1,0:T(8,128)S(1)}, u32[]{:S(2)}, u32[]{:S(2)}) collective-permute-start(f32[200,256]{1,0:T(8,128)S(1)} %get-tuple-element.31), channel_id=1, source_target_pairs={{0,2},{1,3},{2,0},{3,1},{4,6},{5,7},{6,4},{7,5},{8,10},{9,11},{10,... | collective-permute-start | bytes 614408 | tf_op jit(solution)/shard_map/ppermute | solution.py:21
  9.4 2.9 %collective-permute-start.5 = (f32[72,256]{1,0:T(8,128)S(1)}, f32[72,256]{1,0:T(8,128)S(1)}, u32[]{:S(2)}, u32[]{:S(2)}) collective-permute-start(f32[72,256]{1,0:T(8,128)S(1)} %collective-permute-done.4.near_ref.near1), channel_id=1, source_target_pairs={{0,1},{1,0},{2,3},{3,2},{4,5},{5,4},{6,7},{7,6},{8,9},{9,8},{10,11... | collective-permute-start | bytes 221192 | tf_op jit(solution)/shard_map/ppermute | solution.py:21
  14.4 2.0 %collective-permute-start.6 = (f32[200,256]{1,0:T(8,128)S(1)}, f32[200,256]{1,0:T(8,128)S(1)}, u32[]{:S(2)}, u32[]{:S(2)}) collective-permute-start(f32[200,256]{1,0:T(8,128)S(1)} %collective-permute-done.3.near_ref.near2), channel_id=1, source_target_pairs={{0,1},{1,0},{2,3},{3,2},{4,5},{5,4},{6,7},{7,6},{8,9},{9,8},{10,11... | collective-permute-start | bytes 614408 | tf_op jit(solution)/shard_map/ppermute | solution.py:21
  17.1 4.1 %collective-permute-start.8 = (f32[72,256]{1,0:T(8,128)S(1)}, f32[72,256]{1,0:T(8,128)S(1)}, u32[]{:S(2)}, u32[]{:S(2)}) collective-permute-start(f32[72,256]{1,0:T(8,128)S(1)} %get-tuple-element.38), channel_id=1, source_target_pairs={{0,4},{1,5},{2,6},{3,7},{4,0},{5,1},{6,2},{7,3},{8,12},{9,13},{10,... | collective-permute-start | bytes 221192 | tf_op jit(solution)/shard_map/ppermute | solution.py:21
  18.4 6.9 %collective-permute-start.7 = (f32[200,256]{1,0:T(8,128)S(1)}, f32[200,256]{1,0:T(8,128)S(1)}, u32[]{:S(2)}, u32[]{:S(2)}) collective-permute-start(f32[200,256]{1,0:T(8,128)S(1)} %get-tuple-element.36), channel_id=1, source_target_pairs={{0,4},{1,5},{2,6},{3,7},{4,0},{5,1},{6,2},{7,3},{8,12},{9,13},{10,... | collective-permute-start | bytes 614408 | tf_op jit(solution)/shard_map/ppermute | solution.py:21
  21.2 2.1 %collective-permute-start.9 = (f32[72,256]{1,0:T(8,128)S(1)}, f32[72,256]{1,0:T(8,128)S(1)}, u32[]{:S(2)}, u32[]{:S(2)}) collective-permute-start(f32[72,256]{1,0:T(8,128)S(1)} %collective-permute-done.8.near_ref.near1), channel_id=1, source_target_pairs={{0,1},{1,0},{2,3},{3,2},{4,5},{5,4},{6,7},{7,6},{8,9},{9,8},{10,11... | collective-permute-start | bytes 221192 | tf_op jit(solution)/shard_map/ppermute | solution.py:21
  25.3 2.0 %collective-permute-start.10 = (f32[200,256]{1,0:T(8,128)S(1)}, f32[200,256]{1,0:T(8,128)S(1)}, u32[]{:S(2)}, u32[]{:S(2)}) collective-permute-start(f32[200,256]{1,0:T(8,128)S(1)} %collective-permute-done.7.near_ref.near2), channel_id=1, source_target_pairs={{0,1},{1,0},{2,3},{3,2},{4,5},{5,4},{6,7},{7,6},{8,9},{9,8},{10,11... | collective-permute-start | bytes 614408 | tf_op jit(solution)/shard_map/ppermute | solution.py:21
  28.1 4.1 %collective-permute-start.11 = (f32[72,256]{1,0:T(8,128)S(1)}, f32[72,256]{1,0:T(8,128)S(1)}, u32[]{:S(2)}, u32[]{:S(2)}) collective-permute-start(f32[72,256]{1,0:T(8,128)S(1)} %get-tuple-element.44), channel_id=1, source_target_pairs={{0,8},{1,9},{2,10},{3,11},{4,12},{5,13},{6,14},{7,15},{8,0},{9,1},... | collective-permute-start | bytes 221192 | tf_op jit(solution)/shard_map/ppermute | solution.py:21
  29.4 6.8 %collective-permute-start.15 = (f32[200,256]{1,0:T(8,128)S(1)}, f32[200,256]{1,0:T(8,128)S(1)}, u32[]{:S(2)}, u32[]{:S(2)}) collective-permute-start(f32[200,256]{1,0:T(8,128)S(1)} %get-tuple-element.50), channel_id=1, source_target_pairs={{0,8},{1,9},{2,10},{3,11},{4,12},{5,13},{6,14},{7,15},{8,0},{9,1},... | collective-permute-start | bytes 614408 | tf_op jit(solution)/shard_map/ppermute | solution.py:21
  32.2 2.0 %collective-permute-start.12 = (f32[72,256]{1,0:T(8,128)S(1)}, f32[72,256]{1,0:T(8,128)S(1)}, u32[]{:S(2)}, u32[]{:S(2)}) collective-permute-start(f32[72,256]{1,0:T(8,128)S(1)} %collective-permute-done.11.near_ref.near1), channel_id=1, source_target_pairs={{0,1},{1,0},{2,3},{3,2},{4,5},{5,4},{6,7},{7,6},{8,9},{9,8},{10,11... | collective-permute-start | bytes 221192 | tf_op jit(solution)/shard_map/ppermute | solution.py:21
  36.3 2.1 %collective-permute-start.16 = (f32[200,256]{1,0:T(8,128)S(1)}, f32[200,256]{1,0:T(8,128)S(1)}, u32[]{:S(2)}, u32[]{:S(2)}) collective-permute-start(f32[200,256]{1,0:T(8,128)S(1)} %collective-permute-done.15.near2.near_ref), channel_id=1, source_target_pairs={{0,1},{1,0},{2,3},{3,2},{4,5},{5,4},{6,7},{7,6},{8,9},{9,8},{10,11... | collective-permute-start | bytes 614408 | tf_op jit(solution)/shard_map/ppermute | solution.py:21
  37.2 4.6 %collective-permute-start.14 = (f32[72,256]{1,0:T(8,128)S(1)}, f32[72,256]{1,0:T(8,128)S(1)}, u32[]{:S(2)}, u32[]{:S(2)}) collective-permute-start(f32[72,256]{1,0:T(8,128)S(1)} %get-tuple-element.47), channel_id=1, source_target_pairs={{0,1},{1,0},{2,3},{3,2},{4,5},{5,4},{6,7},{7,6},{8,16},{9,17},{10,... | collective-permute-start | bytes 221192 | tf_op jit(solution)/shard_map/ppermute | solution.py:29
  37.4 4.5 %collective-permute-start.13 = (f32[72,256]{1,0:T(8,128)S(1)}, f32[72,256]{1,0:T(8,128)S(1)}, u32[]{:S(2)}, u32[]{:S(2)}) collective-permute-start(f32[72,256]{1,0:T(8,128)S(1)} %get-tuple-element.47), channel_id=1, source_target_pairs={{0,1},{1,0},{2,3},{3,2},{4,5},{5,4},{6,7},{7,6},{8,24},{9,25},{10,... | collective-permute-start | bytes 221192 | tf_op jit(solution)/shard_map/ppermute | solution.py:29
  39.0 8.9 %collective-permute-start.18 = (f32[200,256]{1,0:T(8,128)S(1)}, f32[200,256]{1,0:T(8,128)S(1)}, u32[]{:S(2)}, u32[]{:S(2)}) collective-permute-start(f32[200,256]{1,0:T(8,128)S(1)} %shard_map.67), channel_id=1, source_target_pairs={{0,1},{1,0},{2,3},{3,2},{4,5},{5,4},{6,7},{7,6},{8,24},{9,25},{10,... | collective-permute-start | bytes 614408 | tf_op jit(solution)/shard_map/ppermute | solution.py:29
  39.4 11.5 %collective-permute-start.17 = (f32[200,256]{1,0:T(8,128)S(1)}, f32[200,256]{1,0:T(8,128)S(1)}, u32[]{:S(2)}, u32[]{:S(2)}) collective-permute-start(f32[200,256]{1,0:T(8,128)S(1)} %shard_map.67), channel_id=1, source_target_pairs={{0,1},{1,0},{2,3},{3,2},{4,5},{5,4},{6,7},{7,6},{8,16},{9,17},{10,... | collective-permute-start | bytes 614408 | tf_op jit(solution)/shard_map/ppermute | solution.py:29
  41.8 4.0 %collective-permute-start.19 = (f32[72,256]{1,0:T(8,128)S(1)}, f32[72,256]{1,0:T(8,128)S(1)}, u32[]{:S(2)}, u32[]{:S(2)}) collective-permute-start(f32[72,256]{1,0:T(8,128)S(1)} %collective-permute-done.14.near2), channel_id=1, source_target_pairs={{0,1},{1,0},{2,3},{3,2},{4,5},{5,4},{6,7},{7,6},{8,9},{9,8},{10,11... | collective-permute-start | bytes 221192 | tf_op jit(solution)/shard_map/ppermute | solution.py:21
  43.0 2.9 %collective-permute-start.20 = (f32[72,256]{1,0:T(8,128)S(1)}, f32[72,256]{1,0:T(8,128)S(1)}, u32[]{:S(2)}, u32[]{:S(2)}) collective-permute-start(f32[72,256]{1,0:T(8,128)S(1)} %collective-permute-done.13.near3), channel_id=1, source_target_pairs={{0,1},{1,0},{2,3},{3,2},{4,5},{5,4},{6,7},{7,6},{8,9},{9,8},{10,11... | collective-permute-start | bytes 221192 | tf_op jit(solution)/shard_map/ppermute | solution.py:21
  50.9 2.5 %collective-permute-start.21 = (f32[200,256]{1,0:T(8,128)S(1)}, f32[200,256]{1,0:T(8,128)S(1)}, u32[]{:S(2)}, u32[]{:S(2)}) collective-permute-start(f32[200,256]{1,0:T(8,128)S(1)} %collective-permute-done.17.near2), channel_id=1, source_target_pairs={{0,1},{1,0},{2,3},{3,2},{4,5},{5,4},{6,7},{7,6},{8,9},{9,8},{10,11... | collective-permute-start | bytes 614408 | tf_op jit(solution)/shard_map/ppermute | solution.py:21
  52.3 1.5 %collective-permute-start.22 = (f32[200,256]{1,0:T(8,128)S(1)}, f32[200,256]{1,0:T(8,128)S(1)}, u32[]{:S(2)}, u32[]{:S(2)}) collective-permute-start(f32[200,256]{1,0:T(8,128)S(1)} %collective-permute-done.18.near3), channel_id=1, source_target_pairs={{0,1},{1,0},{2,3},{3,2},{4,5},{5,4},{6,7},{7,6},{8,9},{9,8},{10,11... | collective-permute-start | bytes 614408 | tf_op jit(solution)/shard_map/ppermute | solution.py:21

commit v4 on v3

--- a/solution.py
+++ b/solution.py
@@ -204,31 +204,55 @@
     return jnp.where(third, near3[...], near2[...]), jnp.where(third, far3[...], far2[...])
 
 
-def last_early_kernel(distance, own_ref, near2, far2, near3, far3, half_ref):
-    me = place()
-    facing = unpack_symmetric(*by_third(distance, me, near2, far2, near3, far3), bit(me, 1), 0)
-    for i, x in enumerate(before_trans((own_ref[0], own_ref[1], own_ref[2]), facing)):
-        half_ref[i] = x
-
-
-def last_kernel(distance, old_ref, half_ref, near2, far2, near3, far3, left_ref, right_ref, trans_ref):
+def last_early_kernel(distance, old_ref, near2, far2, near3, far3, half_ref, right_ref):
+    me = place()
+    right_ref[0] = old_ref[1]
+
+    @pl.when(bit(me, distance))
+    def _():
+        facing = unpack_symmetric(*by_third(distance, me, near2, far2, near3, far3), bit(me, 1), 0)
+        leading, mirror, right = before_trans((old_ref[0], old_ref[1], old_ref[2]), facing)
+        half_ref[0] = leading
+        half_ref[1] = mirror
+        right_ref[0] = right
+
+
+def last_kernel(distance, old_ref, half_ref, near2, far2, near3, far3, left_out, trans_out, left_ref, trans_ref, sems):
     me = place()
     upper = bit(me, distance)
-    into, away = unpack_second(*by_third(distance, me, near2, far2, near3, far3), bit(me, 1))
-    trans, left = after_trans(half_ref[0], half_ref[1], away, into)
-    right_ref[0] = jnp.where(upper, half_ref[2], old_ref[1])
-    trans_ref[0] = jnp.where(upper, trans, old_ref[2])
-    left_ref[0] = jnp.where(upper, left, old_ref[0])
-
-
-def call(kernel, products, outs, *args):
+    left_copy = pltpu.make_async_copy(left_ref, left_out, sems.at[0])
+    trans_copy = pltpu.make_async_copy(trans_ref, trans_out, sems.at[1])
+
+    @pl.when(upper)
+    def _():
+        into, away = unpack_second(*by_third(distance, me, near2, far2, near3, far3), bit(me, 1))
+        q = split(into)
+        trans_ref[0] = dot3(split(half_ref[0]), q)
+        trans_copy.start()
+        bounced = split(dot3(split(half_ref[1]), q))
+        left_ref[0] = away + dot3(split(into.T), bounced)
+        left_copy.start()
+
+    @pl.when(jnp.logical_not(upper))
+    def _():
+        trans_ref[0] = old_ref[2]
+        trans_copy.start()
+        left_ref[0] = old_ref[0]
+        left_copy.start()
+
+    trans_copy.wait()
+    left_copy.wait()
+
+
+def call(kernel, products, outs, *args, out_space=pltpu.VMEM, scratch=()):
     vmem = pl.BlockSpec(memory_space=pltpu.VMEM)
     m = args[0].shape[-1]
     return pl.pallas_call(
         kernel,
         out_shape=[jax.ShapeDtypeStruct(s, F32) for s in outs],
         in_specs=[vmem] * len(args),
-        out_specs=[vmem] * len(outs),
+        out_specs=[pl.BlockSpec(memory_space=out_space)] * len(outs),
+        scratch_shapes=scratch,
         cost_estimate=pl.CostEstimate(flops=2 * products * m**3, bytes_accessed=4 * m**2 * len(args), transcendentals=0),
         compiler_params=pltpu.CompilerParams(vmem_limit_bytes=40 * 2**20),
     )(*args)
@@ -268,10 +292,17 @@
     first3, first2, prefix = lax.optimization_barrier((first3, first2, prefix))
     (prefix,) = pending(prefix)
     args = prefix, first2, swap(first2, 1), first3, swap(first3, 1)
-    (halfway,) = call(functools.partial(last_early_kernel, distance), 27, [stack], *args)
-    near2, near3, halfway = lax.optimization_barrier((near2, near3, halfway))
-    args = prefix, halfway, near2, swap(near2, 1), near3, swap(near3, 1)
-    return tuple(call(functools.partial(last_kernel, distance), 9, [(1, m, m)] * 3, *args))
+    outs = [(2, m, m), (1, m, m)]
+    halfway, right = call(functools.partial(last_early_kernel, distance), 27, outs, *args)
+    near3, halfway = lax.optimization_barrier((near3, halfway))
+    far3 = swap(near3, 1)
+    near2, far3 = lax.optimization_barrier((near2, far3))
+    args = prefix, halfway, near2, swap(near2, 1), near3, far3
+    one = (1, m, m)
+    scratch = [pltpu.VMEM(one, F32), pltpu.VMEM(one, F32), pltpu.SemaphoreType.DMA((2,))]
+    kernel = functools.partial(last_kernel, distance)
+    left, trans = call(kernel, 9, [one, one], *args, out_space=pltpu.HBM, scratch=scratch)
+    return left, right, trans
 
 
 def solution(mesh):

time: 56.1 us -> 55.3 us (0.986)
  Pallas kernels: 22.1 us -> 22.8 us
  waiting for transfers between devices: 12.2 us -> 11.6 us
    ppermute x4, waiting for transfers between devices: 2.99 us -> 2.12 us  [pair(): lax.ppermute(block, AXES, [(i, step.get(i // quarter, lambda i: i ^ 1)(i)...]
    pallas_call x12, Pallas kernels: 22.1 us -> 22.8 us  [call(): pl.pallas_call(kernel, out_shape=[jax.ShapeDtypeStruct(s, F32) for s in o...]
  transfers between devices with their start and end apart: 23 -> 23, of which waited for: 12 -> 13; matrix products, arithmetic and copies ran while one was open for 2% -> 2% of each run, Pallas kernels for 30% -> 32%
where the time goes in v4:
time: 55.3 us; the launch traced here: 54.9 us
  Pallas kernels  22.8 us (41%)
  starting transfers between devices  18.4 us (33%)
  waiting for transfers between devices  11.6 us (21%)
  other arithmetic  1.16 us (2%)
  between operations  0.95 us (2%)
    pallas_call x12, Pallas kernels, call(): pl.pallas_call(kernel, out_shape=[jax.ShapeDtypeStruct(s, F32) for s in o...  22.8 us
    ppermute x19, starting transfers between devices, swap(): return lax.ppermute(block, AXES, [(i, i ^ distance) for i in range(count)])  15.6 us
    ppermute x19, waiting for transfers between devices, swap(): return lax.ppermute(block, AXES, [(i, i ^ distance) for i in range(count)])  9.48 us
    ppermute x4, starting transfers between devices, pair(): lax.ppermute(block, AXES, [(i, step.get(i // quarter, lambda i: i ^ 1)(i)...  2.82 us
    ppermute x4, waiting for transfers between devices, pair(): lax.ppermute(block, AXES, [(i, step.get(i // quarter, lambda i: i ^ 1)(i)...  2.12 us
    concatenate x1, other arithmetic, shards(): section = jnp.concatenate(sections, 0)  1.16 us
  transfers between devices with their start and end apart: 23, of which 13 were waited for; matrix products, arithmetic and copies ran while one was open for 2% of the time, Pallas kernels for 32%

profile of v4, /device:TPU:17, one launch (start us, length us, event | category | flops | bytes accessed | tf_op | source)
XLA Modules:
  0.0 54.9 jit_solution(4180188970489378590)
XLA Ops:
  0.6 0.7 %collective-permute-start = (f32[1,256,256]{2,1,0:T(8,128)}, f32[1,256,256]{2,1,0:T(8,128)S(1)}, u32[]{:S(2)}, u32[]{:S(2)}) collective-permute-start(f32[1,256,256]{2,1,0:T(8,128)} %param.3), channel_id=1, source_target_pairs={{0,1},{1,0},{2,3},{3,2},{4,5},{5,4},{6,7},{7,6},{8,9},{9,8},{10,11... | collective-permute-start | bytes 786440 | tf_op jit(solution)/shard_map/ppermute | solution.py:21
  1.9 1.2 %pad_maximum_fusion.section_ref = f32[3,256,256]{2,1,0:T(8,128)S(1)} fusion(f32[1,256,256]{2,1,0:T(8,128)} %param.5, f32[1,256,256]{2,1,0:T(8,128)} %param.4, f32[1,256,256]{2,1,0:T(8,128)} %param.3), kind=kLoop, calls=%fused_computation | loop fusion | flops 393216 | bytes 1572864 | tf_op jit(solution)/shard_map/concatenate | solution.py:268
  3.5 2.6 %shard_map.58 = (f32[3,256,256]{2,1,0:T(8,128)S(1)}, f32[72,256]{1,0:T(8,128)S(1)}, f32[200,256]{1,0:T(8,128)S(1)}, f32[3,256,256]{2,1,0:T(8,128)S(1)}) custom-call(f32[3,256,256]{2,1,0:T(8,128)S(1)} %pad_maximum_fusion.section_ref, f32[1,256,256]{2,1,0:T(8,128)S(1)} %collective-permute-done.got1, f32[1,256,256]{2,1,0:T(8,128)S(1)} %collective-permute-done.1.got2, ...), custom_call_target="tpu_custom_call" | custom-call | flops 1207959552 | bytes 1048576 | tf_op jit(solution)/shard_map/pallas_call | solution.py:250
  6.1 1.3 %collective-permute-start.4 = (f32[72,256]{1,0:T(8,128)S(1)}, f32[72,256]{1,0:T(8,128)S(1)}, u32[]{:S(2)}, u32[]{:S(2)}) collective-permute-start(f32[72,256]{1,0:T(8,128)S(1)} %get-tuple-element.38), channel_id=1, source_target_pairs={{0,2},{1,3},{2,0},{3,1},{4,6},{5,7},{6,4},{7,5},{8,10},{9,11},{10,... | collective-permute-start | bytes 221192 | tf_op jit(solution)/shard_map/ppermute | solution.py:21
  7.7 1.7 %collective-permute-done.4.near_ref.near1 = f32[72,256]{1,0:T(8,128)S(1)} collective-permute-done((f32[72,256]{1,0:T(8,128)S(1)}, f32[72,256]{1,0:T(8,128)S(1)}, u32[]{:S(2)}, u32[]{:S(2)}) %collective-permute-start.4) | collective-permute-done | bytes 73760 | tf_op jit(solution)/shard_map/ppermute | solution.py:21
  9.4 2.0 %collective-permute-start.5 = (f32[72,256]{1,0:T(8,128)S(1)}, f32[72,256]{1,0:T(8,128)S(1)}, u32[]{:S(2)}, u32[]{:S(2)}) collective-permute-start(f32[72,256]{1,0:T(8,128)S(1)} %collective-permute-done.4.near_ref.near1), channel_id=1, source_target_pairs={{0,1},{1,0},{2,3},{3,2},{4,5},{5,4},{6,7},{7,6},{8,9},{9,8},{10,11... | collective-permute-start | bytes 221192 | tf_op jit(solution)/shard_map/ppermute | solution.py:21
  11.4 0.9 %collective-permute-done.5.far_ref.far1 = f32[72,256]{1,0:T(8,128)S(1)} collective-permute-done((f32[72,256]{1,0:T(8,128)S(1)}, f32[72,256]{1,0:T(8,128)S(1)}, u32[]{:S(2)}, u32[]{:S(2)}) %collective-permute-start.5) | collective-permute-done | bytes 73760 | tf_op jit(solution)/shard_map/ppermute | solution.py:21
  12.3 2.1 %shard_map.59.half_ref = f32[3,256,256]{2,1,0:T(8,128)S(1)} custom-call(f32[3,256,256]{2,1,0:T(8,128)S(1)} %get-tuple-element.37.own_ref, f32[72,256]{1,0:T(8,128)S(1)} %collective-permute-done.4.near_ref.near1, f32[72,256]{1,0:T(8,128)S(1)} %collective-permute-done.5.far_ref.far1), custom_call_target="tpu_custom_call" | custom-call | flops 905969664 | bytes 786432 | tf_op jit(solution)/shard_map/pallas_call | solution.py:250
  14.4 0.9 %collective-permute-start.6 = (f32[200,256]{1,0:T(8,128)S(1)}, f32[200,256]{1,0:T(8,128)S(1)}, u32[]{:S(2)}, u32[]{:S(2)}) collective-permute-start(f32[200,256]{1,0:T(8,128)S(1)} %collective-permute-done.3.near_ref.near2), channel_id=1, source_target_pairs={{0,1},{1,0},{2,3},{3,2},{4,5},{5,4},{6,7},{7,6},{8,9},{9,8},{10,11... | collective-permute-start | bytes 614408 | tf_op jit(solution)/shard_map/ppermute | solution.py:21
  15.3 1.1 %collective-permute-done.6.far_ref.far2 = f32[200,256]{1,0:T(8,128)S(1)} collective-permute-done((f32[200,256]{1,0:T(8,128)S(1)}, f32[200,256]{1,0:T(8,128)S(1)}, u32[]{:S(2)}, u32[]{:S(2)}) %collective-permute-start.6) | collective-permute-done | bytes 204832 | tf_op jit(solution)/shard_map/ppermute | solution.py:21
  17.1 1.3 %collective-permute-start.8 = (f32[72,256]{1,0:T(8,128)S(1)}, f32[72,256]{1,0:T(8,128)S(1)}, u32[]{:S(2)}, u32[]{:S(2)}) collective-permute-start(f32[72,256]{1,0:T(8,128)S(1)} %get-tuple-element.43), channel_id=1, source_target_pairs={{0,4},{1,5},{2,6},{3,7},{4,0},{5,1},{6,2},{7,3},{8,12},{9,13},{10,... | collective-permute-start | bytes 221192 | tf_op jit(solution)/shard_map/ppermute | solution.py:21
  18.6 2.6 %shard_map.61.old_ref = f32[3,256,256]{2,1,0:T(8,128)S(1)} custom-call(f32[3,256,256]{2,1,0:T(8,128)S(1)} %get-tuple-element.44.old_ref, f32[72,256]{1,0:T(8,128)S(1)} %collective-permute-done.4.near_ref.near1, f32[72,256]{1,0:T(8,128)S(1)} %collective-permute-done.5.far_ref.far1, f32[200,256]{1,0:T(8,128)S(1)} %collective-permute-done.3.near_ref.near2, ...), custom_call_target="tpu_custom_call" | custom-call | flops 1207959552 | bytes 1310720 | tf_op jit(solution)/shard_map/pallas_call | solution.py:250
  21.2 1.2 %collective-permute-start.9 = (f32[72,256]{1,0:T(8,128)S(1)}, f32[72,256]{1,0:T(8,128)S(1)}, u32[]{:S(2)}, u32[]{:S(2)}) collective-permute-start(f32[72,256]{1,0:T(8,128)S(1)} %collective-permute-done.8.near_ref.near1), channel_id=1, source_target_pairs={{0,1},{1,0},{2,3},{3,2},{4,5},{5,4},{6,7},{7,6},{8,9},{9,8},{10,11... | collective-permute-start | bytes 221192 | tf_op jit(solution)/shard_map/ppermute | solution.py:21
  22.3 0.9 %collective-permute-done.9.far_ref.far1 = f32[72,256]{1,0:T(8,128)S(1)} collective-permute-done((f32[72,256]{1,0:T(8,128)S(1)}, f32[72,256]{1,0:T(8,128)S(1)}, u32[]{:S(2)}, u32[]{:S(2)}) %collective-permute-start.9) | collective-permute-done | bytes 73760 | tf_op jit(solution)/shard_map/ppermute | solution.py:21
  23.2 2.1 %shard_map.62.half_ref = f32[3,256,256]{2,1,0:T(8,128)S(1)} custom-call(f32[3,256,256]{2,1,0:T(8,128)S(1)} %get-tuple-element.42.own_ref, f32[72,256]{1,0:T(8,128)S(1)} %collective-permute-done.8.near_ref.near1, f32[72,256]{1,0:T(8,128)S(1)} %collective-permute-done.9.far_ref.far1), custom_call_target="tpu_custom_call" | custom-call | flops 905969664 | bytes 786432 | tf_op jit(solution)/shard_map/pallas_call | solution.py:250
  25.3 0.9 %collective-permute-start.10 = (f32[200,256]{1,0:T(8,128)S(1)}, f32[200,256]{1,0:T(8,128)S(1)}, u32[]{:S(2)}, u32[]{:S(2)}) collective-permute-start(f32[200,256]{1,0:T(8,128)S(1)} %collective-permute-done.7.near_ref.near2), channel_id=1, source_target_pairs={{0,1},{1,0},{2,3},{3,2},{4,5},{5,4},{6,7},{7,6},{8,9},{9,8},{10,11... | collective-permute-start | bytes 614408 | tf_op jit(solution)/shard_map/ppermute | solution.py:21
  26.3 1.1 %collective-permute-done.10.far_ref.far2 = f32[200,256]{1,0:T(8,128)S(1)} collective-permute-done((f32[200,256]{1,0:T(8,128)S(1)}, f32[200,256]{1,0:T(8,128)S(1)}, u32[]{:S(2)}, u32[]{:S(2)}) %collective-permute-start.10) | collective-permute-done | bytes 204832 | tf_op jit(solution)/shard_map/ppermute | solution.py:21
  28.1 1.4 %collective-permute-start.11 = (f32[72,256]{1,0:T(8,128)S(1)}, f32[72,256]{1,0:T(8,128)S(1)}, u32[]{:S(2)}, u32[]{:S(2)}) collective-permute-start(f32[72,256]{1,0:T(8,128)S(1)} %get-tuple-element.49), channel_id=1, source_target_pairs={{0,8},{1,9},{2,10},{3,11},{4,12},{5,13},{6,14},{7,15},{8,0},{9,1},... | collective-permute-start | bytes 221192 | tf_op jit(solution)/shard_map/ppermute | solution.py:21
  29.6 2.6 %shard_map.64.old_ref = f32[3,256,256]{2,1,0:T(8,128)S(1)} custom-call(f32[3,256,256]{2,1,0:T(8,128)S(1)} %shard_map.61.old_ref, f32[72,256]{1,0:T(8,128)S(1)} %collective-permute-done.8.near_ref.near1, f32[72,256]{1,0:T(8,128)S(1)} %collective-permute-done.9.far_ref.far1, f32[200,256]{1,0:T(8,128)S(1)} %collective-permute-done.7.near_ref.near2, ...), custom_call_target="tpu_custom_call" | custom-call | flops 1207959552 | bytes 1310720 | tf_op jit(solution)/shard_map/pallas_call | solution.py:250
  32.2 1.1 %collective-permute-start.12 = (f32[72,256]{1,0:T(8,128)S(1)}, f32[72,256]{1,0:T(8,128)S(1)}, u32[]{:S(2)}, u32[]{:S(2)}) collective-permute-start(f32[72,256]{1,0:T(8,128)S(1)} %collective-permute-done.11.near_ref.near1), channel_id=1, source_target_pairs={{0,1},{1,0},{2,3},{3,2},{4,5},{5,4},{6,7},{7,6},{8,9},{9,8},{10,11... | collective-permute-start | bytes 221192 | tf_op jit(solution)/shard_map/ppermute | solution.py:21
  33.2 0.9 %collective-permute-done.12.far_ref.far1 = f32[72,256]{1,0:T(8,128)S(1)} collective-permute-done((f32[72,256]{1,0:T(8,128)S(1)}, f32[72,256]{1,0:T(8,128)S(1)}, u32[]{:S(2)}, u32[]{:S(2)}) %collective-permute-start.12) | collective-permute-done | bytes 73760 | tf_op jit(solution)/shard_map/ppermute | solution.py:21
  34.2 2.1 %shard_map.65 = (f32[3,256,256]{2,1,0:T(8,128)S(1)}, f32[72,256]{1,0:T(8,128)S(1)}) custom-call(f32[3,256,256]{2,1,0:T(8,128)S(1)} %get-tuple-element.48.own_ref, f32[72,256]{1,0:T(8,128)S(1)} %collective-permute-done.11.near_ref.near1, f32[72,256]{1,0:T(8,128)S(1)} %collective-permute-done.12.far_ref.far1), custom_call_target="tpu_custom_call" | custom-call | flops 905969664 | bytes 786432 | tf_op jit(solution)/shard_map/pallas_call | solution.py:250
  36.3 1.0 %collective-permute-start.16 = (f32[200,256]{1,0:T(8,128)S(1)}, f32[200,256]{1,0:T(8,128)S(1)}, u32[]{:S(2)}, u32[]{:S(2)}) collective-permute-start(f32[200,256]{1,0:T(8,128)S(1)} %collective-permute-done.15.near2.near_ref), channel_id=1, source_target_pairs={{0,1},{1,0},{2,3},{3,2},{4,5},{5,4},{6,7},{7,6},{8,9},{9,8},{10,11... | collective-permute-start | bytes 614408 | tf_op jit(solution)/shard_map/ppermute | solution.py:21
  39.4 1.7 %collective-permute-done.14.near2 = f32[72,256]{1,0:T(8,128)S(1)} collective-permute-done((f32[72,256]{1,0:T(8,128)S(1)}, f32[72,256]{1,0:T(8,128)S(1)}, u32[]{:S(2)}, u32[]{:S(2)}) %collective-permute-start.14) | collective-permute-done | bytes 73760 | tf_op jit(solution)/shard_map/ppermute | solution.py:29
  41.1 1.2 %collective-permute-start.18 = (f32[72,256]{1,0:T(8,128)S(1)}, f32[72,256]{1,0:T(8,128)S(1)}, u32[]{:S(2)}, u32[]{:S(2)}) collective-permute-start(f32[72,256]{1,0:T(8,128)S(1)} %collective-permute-done.14.near2), channel_id=1, source_target_pairs={{0,1},{1,0},{2,3},{3,2},{4,5},{5,4},{6,7},{7,6},{8,9},{9,8},{10,11... | collective-permute-start | bytes 221192 | tf_op jit(solution)/shard_map/ppermute | solution.py:21
  42.3 2.0 %collective-permute-start.20 = (f32[200,256]{1,0:T(8,128)S(1)}, f32[200,256]{1,0:T(8,128)S(1)}, u32[]{:S(2)}, u32[]{:S(2)}) collective-permute-start(f32[200,256]{1,0:T(8,128)S(1)} %shard_map.67), channel_id=1, source_target_pairs={{0,1},{1,0},{2,3},{3,2},{4,5},{5,4},{6,7},{7,6},{8,16},{9,17},{10,... | collective-permute-start | bytes 614408 | tf_op jit(solution)/shard_map/ppermute | solution.py:29
  44.3 2.6 %shard_map.66.old_ref = f32[3,256,256]{2,1,0:T(8,128)S(1)} custom-call(f32[3,256,256]{2,1,0:T(8,128)S(1)} %shard_map.64.old_ref, f32[72,256]{1,0:T(8,128)S(1)} %collective-permute-done.11.near_ref.near1, f32[72,256]{1,0:T(8,128)S(1)} %collective-permute-done.12.far_ref.far1, f32[200,256]{1,0:T(8,128)S(1)} %collective-permute-done.15.near2.near_ref, ...), custom_call_target="tpu_custom_call" | custom-call | flops 1207959552 | bytes 1310720 | tf_op jit(solution)/shard_map/pallas_call | solution.py:250
  46.9 2.8 %shard_map.68 = (f32[2,256,256]{2,1,0:T(8,128)S(1)}, f32[1,256,256]{2,1,0:T(8,128)}) custom-call(f32[3,256,256]{2,1,0:T(8,128)S(1)} %shard_map.66.old_ref, f32[72,256]{1,0:T(8,128)S(1)} %collective-permute-done.14.near2, f32[72,256]{1,0:T(8,128)S(1)} %collective-permute-done.18.far2, f32[72,256]{1,0:T(8,128)S(1)} %collective-permute-done.13.near3, ...), custom_call_target="tpu_custom_call" | custom-call | flops 905969664 | bytes 1310720 | tf_op jit(solution)/shard_map/pallas_call | solution.py:250
  49.7 0.8 %collective-permute-start.21 = (f32[200,256]{1,0:T(8,128)S(1)}, f32[200,256]{1,0:T(8,128)S(1)}, u32[]{:S(2)}, u32[]{:S(2)}) collective-permute-start(f32[200,256]{1,0:T(8,128)S(1)} %collective-permute-done.17.near3), channel_id=1, source_target_pairs={{0,1},{1,0},{2,3},{3,2},{4,5},{5,4},{6,7},{7,6},{8,9},{9,8},{10,11... | collective-permute-start | bytes 614408 | tf_op jit(solution)/shard_map/ppermute | solution.py:21
  51.6 0.7 %collective-permute-start.22 = (f32[200,256]{1,0:T(8,128)S(1)}, f32[200,256]{1,0:T(8,128)S(1)}, u32[]{:S(2)}, u32[]{:S(2)}) collective-permute-start(f32[200,256]{1,0:T(8,128)S(1)} %collective-permute-done.20.near2), channel_id=1, source_target_pairs={{0,1},{1,0},{2,3},{3,2},{4,5},{5,4},{6,7},{7,6},{8,9},{9,8},{10,11... | collective-permute-start | bytes 614408 | tf_op jit(solution)/shard_map/ppermute | solution.py:21
  52.3 1.1 %collective-permute-done.22.far2 = f32[200,256]{1,0:T(8,128)S(1)} collective-permute-done((f32[200,256]{1,0:T(8,128)S(1)}, f32[200,256]{1,0:T(8,128)S(1)}, u32[]{:S(2)}, u32[]{:S(2)}) %collective-permute-start.22) | collective-permute-done | bytes 204832 | tf_op jit(solution)/shard_map/ppermute | solution.py:21
  53.4 1.4 %shard_map.69 = (f32[1,256,256]{2,1,0:T(8,128)}, f32[1,256,256]{2,1,0:T(8,128)}) custom-call(f32[3,256,256]{2,1,0:T(8,128)S(1)} %shard_map.66.old_ref, f32[2,256,256]{2,1,0:T(8,128)S(1)} %get-tuple-element.62.half_ref, f32[200,256]{1,0:T(8,128)S(1)} %collective-permute-done.20.near2, f32[200,256]{1,0:T(8,128)S(1)} %collective-permute-done.22.far2, ...), custom_call_target="tpu_custom_call" | custom-call | flops 301989888 | bytes 1572864 | tf_op jit(solution)/shard_map/pallas_call | solution.py:250
  (27 shorter events, 6.4 us)
Async XLA Ops:
  0.6 2.4 %collective-permute-start = (f32[1,256,256]{2,1,0:T(8,128)}, f32[1,256,256]{2,1,0:T(8,128)S(1)}, u32[]{:S(2)}, u32[]{:S(2)}) collective-permute-start(f32[1,256,256]{2,1,0:T(8,128)} %param.3), channel_id=1, source_target_pairs={{0,1},{1,0},{2,3},{3,2},{4,5},{5,4},{6,7},{7,6},{8,9},{9,8},{10,11... | collective-permute-start | bytes 786440 | tf_op jit(solution)/shard_map/ppermute | solution.py:21
  1.4 1.7 %collective-permute-start.1 = (f32[1,256,256]{2,1,0:T(8,128)}, f32[1,256,256]{2,1,0:T(8,128)S(1)}, u32[]{:S(2)}, u32[]{:S(2)}) collective-permute-start(f32[1,256,256]{2,1,0:T(8,128)} %param.4), channel_id=1, source_target_pairs={{0,1},{1,0},{2,3},{3,2},{4,5},{5,4},{6,7},{7,6},{8,9},{9,8},{10,11... | collective-permute-start | bytes 786440 | tf_op jit(solution)/shard_map/ppermute | solution.py:21
  1.4 2.0 %collective-permute-start.2 = (f32[1,256,256]{2,1,0:T(8,128)}, f32[1,256,256]{2,1,0:T(8,128)S(1)}, u32[]{:S(2)}, u32[]{:S(2)}) collective-permute-start(f32[1,256,256]{2,1,0:T(8,128)} %param.5), channel_id=1, source_target_pairs={{0,1},{1,0},{2,3},{3,2},{4,5},{5,4},{6,7},{7,6},{8,9},{9,8},{10,11... | collective-permute-start | bytes 786440 | tf_op jit(solution)/shard_map/ppermute | solution.py:21
  6.1 3.3 %collective-permute-start.4 = (f32[72,256]{1,0:T(8,128)S(1)}, f32[72,256]{1,0:T(8,128)S(1)}, u32[]{:S(2)}, u32[]{:S(2)}) collective-permute-start(f32[72,256]{1,0:T(8,128)S(1)} %get-tuple-element.38), channel_id=1, source_target_pairs={{0,2},{1,3},{2,0},{3,1},{4,6},{5,7},{6,4},{7,5},{8,10},{9,11},{10,... | collective-permute-start | bytes 221192 | tf_op jit(solution)/shard_map/ppermute | solution.py:21
  7.4 7.0 %collective-permute-start.3 = (f32[200,256]{1,0:T(8,128)S(1)}, f32[200,256]{1,0:T(8,128)S(1)}, u32[]{:S(2)}, u32[]{:S(2)}) collective-permute-start(f32[200,256]{1,0:T(8,128)S(1)} %get-tuple-element.36), channel_id=1, source_target_pairs={{0,2},{1,3},{2,0},{3,1},{4,6},{5,7},{6,4},{7,5},{8,10},{9,11},{10,... | collective-permute-start | bytes 614408 | tf_op jit(solution)/shard_map/ppermute | solution.py:21
  9.4 2.9 %collective-permute-start.5 = (f32[72,256]{1,0:T(8,128)S(1)}, f32[72,256]{1,0:T(8,128)S(1)}, u32[]{:S(2)}, u32[]{:S(2)}) collective-permute-start(f32[72,256]{1,0:T(8,128)S(1)} %collective-permute-done.4.near_ref.near1), channel_id=1, source_target_pairs={{0,1},{1,0},{2,3},{3,2},{4,5},{5,4},{6,7},{7,6},{8,9},{9,8},{10,11... | collective-permute-start | bytes 221192 | tf_op jit(solution)/shard_map/ppermute | solution.py:21
  14.4 2.0 %collective-permute-start.6 = (f32[200,256]{1,0:T(8,128)S(1)}, f32[200,256]{1,0:T(8,128)S(1)}, u32[]{:S(2)}, u32[]{:S(2)}) collective-permute-start(f32[200,256]{1,0:T(8,128)S(1)} %collective-permute-done.3.near_ref.near2), channel_id=1, source_target_pairs={{0,1},{1,0},{2,3},{3,2},{4,5},{5,4},{6,7},{7,6},{8,9},{9,8},{10,11... | collective-permute-start | bytes 614408 | tf_op jit(solution)/shard_map/ppermute | solution.py:21
  17.1 4.1 %collective-permute-start.8 = (f32[72,256]{1,0:T(8,128)S(1)}, f32[72,256]{1,0:T(8,128)S(1)}, u32[]{:S(2)}, u32[]{:S(2)}) collective-permute-start(f32[72,256]{1,0:T(8,128)S(1)} %get-tuple-element.43), channel_id=1, source_target_pairs={{0,4},{1,5},{2,6},{3,7},{4,0},{5,1},{6,2},{7,3},{8,12},{9,13},{10,... | collective-permute-start | bytes 221192 | tf_op jit(solution)/shard_map/ppermute | solution.py:21
  18.4 6.9 %collective-permute-start.7 = (f32[200,256]{1,0:T(8,128)S(1)}, f32[200,256]{1,0:T(8,128)S(1)}, u32[]{:S(2)}, u32[]{:S(2)}) collective-permute-start(f32[200,256]{1,0:T(8,128)S(1)} %get-tuple-element.41), channel_id=1, source_target_pairs={{0,4},{1,5},{2,6},{3,7},{4,0},{5,1},{6,2},{7,3},{8,12},{9,13},{10,... | collective-permute-start | bytes 614408 | tf_op jit(solution)/shard_map/ppermute | solution.py:21
  21.2 2.1 %collective-permute-start.9 = (f32[72,256]{1,0:T(8,128)S(1)}, f32[72,256]{1,0:T(8,128)S(1)}, u32[]{:S(2)}, u32[]{:S(2)}) collective-permute-start(f32[72,256]{1,0:T(8,128)S(1)} %collective-permute-done.8.near_ref.near1), channel_id=1, source_target_pairs={{0,1},{1,0},{2,3},{3,2},{4,5},{5,4},{6,7},{7,6},{8,9},{9,8},{10,11... | collective-permute-start | bytes 221192 | tf_op jit(solution)/shard_map/ppermute | solution.py:21
  25.3 2.0 %collective-permute-start.10 = (f32[200,256]{1,0:T(8,128)S(1)}, f32[200,256]{1,0:T(8,128)S(1)}, u32[]{:S(2)}, u32[]{:S(2)}) collective-permute-start(f32[200,256]{1,0:T(8,128)S(1)} %collective-permute-done.7.near_ref.near2), channel_id=1, source_target_pairs={{0,1},{1,0},{2,3},{3,2},{4,5},{5,4},{6,7},{7,6},{8,9},{9,8},{10,11... | collective-permute-start | bytes 614408 | tf_op jit(solution)/shard_map/ppermute | solution.py:21
  28.1 4.1 %collective-permute-start.11 = (f32[72,256]{1,0:T(8,128)S(1)}, f32[72,256]{1,0:T(8,128)S(1)}, u32[]{:S(2)}, u32[]{:S(2)}) collective-permute-start(f32[72,256]{1,0:T(8,128)S(1)} %get-tuple-element.49), channel_id=1, source_target_pairs={{0,8},{1,9},{2,10},{3,11},{4,12},{5,13},{6,14},{7,15},{8,0},{9,1},... | collective-permute-start | bytes 221192 | tf_op jit(solution)/shard_map/ppermute | solution.py:21
  29.4 6.8 %collective-permute-start.15 = (f32[200,256]{1,0:T(8,128)S(1)}, f32[200,256]{1,0:T(8,128)S(1)}, u32[]{:S(2)}, u32[]{:S(2)}) collective-permute-start(f32[200,256]{1,0:T(8,128)S(1)} %get-tuple-element.55), channel_id=1, source_target_pairs={{0,8},{1,9},{2,10},{3,11},{4,12},{5,13},{6,14},{7,15},{8,0},{9,1},... | collective-permute-start | bytes 614408 | tf_op jit(solution)/shard_map/ppermute | solution.py:21
  32.2 2.0 %collective-permute-start.12 = (f32[72,256]{1,0:T(8,128)S(1)}, f32[72,256]{1,0:T(8,128)S(1)}, u32[]{:S(2)}, u32[]{:S(2)}) collective-permute-start(f32[72,256]{1,0:T(8,128)S(1)} %collective-permute-done.11.near_ref.near1), channel_id=1, source_target_pairs={{0,1},{1,0},{2,3},{3,2},{4,5},{5,4},{6,7},{7,6},{8,9},{9,8},{10,11... | collective-permute-start | bytes 221192 | tf_op jit(solution)/shard_map/ppermute | solution.py:21
  36.3 2.1 %collective-permute-start.16 = (f32[200,256]{1,0:T(8,128)S(1)}, f32[200,256]{1,0:T(8,128)S(1)}, u32[]{:S(2)}, u32[]{:S(2)}) collective-permute-start(f32[200,256]{1,0:T(8,128)S(1)} %collective-permute-done.15.near2.near_ref), channel_id=1, source_target_pairs={{0,1},{1,0},{2,3},{3,2},{4,5},{5,4},{6,7},{7,6},{8,9},{9,8},{10,11... | collective-permute-start | bytes 614408 | tf_op jit(solution)/shard_map/ppermute | solution.py:21
  37.2 3.9 %collective-permute-start.14 = (f32[72,256]{1,0:T(8,128)S(1)}, f32[72,256]{1,0:T(8,128)S(1)}, u32[]{:S(2)}, u32[]{:S(2)}) collective-permute-start(f32[72,256]{1,0:T(8,128)S(1)} %get-tuple-element.52), channel_id=1, source_target_pairs={{0,1},{1,0},{2,3},{3,2},{4,5},{5,4},{6,7},{7,6},{8,16},{9,17},{10,... | collective-permute-start | bytes 221192 | tf_op jit(solution)/shard_map/ppermute | solution.py:29
  37.4 3.8 %collective-permute-start.13 = (f32[72,256]{1,0:T(8,128)S(1)}, f32[72,256]{1,0:T(8,128)S(1)}, u32[]{:S(2)}, u32[]{:S(2)}) collective-permute-start(f32[72,256]{1,0:T(8,128)S(1)} %get-tuple-element.52), channel_id=1, source_target_pairs={{0,1},{1,0},{2,3},{3,2},{4,5},{5,4},{6,7},{7,6},{8,24},{9,25},{10,... | collective-permute-start | bytes 221192 | tf_op jit(solution)/shard_map/ppermute | solution.py:29
  39.0 10.7 %collective-permute-start.17 = (f32[200,256]{1,0:T(8,128)S(1)}, f32[200,256]{1,0:T(8,128)S(1)}, u32[]{:S(2)}, u32[]{:S(2)}) collective-permute-start(f32[200,256]{1,0:T(8,128)S(1)} %shard_map.67), channel_id=1, source_target_pairs={{0,1},{1,0},{2,3},{3,2},{4,5},{5,4},{6,7},{7,6},{8,24},{9,25},{10,... | collective-permute-start | bytes 614408 | tf_op jit(solution)/shard_map/ppermute | solution.py:29
  41.1 5.7 %collective-permute-start.18 = (f32[72,256]{1,0:T(8,128)S(1)}, f32[72,256]{1,0:T(8,128)S(1)}, u32[]{:S(2)}, u32[]{:S(2)}) collective-permute-start(f32[72,256]{1,0:T(8,128)S(1)} %collective-permute-done.14.near2), channel_id=1, source_target_pairs={{0,1},{1,0},{2,3},{3,2},{4,5},{5,4},{6,7},{7,6},{8,9},{9,8},{10,11... | collective-permute-start | bytes 221192 | tf_op jit(solution)/shard_map/ppermute | solution.py:21
  42.3 4.6 %collective-permute-start.19 = (f32[72,256]{1,0:T(8,128)S(1)}, f32[72,256]{1,0:T(8,128)S(1)}, u32[]{:S(2)}, u32[]{:S(2)}) collective-permute-start(f32[72,256]{1,0:T(8,128)S(1)} %collective-permute-done.13.near3), channel_id=1, source_target_pairs={{0,1},{1,0},{2,3},{3,2},{4,5},{5,4},{6,7},{7,6},{8,9},{9,8},{10,11... | collective-permute-start | bytes 221192 | tf_op jit(solution)/shard_map/ppermute | solution.py:21
  42.3 8.6 %collective-permute-start.20 = (f32[200,256]{1,0:T(8,128)S(1)}, f32[200,256]{1,0:T(8,128)S(1)}, u32[]{:S(2)}, u32[]{:S(2)}) collective-permute-start(f32[200,256]{1,0:T(8,128)S(1)} %shard_map.67), channel_id=1, source_target_pairs={{0,1},{1,0},{2,3},{3,2},{4,5},{5,4},{6,7},{7,6},{8,16},{9,17},{10,... | collective-permute-start | bytes 614408 | tf_op jit(solution)/shard_map/ppermute | solution.py:29
  49.7 1.9 %collective-permute-start.21 = (f32[200,256]{1,0:T(8,128)S(1)}, f32[200,256]{1,0:T(8,128)S(1)}, u32[]{:S(2)}, u32[]{:S(2)}) collective-permute-start(f32[200,256]{1,0:T(8,128)S(1)} %collective-permute-done.17.near3), channel_id=1, source_target_pairs={{0,1},{1,0},{2,3},{3,2},{4,5},{5,4},{6,7},{7,6},{8,9},{9,8},{10,11... | collective-permute-start | bytes 614408 | tf_op jit(solution)/shard_map/ppermute | solution.py:21
  51.6 1.8 %collective-permute-start.22 = (f32[200,256]{1,0:T(8,128)S(1)}, f32[200,256]{1,0:T(8,128)S(1)}, u32[]{:S(2)}, u32[]{:S(2)}) collective-permute-start(f32[200,256]{1,0:T(8,128)S(1)} %collective-permute-done.20.near2), channel_id=1, source_target_pairs={{0,1},{1,0},{2,3},{3,2},{4,5},{5,4},{6,7},{7,6},{8,9},{9,8},{10,11... | collective-permute-start | bytes 614408 | tf_op jit(solution)/shard_map/ppermute | solution.py:21

commit v5 on v4

--- a/solution.py
+++ b/solution.py
@@ -166,11 +166,13 @@
         half_ref[i] = x
 
 
-def final_kernel(half_ref, near_ref, far_ref, second_ref):
-    core = bit(place(), 1)
+def final_kernel(distance, half_ref, near_ref, far_ref, second_ref):
+    me = place()
+    core, upper = bit(me, 1), bit(me, distance)
     into, away = unpack_second(near_ref, far_ref, core)
     trans, other_side = after_trans(half_ref[0], half_ref[1], away, into)
-    pack_second(trans, other_side, core, second_ref)
+    left = jnp.where(upper, other_side, half_ref[2])
+    pack_second(jnp.where(upper, trans, trans.T), left, core, second_ref)
 
 
 def pack_second(back, away, core, ref):
@@ -204,42 +206,43 @@
     return jnp.where(third, near3[...], near2[...]), jnp.where(third, far3[...], far2[...])
 
 
-def last_early_kernel(distance, old_ref, near2, far2, near3, far3, half_ref, right_ref):
-    me = place()
-    right_ref[0] = old_ref[1]
+def last_early_kernel(distance, old_ref, near2, far2, near3, far3, half_ref):
+    me = place()
 
     @pl.when(bit(me, distance))
     def _():
         facing = unpack_symmetric(*by_third(distance, me, near2, far2, near3, far3), bit(me, 1), 0)
-        leading, mirror, right = before_trans((old_ref[0], old_ref[1], old_ref[2]), facing)
-        half_ref[0] = leading
-        half_ref[1] = mirror
-        right_ref[0] = right
-
-
-def last_kernel(distance, old_ref, half_ref, near2, far2, near3, far3, left_out, trans_out, left_ref, trans_ref, sems):
+        for i, x in enumerate(before_trans((old_ref[0], old_ref[1], old_ref[2]), facing)):
+            half_ref[i] = x
+
+
+def last_kernel(distance, old_ref, half_ref, near_ref, far_ref, left_out, right_out, trans_out, new_ref, sems):
     me = place()
     upper = bit(me, distance)
-    left_copy = pltpu.make_async_copy(left_ref, left_out, sems.at[0])
-    trans_copy = pltpu.make_async_copy(trans_ref, trans_out, sems.at[1])
+    left_copy = pltpu.make_async_copy(new_ref.at[0:1], left_out, sems.at[0])
+    trans_copy = pltpu.make_async_copy(new_ref.at[2:3], trans_out, sems.at[1])
+    right_copy = pltpu.make_async_copy(new_ref.at[1:2], right_out, sems.at[2])
+    new_ref[1] = jnp.where(upper, half_ref[2], old_ref[1])
+    right_copy.start()
 
     @pl.when(upper)
     def _():
-        into, away = unpack_second(*by_third(distance, me, near2, far2, near3, far3), bit(me, 1))
+        into, away = unpack_second(near_ref, far_ref, bit(me, 1))
         q = split(into)
-        trans_ref[0] = dot3(split(half_ref[0]), q)
+        new_ref[2] = dot3(split(half_ref[0]), q)
         trans_copy.start()
         bounced = split(dot3(split(half_ref[1]), q))
-        left_ref[0] = away + dot3(split(into.T), bounced)
+        new_ref[0] = away + dot3(split(into.T), bounced)
         left_copy.start()
 
     @pl.when(jnp.logical_not(upper))
     def _():
-        trans_ref[0] = old_ref[2]
+        new_ref[2] = old_ref[2]
         trans_copy.start()
-        left_ref[0] = old_ref[0]
+        new_ref[0] = old_ref[0]
         left_copy.start()
 
+    right_copy.wait()
     trans_copy.wait()
     left_copy.wait()
 
@@ -284,25 +287,20 @@
         if level < levels - 2:
             send1, send2, own = call(bind(late_kernel), 9, [first, second, stack], halfway, near2, far2)
 
-    distance *= 2
     (send1,) = sends
     first3, first2 = pair(send1, 1, 3), pair(send1, 1, 2)
-    (send2,) = call(final_kernel, 9, [second], halfway, near2, far2)
-    near3, near2 = pair(send2, 1, 3), pair(send2, 1, 2)
+    (send2,) = call(bind(final_kernel), 9, [second], halfway, near2, far2)
+    distance *= 2
+    near2 = swap(send2, distance)
     first3, first2, prefix = lax.optimization_barrier((first3, first2, prefix))
     (prefix,) = pending(prefix)
     args = prefix, first2, swap(first2, 1), first3, swap(first3, 1)
-    outs = [(2, m, m), (1, m, m)]
-    halfway, right = call(functools.partial(last_early_kernel, distance), 27, outs, *args)
-    near3, halfway = lax.optimization_barrier((near3, halfway))
-    far3 = swap(near3, 1)
-    near2, far3 = lax.optimization_barrier((near2, far3))
-    args = prefix, halfway, near2, swap(near2, 1), near3, far3
-    one = (1, m, m)
-    scratch = [pltpu.VMEM(one, F32), pltpu.VMEM(one, F32), pltpu.SemaphoreType.DMA((2,))]
+    (halfway,) = call(functools.partial(last_early_kernel, distance), 27, [stack], *args)
+    near2, halfway = lax.optimization_barrier((near2, halfway))
+    args = prefix, halfway, near2, swap(near2, 1)
+    scratch = [pltpu.VMEM(stack, F32), pltpu.SemaphoreType.DMA((3,))]
     kernel = functools.partial(last_kernel, distance)
-    left, trans = call(kernel, 9, [one, one], *args, out_space=pltpu.HBM, scratch=scratch)
-    return left, right, trans
+    return tuple(call(kernel, 9, [(1, m, m)] * 3, *args, out_space=pltpu.HBM, scratch=scratch))
 
 
 def solution(mesh):

time: 55.3 us -> 56.9 us (1.029)
  the two profiles are of different devices: /device:TPU:17 before, /device:TPU:0 now
where the time goes in v5:
time: 56.9 us; the launch traced here: 56.7 us
  waiting for transfers between devices  22.8 us (40%)
  Pallas kernels  19.6 us (34%)
  starting transfers between devices  12.3 us (22%)
  other arithmetic  1.16 us (2%)
  between operations  0.95 us (2%)
    ppermute x19, waiting for transfers between devices, swap(): return lax.ppermute(block, AXES, [(i, i ^ distance) for i in range(count)])  22.8 us
    pallas_call x12, Pallas kernels, call(): pl.pallas_call(kernel, out_shape=[jax.ShapeDtypeStruct(s, F32) for s in o...  19.6 us
    ppermute x19, starting transfers between devices, swap(): return lax.ppermute(block, AXES, [(i, i ^ distance) for i in range(count)])  11.7 us
    concatenate x1, other arithmetic, shards(): section = jnp.concatenate(sections, 0)  1.16 us
  transfers between devices with their start and end apart: 21, of which 14 were waited for; matrix products, arithmetic and copies ran while one was open for 2% of the time, Pallas kernels for 26%

profile of v5, /device:TPU:0, one launch (start us, length us, event | category | flops | bytes accessed | tf_op | source)
XLA Modules:
  0.0 56.7 jit_solution(5536635298181926243)
XLA Ops:
  0.6 0.5 collective-permute-start
  1.2 0.4 collective-permute-start.2
  1.7 1.2 %pad_maximum_fusion.section_ref = f32[3,256,256]{2,1,0:T(8,128)S(1)} fusion(f32[1,256,256]{2,1,0:T(8,128)} %param.5, f32[1,256,256]{2,1,0:T(8,128)} %param.4, f32[1,256,256]{2,1,0:T(8,128)} %param.3), kind=kLoop, calls=%fused_computation | loop fusion | flops 393216 | bytes 1572864 | tf_op jit(solution)/shard_map/concatenate | solution.py:271
  3.3 2.6 %shard_map.58 = (f32[3,256,256]{2,1,0:T(8,128)S(1)}, f32[72,256]{1,0:T(8,128)S(1)}, f32[200,256]{1,0:T(8,128)S(1)}, f32[3,256,256]{2,1,0:T(8,128)S(1)}) custom-call(f32[3,256,256]{2,1,0:T(8,128)S(1)} %pad_maximum_fusion.section_ref, f32[1,256,256]{2,1,0:T(8,128)S(1)} %collective-permute-done.got1, f32[1,256,256]{2,1,0:T(8,128)S(1)} %collective-permute-done.1.got2, ...), custom_call_target="tpu_custom_call" | custom-call | flops 1207959552 | bytes 1048576 | tf_op jit(solution)/shard_map/pallas_call | solution.py:253
  5.9 2.9 %collective-permute-start.4 = (f32[72,256]{1,0:T(8,128)S(1)}, f32[72,256]{1,0:T(8,128)S(1)}, u32[]{:S(2)}, u32[]{:S(2)}) collective-permute-start(f32[72,256]{1,0:T(8,128)S(1)} %get-tuple-element.32), channel_id=1, source_target_pairs={{0,2},{1,3},{2,0},{3,1},{4,6},{5,7},{6,4},{7,5},{8,10},{9,11},{10,... | collective-permute-start | bytes 221192 | tf_op jit(solution)/shard_map/ppermute | solution.py:21
  8.9 2.6 %collective-permute-done.4.near_ref.near1 = f32[72,256]{1,0:T(8,128)S(1)} collective-permute-done((f32[72,256]{1,0:T(8,128)S(1)}, f32[72,256]{1,0:T(8,128)S(1)}, u32[]{:S(2)}, u32[]{:S(2)}) %collective-permute-start.4) | collective-permute-done | bytes 73760 | tf_op jit(solution)/shard_map/ppermute | solution.py:21
  11.5 1.3 %collective-permute-done.5.far_ref.far1 = f32[72,256]{1,0:T(8,128)S(1)} collective-permute-done((f32[72,256]{1,0:T(8,128)S(1)}, f32[72,256]{1,0:T(8,128)S(1)}, u32[]{:S(2)}, u32[]{:S(2)}) %collective-permute-start.5) | collective-permute-done | bytes 73760 | tf_op jit(solution)/shard_map/ppermute | solution.py:21
  12.8 2.1 %shard_map.59.half_ref = f32[3,256,256]{2,1,0:T(8,128)S(1)} custom-call(f32[3,256,256]{2,1,0:T(8,128)S(1)} %get-tuple-element.31.own_ref, f32[72,256]{1,0:T(8,128)S(1)} %collective-permute-done.4.near_ref.near1, f32[72,256]{1,0:T(8,128)S(1)} %collective-permute-done.5.far_ref.far1), custom_call_target="tpu_custom_call" | custom-call | flops 905969664 | bytes 786432 | tf_op jit(solution)/shard_map/pallas_call | solution.py:253
  14.8 0.9 %collective-permute-done.3.near_ref.near2 = f32[200,256]{1,0:T(8,128)S(1)} collective-permute-done((f32[200,256]{1,0:T(8,128)S(1)}, f32[200,256]{1,0:T(8,128)S(1)}, u32[]{:S(2)}, u32[]{:S(2)}) %collective-permute-start.3) | collective-permute-done | bytes 204832 | tf_op jit(solution)/shard_map/ppermute | solution.py:21
  15.8 1.5 %collective-permute-done.6.far_ref.far2 = f32[200,256]{1,0:T(8,128)S(1)} collective-permute-done((f32[200,256]{1,0:T(8,128)S(1)}, f32[200,256]{1,0:T(8,128)S(1)}, u32[]{:S(2)}, u32[]{:S(2)}) %collective-permute-start.6) | collective-permute-done | bytes 204832 | tf_op jit(solution)/shard_map/ppermute | solution.py:21
  17.2 0.7 %shard_map.60 = (f32[72,256]{1,0:T(8,128)S(1)}, f32[200,256]{1,0:T(8,128)S(1)}, f32[3,256,256]{2,1,0:T(8,128)S(1)}) custom-call(f32[3,256,256]{2,1,0:T(8,128)S(1)} %shard_map.59.half_ref, f32[200,256]{1,0:T(8,128)S(1)} %collective-permute-done.3.near_ref.near2, f32[200,256]{1,0:T(8,128)S(1)} %collective-permute-done.6.far_ref.far2), custom_call_target="tpu_custom_call" | custom-call | flops 301989888 | bytes 786432 | tf_op jit(solution)/shard_map/pallas_call | solution.py:253
  17.9 1.9 %collective-permute-start.8 = (f32[72,256]{1,0:T(8,128)S(1)}, f32[72,256]{1,0:T(8,128)S(1)}, u32[]{:S(2)}, u32[]{:S(2)}) collective-permute-start(f32[72,256]{1,0:T(8,128)S(1)} %get-tuple-element.37), channel_id=1, source_target_pairs={{0,4},{1,5},{2,6},{3,7},{4,0},{5,1},{6,2},{7,3},{8,12},{9,13},{10,... | collective-permute-start | bytes 221192 | tf_op jit(solution)/shard_map/ppermute | solution.py:21
  20.0 2.6 %shard_map.61.old_ref = f32[3,256,256]{2,1,0:T(8,128)S(1)} custom-call(f32[3,256,256]{2,1,0:T(8,128)S(1)} %get-tuple-element.38.old_ref, f32[72,256]{1,0:T(8,128)S(1)} %collective-permute-done.4.near_ref.near1, f32[72,256]{1,0:T(8,128)S(1)} %collective-permute-done.5.far_ref.far1, f32[200,256]{1,0:T(8,128)S(1)} %collective-permute-done.3.near_ref.near2, ...), custom_call_target="tpu_custom_call" | custom-call | flops 1207959552 | bytes 1310720 | tf_op jit(solution)/shard_map/pallas_call | solution.py:253
  22.7 1.3 %collective-permute-done.9.far_ref.far1 = f32[72,256]{1,0:T(8,128)S(1)} collective-permute-done((f32[72,256]{1,0:T(8,128)S(1)}, f32[72,256]{1,0:T(8,128)S(1)}, u32[]{:S(2)}, u32[]{:S(2)}) %collective-permute-start.9) | collective-permute-done | bytes 73760 | tf_op jit(solution)/shard_map/ppermute | solution.py:21
  23.9 2.1 %shard_map.62.half_ref = f32[3,256,256]{2,1,0:T(8,128)S(1)} custom-call(f32[3,256,256]{2,1,0:T(8,128)S(1)} %get-tuple-element.36.own_ref, f32[72,256]{1,0:T(8,128)S(1)} %collective-permute-done.8.near_ref.near1, f32[72,256]{1,0:T(8,128)S(1)} %collective-permute-done.9.far_ref.far1), custom_call_target="tpu_custom_call" | custom-call | flops 905969664 | bytes 786432 | tf_op jit(solution)/shard_map/pallas_call | solution.py:253
  26.0 0.8 %collective-permute-done.7.near_ref.near2 = f32[200,256]{1,0:T(8,128)S(1)} collective-permute-done((f32[200,256]{1,0:T(8,128)S(1)}, f32[200,256]{1,0:T(8,128)S(1)}, u32[]{:S(2)}, u32[]{:S(2)}) %collective-permute-start.7) | collective-permute-done | bytes 204832 | tf_op jit(solution)/shard_map/ppermute | solution.py:21
  26.8 1.5 %collective-permute-done.10.far_ref.far2 = f32[200,256]{1,0:T(8,128)S(1)} collective-permute-done((f32[200,256]{1,0:T(8,128)S(1)}, f32[200,256]{1,0:T(8,128)S(1)}, u32[]{:S(2)}, u32[]{:S(2)}) %collective-permute-start.10) | collective-permute-done | bytes 204832 | tf_op jit(solution)/shard_map/ppermute | solution.py:21
  28.2 0.7 %shard_map.63 = (f32[72,256]{1,0:T(8,128)S(1)}, f32[200,256]{1,0:T(8,128)S(1)}, f32[3,256,256]{2,1,0:T(8,128)S(1)}) custom-call(f32[3,256,256]{2,1,0:T(8,128)S(1)} %shard_map.62.half_ref, f32[200,256]{1,0:T(8,128)S(1)} %collective-permute-done.7.near_ref.near2, f32[200,256]{1,0:T(8,128)S(1)} %collective-permute-done.10.far_ref.far2), custom_call_target="tpu_custom_call" | custom-call | flops 301989888 | bytes 786432 | tf_op jit(solution)/shard_map/pallas_call | solution.py:253
  28.9 1.9 %collective-permute-start.11 = (f32[72,256]{1,0:T(8,128)S(1)}, f32[72,256]{1,0:T(8,128)S(1)}, u32[]{:S(2)}, u32[]{:S(2)}) collective-permute-start(f32[72,256]{1,0:T(8,128)S(1)} %get-tuple-element.43), channel_id=1, source_target_pairs={{0,8},{1,9},{2,10},{3,11},{4,12},{5,13},{6,14},{7,15},{8,0},{9,1},... | collective-permute-start | bytes 221192 | tf_op jit(solution)/shard_map/ppermute | solution.py:21
  31.0 2.6 %shard_map.64.old_ref = f32[3,256,256]{2,1,0:T(8,128)S(1)} custom-call(f32[3,256,256]{2,1,0:T(8,128)S(1)} %shard_map.61.old_ref, f32[72,256]{1,0:T(8,128)S(1)} %collective-permute-done.8.near_ref.near1, f32[72,256]{1,0:T(8,128)S(1)} %collective-permute-done.9.far_ref.far1, f32[200,256]{1,0:T(8,128)S(1)} %collective-permute-done.7.near_ref.near2, ...), custom_call_target="tpu_custom_call" | custom-call | flops 1207959552 | bytes 1310720 | tf_op jit(solution)/shard_map/pallas_call | solution.py:253
  33.7 1.3 %collective-permute-done.12.far_ref.far1 = f32[72,256]{1,0:T(8,128)S(1)} collective-permute-done((f32[72,256]{1,0:T(8,128)S(1)}, f32[72,256]{1,0:T(8,128)S(1)}, u32[]{:S(2)}, u32[]{:S(2)}) %collective-permute-start.12) | collective-permute-done | bytes 73760 | tf_op jit(solution)/shard_map/ppermute | solution.py:21
  34.9 2.1 %shard_map.65 = (f32[3,256,256]{2,1,0:T(8,128)S(1)}, f32[72,256]{1,0:T(8,128)S(1)}) custom-call(f32[3,256,256]{2,1,0:T(8,128)S(1)} %get-tuple-element.42.own_ref, f32[72,256]{1,0:T(8,128)S(1)} %collective-permute-done.11.near_ref.near1, f32[72,256]{1,0:T(8,128)S(1)} %collective-permute-done.12.far_ref.far1), custom_call_target="tpu_custom_call" | custom-call | flops 905969664 | bytes 786432 | tf_op jit(solution)/shard_map/pallas_call | solution.py:253
  37.0 0.8 %collective-permute-done.15.near2.near_ref = f32[200,256]{1,0:T(8,128)S(1)} collective-permute-done((f32[200,256]{1,0:T(8,128)S(1)}, f32[200,256]{1,0:T(8,128)S(1)}, u32[]{:S(2)}, u32[]{:S(2)}) %collective-permute-start.15) | collective-permute-done | bytes 204832 | tf_op jit(solution)/shard_map/ppermute | solution.py:21
  37.8 0.5 collective-permute-start.14
  38.3 0.9 %collective-permute-done.16.far2.far_ref = f32[200,256]{1,0:T(8,128)S(1)} collective-permute-done((f32[200,256]{1,0:T(8,128)S(1)}, f32[200,256]{1,0:T(8,128)S(1)}, u32[]{:S(2)}, u32[]{:S(2)}) %collective-permute-start.16) | collective-permute-done | bytes 204832 | tf_op jit(solution)/shard_map/ppermute | solution.py:21
  39.3 0.7 %shard_map.67 = f32[200,256]{1,0:T(8,128)S(1)} custom-call(f32[3,256,256]{2,1,0:T(8,128)S(1)} %get-tuple-element.52.half_ref, f32[200,256]{1,0:T(8,128)S(1)} %collective-permute-done.15.near2.near_ref, f32[200,256]{1,0:T(8,128)S(1)} %collective-permute-done.16.far2.far_ref), custom_call_target="tpu_custom_call" | custom-call | flops 301989888 | bytes 786432 | tf_op jit(solution)/shard_map/pallas_call | solution.py:253
  40.0 2.9 %collective-permute-start.17 = (f32[200,256]{1,0:T(8,128)S(1)}, f32[200,256]{1,0:T(8,128)S(1)}, u32[]{:S(2)}, u32[]{:S(2)}) collective-permute-start(f32[200,256]{1,0:T(8,128)S(1)} %shard_map.67), channel_id=1, source_target_pairs={{0,16},{1,17},{2,18},{3,19},{4,20},{5,21},{6,22},{7,23},{8,24},{9,... | collective-permute-start | bytes 614408 | tf_op jit(solution)/shard_map/ppermute | solution.py:21
  42.8 0.5 collective-permute-start.19
  43.3 2.6 %shard_map.66.old_ref = f32[3,256,256]{2,1,0:T(8,128)S(1)} custom-call(f32[3,256,256]{2,1,0:T(8,128)S(1)} %shard_map.64.old_ref, f32[72,256]{1,0:T(8,128)S(1)} %collective-permute-done.11.near_ref.near1, f32[72,256]{1,0:T(8,128)S(1)} %collective-permute-done.12.far_ref.far1, f32[200,256]{1,0:T(8,128)S(1)} %collective-permute-done.15.near2.near_ref, ...), custom_call_target="tpu_custom_call" | custom-call | flops 1207959552 | bytes 1310720 | tf_op jit(solution)/shard_map/pallas_call | solution.py:253
  46.0 8.2 %collective-permute-done.17.near_ref = f32[200,256]{1,0:T(8,128)S(1)} collective-permute-done((f32[200,256]{1,0:T(8,128)S(1)}, f32[200,256]{1,0:T(8,128)S(1)}, u32[]{:S(2)}, u32[]{:S(2)}) %collective-permute-start.17) | collective-permute-done | bytes 204832 | tf_op jit(solution)/shard_map/ppermute | solution.py:21
  54.2 1.5 %collective-permute-done.20.far_ref = f32[200,256]{1,0:T(8,128)S(1)} collective-permute-done((f32[200,256]{1,0:T(8,128)S(1)}, f32[200,256]{1,0:T(8,128)S(1)}, u32[]{:S(2)}, u32[]{:S(2)}) %collective-permute-start.20) | collective-permute-done | bytes 204832 | tf_op jit(solution)/shard_map/ppermute | solution.py:21
  55.6 0.9 %shard_map.69 = (f32[1,256,256]{2,1,0:T(8,128)}, f32[1,256,256]{2,1,0:T(8,128)}, f32[1,256,256]{2,1,0:T(8,128)}) custom-call(f32[3,256,256]{2,1,0:T(8,128)S(1)} %shard_map.66.old_ref, f32[3,256,256]{2,1,0:T(8,128)S(1)} %shard_map.68.half_ref, f32[200,256]{1,0:T(8,128)S(1)} %collective-permute-done.17.near_ref, f32[200,256]{1,0:T(8,128)S(1)} %collective-permute-done.20.far_ref), custom_call_target="tpu_custom_call" | custom-call | flops 301989888 | bytes 1048576 | tf_op jit(solution)/shard_map/pallas_call | solution.py:253
  (23 shorter events, 1.2 us)
Async XLA Ops:
  0.6 2.2 %collective-permute-start = (f32[1,256,256]{2,1,0:T(8,128)}, f32[1,256,256]{2,1,0:T(8,128)S(1)}, u32[]{:S(2)}, u32[]{:S(2)}) collective-permute-start(f32[1,256,256]{2,1,0:T(8,128)} %param.3), channel_id=1, source_target_pairs={{0,1},{1,0},{2,3},{3,2},{4,5},{5,4},{6,7},{7,6},{8,9},{9,8},{10,11... | collective-permute-start | bytes 786440 | tf_op jit(solution)/shard_map/ppermute | solution.py:21
  1.1 1.7 %collective-permute-start.1 = (f32[1,256,256]{2,1,0:T(8,128)}, f32[1,256,256]{2,1,0:T(8,128)S(1)}, u32[]{:S(2)}, u32[]{:S(2)}) collective-permute-start(f32[1,256,256]{2,1,0:T(8,128)} %param.4), channel_id=1, source_target_pairs={{0,1},{1,0},{2,3},{3,2},{4,5},{5,4},{6,7},{7,6},{8,9},{9,8},{10,11... | collective-permute-start | bytes 786440 | tf_op jit(solution)/shard_map/ppermute | solution.py:21
  1.2 2.0 %collective-permute-start.2 = (f32[1,256,256]{2,1,0:T(8,128)}, f32[1,256,256]{2,1,0:T(8,128)S(1)}, u32[]{:S(2)}, u32[]{:S(2)}) collective-permute-start(f32[1,256,256]{2,1,0:T(8,128)} %param.5), channel_id=1, source_target_pairs={{0,1},{1,0},{2,3},{3,2},{4,5},{5,4},{6,7},{7,6},{8,9},{9,8},{10,11... | collective-permute-start | bytes 786440 | tf_op jit(solution)/shard_map/ppermute | solution.py:21
  5.9 5.6 %collective-permute-start.4 = (f32[72,256]{1,0:T(8,128)S(1)}, f32[72,256]{1,0:T(8,128)S(1)}, u32[]{:S(2)}, u32[]{:S(2)}) collective-permute-start(f32[72,256]{1,0:T(8,128)S(1)} %get-tuple-element.32), channel_id=1, source_target_pairs={{0,2},{1,3},{2,0},{3,1},{4,6},{5,7},{6,4},{7,5},{8,10},{9,11},{10,... | collective-permute-start | bytes 221192 | tf_op jit(solution)/shard_map/ppermute | solution.py:21
  8.8 7.0 %collective-permute-start.3 = (f32[200,256]{1,0:T(8,128)S(1)}, f32[200,256]{1,0:T(8,128)S(1)}, u32[]{:S(2)}, u32[]{:S(2)}) collective-permute-start(f32[200,256]{1,0:T(8,128)S(1)} %get-tuple-element.30), channel_id=1, source_target_pairs={{0,2},{1,3},{2,0},{3,1},{4,6},{5,7},{6,4},{7,5},{8,10},{9,11},{10,... | collective-permute-start | bytes 614408 | tf_op jit(solution)/shard_map/ppermute | solution.py:21
  11.5 1.3 %collective-permute-start.5 = (f32[72,256]{1,0:T(8,128)S(1)}, f32[72,256]{1,0:T(8,128)S(1)}, u32[]{:S(2)}, u32[]{:S(2)}) collective-permute-start(f32[72,256]{1,0:T(8,128)S(1)} %collective-permute-done.4.near_ref.near1), channel_id=1, source_target_pairs={{0,1},{1,0},{2,3},{3,2},{4,5},{5,4},{6,7},{7,6},{8,9},{9,8},{10,11... | collective-permute-start | bytes 221192 | tf_op jit(solution)/shard_map/ppermute | solution.py:21
  15.8 1.5 %collective-permute-start.6 = (f32[200,256]{1,0:T(8,128)S(1)}, f32[200,256]{1,0:T(8,128)S(1)}, u32[]{:S(2)}, u32[]{:S(2)}) collective-permute-start(f32[200,256]{1,0:T(8,128)S(1)} %collective-permute-done.3.near_ref.near2), channel_id=1, source_target_pairs={{0,1},{1,0},{2,3},{3,2},{4,5},{5,4},{6,7},{7,6},{8,9},{9,8},{10,11... | collective-permute-start | bytes 614408 | tf_op jit(solution)/shard_map/ppermute | solution.py:21
  17.9 4.7 %collective-permute-start.8 = (f32[72,256]{1,0:T(8,128)S(1)}, f32[72,256]{1,0:T(8,128)S(1)}, u32[]{:S(2)}, u32[]{:S(2)}) collective-permute-start(f32[72,256]{1,0:T(8,128)S(1)} %get-tuple-element.37), channel_id=1, source_target_pairs={{0,4},{1,5},{2,6},{3,7},{4,0},{5,1},{6,2},{7,3},{8,12},{9,13},{10,... | collective-permute-start | bytes 221192 | tf_op jit(solution)/shard_map/ppermute | solution.py:21
  19.8 7.0 %collective-permute-start.7 = (f32[200,256]{1,0:T(8,128)S(1)}, f32[200,256]{1,0:T(8,128)S(1)}, u32[]{:S(2)}, u32[]{:S(2)}) collective-permute-start(f32[200,256]{1,0:T(8,128)S(1)} %get-tuple-element.35), channel_id=1, source_target_pairs={{0,4},{1,5},{2,6},{3,7},{4,0},{5,1},{6,2},{7,3},{8,12},{9,13},{10,... | collective-permute-start | bytes 614408 | tf_op jit(solution)/shard_map/ppermute | solution.py:21
  22.6 1.3 %collective-permute-start.9 = (f32[72,256]{1,0:T(8,128)S(1)}, f32[72,256]{1,0:T(8,128)S(1)}, u32[]{:S(2)}, u32[]{:S(2)}) collective-permute-start(f32[72,256]{1,0:T(8,128)S(1)} %collective-permute-done.8.near_ref.near1), channel_id=1, source_target_pairs={{0,1},{1,0},{2,3},{3,2},{4,5},{5,4},{6,7},{7,6},{8,9},{9,8},{10,11... | collective-permute-start | bytes 221192 | tf_op jit(solution)/shard_map/ppermute | solution.py:21
  26.8 1.5 %collective-permute-start.10 = (f32[200,256]{1,0:T(8,128)S(1)}, f32[200,256]{1,0:T(8,128)S(1)}, u32[]{:S(2)}, u32[]{:S(2)}) collective-permute-start(f32[200,256]{1,0:T(8,128)S(1)} %collective-permute-done.7.near_ref.near2), channel_id=1, source_target_pairs={{0,1},{1,0},{2,3},{3,2},{4,5},{5,4},{6,7},{7,6},{8,9},{9,8},{10,11... | collective-permute-start | bytes 614408 | tf_op jit(solution)/shard_map/ppermute | solution.py:21
  28.9 4.7 %collective-permute-start.11 = (f32[72,256]{1,0:T(8,128)S(1)}, f32[72,256]{1,0:T(8,128)S(1)}, u32[]{:S(2)}, u32[]{:S(2)}) collective-permute-start(f32[72,256]{1,0:T(8,128)S(1)} %get-tuple-element.43), channel_id=1, source_target_pairs={{0,8},{1,9},{2,10},{3,11},{4,12},{5,13},{6,14},{7,15},{8,0},{9,1},... | collective-permute-start | bytes 221192 | tf_op jit(solution)/shard_map/ppermute | solution.py:21
  30.8 7.0 %collective-permute-start.15 = (f32[200,256]{1,0:T(8,128)S(1)}, f32[200,256]{1,0:T(8,128)S(1)}, u32[]{:S(2)}, u32[]{:S(2)}) collective-permute-start(f32[200,256]{1,0:T(8,128)S(1)} %get-tuple-element.49), channel_id=1, source_target_pairs={{0,8},{1,9},{2,10},{3,11},{4,12},{5,13},{6,14},{7,15},{8,0},{9,1},... | collective-permute-start | bytes 614408 | tf_op jit(solution)/shard_map/ppermute | solution.py:21
  33.6 1.3 %collective-permute-start.12 = (f32[72,256]{1,0:T(8,128)S(1)}, f32[72,256]{1,0:T(8,128)S(1)}, u32[]{:S(2)}, u32[]{:S(2)}) collective-permute-start(f32[72,256]{1,0:T(8,128)S(1)} %collective-permute-done.11.near_ref.near1), channel_id=1, source_target_pairs={{0,1},{1,0},{2,3},{3,2},{4,5},{5,4},{6,7},{7,6},{8,9},{9,8},{10,11... | collective-permute-start | bytes 221192 | tf_op jit(solution)/shard_map/ppermute | solution.py:21
  37.8 1.5 %collective-permute-start.16 = (f32[200,256]{1,0:T(8,128)S(1)}, f32[200,256]{1,0:T(8,128)S(1)}, u32[]{:S(2)}, u32[]{:S(2)}) collective-permute-start(f32[200,256]{1,0:T(8,128)S(1)} %collective-permute-done.15.near2.near_ref), channel_id=1, source_target_pairs={{0,1},{1,0},{2,3},{3,2},{4,5},{5,4},{6,7},{7,6},{8,9},{9,8},{10,11... | collective-permute-start | bytes 614408 | tf_op jit(solution)/shard_map/ppermute | solution.py:21
  37.8 5.0 %collective-permute-start.14 = (f32[72,256]{1,0:T(8,128)S(1)}, f32[72,256]{1,0:T(8,128)S(1)}, u32[]{:S(2)}, u32[]{:S(2)}) collective-permute-start(f32[72,256]{1,0:T(8,128)S(1)} %get-tuple-element.46), channel_id=1, source_target_pairs={{0,1},{1,0},{2,3},{3,2},{4,5},{5,4},{6,7},{7,6},{8,16},{9,17},{10,... | collective-permute-start | bytes 221192 | tf_op jit(solution)/shard_map/ppermute | solution.py:29
  38.3 4.5 %collective-permute-start.13 = (f32[72,256]{1,0:T(8,128)S(1)}, f32[72,256]{1,0:T(8,128)S(1)}, u32[]{:S(2)}, u32[]{:S(2)}) collective-permute-start(f32[72,256]{1,0:T(8,128)S(1)} %get-tuple-element.46), channel_id=1, source_target_pairs={{0,1},{1,0},{2,3},{3,2},{4,5},{5,4},{6,7},{7,6},{8,24},{9,25},{10,... | collective-permute-start | bytes 221192 | tf_op jit(solution)/shard_map/ppermute | solution.py:29
  40.0 14.2 %collective-permute-start.17 = (f32[200,256]{1,0:T(8,128)S(1)}, f32[200,256]{1,0:T(8,128)S(1)}, u32[]{:S(2)}, u32[]{:S(2)}) collective-permute-start(f32[200,256]{1,0:T(8,128)S(1)} %shard_map.67), channel_id=1, source_target_pairs={{0,16},{1,17},{2,18},{3,19},{4,20},{5,21},{6,22},{7,23},{8,24},{9,... | collective-permute-start | bytes 614408 | tf_op jit(solution)/shard_map/ppermute | solution.py:21
  42.8 3.1 %collective-permute-start.18 = (f32[72,256]{1,0:T(8,128)S(1)}, f32[72,256]{1,0:T(8,128)S(1)}, u32[]{:S(2)}, u32[]{:S(2)}) collective-permute-start(f32[72,256]{1,0:T(8,128)S(1)} %collective-permute-done.14.near2), channel_id=1, source_target_pairs={{0,1},{1,0},{2,3},{3,2},{4,5},{5,4},{6,7},{7,6},{8,9},{9,8},{10,11... | collective-permute-start | bytes 221192 | tf_op jit(solution)/shard_map/ppermute | solution.py:21
  42.8 3.1 %collective-permute-start.19 = (f32[72,256]{1,0:T(8,128)S(1)}, f32[72,256]{1,0:T(8,128)S(1)}, u32[]{:S(2)}, u32[]{:S(2)}) collective-permute-start(f32[72,256]{1,0:T(8,128)S(1)} %collective-permute-done.13.near3), channel_id=1, source_target_pairs={{0,1},{1,0},{2,3},{3,2},{4,5},{5,4},{6,7},{7,6},{8,9},{9,8},{10,11... | collective-permute-start | bytes 221192 | tf_op jit(solution)/shard_map/ppermute | solution.py:21
  54.2 1.5 %collective-permute-start.20 = (f32[200,256]{1,0:T(8,128)S(1)}, f32[200,256]{1,0:T(8,128)S(1)}, u32[]{:S(2)}, u32[]{:S(2)}) collective-permute-start(f32[200,256]{1,0:T(8,128)S(1)} %collective-permute-done.17.near_ref), channel_id=1, source_target_pairs={{0,1},{1,0},{2,3},{3,2},{4,5},{5,4},{6,7},{7,6},{8,9},{9,8},{10,11... | collective-permute-start | bytes 614408 | tf_op jit(solution)/shard_map/ppermute | solution.py:21

commit v6 on v5

--- a/solution.py
+++ b/solution.py
@@ -27,6 +27,11 @@
     shift = (second - first) * quarter
     step = {first: lambda i: i + shift, second: lambda i: i - shift}
     return lax.ppermute(block, AXES, [(i, step.get(i // quarter, lambda i: i ^ 1)(i)) for i in range(count)])
+
+
+def give(block, first, second):
+    quarter = lax.axis_size(AXES) // 4
+    return lax.ppermute(block, AXES, [(first * quarter + i, second * quarter + i) for i in range(quarter)])
 
 
 def split(x):
@@ -166,13 +171,11 @@
         half_ref[i] = x
 
 
-def final_kernel(distance, half_ref, near_ref, far_ref, second_ref):
-    me = place()
-    core, upper = bit(me, 1), bit(me, distance)
+def final_kernel(half_ref, near_ref, far_ref, second_ref):
+    core = bit(place(), 1)
     into, away = unpack_second(near_ref, far_ref, core)
     trans, other_side = after_trans(half_ref[0], half_ref[1], away, into)
-    left = jnp.where(upper, other_side, half_ref[2])
-    pack_second(jnp.where(upper, trans, trans.T), left, core, second_ref)
+    pack_second(trans, other_side, core, second_ref)
 
 
 def pack_second(back, away, core, ref):
@@ -216,7 +219,7 @@
             half_ref[i] = x
 
 
-def last_kernel(distance, old_ref, half_ref, near_ref, far_ref, left_out, right_out, trans_out, new_ref, sems):
+def last_kernel(distance, old_ref, half_ref, near2, far2, near3, far3, left_out, right_out, trans_out, new_ref, sems):
     me = place()
     upper = bit(me, distance)
     left_copy = pltpu.make_async_copy(new_ref.at[0:1], left_out, sems.at[0])
@@ -227,7 +230,7 @@
 
     @pl.when(upper)
     def _():
-        into, away = unpack_second(near_ref, far_ref, bit(me, 1))
+        into, away = unpack_second(*by_third(distance, me, near2, far2, near3, far3), bit(me, 1))
         q = split(into)
         new_ref[2] = dot3(split(half_ref[0]), q)
         trans_copy.start()
@@ -287,17 +290,19 @@
         if level < levels - 2:
             send1, send2, own = call(bind(late_kernel), 9, [first, second, stack], halfway, near2, far2)
 
+    distance *= 2
     (send1,) = sends
     first3, first2 = pair(send1, 1, 3), pair(send1, 1, 2)
-    (send2,) = call(bind(final_kernel), 9, [second], halfway, near2, far2)
-    distance *= 2
-    near2 = swap(send2, distance)
+    (send2,) = call(final_kernel, 9, [second], halfway, near2, far2)
+    near3, near2 = give(send2, 1, 3), give(send2, 1, 2)
     first3, first2, prefix = lax.optimization_barrier((first3, first2, prefix))
     (prefix,) = pending(prefix)
     args = prefix, first2, swap(first2, 1), first3, swap(first3, 1)
     (halfway,) = call(functools.partial(last_early_kernel, distance), 27, [stack], *args)
-    near2, halfway = lax.optimization_barrier((near2, halfway))
-    args = prefix, halfway, near2, swap(near2, 1)
+    near3, halfway = lax.optimization_barrier((near3, halfway))
+    far3 = swap(near3, 1)
+    near2, far3 = lax.optimization_barrier((near2, far3))
+    args = prefix, halfway, near2, swap(near2, 1), near3, far3
     scratch = [pltpu.VMEM(stack, F32), pltpu.SemaphoreType.DMA((3,))]
     kernel = functools.partial(last_kernel, distance)
     return tuple(call(kernel, 9, [(1, m, m)] * 3, *args, out_space=pltpu.HBM, scratch=scratch))

time: 56.9 us -> 56.9 us (level)
  the two profiles are of different devices: /device:TPU:0 before, /device:TPU:17 now
where the time goes in v6:
time: 56.9 us; the launch traced here: 56.7 us
  Pallas kernels  22.1 us (39%)
  starting transfers between devices  18.6 us (33%)
  waiting for transfers between devices  13.9 us (24%)
  other arithmetic  1.16 us (2%)
  between operations  0.98 us (2%)
    pallas_call x12, Pallas kernels, call(): pl.pallas_call(kernel, out_shape=[jax.ShapeDtypeStruct(s, F32) for s in o...  22.1 us
    ppermute x19, starting transfers between devices, swap(): return lax.ppermute(block, AXES, [(i, i ^ distance) for i in range(count)])  16.1 us
    ppermute x19, waiting for transfers between devices, swap(): return lax.ppermute(block, AXES, [(i, i ^ distance) for i in range(count)])  8.81 us
    ppermute x2, waiting for transfers between devices, give(): lax.ppermute(block, AXES, [(first * quarter + i, second * quarter + i) fo...  3.77 us
    ppermute x2, starting transfers between devices, give(): lax.ppermute(block, AXES, [(first * quarter + i, second * quarter + i) fo...  2.13 us
    ppermute x2, waiting for transfers between devices, pair(): lax.ppermute(block, AXES, [(i, step.get(i // quarter, lambda i: i ^ 1)(i)...  1.27 us
    concatenate x1, other arithmetic, shards(): section = jnp.concatenate(sections, 0)  1.16 us
  transfers between devices with their start and end apart: 23, of which 12 were waited for; matrix products, arithmetic and copies ran while one was open for 2% of the time, Pallas kernels for 29%

profile of v6, /device:TPU:17, one launch (start us, length us, event | category | flops | bytes accessed | tf_op | source)
XLA Modules:
  0.0 56.7 jit_solution(5416486304284047768)
XLA Ops:
  1.9 1.2 %pad_maximum_fusion.section_ref = f32[3,256,256]{2,1,0:T(8,128)S(1)} fusion(f32[1,256,256]{2,1,0:T(8,128)} %param.5, f32[1,256,256]{2,1,0:T(8,128)} %param.4, f32[1,256,256]{2,1,0:T(8,128)} %param.3), kind=kLoop, calls=%fused_computation | loop fusion | flops 393216 | bytes 1572864 | tf_op jit(solution)/shard_map/concatenate | solution.py:274
  3.5 2.6 %shard_map.58 = (f32[3,256,256]{2,1,0:T(8,128)S(1)}, f32[72,256]{1,0:T(8,128)S(1)}, f32[200,256]{1,0:T(8,128)S(1)}, f32[3,256,256]{2,1,0:T(8,128)S(1)}) custom-call(f32[3,256,256]{2,1,0:T(8,128)S(1)} %pad_maximum_fusion.section_ref, f32[1,256,256]{2,1,0:T(8,128)S(1)} %collective-permute-done.got1, f32[1,256,256]{2,1,0:T(8,128)S(1)} %collective-permute-done.1.got2, ...), custom_call_target="tpu_custom_call" | custom-call | flops 1207959552 | bytes 1048576 | tf_op jit(solution)/shard_map/pallas_call | solution.py:256
  6.1 1.3 %collective-permute-start.4 = (f32[72,256]{1,0:T(8,128)S(1)}, f32[72,256]{1,0:T(8,128)S(1)}, u32[]{:S(2)}, u32[]{:S(2)}) collective-permute-start(f32[72,256]{1,0:T(8,128)S(1)} %get-tuple-element.34), channel_id=1, source_target_pairs={{0,2},{1,3},{2,0},{3,1},{4,6},{5,7},{6,4},{7,5},{8,10},{9,11},{10,... | collective-permute-start | bytes 221192 | tf_op jit(solution)/shard_map/ppermute | solution.py:21
  7.7 1.7 %collective-permute-done.4.near_ref.near1 = f32[72,256]{1,0:T(8,128)S(1)} collective-permute-done((f32[72,256]{1,0:T(8,128)S(1)}, f32[72,256]{1,0:T(8,128)S(1)}, u32[]{:S(2)}, u32[]{:S(2)}) %collective-permute-start.4) | collective-permute-done | bytes 73760 | tf_op jit(solution)/shard_map/ppermute | solution.py:21
  9.4 2.0 %collective-permute-start.5 = (f32[72,256]{1,0:T(8,128)S(1)}, f32[72,256]{1,0:T(8,128)S(1)}, u32[]{:S(2)}, u32[]{:S(2)}) collective-permute-start(f32[72,256]{1,0:T(8,128)S(1)} %collective-permute-done.4.near_ref.near1), channel_id=1, source_target_pairs={{0,1},{1,0},{2,3},{3,2},{4,5},{5,4},{6,7},{7,6},{8,9},{9,8},{10,11... | collective-permute-start | bytes 221192 | tf_op jit(solution)/shard_map/ppermute | solution.py:21
  11.4 0.9 %collective-permute-done.5.far_ref.far1 = f32[72,256]{1,0:T(8,128)S(1)} collective-permute-done((f32[72,256]{1,0:T(8,128)S(1)}, f32[72,256]{1,0:T(8,128)S(1)}, u32[]{:S(2)}, u32[]{:S(2)}) %collective-permute-start.5) | collective-permute-done | bytes 73760 | tf_op jit(solution)/shard_map/ppermute | solution.py:21
  12.3 2.1 %shard_map.59.half_ref = f32[3,256,256]{2,1,0:T(8,128)S(1)} custom-call(f32[3,256,256]{2,1,0:T(8,128)S(1)} %get-tuple-element.33.own_ref, f32[72,256]{1,0:T(8,128)S(1)} %collective-permute-done.4.near_ref.near1, f32[72,256]{1,0:T(8,128)S(1)} %collective-permute-done.5.far_ref.far1), custom_call_target="tpu_custom_call" | custom-call | flops 905969664 | bytes 786432 | tf_op jit(solution)/shard_map/pallas_call | solution.py:256
  14.4 0.9 %collective-permute-start.6 = (f32[200,256]{1,0:T(8,128)S(1)}, f32[200,256]{1,0:T(8,128)S(1)}, u32[]{:S(2)}, u32[]{:S(2)}) collective-permute-start(f32[200,256]{1,0:T(8,128)S(1)} %collective-permute-done.3.near_ref.near2), channel_id=1, source_target_pairs={{0,1},{1,0},{2,3},{3,2},{4,5},{5,4},{6,7},{7,6},{8,9},{9,8},{10,11... | collective-permute-start | bytes 614408 | tf_op jit(solution)/shard_map/ppermute | solution.py:21
  15.3 1.1 %collective-permute-done.6.far_ref.far2 = f32[200,256]{1,0:T(8,128)S(1)} collective-permute-done((f32[200,256]{1,0:T(8,128)S(1)}, f32[200,256]{1,0:T(8,128)S(1)}, u32[]{:S(2)}, u32[]{:S(2)}) %collective-permute-start.6) | collective-permute-done | bytes 204832 | tf_op jit(solution)/shard_map/ppermute | solution.py:21
  17.1 1.3 %collective-permute-start.8 = (f32[72,256]{1,0:T(8,128)S(1)}, f32[72,256]{1,0:T(8,128)S(1)}, u32[]{:S(2)}, u32[]{:S(2)}) collective-permute-start(f32[72,256]{1,0:T(8,128)S(1)} %get-tuple-element.39), channel_id=1, source_target_pairs={{0,4},{1,5},{2,6},{3,7},{4,0},{5,1},{6,2},{7,3},{8,12},{9,13},{10,... | collective-permute-start | bytes 221192 | tf_op jit(solution)/shard_map/ppermute | solution.py:21
  18.6 2.6 %shard_map.61.old_ref = f32[3,256,256]{2,1,0:T(8,128)S(1)} custom-call(f32[3,256,256]{2,1,0:T(8,128)S(1)} %get-tuple-element.40.old_ref, f32[72,256]{1,0:T(8,128)S(1)} %collective-permute-done.4.near_ref.near1, f32[72,256]{1,0:T(8,128)S(1)} %collective-permute-done.5.far_ref.far1, f32[200,256]{1,0:T(8,128)S(1)} %collective-permute-done.3.near_ref.near2, ...), custom_call_target="tpu_custom_call" | custom-call | flops 1207959552 | bytes 1310720 | tf_op jit(solution)/shard_map/pallas_call | solution.py:256
  21.2 1.2 %collective-permute-start.9 = (f32[72,256]{1,0:T(8,128)S(1)}, f32[72,256]{1,0:T(8,128)S(1)}, u32[]{:S(2)}, u32[]{:S(2)}) collective-permute-start(f32[72,256]{1,0:T(8,128)S(1)} %collective-permute-done.8.near_ref.near1), channel_id=1, source_target_pairs={{0,1},{1,0},{2,3},{3,2},{4,5},{5,4},{6,7},{7,6},{8,9},{9,8},{10,11... | collective-permute-start | bytes 221192 | tf_op jit(solution)/shard_map/ppermute | solution.py:21
  22.3 0.9 %collective-permute-done.9.far_ref.far1 = f32[72,256]{1,0:T(8,128)S(1)} collective-permute-done((f32[72,256]{1,0:T(8,128)S(1)}, f32[72,256]{1,0:T(8,128)S(1)}, u32[]{:S(2)}, u32[]{:S(2)}) %collective-permute-start.9) | collective-permute-done | bytes 73760 | tf_op jit(solution)/shard_map/ppermute | solution.py:21
  23.2 2.1 %shard_map.62.half_ref = f32[3,256,256]{2,1,0:T(8,128)S(1)} custom-call(f32[3,256,256]{2,1,0:T(8,128)S(1)} %get-tuple-element.38.own_ref, f32[72,256]{1,0:T(8,128)S(1)} %collective-permute-done.8.near_ref.near1, f32[72,256]{1,0:T(8,128)S(1)} %collective-permute-done.9.far_ref.far1), custom_call_target="tpu_custom_call" | custom-call | flops 905969664 | bytes 786432 | tf_op jit(solution)/shard_map/pallas_call | solution.py:256
  25.3 0.9 %collective-permute-start.10 = (f32[200,256]{1,0:T(8,128)S(1)}, f32[200,256]{1,0:T(8,128)S(1)}, u32[]{:S(2)}, u32[]{:S(2)}) collective-permute-start(f32[200,256]{1,0:T(8,128)S(1)} %collective-permute-done.7.near_ref.near2), channel_id=1, source_target_pairs={{0,1},{1,0},{2,3},{3,2},{4,5},{5,4},{6,7},{7,6},{8,9},{9,8},{10,11... | collective-permute-start | bytes 614408 | tf_op jit(solution)/shard_map/ppermute | solution.py:21
  26.3 1.1 %collective-permute-done.10.far_ref.far2 = f32[200,256]{1,0:T(8,128)S(1)} collective-permute-done((f32[200,256]{1,0:T(8,128)S(1)}, f32[200,256]{1,0:T(8,128)S(1)}, u32[]{:S(2)}, u32[]{:S(2)}) %collective-permute-start.10) | collective-permute-done | bytes 204832 | tf_op jit(solution)/shard_map/ppermute | solution.py:21
  28.1 1.4 %collective-permute-start.11 = (f32[72,256]{1,0:T(8,128)S(1)}, f32[72,256]{1,0:T(8,128)S(1)}, u32[]{:S(2)}, u32[]{:S(2)}) collective-permute-start(f32[72,256]{1,0:T(8,128)S(1)} %get-tuple-element.45), channel_id=1, source_target_pairs={{0,8},{1,9},{2,10},{3,11},{4,12},{5,13},{6,14},{7,15},{8,0},{9,1},... | collective-permute-start | bytes 221192 | tf_op jit(solution)/shard_map/ppermute | solution.py:21
  29.6 2.6 %shard_map.64.old_ref = f32[3,256,256]{2,1,0:T(8,128)S(1)} custom-call(f32[3,256,256]{2,1,0:T(8,128)S(1)} %shard_map.61.old_ref, f32[72,256]{1,0:T(8,128)S(1)} %collective-permute-done.8.near_ref.near1, f32[72,256]{1,0:T(8,128)S(1)} %collective-permute-done.9.far_ref.far1, f32[200,256]{1,0:T(8,128)S(1)} %collective-permute-done.7.near_ref.near2, ...), custom_call_target="tpu_custom_call" | custom-call | flops 1207959552 | bytes 1310720 | tf_op jit(solution)/shard_map/pallas_call | solution.py:256
  32.2 1.1 %collective-permute-start.12 = (f32[72,256]{1,0:T(8,128)S(1)}, f32[72,256]{1,0:T(8,128)S(1)}, u32[]{:S(2)}, u32[]{:S(2)}) collective-permute-start(f32[72,256]{1,0:T(8,128)S(1)} %collective-permute-done.11.near_ref.near1), channel_id=1, source_target_pairs={{0,1},{1,0},{2,3},{3,2},{4,5},{5,4},{6,7},{7,6},{8,9},{9,8},{10,11... | collective-permute-start | bytes 221192 | tf_op jit(solution)/shard_map/ppermute | solution.py:21
  33.2 0.9 %collective-permute-done.12.far_ref.far1 = f32[72,256]{1,0:T(8,128)S(1)} collective-permute-done((f32[72,256]{1,0:T(8,128)S(1)}, f32[72,256]{1,0:T(8,128)S(1)}, u32[]{:S(2)}, u32[]{:S(2)}) %collective-permute-start.12) | collective-permute-done | bytes 73760 | tf_op jit(solution)/shard_map/ppermute | solution.py:21
  34.2 2.1 %shard_map.65 = (f32[3,256,256]{2,1,0:T(8,128)S(1)}, f32[72,256]{1,0:T(8,128)S(1)}) custom-call(f32[3,256,256]{2,1,0:T(8,128)S(1)} %get-tuple-element.44.own_ref, f32[72,256]{1,0:T(8,128)S(1)} %collective-permute-done.11.near_ref.near1, f32[72,256]{1,0:T(8,128)S(1)} %collective-permute-done.12.far_ref.far1), custom_call_target="tpu_custom_call" | custom-call | flops 905969664 | bytes 786432 | tf_op jit(solution)/shard_map/pallas_call | solution.py:256
  36.3 1.0 %collective-permute-start.16 = (f32[200,256]{1,0:T(8,128)S(1)}, f32[200,256]{1,0:T(8,128)S(1)}, u32[]{:S(2)}, u32[]{:S(2)}) collective-permute-start(f32[200,256]{1,0:T(8,128)S(1)} %collective-permute-done.15.near2.near_ref), channel_id=1, source_target_pairs={{0,1},{1,0},{2,3},{3,2},{4,5},{5,4},{6,7},{7,6},{8,9},{9,8},{10,11... | collective-permute-start | bytes 614408 | tf_op jit(solution)/shard_map/ppermute | solution.py:21
  39.0 0.9 %collective-permute-start.17 = (f32[200,256]{1,0:T(8,128)S(1)}, f32[200,256]{1,0:T(8,128)S(1)}, u32[]{:S(2)}, u32[]{:S(2)}) collective-permute-start(f32[200,256]{1,0:T(8,128)S(1)} %shard_map.67), channel_id=1, source_target_pairs={{8,24},{9,25},{10,26},{11,27},{12,28},{13,29},{14,30},{15,31}} | collective-permute-start | bytes 614408 | tf_op jit(solution)/shard_map/ppermute | solution.py:34
  39.9 1.3 %collective-permute-done.14.near2 = f32[72,256]{1,0:T(8,128)S(1)} collective-permute-done((f32[72,256]{1,0:T(8,128)S(1)}, f32[72,256]{1,0:T(8,128)S(1)}, u32[]{:S(2)}, u32[]{:S(2)}) %collective-permute-start.14) | collective-permute-done | bytes 73760 | tf_op jit(solution)/shard_map/ppermute | solution.py:29
  41.1 1.2 %collective-permute-start.18 = (f32[72,256]{1,0:T(8,128)S(1)}, f32[72,256]{1,0:T(8,128)S(1)}, u32[]{:S(2)}, u32[]{:S(2)}) collective-permute-start(f32[72,256]{1,0:T(8,128)S(1)} %collective-permute-done.14.near2), channel_id=1, source_target_pairs={{0,1},{1,0},{2,3},{3,2},{4,5},{5,4},{6,7},{7,6},{8,9},{9,8},{10,11... | collective-permute-start | bytes 221192 | tf_op jit(solution)/shard_map/ppermute | solution.py:21
  42.3 1.3 %collective-permute-start.20 = (f32[200,256]{1,0:T(8,128)S(1)}, f32[200,256]{1,0:T(8,128)S(1)}, u32[]{:S(2)}, u32[]{:S(2)}) collective-permute-start(f32[200,256]{1,0:T(8,128)S(1)} %shard_map.67), channel_id=1, source_target_pairs={{8,16},{9,17},{10,18},{11,19},{12,20},{13,21},{14,22},{15,23}} | collective-permute-start | bytes 614408 | tf_op jit(solution)/shard_map/ppermute | solution.py:34
  43.6 2.6 %shard_map.66.old_ref = f32[3,256,256]{2,1,0:T(8,128)S(1)} custom-call(f32[3,256,256]{2,1,0:T(8,128)S(1)} %shard_map.64.old_ref, f32[72,256]{1,0:T(8,128)S(1)} %collective-permute-done.11.near_ref.near1, f32[72,256]{1,0:T(8,128)S(1)} %collective-permute-done.12.far_ref.far1, f32[200,256]{1,0:T(8,128)S(1)} %collective-permute-done.15.near2.near_ref, ...), custom_call_target="tpu_custom_call" | custom-call | flops 1207959552 | bytes 1310720 | tf_op jit(solution)/shard_map/pallas_call | solution.py:256
  46.2 2.1 %shard_map.68.half_ref = f32[3,256,256]{2,1,0:T(8,128)S(1)} custom-call(f32[3,256,256]{2,1,0:T(8,128)S(1)} %shard_map.66.old_ref, f32[72,256]{1,0:T(8,128)S(1)} %collective-permute-done.14.near2, f32[72,256]{1,0:T(8,128)S(1)} %collective-permute-done.18.far2, f32[72,256]{1,0:T(8,128)S(1)} %collective-permute-done.13.near3, ...), custom_call_target="tpu_custom_call" | custom-call | flops 905969664 | bytes 1310720 | tf_op jit(solution)/shard_map/pallas_call | solution.py:256
  48.9 3.8 %collective-permute-done.20.near2 = f32[200,256]{1,0:T(8,128)S(1)} collective-permute-done((f32[200,256]{1,0:T(8,128)S(1)}, f32[200,256]{1,0:T(8,128)S(1)}, u32[]{:S(2)}, u32[]{:S(2)}) %collective-permute-start.20) | collective-permute-done | bytes 204832 | tf_op jit(solution)/shard_map/ppermute | solution.py:34
  52.6 1.4 %collective-permute-start.22 = (f32[200,256]{1,0:T(8,128)S(1)}, f32[200,256]{1,0:T(8,128)S(1)}, u32[]{:S(2)}, u32[]{:S(2)}) collective-permute-start(f32[200,256]{1,0:T(8,128)S(1)} %collective-permute-done.20.near2), channel_id=1, source_target_pairs={{0,1},{1,0},{2,3},{3,2},{4,5},{5,4},{6,7},{7,6},{8,9},{9,8},{10,11... | collective-permute-start | bytes 614408 | tf_op jit(solution)/shard_map/ppermute | solution.py:21
  54.1 1.1 %collective-permute-done.22.far2 = f32[200,256]{1,0:T(8,128)S(1)} collective-permute-done((f32[200,256]{1,0:T(8,128)S(1)}, f32[200,256]{1,0:T(8,128)S(1)}, u32[]{:S(2)}, u32[]{:S(2)}) %collective-permute-start.22) | collective-permute-done | bytes 204832 | tf_op jit(solution)/shard_map/ppermute | solution.py:21
  55.1 1.4 %shard_map.69 = (f32[1,256,256]{2,1,0:T(8,128)}, f32[1,256,256]{2,1,0:T(8,128)}, f32[1,256,256]{2,1,0:T(8,128)}) custom-call(f32[3,256,256]{2,1,0:T(8,128)S(1)} %shard_map.66.old_ref, f32[3,256,256]{2,1,0:T(8,128)S(1)} %shard_map.68.half_ref, f32[200,256]{1,0:T(8,128)S(1)} %collective-permute-done.20.near2, f32[200,256]{1,0:T(8,128)S(1)} %collective-permute-done.22.far2, ...), custom_call_target="tpu_custom_call" | custom-call | flops 301989888 | bytes 1572864 | tf_op jit(solution)/shard_map/pallas_call | solution.py:256
  (27 shorter events, 6.1 us)
Async XLA Ops:
  0.6 2.4 %collective-permute-start = (f32[1,256,256]{2,1,0:T(8,128)}, f32[1,256,256]{2,1,0:T(8,128)S(1)}, u32[]{:S(2)}, u32[]{:S(2)}) collective-permute-start(f32[1,256,256]{2,1,0:T(8,128)} %param.3), channel_id=1, source_target_pairs={{0,1},{1,0},{2,3},{3,2},{4,5},{5,4},{6,7},{7,6},{8,9},{9,8},{10,11... | collective-permute-start | bytes 786440 | tf_op jit(solution)/shard_map/ppermute | solution.py:21
  1.4 1.7 %collective-permute-start.1 = (f32[1,256,256]{2,1,0:T(8,128)}, f32[1,256,256]{2,1,0:T(8,128)S(1)}, u32[]{:S(2)}, u32[]{:S(2)}) collective-permute-start(f32[1,256,256]{2,1,0:T(8,128)} %param.4), channel_id=1, source_target_pairs={{0,1},{1,0},{2,3},{3,2},{4,5},{5,4},{6,7},{7,6},{8,9},{9,8},{10,11... | collective-permute-start | bytes 786440 | tf_op jit(solution)/shard_map/ppermute | solution.py:21
  1.4 2.0 %collective-permute-start.2 = (f32[1,256,256]{2,1,0:T(8,128)}, f32[1,256,256]{2,1,0:T(8,128)S(1)}, u32[]{:S(2)}, u32[]{:S(2)}) collective-permute-start(f32[1,256,256]{2,1,0:T(8,128)} %param.5), channel_id=1, source_target_pairs={{0,1},{1,0},{2,3},{3,2},{4,5},{5,4},{6,7},{7,6},{8,9},{9,8},{10,11... | collective-permute-start | bytes 786440 | tf_op jit(solution)/shard_map/ppermute | solution.py:21
  6.1 3.3 %collective-permute-start.4 = (f32[72,256]{1,0:T(8,128)S(1)}, f32[72,256]{1,0:T(8,128)S(1)}, u32[]{:S(2)}, u32[]{:S(2)}) collective-permute-start(f32[72,256]{1,0:T(8,128)S(1)} %get-tuple-element.34), channel_id=1, source_target_pairs={{0,2},{1,3},{2,0},{3,1},{4,6},{5,7},{6,4},{7,5},{8,10},{9,11},{10,... | collective-permute-start | bytes 221192 | tf_op jit(solution)/shard_map/ppermute | solution.py:21
  7.4 7.0 %collective-permute-start.3 = (f32[200,256]{1,0:T(8,128)S(1)}, f32[200,256]{1,0:T(8,128)S(1)}, u32[]{:S(2)}, u32[]{:S(2)}) collective-permute-start(f32[200,256]{1,0:T(8,128)S(1)} %get-tuple-element.32), channel_id=1, source_target_pairs={{0,2},{1,3},{2,0},{3,1},{4,6},{5,7},{6,4},{7,5},{8,10},{9,11},{10,... | collective-permute-start | bytes 614408 | tf_op jit(solution)/shard_map/ppermute | solution.py:21
  9.4 2.9 %collective-permute-start.5 = (f32[72,256]{1,0:T(8,128)S(1)}, f32[72,256]{1,0:T(8,128)S(1)}, u32[]{:S(2)}, u32[]{:S(2)}) collective-permute-start(f32[72,256]{1,0:T(8,128)S(1)} %collective-permute-done.4.near_ref.near1), channel_id=1, source_target_pairs={{0,1},{1,0},{2,3},{3,2},{4,5},{5,4},{6,7},{7,6},{8,9},{9,8},{10,11... | collective-permute-start | bytes 221192 | tf_op jit(solution)/shard_map/ppermute | solution.py:21
  14.4 2.0 %collective-permute-start.6 = (f32[200,256]{1,0:T(8,128)S(1)}, f32[200,256]{1,0:T(8,128)S(1)}, u32[]{:S(2)}, u32[]{:S(2)}) collective-permute-start(f32[200,256]{1,0:T(8,128)S(1)} %collective-permute-done.3.near_ref.near2), channel_id=1, source_target_pairs={{0,1},{1,0},{2,3},{3,2},{4,5},{5,4},{6,7},{7,6},{8,9},{9,8},{10,11... | collective-permute-start | bytes 614408 | tf_op jit(solution)/shard_map/ppermute | solution.py:21
  17.1 4.1 %collective-permute-start.8 = (f32[72,256]{1,0:T(8,128)S(1)}, f32[72,256]{1,0:T(8,128)S(1)}, u32[]{:S(2)}, u32[]{:S(2)}) collective-permute-start(f32[72,256]{1,0:T(8,128)S(1)} %get-tuple-element.39), channel_id=1, source_target_pairs={{0,4},{1,5},{2,6},{3,7},{4,0},{5,1},{6,2},{7,3},{8,12},{9,13},{10,... | collective-permute-start | bytes 221192 | tf_op jit(solution)/shard_map/ppermute | solution.py:21
  18.4 6.9 %collective-permute-start.7 = (f32[200,256]{1,0:T(8,128)S(1)}, f32[200,256]{1,0:T(8,128)S(1)}, u32[]{:S(2)}, u32[]{:S(2)}) collective-permute-start(f32[200,256]{1,0:T(8,128)S(1)} %get-tuple-element.37), channel_id=1, source_target_pairs={{0,4},{1,5},{2,6},{3,7},{4,0},{5,1},{6,2},{7,3},{8,12},{9,13},{10,... | collective-permute-start | bytes 614408 | tf_op jit(solution)/shard_map/ppermute | solution.py:21
  21.2 2.1 %collective-permute-start.9 = (f32[72,256]{1,0:T(8,128)S(1)}, f32[72,256]{1,0:T(8,128)S(1)}, u32[]{:S(2)}, u32[]{:S(2)}) collective-permute-start(f32[72,256]{1,0:T(8,128)S(1)} %collective-permute-done.8.near_ref.near1), channel_id=1, source_target_pairs={{0,1},{1,0},{2,3},{3,2},{4,5},{5,4},{6,7},{7,6},{8,9},{9,8},{10,11... | collective-permute-start | bytes 221192 | tf_op jit(solution)/shard_map/ppermute | solution.py:21
  25.3 2.0 %collective-permute-start.10 = (f32[200,256]{1,0:T(8,128)S(1)}, f32[200,256]{1,0:T(8,128)S(1)}, u32[]{:S(2)}, u32[]{:S(2)}) collective-permute-start(f32[200,256]{1,0:T(8,128)S(1)} %collective-permute-done.7.near_ref.near2), channel_id=1, source_target_pairs={{0,1},{1,0},{2,3},{3,2},{4,5},{5,4},{6,7},{7,6},{8,9},{9,8},{10,11... | collective-permute-start | bytes 614408 | tf_op jit(solution)/shard_map/ppermute | solution.py:21
  28.1 4.1 %collective-permute-start.11 = (f32[72,256]{1,0:T(8,128)S(1)}, f32[72,256]{1,0:T(8,128)S(1)}, u32[]{:S(2)}, u32[]{:S(2)}) collective-permute-start(f32[72,256]{1,0:T(8,128)S(1)} %get-tuple-element.45), channel_id=1, source_target_pairs={{0,8},{1,9},{2,10},{3,11},{4,12},{5,13},{6,14},{7,15},{8,0},{9,1},... | collective-permute-start | bytes 221192 | tf_op jit(solution)/shard_map/ppermute | solution.py:21
  29.4 6.8 %collective-permute-start.15 = (f32[200,256]{1,0:T(8,128)S(1)}, f32[200,256]{1,0:T(8,128)S(1)}, u32[]{:S(2)}, u32[]{:S(2)}) collective-permute-start(f32[200,256]{1,0:T(8,128)S(1)} %get-tuple-element.51), channel_id=1, source_target_pairs={{0,8},{1,9},{2,10},{3,11},{4,12},{5,13},{6,14},{7,15},{8,0},{9,1},... | collective-permute-start | bytes 614408 | tf_op jit(solution)/shard_map/ppermute | solution.py:21
  32.2 2.0 %collective-permute-start.12 = (f32[72,256]{1,0:T(8,128)S(1)}, f32[72,256]{1,0:T(8,128)S(1)}, u32[]{:S(2)}, u32[]{:S(2)}) collective-permute-start(f32[72,256]{1,0:T(8,128)S(1)} %collective-permute-done.11.near_ref.near1), channel_id=1, source_target_pairs={{0,1},{1,0},{2,3},{3,2},{4,5},{5,4},{6,7},{7,6},{8,9},{9,8},{10,11... | collective-permute-start | bytes 221192 | tf_op jit(solution)/shard_map/ppermute | solution.py:21
  36.3 2.1 %collective-permute-start.16 = (f32[200,256]{1,0:T(8,128)S(1)}, f32[200,256]{1,0:T(8,128)S(1)}, u32[]{:S(2)}, u32[]{:S(2)}) collective-permute-start(f32[200,256]{1,0:T(8,128)S(1)} %collective-permute-done.15.near2.near_ref), channel_id=1, source_target_pairs={{0,1},{1,0},{2,3},{3,2},{4,5},{5,4},{6,7},{7,6},{8,9},{9,8},{10,11... | collective-permute-start | bytes 614408 | tf_op jit(solution)/shard_map/ppermute | solution.py:21
  37.2 3.9 %collective-permute-start.14 = (f32[72,256]{1,0:T(8,128)S(1)}, f32[72,256]{1,0:T(8,128)S(1)}, u32[]{:S(2)}, u32[]{:S(2)}) collective-permute-start(f32[72,256]{1,0:T(8,128)S(1)} %get-tuple-element.48), channel_id=1, source_target_pairs={{0,1},{1,0},{2,3},{3,2},{4,5},{5,4},{6,7},{7,6},{8,16},{9,17},{10,... | collective-permute-start | bytes 221192 | tf_op jit(solution)/shard_map/ppermute | solution.py:29
  37.4 3.8 %collective-permute-start.13 = (f32[72,256]{1,0:T(8,128)S(1)}, f32[72,256]{1,0:T(8,128)S(1)}, u32[]{:S(2)}, u32[]{:S(2)}) collective-permute-start(f32[72,256]{1,0:T(8,128)S(1)} %get-tuple-element.48), channel_id=1, source_target_pairs={{0,1},{1,0},{2,3},{3,2},{4,5},{5,4},{6,7},{7,6},{8,24},{9,25},{10,... | collective-permute-start | bytes 221192 | tf_op jit(solution)/shard_map/ppermute | solution.py:29
  39.0 9.3 %collective-permute-start.17 = (f32[200,256]{1,0:T(8,128)S(1)}, f32[200,256]{1,0:T(8,128)S(1)}, u32[]{:S(2)}, u32[]{:S(2)}) collective-permute-start(f32[200,256]{1,0:T(8,128)S(1)} %shard_map.67), channel_id=1, source_target_pairs={{8,24},{9,25},{10,26},{11,27},{12,28},{13,29},{14,30},{15,31}} | collective-permute-start | bytes 614408 | tf_op jit(solution)/shard_map/ppermute | solution.py:34
  41.1 5.1 %collective-permute-start.18 = (f32[72,256]{1,0:T(8,128)S(1)}, f32[72,256]{1,0:T(8,128)S(1)}, u32[]{:S(2)}, u32[]{:S(2)}) collective-permute-start(f32[72,256]{1,0:T(8,128)S(1)} %collective-permute-done.14.near2), channel_id=1, source_target_pairs={{0,1},{1,0},{2,3},{3,2},{4,5},{5,4},{6,7},{7,6},{8,9},{9,8},{10,11... | collective-permute-start | bytes 221192 | tf_op jit(solution)/shard_map/ppermute | solution.py:21
  42.3 3.9 %collective-permute-start.19 = (f32[72,256]{1,0:T(8,128)S(1)}, f32[72,256]{1,0:T(8,128)S(1)}, u32[]{:S(2)}, u32[]{:S(2)}) collective-permute-start(f32[72,256]{1,0:T(8,128)S(1)} %collective-permute-done.13.near3), channel_id=1, source_target_pairs={{0,1},{1,0},{2,3},{3,2},{4,5},{5,4},{6,7},{7,6},{8,9},{9,8},{10,11... | collective-permute-start | bytes 221192 | tf_op jit(solution)/shard_map/ppermute | solution.py:21
  42.3 10.3 %collective-permute-start.20 = (f32[200,256]{1,0:T(8,128)S(1)}, f32[200,256]{1,0:T(8,128)S(1)}, u32[]{:S(2)}, u32[]{:S(2)}) collective-permute-start(f32[200,256]{1,0:T(8,128)S(1)} %shard_map.67), channel_id=1, source_target_pairs={{8,16},{9,17},{10,18},{11,19},{12,20},{13,21},{14,22},{15,23}} | collective-permute-start | bytes 614408 | tf_op jit(solution)/shard_map/ppermute | solution.py:34
  48.3 4.3 %collective-permute-start.21 = (f32[200,256]{1,0:T(8,128)S(1)}, f32[200,256]{1,0:T(8,128)S(1)}, u32[]{:S(2)}, u32[]{:S(2)}) collective-permute-start(f32[200,256]{1,0:T(8,128)S(1)} %collective-permute-done.17.near3), channel_id=1, source_target_pairs={{0,1},{1,0},{2,3},{3,2},{4,5},{5,4},{6,7},{7,6},{8,9},{9,8},{10,11... | collective-permute-start | bytes 614408 | tf_op jit(solution)/shard_map/ppermute | solution.py:21
  52.6 2.5 %collective-permute-start.22 = (f32[200,256]{1,0:T(8,128)S(1)}, f32[200,256]{1,0:T(8,128)S(1)}, u32[]{:S(2)}, u32[]{:S(2)}) collective-permute-start(f32[200,256]{1,0:T(8,128)S(1)} %collective-permute-done.20.near2), channel_id=1, source_target_pairs={{0,1},{1,0},{2,3},{3,2},{4,5},{5,4},{6,7},{7,6},{8,9},{9,8},{10,11... | collective-permute-start | bytes 614408 | tf_op jit(solution)/shard_map/ppermute | solution.py:21

commit v7 on v3

--- a/solution.py
+++ b/solution.py
@@ -204,34 +204,60 @@
     return jnp.where(third, near3[...], near2[...]), jnp.where(third, far3[...], far2[...])
 
 
-def last_early_kernel(distance, own_ref, near2, far2, near3, far3, half_ref):
-    me = place()
-    facing = unpack_symmetric(*by_third(distance, me, near2, far2, near3, far3), bit(me, 1), 0)
-    for i, x in enumerate(before_trans((own_ref[0], own_ref[1], own_ref[2]), facing)):
-        half_ref[i] = x
-
-
-def last_kernel(distance, old_ref, half_ref, near2, far2, near3, far3, left_ref, right_ref, trans_ref):
+def last_early_kernel(distance, old_ref, near2, far2, near3, far3, half_ref, left_out, right_out, trans_out, sems):
     me = place()
     upper = bit(me, distance)
-    into, away = unpack_second(*by_third(distance, me, near2, far2, near3, far3), bit(me, 1))
-    trans, left = after_trans(half_ref[0], half_ref[1], away, into)
-    right_ref[0] = jnp.where(upper, half_ref[2], old_ref[1])
-    trans_ref[0] = jnp.where(upper, trans, old_ref[2])
-    left_ref[0] = jnp.where(upper, left, old_ref[0])
-
-
-def call(kernel, products, outs, *args):
-    vmem = pl.BlockSpec(memory_space=pltpu.VMEM)
+
+    @pl.when(upper)
+    def _():
+        facing = unpack_symmetric(*by_third(distance, me, near2, far2, near3, far3), bit(me, 1), 0)
+        for i, x in enumerate(before_trans((old_ref[0], old_ref[1], old_ref[2]), facing)):
+            half_ref[i] = x
+
+    @pl.when(jnp.logical_not(upper))
+    def _():
+        outs = left_out, right_out, trans_out
+        copies = [pltpu.make_async_copy(old_ref.at[i : i + 1], out, sems.at[i]) for i, out in enumerate(outs)]
+        for copy in copies:
+            copy.start()
+        for copy in copies:
+            copy.wait()
+
+
+def last_kernel(distance, half_ref, near2, far2, near3, far3, _l, _r, _t, left_out, right_out, trans_out, new_ref, sems):
+    me = place()
+
+    @pl.when(bit(me, distance))
+    def _():
+        right_copy = pltpu.make_async_copy(half_ref.at[2:3], right_out, sems.at[0])
+        trans_copy = pltpu.make_async_copy(new_ref.at[0:1], trans_out, sems.at[1])
+        left_copy = pltpu.make_async_copy(new_ref.at[1:2], left_out, sems.at[2])
+        right_copy.start()
+        into, away = unpack_second(*by_third(distance, me, near2, far2, near3, far3), bit(me, 1))
+        q = split(into)
+        new_ref[0] = dot3(split(half_ref[0]), q)
+        trans_copy.start()
+        bounced = split(dot3(split(half_ref[1]), q))
+        new_ref[1] = away + dot3(split(into.T), bounced)
+        left_copy.start()
+        right_copy.wait()
+        trans_copy.wait()
+        left_copy.wait()
+
+
+def call(kernel, products, outs, *args, given=(), copied=0, scratch=()):
+    vmem, hbm = pl.BlockSpec(memory_space=pltpu.VMEM), pl.BlockSpec(memory_space=pltpu.HBM)
     m = args[0].shape[-1]
     return pl.pallas_call(
         kernel,
         out_shape=[jax.ShapeDtypeStruct(s, F32) for s in outs],
-        in_specs=[vmem] * len(args),
-        out_specs=[vmem] * len(outs),
+        in_specs=[vmem] * len(args) + [hbm] * len(given),
+        out_specs=[vmem] * (len(outs) - copied) + [hbm] * copied,
+        input_output_aliases={len(args) + i: len(outs) - copied + i for i in range(len(given))},
+        scratch_shapes=scratch,
         cost_estimate=pl.CostEstimate(flops=2 * products * m**3, bytes_accessed=4 * m**2 * len(args), transcendentals=0),
         compiler_params=pltpu.CompilerParams(vmem_limit_bytes=40 * 2**20),
-    )(*args)
+    )(*args, *given)
 
 
 def shards(refl_left, refl_right, trans):
@@ -268,10 +294,15 @@
     first3, first2, prefix = lax.optimization_barrier((first3, first2, prefix))
     (prefix,) = pending(prefix)
     args = prefix, first2, swap(first2, 1), first3, swap(first3, 1)
-    (halfway,) = call(functools.partial(last_early_kernel, distance), 27, [stack], *args)
-    near2, near3, halfway = lax.optimization_barrier((near2, near3, halfway))
-    args = prefix, halfway, near2, swap(near2, 1), near3, swap(near3, 1)
-    return tuple(call(functools.partial(last_kernel, distance), 9, [(1, m, m)] * 3, *args))
+    one, sems = (1, m, m), pltpu.SemaphoreType.DMA((3,))
+    kernel = functools.partial(last_early_kernel, distance)
+    halfway, *given = call(kernel, 27, [stack, one, one, one], *args, copied=3, scratch=[sems])
+    near3, halfway = lax.optimization_barrier((near3, halfway))
+    far3 = swap(near3, 1)
+    near2, far3 = lax.optimization_barrier((near2, far3))
+    args = halfway, near2, swap(near2, 1), near3, far3
+    scratch = [pltpu.VMEM((2, m, m), F32), sems]
+    return tuple(call(functools.partial(last_kernel, distance), 9, [one] * 3, *args, given=given, copied=3, scratch=scratch))
 
 
 def solution(mesh):

time: 56.1 us -> 55.1 us (0.982); the launches traced: 55.2 us -> 54.9 us
  waiting for transfers between devices: 12.2 us -> 11.6 us
    ppermute x19, starting transfers between devices: 15.7 us -> 16.3 us  [swap(): return lax.ppermute(block, AXES, [(i, i ^ distance) for i in range(count)])]
where the time goes in v7:
time: 55.1 us; the launch traced here: 54.9 us
  Pallas kernels  22.1 us (40%)
  starting transfers between devices  19.1 us (35%)
  waiting for transfers between devices  11.6 us (21%)
  other arithmetic  1.16 us (2%)
  between operations  0.96 us (2%)
    pallas_call x12, Pallas kernels, call(): pl.pallas_call(kernel, out_shape=[jax.ShapeDtypeStruct(s, F32) for s in o...  22.1 us
    ppermute x19, starting transfers between devices, swap(): return lax.ppermute(block, AXES, [(i, i ^ distance) for i in range(count)])  16.3 us
    ppermute x19, waiting for transfers between devices, swap(): return lax.ppermute(block, AXES, [(i, i ^ distance) for i in range(count)])  8.85 us
    ppermute x4, starting transfers between devices, pair(): lax.ppermute(block, AXES, [(i, step.get(i // quarter, lambda i: i ^ 1)(i)...  2.84 us
    ppermute x4, waiting for transfers between devices, pair(): lax.ppermute(block, AXES, [(i, step.get(i // quarter, lambda i: i ^ 1)(i)...  2.74 us
    concatenate x1, other arithmetic, shards(): section = jnp.concatenate(sections, 0)  1.16 us
  transfers between devices with their start and end apart: 23, of which 12 were waited for; matrix products, arithmetic and copies ran while one was open for 2% of the time, Pallas kernels for 30%

profile of v7, /device:TPU:17, one launch (start us, length us, event | category | flops | bytes accessed | tf_op | source)
XLA Modules:
  0.0 54.9 jit_solution(5834506874818356470)
XLA Ops:
  1.9 1.2 %pad_maximum_fusion.section_ref = f32[3,256,256]{2,1,0:T(8,128)S(1)} fusion(f32[1,256,256]{2,1,0:T(8,128)} %param.5, f32[1,256,256]{2,1,0:T(8,128)} %param.4, f32[1,256,256]{2,1,0:T(8,128)} %param.3), kind=kLoop, calls=%fused_computation | loop fusion | flops 393216 | bytes 1572864 | tf_op jit(solution)/shard_map/concatenate | solution.py:270
  3.5 2.6 %shard_map.58 = (f32[3,256,256]{2,1,0:T(8,128)S(1)}, f32[72,256]{1,0:T(8,128)S(1)}, f32[200,256]{1,0:T(8,128)S(1)}, f32[3,256,256]{2,1,0:T(8,128)S(1)}) custom-call(f32[3,256,256]{2,1,0:T(8,128)S(1)} %pad_maximum_fusion.section_ref, f32[1,256,256]{2,1,0:T(8,128)S(1)} %collective-permute-done.got1, f32[1,256,256]{2,1,0:T(8,128)S(1)} %collective-permute-done.1.got2, ...), custom_call_target="tpu_custom_call" | custom-call | flops 1207959552 | bytes 1048576 | tf_op jit(solution)/shard_map/pallas_call | solution.py:251
  6.1 1.3 %collective-permute-start.4 = (f32[72,256]{1,0:T(8,128)S(1)}, f32[72,256]{1,0:T(8,128)S(1)}, u32[]{:S(2)}, u32[]{:S(2)}) collective-permute-start(f32[72,256]{1,0:T(8,128)S(1)} %get-tuple-element.38), channel_id=1, source_target_pairs={{0,2},{1,3},{2,0},{3,1},{4,6},{5,7},{6,4},{7,5},{8,10},{9,11},{10,... | collective-permute-start | bytes 221192 | tf_op jit(solution)/shard_map/ppermute | solution.py:21
  7.7 1.7 %collective-permute-done.4.near_ref.near1 = f32[72,256]{1,0:T(8,128)S(1)} collective-permute-done((f32[72,256]{1,0:T(8,128)S(1)}, f32[72,256]{1,0:T(8,128)S(1)}, u32[]{:S(2)}, u32[]{:S(2)}) %collective-permute-start.4) | collective-permute-done | bytes 73760 | tf_op jit(solution)/shard_map/ppermute | solution.py:21
  9.4 2.0 %collective-permute-start.5 = (f32[72,256]{1,0:T(8,128)S(1)}, f32[72,256]{1,0:T(8,128)S(1)}, u32[]{:S(2)}, u32[]{:S(2)}) collective-permute-start(f32[72,256]{1,0:T(8,128)S(1)} %collective-permute-done.4.near_ref.near1), channel_id=1, source_target_pairs={{0,1},{1,0},{2,3},{3,2},{4,5},{5,4},{6,7},{7,6},{8,9},{9,8},{10,11... | collective-permute-start | bytes 221192 | tf_op jit(solution)/shard_map/ppermute | solution.py:21
  11.4 0.9 %collective-permute-done.5.far_ref.far1 = f32[72,256]{1,0:T(8,128)S(1)} collective-permute-done((f32[72,256]{1,0:T(8,128)S(1)}, f32[72,256]{1,0:T(8,128)S(1)}, u32[]{:S(2)}, u32[]{:S(2)}) %collective-permute-start.5) | collective-permute-done | bytes 73760 | tf_op jit(solution)/shard_map/ppermute | solution.py:21
  12.3 2.1 %shard_map.59.half_ref = f32[3,256,256]{2,1,0:T(8,128)S(1)} custom-call(f32[3,256,256]{2,1,0:T(8,128)S(1)} %get-tuple-element.37.own_ref, f32[72,256]{1,0:T(8,128)S(1)} %collective-permute-done.4.near_ref.near1, f32[72,256]{1,0:T(8,128)S(1)} %collective-permute-done.5.far_ref.far1), custom_call_target="tpu_custom_call" | custom-call | flops 905969664 | bytes 786432 | tf_op jit(solution)/shard_map/pallas_call | solution.py:251
  14.4 0.9 %collective-permute-start.6 = (f32[200,256]{1,0:T(8,128)S(1)}, f32[200,256]{1,0:T(8,128)S(1)}, u32[]{:S(2)}, u32[]{:S(2)}) collective-permute-start(f32[200,256]{1,0:T(8,128)S(1)} %collective-permute-done.3.near_ref.near2), channel_id=1, source_target_pairs={{0,1},{1,0},{2,3},{3,2},{4,5},{5,4},{6,7},{7,6},{8,9},{9,8},{10,11... | collective-permute-start | bytes 614408 | tf_op jit(solution)/shard_map/ppermute | solution.py:21
  15.3 1.1 %collective-permute-done.6.far_ref.far2 = f32[200,256]{1,0:T(8,128)S(1)} collective-permute-done((f32[200,256]{1,0:T(8,128)S(1)}, f32[200,256]{1,0:T(8,128)S(1)}, u32[]{:S(2)}, u32[]{:S(2)}) %collective-permute-start.6) | collective-permute-done | bytes 204832 | tf_op jit(solution)/shard_map/ppermute | solution.py:21
  17.1 1.3 %collective-permute-start.8 = (f32[72,256]{1,0:T(8,128)S(1)}, f32[72,256]{1,0:T(8,128)S(1)}, u32[]{:S(2)}, u32[]{:S(2)}) collective-permute-start(f32[72,256]{1,0:T(8,128)S(1)} %get-tuple-element.43), channel_id=1, source_target_pairs={{0,4},{1,5},{2,6},{3,7},{4,0},{5,1},{6,2},{7,3},{8,12},{9,13},{10,... | collective-permute-start | bytes 221192 | tf_op jit(solution)/shard_map/ppermute | solution.py:21
  18.6 2.6 %shard_map.61.old_ref = f32[3,256,256]{2,1,0:T(8,128)S(1)} custom-call(f32[3,256,256]{2,1,0:T(8,128)S(1)} %get-tuple-element.44.old_ref, f32[72,256]{1,0:T(8,128)S(1)} %collective-permute-done.4.near_ref.near1, f32[72,256]{1,0:T(8,128)S(1)} %collective-permute-done.5.far_ref.far1, f32[200,256]{1,0:T(8,128)S(1)} %collective-permute-done.3.near_ref.near2, ...), custom_call_target="tpu_custom_call" | custom-call | flops 1207959552 | bytes 1310720 | tf_op jit(solution)/shard_map/pallas_call | solution.py:251
  21.2 1.2 %collective-permute-start.9 = (f32[72,256]{1,0:T(8,128)S(1)}, f32[72,256]{1,0:T(8,128)S(1)}, u32[]{:S(2)}, u32[]{:S(2)}) collective-permute-start(f32[72,256]{1,0:T(8,128)S(1)} %collective-permute-done.8.near_ref.near1), channel_id=1, source_target_pairs={{0,1},{1,0},{2,3},{3,2},{4,5},{5,4},{6,7},{7,6},{8,9},{9,8},{10,11... | collective-permute-start | bytes 221192 | tf_op jit(solution)/shard_map/ppermute | solution.py:21
  22.3 0.9 %collective-permute-done.9.far_ref.far1 = f32[72,256]{1,0:T(8,128)S(1)} collective-permute-done((f32[72,256]{1,0:T(8,128)S(1)}, f32[72,256]{1,0:T(8,128)S(1)}, u32[]{:S(2)}, u32[]{:S(2)}) %collective-permute-start.9) | collective-permute-done | bytes 73760 | tf_op jit(solution)/shard_map/ppermute | solution.py:21
  23.2 2.1 %shard_map.62.half_ref = f32[3,256,256]{2,1,0:T(8,128)S(1)} custom-call(f32[3,256,256]{2,1,0:T(8,128)S(1)} %get-tuple-element.42.own_ref, f32[72,256]{1,0:T(8,128)S(1)} %collective-permute-done.8.near_ref.near1, f32[72,256]{1,0:T(8,128)S(1)} %collective-permute-done.9.far_ref.far1), custom_call_target="tpu_custom_call" | custom-call | flops 905969664 | bytes 786432 | tf_op jit(solution)/shard_map/pallas_call | solution.py:251
  25.3 0.9 %collective-permute-start.10 = (f32[200,256]{1,0:T(8,128)S(1)}, f32[200,256]{1,0:T(8,128)S(1)}, u32[]{:S(2)}, u32[]{:S(2)}) collective-permute-start(f32[200,256]{1,0:T(8,128)S(1)} %collective-permute-done.7.near_ref.near2), channel_id=1, source_target_pairs={{0,1},{1,0},{2,3},{3,2},{4,5},{5,4},{6,7},{7,6},{8,9},{9,8},{10,11... | collective-permute-start | bytes 614408 | tf_op jit(solution)/shard_map/ppermute | solution.py:21
  26.3 1.1 %collective-permute-done.10.far_ref.far2 = f32[200,256]{1,0:T(8,128)S(1)} collective-permute-done((f32[200,256]{1,0:T(8,128)S(1)}, f32[200,256]{1,0:T(8,128)S(1)}, u32[]{:S(2)}, u32[]{:S(2)}) %collective-permute-start.10) | collective-permute-done | bytes 204832 | tf_op jit(solution)/shard_map/ppermute | solution.py:21
  28.1 1.4 %collective-permute-start.12 = (f32[72,256]{1,0:T(8,128)S(1)}, f32[72,256]{1,0:T(8,128)S(1)}, u32[]{:S(2)}, u32[]{:S(2)}) collective-permute-start(f32[72,256]{1,0:T(8,128)S(1)} %get-tuple-element.50), channel_id=1, source_target_pairs={{0,8},{1,9},{2,10},{3,11},{4,12},{5,13},{6,14},{7,15},{8,0},{9,1},... | collective-permute-start | bytes 221192 | tf_op jit(solution)/shard_map/ppermute | solution.py:21
  29.6 2.6 %shard_map.64.old_ref = f32[3,256,256]{2,1,0:T(8,128)S(1)} custom-call(f32[3,256,256]{2,1,0:T(8,128)S(1)} %shard_map.61.old_ref, f32[72,256]{1,0:T(8,128)S(1)} %collective-permute-done.8.near_ref.near1, f32[72,256]{1,0:T(8,128)S(1)} %collective-permute-done.9.far_ref.far1, f32[200,256]{1,0:T(8,128)S(1)} %collective-permute-done.7.near_ref.near2, ...), custom_call_target="tpu_custom_call" | custom-call | flops 1207959552 | bytes 1310720 | tf_op jit(solution)/shard_map/pallas_call | solution.py:251
  32.2 1.1 %collective-permute-start.13 = (f32[72,256]{1,0:T(8,128)S(1)}, f32[72,256]{1,0:T(8,128)S(1)}, u32[]{:S(2)}, u32[]{:S(2)}) collective-permute-start(f32[72,256]{1,0:T(8,128)S(1)} %collective-permute-done.12.near_ref.near1), channel_id=1, source_target_pairs={{0,1},{1,0},{2,3},{3,2},{4,5},{5,4},{6,7},{7,6},{8,9},{9,8},{10,11... | collective-permute-start | bytes 221192 | tf_op jit(solution)/shard_map/ppermute | solution.py:21
  33.2 0.9 %collective-permute-done.13.far_ref.far1 = f32[72,256]{1,0:T(8,128)S(1)} collective-permute-done((f32[72,256]{1,0:T(8,128)S(1)}, f32[72,256]{1,0:T(8,128)S(1)}, u32[]{:S(2)}, u32[]{:S(2)}) %collective-permute-start.13) | collective-permute-done | bytes 73760 | tf_op jit(solution)/shard_map/ppermute | solution.py:21
  34.2 2.1 %shard_map.65 = (f32[3,256,256]{2,1,0:T(8,128)S(1)}, f32[72,256]{1,0:T(8,128)S(1)}) custom-call(f32[3,256,256]{2,1,0:T(8,128)S(1)} %get-tuple-element.49.own_ref, f32[72,256]{1,0:T(8,128)S(1)} %collective-permute-done.12.near_ref.near1, f32[72,256]{1,0:T(8,128)S(1)} %collective-permute-done.13.far_ref.far1), custom_call_target="tpu_custom_call" | custom-call | flops 905969664 | bytes 786432 | tf_op jit(solution)/shard_map/pallas_call | solution.py:251
  36.3 1.0 %collective-permute-start.14 = (f32[200,256]{1,0:T(8,128)S(1)}, f32[200,256]{1,0:T(8,128)S(1)}, u32[]{:S(2)}, u32[]{:S(2)}) collective-permute-start(f32[200,256]{1,0:T(8,128)S(1)} %collective-permute-done.11.near_ref.near2), channel_id=1, source_target_pairs={{0,1},{1,0},{2,3},{3,2},{4,5},{5,4},{6,7},{7,6},{8,9},{9,8},{10,11... | collective-permute-start | bytes 614408 | tf_op jit(solution)/shard_map/ppermute | solution.py:21
  39.4 1.7 %collective-permute-done.17.near2 = f32[72,256]{1,0:T(8,128)S(1)} collective-permute-done((f32[72,256]{1,0:T(8,128)S(1)}, f32[72,256]{1,0:T(8,128)S(1)}, u32[]{:S(2)}, u32[]{:S(2)}) %collective-permute-start.17) | collective-permute-done | bytes 73760 | tf_op jit(solution)/shard_map/ppermute | solution.py:29
  41.1 1.2 %collective-permute-start.18 = (f32[72,256]{1,0:T(8,128)S(1)}, f32[72,256]{1,0:T(8,128)S(1)}, u32[]{:S(2)}, u32[]{:S(2)}) collective-permute-start(f32[72,256]{1,0:T(8,128)S(1)} %collective-permute-done.17.near2), channel_id=1, source_target_pairs={{0,1},{1,0},{2,3},{3,2},{4,5},{5,4},{6,7},{7,6},{8,9},{9,8},{10,11... | collective-permute-start | bytes 221192 | tf_op jit(solution)/shard_map/ppermute | solution.py:21
  42.3 2.0 %collective-permute-start.20 = (f32[200,256]{1,0:T(8,128)S(1)}, f32[200,256]{1,0:T(8,128)S(1)}, u32[]{:S(2)}, u32[]{:S(2)}) collective-permute-start(f32[200,256]{1,0:T(8,128)S(1)} %shard_map.66), channel_id=1, source_target_pairs={{0,1},{1,0},{2,3},{3,2},{4,5},{5,4},{6,7},{7,6},{8,16},{9,17},{10,... | collective-permute-start | bytes 614408 | tf_op jit(solution)/shard_map/ppermute | solution.py:29
  44.3 2.6 %shard_map.67.old_ref = f32[3,256,256]{2,1,0:T(8,128)S(1)} custom-call(f32[3,256,256]{2,1,0:T(8,128)S(1)} %shard_map.64.old_ref, f32[72,256]{1,0:T(8,128)S(1)} %collective-permute-done.12.near_ref.near1, f32[72,256]{1,0:T(8,128)S(1)} %collective-permute-done.13.far_ref.far1, f32[200,256]{1,0:T(8,128)S(1)} %collective-permute-done.11.near_ref.near2, ...), custom_call_target="tpu_custom_call" | custom-call | flops 1207959552 | bytes 1310720 | tf_op jit(solution)/shard_map/pallas_call | solution.py:251
  46.9 2.1 %shard_map.68 = (f32[3,256,256]{2,1,0:T(8,128)S(1)}, f32[1,256,256]{2,1,0:T(8,128)}, f32[1,256,256]{2,1,0:T(8,128)}, f32[1,256,256]{2,1,0:T(8,128)}) custom-call(f32[3,256,256]{2,1,0:T(8,128)S(1)} %shard_map.67.old_ref, f32[72,256]{1,0:T(8,128)S(1)} %collective-permute-done.17.near2, f32[72,256]{1,0:T(8,128)S(1)} %collective-permute-done.18.far2, ...), custom_call_target="tpu_custom_call" | custom-call | flops 905969664 | bytes 1310720 | tf_op jit(solution)/shard_map/pallas_call | solution.py:251
  49.0 0.9 %collective-permute-start.21 = (f32[200,256]{1,0:T(8,128)S(1)}, f32[200,256]{1,0:T(8,128)S(1)}, u32[]{:S(2)}, u32[]{:S(2)}) collective-permute-start(f32[200,256]{1,0:T(8,128)S(1)} %collective-permute-done.15.near3), channel_id=1, source_target_pairs={{0,1},{1,0},{2,3},{3,2},{4,5},{5,4},{6,7},{7,6},{8,9},{9,8},{10,11... | collective-permute-start | bytes 614408 | tf_op jit(solution)/shard_map/ppermute | solution.py:21
  49.9 1.0 %collective-permute-done.20.near2 = f32[200,256]{1,0:T(8,128)S(1)} collective-permute-done((f32[200,256]{1,0:T(8,128)S(1)}, f32[200,256]{1,0:T(8,128)S(1)}, u32[]{:S(2)}, u32[]{:S(2)}) %collective-permute-start.20) | collective-permute-done | bytes 204832 | tf_op jit(solution)/shard_map/ppermute | solution.py:29
  50.9 1.3 %collective-permute-start.22 = (f32[200,256]{1,0:T(8,128)S(1)}, f32[200,256]{1,0:T(8,128)S(1)}, u32[]{:S(2)}, u32[]{:S(2)}) collective-permute-start(f32[200,256]{1,0:T(8,128)S(1)} %collective-permute-done.20.near2), channel_id=1, source_target_pairs={{0,1},{1,0},{2,3},{3,2},{4,5},{5,4},{6,7},{7,6},{8,9},{9,8},{10,11... | collective-permute-start | bytes 614408 | tf_op jit(solution)/shard_map/ppermute | solution.py:21
  52.3 1.1 %collective-permute-done.22.far2 = f32[200,256]{1,0:T(8,128)S(1)} collective-permute-done((f32[200,256]{1,0:T(8,128)S(1)}, f32[200,256]{1,0:T(8,128)S(1)}, u32[]{:S(2)}, u32[]{:S(2)}) %collective-permute-start.22) | collective-permute-done | bytes 204832 | tf_op jit(solution)/shard_map/ppermute | solution.py:21
  53.4 1.4 %shard_map.69 = (f32[1,256,256]{2,1,0:T(8,128)}, f32[1,256,256]{2,1,0:T(8,128)}, f32[1,256,256]{2,1,0:T(8,128)}) custom-call(f32[3,256,256]{2,1,0:T(8,128)S(1)} %get-tuple-element.62.half_ref, f32[200,256]{1,0:T(8,128)S(1)} %collective-permute-done.20.near2, ...), custom_call_target="tpu_custom_call", output_to_operand_aliasing={{0}: (5, {}), {1}: (6, {}), {2}: (7, {})} | custom-call | flops 301989888 | bytes 1310720 | tf_op jit(solution)/shard_map/pallas_call | solution.py:251
  (27 shorter events, 6.1 us)
Async XLA Ops:
  0.6 2.4 %collective-permute-start = (f32[1,256,256]{2,1,0:T(8,128)}, f32[1,256,256]{2,1,0:T(8,128)S(1)}, u32[]{:S(2)}, u32[]{:S(2)}) collective-permute-start(f32[1,256,256]{2,1,0:T(8,128)} %param.3), channel_id=1, source_target_pairs={{0,1},{1,0},{2,3},{3,2},{4,5},{5,4},{6,7},{7,6},{8,9},{9,8},{10,11... | collective-permute-start | bytes 786440 | tf_op jit(solution)/shard_map/ppermute | solution.py:21
  1.4 1.7 %collective-permute-start.1 = (f32[1,256,256]{2,1,0:T(8,128)}, f32[1,256,256]{2,1,0:T(8,128)S(1)}, u32[]{:S(2)}, u32[]{:S(2)}) collective-permute-start(f32[1,256,256]{2,1,0:T(8,128)} %param.4), channel_id=1, source_target_pairs={{0,1},{1,0},{2,3},{3,2},{4,5},{5,4},{6,7},{7,6},{8,9},{9,8},{10,11... | collective-permute-start | bytes 786440 | tf_op jit(solution)/shard_map/ppermute | solution.py:21
  1.4 2.0 %collective-permute-start.2 = (f32[1,256,256]{2,1,0:T(8,128)}, f32[1,256,256]{2,1,0:T(8,128)S(1)}, u32[]{:S(2)}, u32[]{:S(2)}) collective-permute-start(f32[1,256,256]{2,1,0:T(8,128)} %param.5), channel_id=1, source_target_pairs={{0,1},{1,0},{2,3},{3,2},{4,5},{5,4},{6,7},{7,6},{8,9},{9,8},{10,11... | collective-permute-start | bytes 786440 | tf_op jit(solution)/shard_map/ppermute | solution.py:21
  6.1 3.3 %collective-permute-start.4 = (f32[72,256]{1,0:T(8,128)S(1)}, f32[72,256]{1,0:T(8,128)S(1)}, u32[]{:S(2)}, u32[]{:S(2)}) collective-permute-start(f32[72,256]{1,0:T(8,128)S(1)} %get-tuple-element.38), channel_id=1, source_target_pairs={{0,2},{1,3},{2,0},{3,1},{4,6},{5,7},{6,4},{7,5},{8,10},{9,11},{10,... | collective-permute-start | bytes 221192 | tf_op jit(solution)/shard_map/ppermute | solution.py:21
  7.4 7.0 %collective-permute-start.3 = (f32[200,256]{1,0:T(8,128)S(1)}, f32[200,256]{1,0:T(8,128)S(1)}, u32[]{:S(2)}, u32[]{:S(2)}) collective-permute-start(f32[200,256]{1,0:T(8,128)S(1)} %get-tuple-element.36), channel_id=1, source_target_pairs={{0,2},{1,3},{2,0},{3,1},{4,6},{5,7},{6,4},{7,5},{8,10},{9,11},{10,... | collective-permute-start | bytes 614408 | tf_op jit(solution)/shard_map/ppermute | solution.py:21
  9.4 2.9 %collective-permute-start.5 = (f32[72,256]{1,0:T(8,128)S(1)}, f32[72,256]{1,0:T(8,128)S(1)}, u32[]{:S(2)}, u32[]{:S(2)}) collective-permute-start(f32[72,256]{1,0:T(8,128)S(1)} %collective-permute-done.4.near_ref.near1), channel_id=1, source_target_pairs={{0,1},{1,0},{2,3},{3,2},{4,5},{5,4},{6,7},{7,6},{8,9},{9,8},{10,11... | collective-permute-start | bytes 221192 | tf_op jit(solution)/shard_map/ppermute | solution.py:21
  14.4 2.0 %collective-permute-start.6 = (f32[200,256]{1,0:T(8,128)S(1)}, f32[200,256]{1,0:T(8,128)S(1)}, u32[]{:S(2)}, u32[]{:S(2)}) collective-permute-start(f32[200,256]{1,0:T(8,128)S(1)} %collective-permute-done.3.near_ref.near2), channel_id=1, source_target_pairs={{0,1},{1,0},{2,3},{3,2},{4,5},{5,4},{6,7},{7,6},{8,9},{9,8},{10,11... | collective-permute-start | bytes 614408 | tf_op jit(solution)/shard_map/ppermute | solution.py:21
  17.1 4.1 %collective-permute-start.8 = (f32[72,256]{1,0:T(8,128)S(1)}, f32[72,256]{1,0:T(8,128)S(1)}, u32[]{:S(2)}, u32[]{:S(2)}) collective-permute-start(f32[72,256]{1,0:T(8,128)S(1)} %get-tuple-element.43), channel_id=1, source_target_pairs={{0,4},{1,5},{2,6},{3,7},{4,0},{5,1},{6,2},{7,3},{8,12},{9,13},{10,... | collective-permute-start | bytes 221192 | tf_op jit(solution)/shard_map/ppermute | solution.py:21
  18.4 6.9 %collective-permute-start.7 = (f32[200,256]{1,0:T(8,128)S(1)}, f32[200,256]{1,0:T(8,128)S(1)}, u32[]{:S(2)}, u32[]{:S(2)}) collective-permute-start(f32[200,256]{1,0:T(8,128)S(1)} %get-tuple-element.41), channel_id=1, source_target_pairs={{0,4},{1,5},{2,6},{3,7},{4,0},{5,1},{6,2},{7,3},{8,12},{9,13},{10,... | collective-permute-start | bytes 614408 | tf_op jit(solution)/shard_map/ppermute | solution.py:21
  21.2 2.1 %collective-permute-start.9 = (f32[72,256]{1,0:T(8,128)S(1)}, f32[72,256]{1,0:T(8,128)S(1)}, u32[]{:S(2)}, u32[]{:S(2)}) collective-permute-start(f32[72,256]{1,0:T(8,128)S(1)} %collective-permute-done.8.near_ref.near1), channel_id=1, source_target_pairs={{0,1},{1,0},{2,3},{3,2},{4,5},{5,4},{6,7},{7,6},{8,9},{9,8},{10,11... | collective-permute-start | bytes 221192 | tf_op jit(solution)/shard_map/ppermute | solution.py:21
  25.3 2.0 %collective-permute-start.10 = (f32[200,256]{1,0:T(8,128)S(1)}, f32[200,256]{1,0:T(8,128)S(1)}, u32[]{:S(2)}, u32[]{:S(2)}) collective-permute-start(f32[200,256]{1,0:T(8,128)S(1)} %collective-permute-done.7.near_ref.near2), channel_id=1, source_target_pairs={{0,1},{1,0},{2,3},{3,2},{4,5},{5,4},{6,7},{7,6},{8,9},{9,8},{10,11... | collective-permute-start | bytes 614408 | tf_op jit(solution)/shard_map/ppermute | solution.py:21
  28.1 4.1 %collective-permute-start.12 = (f32[72,256]{1,0:T(8,128)S(1)}, f32[72,256]{1,0:T(8,128)S(1)}, u32[]{:S(2)}, u32[]{:S(2)}) collective-permute-start(f32[72,256]{1,0:T(8,128)S(1)} %get-tuple-element.50), channel_id=1, source_target_pairs={{0,8},{1,9},{2,10},{3,11},{4,12},{5,13},{6,14},{7,15},{8,0},{9,1},... | collective-permute-start | bytes 221192 | tf_op jit(solution)/shard_map/ppermute | solution.py:21
  29.4 6.8 %collective-permute-start.11 = (f32[200,256]{1,0:T(8,128)S(1)}, f32[200,256]{1,0:T(8,128)S(1)}, u32[]{:S(2)}, u32[]{:S(2)}) collective-permute-start(f32[200,256]{1,0:T(8,128)S(1)} %get-tuple-element.48), channel_id=1, source_target_pairs={{0,8},{1,9},{2,10},{3,11},{4,12},{5,13},{6,14},{7,15},{8,0},{9,1},... | collective-permute-start | bytes 614408 | tf_op jit(solution)/shard_map/ppermute | solution.py:21
  32.2 2.0 %collective-permute-start.13 = (f32[72,256]{1,0:T(8,128)S(1)}, f32[72,256]{1,0:T(8,128)S(1)}, u32[]{:S(2)}, u32[]{:S(2)}) collective-permute-start(f32[72,256]{1,0:T(8,128)S(1)} %collective-permute-done.12.near_ref.near1), channel_id=1, source_target_pairs={{0,1},{1,0},{2,3},{3,2},{4,5},{5,4},{6,7},{7,6},{8,9},{9,8},{10,11... | collective-permute-start | bytes 221192 | tf_op jit(solution)/shard_map/ppermute | solution.py:21
  36.3 2.0 %collective-permute-start.14 = (f32[200,256]{1,0:T(8,128)S(1)}, f32[200,256]{1,0:T(8,128)S(1)}, u32[]{:S(2)}, u32[]{:S(2)}) collective-permute-start(f32[200,256]{1,0:T(8,128)S(1)} %collective-permute-done.11.near_ref.near2), channel_id=1, source_target_pairs={{0,1},{1,0},{2,3},{3,2},{4,5},{5,4},{6,7},{7,6},{8,9},{9,8},{10,11... | collective-permute-start | bytes 614408 | tf_op jit(solution)/shard_map/ppermute | solution.py:21
  37.2 3.9 %collective-permute-start.17 = (f32[72,256]{1,0:T(8,128)S(1)}, f32[72,256]{1,0:T(8,128)S(1)}, u32[]{:S(2)}, u32[]{:S(2)}) collective-permute-start(f32[72,256]{1,0:T(8,128)S(1)} %get-tuple-element.56), channel_id=1, source_target_pairs={{0,1},{1,0},{2,3},{3,2},{4,5},{5,4},{6,7},{7,6},{8,16},{9,17},{10,... | collective-permute-start | bytes 221192 | tf_op jit(solution)/shard_map/ppermute | solution.py:29
  37.4 3.8 %collective-permute-start.16 = (f32[72,256]{1,0:T(8,128)S(1)}, f32[72,256]{1,0:T(8,128)S(1)}, u32[]{:S(2)}, u32[]{:S(2)}) collective-permute-start(f32[72,256]{1,0:T(8,128)S(1)} %get-tuple-element.56), channel_id=1, source_target_pairs={{0,1},{1,0},{2,3},{3,2},{4,5},{5,4},{6,7},{7,6},{8,24},{9,25},{10,... | collective-permute-start | bytes 221192 | tf_op jit(solution)/shard_map/ppermute | solution.py:29
  39.0 10.0 %collective-permute-start.15 = (f32[200,256]{1,0:T(8,128)S(1)}, f32[200,256]{1,0:T(8,128)S(1)}, u32[]{:S(2)}, u32[]{:S(2)}) collective-permute-start(f32[200,256]{1,0:T(8,128)S(1)} %shard_map.66), channel_id=1, source_target_pairs={{0,1},{1,0},{2,3},{3,2},{4,5},{5,4},{6,7},{7,6},{8,24},{9,25},{10,... | collective-permute-start | bytes 614408 | tf_op jit(solution)/shard_map/ppermute | solution.py:29
  41.1 5.7 %collective-permute-start.18 = (f32[72,256]{1,0:T(8,128)S(1)}, f32[72,256]{1,0:T(8,128)S(1)}, u32[]{:S(2)}, u32[]{:S(2)}) collective-permute-start(f32[72,256]{1,0:T(8,128)S(1)} %collective-permute-done.17.near2), channel_id=1, source_target_pairs={{0,1},{1,0},{2,3},{3,2},{4,5},{5,4},{6,7},{7,6},{8,9},{9,8},{10,11... | collective-permute-start | bytes 221192 | tf_op jit(solution)/shard_map/ppermute | solution.py:21
  42.3 4.6 %collective-permute-start.19 = (f32[72,256]{1,0:T(8,128)S(1)}, f32[72,256]{1,0:T(8,128)S(1)}, u32[]{:S(2)}, u32[]{:S(2)}) collective-permute-start(f32[72,256]{1,0:T(8,128)S(1)} %collective-permute-done.16.near3), channel_id=1, source_target_pairs={{0,1},{1,0},{2,3},{3,2},{4,5},{5,4},{6,7},{7,6},{8,9},{9,8},{10,11... | collective-permute-start | bytes 221192 | tf_op jit(solution)/shard_map/ppermute | solution.py:21
  42.3 8.6 %collective-permute-start.20 = (f32[200,256]{1,0:T(8,128)S(1)}, f32[200,256]{1,0:T(8,128)S(1)}, u32[]{:S(2)}, u32[]{:S(2)}) collective-permute-start(f32[200,256]{1,0:T(8,128)S(1)} %shard_map.66), channel_id=1, source_target_pairs={{0,1},{1,0},{2,3},{3,2},{4,5},{5,4},{6,7},{7,6},{8,16},{9,17},{10,... | collective-permute-start | bytes 614408 | tf_op jit(solution)/shard_map/ppermute | solution.py:29
  49.0 1.9 %collective-permute-start.21 = (f32[200,256]{1,0:T(8,128)S(1)}, f32[200,256]{1,0:T(8,128)S(1)}, u32[]{:S(2)}, u32[]{:S(2)}) collective-permute-start(f32[200,256]{1,0:T(8,128)S(1)} %collective-permute-done.15.near3), channel_id=1, source_target_pairs={{0,1},{1,0},{2,3},{3,2},{4,5},{5,4},{6,7},{7,6},{8,9},{9,8},{10,11... | collective-permute-start | bytes 614408 | tf_op jit(solution)/shard_map/ppermute | solution.py:21
  50.9 2.4 %collective-permute-start.22 = (f32[200,256]{1,0:T(8,128)S(1)}, f32[200,256]{1,0:T(8,128)S(1)}, u32[]{:S(2)}, u32[]{:S(2)}) collective-permute-start(f32[200,256]{1,0:T(8,128)S(1)} %collective-permute-done.20.near2), channel_id=1, source_target_pairs={{0,1},{1,0},{2,3},{3,2},{4,5},{5,4},{6,7},{7,6},{8,9},{9,8},{10,11... | collective-permute-start | bytes 614408 | tf_op jit(solution)/shard_map/ppermute | solution.py:21

commit v8 on v7

--- a/solution.py
+++ b/solution.py
@@ -94,16 +94,27 @@
     return row > col, row < col
 
 
-def pack_symmetric(x, core, ref, start):
+def symmetric_rows(x):
     h = x.shape[0] // 2
-    q = h // 2
     below, above = lower_upper(h)
     a, b, c = x[:h, :h], x[:h, h:], x[h:, h:]
     diagonal = jnp.sum(jnp.where(below | above, 0.0, c), axis=0, keepdims=True)
-    both = jnp.concatenate([b, jnp.where(above, c, a)], 1)
-    ref[start : start + q, :] = jnp.where(core, both[q:], both[:q])
-    diagonal = jnp.concatenate([diagonal, diagonal], 1)
-    ref[start + q : start + q + PAD, :] = jnp.broadcast_to(diagonal, (PAD, 2 * h))
+    return jnp.concatenate([b, jnp.where(above, c, a)], 1), diagonal
+
+
+def store_half(rows, core, ref, start):
+    q = rows.shape[0] // 2
+    ref[start : start + q, :] = jnp.where(core, rows[q:], rows[:q])
+
+
+def store_diagonals(one, two, ref, start):
+    ref[start : start + PAD, :] = jnp.broadcast_to(jnp.concatenate([one, two], 1), (PAD, 2 * one.shape[1]))
+
+
+def pack_symmetric(x, core, ref, start):
+    rows, diagonal = symmetric_rows(x)
+    store_half(rows, core, ref, start)
+    store_diagonals(diagonal, diagonal, ref, start + rows.shape[0] // 2)
 
 
 def joined(near_ref, far_ref, core, lo, hi):
@@ -111,12 +122,13 @@
     return jnp.concatenate([jnp.where(core, far, near), jnp.where(core, near, far)], 0)
 
 
-def unpack_symmetric(near_ref, far_ref, core, start):
+def unpack_symmetric(near_ref, far_ref, core, start, diagonal=None):
     h = near_ref.shape[1] // 2
     q = h // 2
     below, above = lower_upper(h)
     both = joined(near_ref, far_ref, core, start, start + q)
-    diagonal = near_ref[start + q : start + q + 1, :h]
+    if diagonal is None:
+        diagonal = near_ref[start + q : start + q + 1, :h]
     b, w = both[:, :h], both[:, h:]
     turned = w.T
     a = jnp.where(above, turned, w)
@@ -124,9 +136,10 @@
     return jnp.concatenate([jnp.concatenate([a, b], 1), jnp.concatenate([b.T, c], 1)], 0)
 
 
-def unpack_second(near_ref, far_ref, core):
+def unpack_second(near_ref, far_ref, core, first_ref=None):
     h = near_ref.shape[1] // 2
-    return joined(near_ref, far_ref, core, 0, h), unpack_symmetric(near_ref, far_ref, core, h)
+    diagonal = None if first_ref is None else first_ref[h // 2 : h // 2 + 1, h:]
+    return joined(near_ref, far_ref, core, 0, h), unpack_symmetric(near_ref, far_ref, core, h, diagonal)
 
 
 def send_total(own_side, other_side, trans, same, core, first_ref, second_ref, own_ref):
@@ -137,8 +150,13 @@
     own_ref[0] = near
     own_ref[1] = away
     own_ref[2] = jnp.where(same, trans, turned)
-    pack_symmetric(near, core, first_ref, 0)
-    pack_second(back, away, core, second_ref)
+    near_rows, near_diagonal = symmetric_rows(near)
+    away_rows, away_diagonal = symmetric_rows(away)
+    h = near_rows.shape[0]
+    store_half(near_rows, core, first_ref, 0)
+    store_diagonals(near_diagonal, away_diagonal, first_ref, h // 2)
+    store_half(back, core, second_ref, 0)
+    store_half(away_rows, core, second_ref, h)
 
 
 def first_kernel(section_ref, got1, got2, got3, prefix_ref, *send_refs):
@@ -166,23 +184,23 @@
         half_ref[i] = x
 
 
-def final_kernel(half_ref, near_ref, far_ref, second_ref):
+def final_kernel(half_ref, near1, near_ref, far_ref, second_ref):
     core = bit(place(), 1)
-    into, away = unpack_second(near_ref, far_ref, core)
+    into, away = unpack_second(near_ref, far_ref, core, near1)
     trans, other_side = after_trans(half_ref[0], half_ref[1], away, into)
     pack_second(trans, other_side, core, second_ref)
 
 
 def pack_second(back, away, core, ref):
     h = back.shape[0] // 2
-    ref[0:h, :] = jnp.where(core, back[h:], back[:h])
+    store_half(back, core, ref, 0)
     pack_symmetric(away, core, ref, h)
 
 
-def late_kernel(distance, half_ref, near_ref, far_ref, *send_refs):
+def late_kernel(distance, half_ref, near1, near_ref, far_ref, *send_refs):
     me = place()
     core = bit(me, 1)
-    into, away = unpack_second(near_ref, far_ref, core)
+    into, away = unpack_second(near_ref, far_ref, core, near1)
     trans, other_side = after_trans(half_ref[0], half_ref[1], away, into)
     same = bit(me, distance) == bit(me, 2 * distance)
     send_total(half_ref[2], other_side, trans, same, core, *send_refs)
@@ -193,7 +211,7 @@
     core, upper = bit(me, 1), bit(me, distance)
     facing = unpack_symmetric(near1, far1, core, 0)
     leading, mirror, right = before_trans((old_ref[0], old_ref[1], old_ref[2]), facing)
-    into, away = unpack_second(near2, far2, core)
+    into, away = unpack_second(near2, far2, core, near1)
     trans, left = after_trans(leading, mirror, away, into)
     for i, x in enumerate((left, right, trans)):
         new_ref[i] = jnp.where(upper, x, old_ref[i])
@@ -264,7 +282,7 @@
     m = trans.shape[1]
     levels = lax.axis_size(AXES).bit_length() - 1
     stack = (3, m, m)
-    first, second = (m // 4 + PAD, m), (m // 2 + m // 4 + PAD, m)
+    first, second, padded = (m // 4 + PAD, m), (m // 2 + m // 4, m), (m // 2 + m // 4 + PAD, m)
     sections = refl_left, refl_right, trans
     got = [swap(x, 1) for x in sections]
     section = jnp.concatenate(sections, 0)
@@ -284,12 +302,12 @@
         far2 = swap(near2, 1)
         pending = lambda old, kernel=bind(prefix_kernel), got=(near1, far1, near2, far2): call(kernel, 36, [stack], old, *got)
         if level < levels - 2:
-            send1, send2, own = call(bind(late_kernel), 9, [first, second, stack], halfway, near2, far2)
+            send1, send2, own = call(bind(late_kernel), 9, [first, second, stack], halfway, near1, near2, far2)
 
     distance *= 2
     (send1,) = sends
     first3, first2 = pair(send1, 1, 3), pair(send1, 1, 2)
-    (send2,) = call(final_kernel, 9, [second], halfway, near2, far2)
+    (send2,) = call(final_kernel, 9, [padded], halfway, near1, near2, far2)
     near3, near2 = pair(send2, 1, 3), pair(send2, 1, 2)
     first3, first2, prefix = lax.optimization_barrier((first3, first2, prefix))
     (prefix,) = pending(prefix)

time: 55.1 us -> 54.6 us (level)
    ppermute x19, starting transfers between devices: 16.3 us -> 15.6 us  [swap(): return lax.ppermute(block, AXES, [(i, i ^ distance) for i in range(count)])]
  transfers between devices with their start and end apart: 23 -> 23, of which waited for: 12 -> 12; matrix products, arithmetic and copies ran while one was open for 2% -> 2% of each run, Pallas kernels for 30% -> 31%
where the time goes in v8:
time: 54.6 us; the launch traced here: 54.4 us
  Pallas kernels  22.2 us (41%)
  starting transfers between devices  18.6 us (34%)
  waiting for transfers between devices  11.4 us (21%)
  other arithmetic  1.16 us (2%)
  between operations  0.96 us (2%)
    pallas_call x12, Pallas kernels, call(): pl.pallas_call(kernel, out_shape=[jax.ShapeDtypeStruct(s, F32) for s in o...  22.2 us
    ppermute x19, starting transfers between devices, swap(): return lax.ppermute(block, AXES, [(i, i ^ distance) for i in range(count)])  15.6 us
    ppermute x19, waiting for transfers between devices, swap(): return lax.ppermute(block, AXES, [(i, i ^ distance) for i in range(count)])  8.68 us
    ppermute x4, starting transfers between devices, pair(): lax.ppermute(block, AXES, [(i, step.get(i // quarter, lambda i: i ^ 1)(i)...  3.01 us
    ppermute x4, waiting for transfers between devices, pair(): lax.ppermute(block, AXES, [(i, step.get(i // quarter, lambda i: i ^ 1)(i)...  2.75 us
    concatenate x1, other arithmetic, shards(): section = jnp.concatenate(sections, 0)  1.16 us
  transfers between devices with their start and end apart: 23, of which 12 were waited for; matrix products, arithmetic and copies ran while one was open for 2% of the time, Pallas kernels for 31%

profile of v8, /device:TPU:17, one launch (start us, length us, event | category | flops | bytes accessed | tf_op | source)
XLA Modules:
  0.0 54.4 jit_solution(15712472641925614113)
XLA Ops:
  0.6 0.7 %collective-permute-start = (f32[1,256,256]{2,1,0:T(8,128)}, f32[1,256,256]{2,1,0:T(8,128)S(1)}, u32[]{:S(2)}, u32[]{:S(2)}) collective-permute-start(f32[1,256,256]{2,1,0:T(8,128)} %param.3), channel_id=1, source_target_pairs={{0,1},{1,0},{2,3},{3,2},{4,5},{5,4},{6,7},{7,6},{8,9},{9,8},{10,11... | collective-permute-start | bytes 786440 | tf_op jit(solution)/shard_map/ppermute | solution.py:21
  1.9 1.2 %pad_maximum_fusion.section_ref = f32[3,256,256]{2,1,0:T(8,128)S(1)} fusion(f32[1,256,256]{2,1,0:T(8,128)} %param.5, f32[1,256,256]{2,1,0:T(8,128)} %param.4, f32[1,256,256]{2,1,0:T(8,128)} %param.3), kind=kLoop, calls=%fused_computation | loop fusion | flops 393216 | bytes 1572864 | tf_op jit(solution)/shard_map/concatenate | solution.py:288
  3.5 2.6 %shard_map.58 = (f32[3,256,256]{2,1,0:T(8,128)S(1)}, f32[72,256]{1,0:T(8,128)S(1)}, f32[192,256]{1,0:T(8,128)S(1)}, f32[3,256,256]{2,1,0:T(8,128)S(1)}) custom-call(f32[3,256,256]{2,1,0:T(8,128)S(1)} %pad_maximum_fusion.section_ref, f32[1,256,256]{2,1,0:T(8,128)S(1)} %collective-permute-done.got1, f32[1,256,256]{2,1,0:T(8,128)S(1)} %collective-permute-done.1.got2, ...), custom_call_target="tpu_custom_call" | custom-call | flops 1207959552 | bytes 1048576 | tf_op jit(solution)/shard_map/pallas_call | solution.py:269
  6.1 1.3 %collective-permute-start.4 = (f32[72,256]{1,0:T(8,128)S(1)}, f32[72,256]{1,0:T(8,128)S(1)}, u32[]{:S(2)}, u32[]{:S(2)}) collective-permute-start(f32[72,256]{1,0:T(8,128)S(1)} %get-tuple-element.38), channel_id=1, source_target_pairs={{0,2},{1,3},{2,0},{3,1},{4,6},{5,7},{6,4},{7,5},{8,10},{9,11},{10,... | collective-permute-start | bytes 221192 | tf_op jit(solution)/shard_map/ppermute | solution.py:21
  7.6 1.7 %collective-permute-done.4.near_ref.near1 = f32[72,256]{1,0:T(8,128)S(1)} collective-permute-done((f32[72,256]{1,0:T(8,128)S(1)}, f32[72,256]{1,0:T(8,128)S(1)}, u32[]{:S(2)}, u32[]{:S(2)}) %collective-permute-start.4) | collective-permute-done | bytes 73760 | tf_op jit(solution)/shard_map/ppermute | solution.py:21
  9.4 2.0 %collective-permute-start.5 = (f32[72,256]{1,0:T(8,128)S(1)}, f32[72,256]{1,0:T(8,128)S(1)}, u32[]{:S(2)}, u32[]{:S(2)}) collective-permute-start(f32[72,256]{1,0:T(8,128)S(1)} %collective-permute-done.4.near_ref.near1), channel_id=1, source_target_pairs={{0,1},{1,0},{2,3},{3,2},{4,5},{5,4},{6,7},{7,6},{8,9},{9,8},{10,11... | collective-permute-start | bytes 221192 | tf_op jit(solution)/shard_map/ppermute | solution.py:21
  11.4 0.9 %collective-permute-done.5.far_ref.far1 = f32[72,256]{1,0:T(8,128)S(1)} collective-permute-done((f32[72,256]{1,0:T(8,128)S(1)}, f32[72,256]{1,0:T(8,128)S(1)}, u32[]{:S(2)}, u32[]{:S(2)}) %collective-permute-start.5) | collective-permute-done | bytes 73760 | tf_op jit(solution)/shard_map/ppermute | solution.py:21
  12.3 2.1 %shard_map.59.half_ref = f32[3,256,256]{2,1,0:T(8,128)S(1)} custom-call(f32[3,256,256]{2,1,0:T(8,128)S(1)} %get-tuple-element.37.own_ref, f32[72,256]{1,0:T(8,128)S(1)} %collective-permute-done.4.near_ref.near1, f32[72,256]{1,0:T(8,128)S(1)} %collective-permute-done.5.far_ref.far1), custom_call_target="tpu_custom_call" | custom-call | flops 905969664 | bytes 786432 | tf_op jit(solution)/shard_map/pallas_call | solution.py:269
  15.1 1.1 %collective-permute-done.6.far_ref.far2 = f32[192,256]{1,0:T(8,128)S(1)} collective-permute-done((f32[192,256]{1,0:T(8,128)S(1)}, f32[192,256]{1,0:T(8,128)S(1)}, u32[]{:S(2)}, u32[]{:S(2)}) %collective-permute-start.6) | collective-permute-done | bytes 196640 | tf_op jit(solution)/shard_map/ppermute | solution.py:21
  16.9 1.3 %collective-permute-start.8 = (f32[72,256]{1,0:T(8,128)S(1)}, f32[72,256]{1,0:T(8,128)S(1)}, u32[]{:S(2)}, u32[]{:S(2)}) collective-permute-start(f32[72,256]{1,0:T(8,128)S(1)} %get-tuple-element.43), channel_id=1, source_target_pairs={{0,4},{1,5},{2,6},{3,7},{4,0},{5,1},{6,2},{7,3},{8,12},{9,13},{10,... | collective-permute-start | bytes 221192 | tf_op jit(solution)/shard_map/ppermute | solution.py:21
  18.4 2.6 %shard_map.61.old_ref = f32[3,256,256]{2,1,0:T(8,128)S(1)} custom-call(f32[3,256,256]{2,1,0:T(8,128)S(1)} %get-tuple-element.44.old_ref, f32[72,256]{1,0:T(8,128)S(1)} %collective-permute-done.4.near_ref.near1, f32[72,256]{1,0:T(8,128)S(1)} %collective-permute-done.5.far_ref.far1, f32[192,256]{1,0:T(8,128)S(1)} %collective-permute-done.3.near_ref.near2, ...), custom_call_target="tpu_custom_call" | custom-call | flops 1207959552 | bytes 1310720 | tf_op jit(solution)/shard_map/pallas_call | solution.py:269
  21.0 1.1 %collective-permute-start.9 = (f32[72,256]{1,0:T(8,128)S(1)}, f32[72,256]{1,0:T(8,128)S(1)}, u32[]{:S(2)}, u32[]{:S(2)}) collective-permute-start(f32[72,256]{1,0:T(8,128)S(1)} %collective-permute-done.8.near_ref.near1), channel_id=1, source_target_pairs={{0,1},{1,0},{2,3},{3,2},{4,5},{5,4},{6,7},{7,6},{8,9},{9,8},{10,11... | collective-permute-start | bytes 221192 | tf_op jit(solution)/shard_map/ppermute | solution.py:21
  22.2 0.9 %collective-permute-done.9.far_ref.far1 = f32[72,256]{1,0:T(8,128)S(1)} collective-permute-done((f32[72,256]{1,0:T(8,128)S(1)}, f32[72,256]{1,0:T(8,128)S(1)}, u32[]{:S(2)}, u32[]{:S(2)}) %collective-permute-start.9) | collective-permute-done | bytes 73760 | tf_op jit(solution)/shard_map/ppermute | solution.py:21
  23.1 2.1 %shard_map.62.half_ref = f32[3,256,256]{2,1,0:T(8,128)S(1)} custom-call(f32[3,256,256]{2,1,0:T(8,128)S(1)} %get-tuple-element.42.own_ref, f32[72,256]{1,0:T(8,128)S(1)} %collective-permute-done.8.near_ref.near1, f32[72,256]{1,0:T(8,128)S(1)} %collective-permute-done.9.far_ref.far1), custom_call_target="tpu_custom_call" | custom-call | flops 905969664 | bytes 786432 | tf_op jit(solution)/shard_map/pallas_call | solution.py:269
  25.2 0.7 %collective-permute-start.10 = (f32[192,256]{1,0:T(8,128)S(1)}, f32[192,256]{1,0:T(8,128)S(1)}, u32[]{:S(2)}, u32[]{:S(2)}) collective-permute-start(f32[192,256]{1,0:T(8,128)S(1)} %collective-permute-done.7.near_ref.near2), channel_id=1, source_target_pairs={{0,1},{1,0},{2,3},{3,2},{4,5},{5,4},{6,7},{7,6},{8,9},{9,8},{10,11... | collective-permute-start | bytes 589832 | tf_op jit(solution)/shard_map/ppermute | solution.py:21
  25.9 1.1 %collective-permute-done.10.far_ref.far2 = f32[192,256]{1,0:T(8,128)S(1)} collective-permute-done((f32[192,256]{1,0:T(8,128)S(1)}, f32[192,256]{1,0:T(8,128)S(1)}, u32[]{:S(2)}, u32[]{:S(2)}) %collective-permute-start.10) | collective-permute-done | bytes 196640 | tf_op jit(solution)/shard_map/ppermute | solution.py:21
  27.7 1.4 %collective-permute-start.12 = (f32[72,256]{1,0:T(8,128)S(1)}, f32[72,256]{1,0:T(8,128)S(1)}, u32[]{:S(2)}, u32[]{:S(2)}) collective-permute-start(f32[72,256]{1,0:T(8,128)S(1)} %get-tuple-element.50), channel_id=1, source_target_pairs={{0,8},{1,9},{2,10},{3,11},{4,12},{5,13},{6,14},{7,15},{8,0},{9,1},... | collective-permute-start | bytes 221192 | tf_op jit(solution)/shard_map/ppermute | solution.py:21
  29.2 2.6 %shard_map.64.old_ref = f32[3,256,256]{2,1,0:T(8,128)S(1)} custom-call(f32[3,256,256]{2,1,0:T(8,128)S(1)} %shard_map.61.old_ref, f32[72,256]{1,0:T(8,128)S(1)} %collective-permute-done.8.near_ref.near1, f32[72,256]{1,0:T(8,128)S(1)} %collective-permute-done.9.far_ref.far1, f32[192,256]{1,0:T(8,128)S(1)} %collective-permute-done.7.near_ref.near2, ...), custom_call_target="tpu_custom_call" | custom-call | flops 1207959552 | bytes 1310720 | tf_op jit(solution)/shard_map/pallas_call | solution.py:269
  31.8 1.1 %collective-permute-start.13 = (f32[72,256]{1,0:T(8,128)S(1)}, f32[72,256]{1,0:T(8,128)S(1)}, u32[]{:S(2)}, u32[]{:S(2)}) collective-permute-start(f32[72,256]{1,0:T(8,128)S(1)} %collective-permute-done.12.near_ref.near1), channel_id=1, source_target_pairs={{0,1},{1,0},{2,3},{3,2},{4,5},{5,4},{6,7},{7,6},{8,9},{9,8},{10,11... | collective-permute-start | bytes 221192 | tf_op jit(solution)/shard_map/ppermute | solution.py:21
  32.9 0.9 %collective-permute-done.13.far_ref.far1 = f32[72,256]{1,0:T(8,128)S(1)} collective-permute-done((f32[72,256]{1,0:T(8,128)S(1)}, f32[72,256]{1,0:T(8,128)S(1)}, u32[]{:S(2)}, u32[]{:S(2)}) %collective-permute-start.13) | collective-permute-done | bytes 73760 | tf_op jit(solution)/shard_map/ppermute | solution.py:21
  33.8 2.1 %shard_map.65 = (f32[3,256,256]{2,1,0:T(8,128)S(1)}, f32[72,256]{1,0:T(8,128)S(1)}) custom-call(f32[3,256,256]{2,1,0:T(8,128)S(1)} %get-tuple-element.49.own_ref, f32[72,256]{1,0:T(8,128)S(1)} %collective-permute-done.12.near_ref.near1, f32[72,256]{1,0:T(8,128)S(1)} %collective-permute-done.13.far_ref.far1), custom_call_target="tpu_custom_call" | custom-call | flops 905969664 | bytes 786432 | tf_op jit(solution)/shard_map/pallas_call | solution.py:269
  35.9 0.8 %collective-permute-start.14 = (f32[192,256]{1,0:T(8,128)S(1)}, f32[192,256]{1,0:T(8,128)S(1)}, u32[]{:S(2)}, u32[]{:S(2)}) collective-permute-start(f32[192,256]{1,0:T(8,128)S(1)} %collective-permute-done.11.near_ref.near2), channel_id=1, source_target_pairs={{0,1},{1,0},{2,3},{3,2},{4,5},{5,4},{6,7},{7,6},{8,9},{9,8},{10,11... | collective-permute-start | bytes 589832 | tf_op jit(solution)/shard_map/ppermute | solution.py:21
  38.9 1.7 %collective-permute-done.17.near2 = f32[72,256]{1,0:T(8,128)S(1)} collective-permute-done((f32[72,256]{1,0:T(8,128)S(1)}, f32[72,256]{1,0:T(8,128)S(1)}, u32[]{:S(2)}, u32[]{:S(2)}) %collective-permute-start.17) | collective-permute-done | bytes 73760 | tf_op jit(solution)/shard_map/ppermute | solution.py:29
  40.6 1.2 %collective-permute-start.18 = (f32[72,256]{1,0:T(8,128)S(1)}, f32[72,256]{1,0:T(8,128)S(1)}, u32[]{:S(2)}, u32[]{:S(2)}) collective-permute-start(f32[72,256]{1,0:T(8,128)S(1)} %collective-permute-done.17.near2), channel_id=1, source_target_pairs={{0,1},{1,0},{2,3},{3,2},{4,5},{5,4},{6,7},{7,6},{8,9},{9,8},{10,11... | collective-permute-start | bytes 221192 | tf_op jit(solution)/shard_map/ppermute | solution.py:21
  41.8 2.0 %collective-permute-start.20 = (f32[200,256]{1,0:T(8,128)S(1)}, f32[200,256]{1,0:T(8,128)S(1)}, u32[]{:S(2)}, u32[]{:S(2)}) collective-permute-start(f32[200,256]{1,0:T(8,128)S(1)} %shard_map.66), channel_id=1, source_target_pairs={{0,1},{1,0},{2,3},{3,2},{4,5},{5,4},{6,7},{7,6},{8,16},{9,17},{10,... | collective-permute-start | bytes 614408 | tf_op jit(solution)/shard_map/ppermute | solution.py:29
  43.7 2.6 %shard_map.67.old_ref = f32[3,256,256]{2,1,0:T(8,128)S(1)} custom-call(f32[3,256,256]{2,1,0:T(8,128)S(1)} %shard_map.64.old_ref, f32[72,256]{1,0:T(8,128)S(1)} %collective-permute-done.12.near_ref.near1, f32[72,256]{1,0:T(8,128)S(1)} %collective-permute-done.13.far_ref.far1, f32[192,256]{1,0:T(8,128)S(1)} %collective-permute-done.11.near_ref.near2, ...), custom_call_target="tpu_custom_call" | custom-call | flops 1207959552 | bytes 1310720 | tf_op jit(solution)/shard_map/pallas_call | solution.py:269
  46.3 2.1 %shard_map.68 = (f32[3,256,256]{2,1,0:T(8,128)S(1)}, f32[1,256,256]{2,1,0:T(8,128)}, f32[1,256,256]{2,1,0:T(8,128)}, f32[1,256,256]{2,1,0:T(8,128)}) custom-call(f32[3,256,256]{2,1,0:T(8,128)S(1)} %shard_map.67.old_ref, f32[72,256]{1,0:T(8,128)S(1)} %collective-permute-done.17.near2, f32[72,256]{1,0:T(8,128)S(1)} %collective-permute-done.18.far2, ...), custom_call_target="tpu_custom_call" | custom-call | flops 905969664 | bytes 1310720 | tf_op jit(solution)/shard_map/pallas_call | solution.py:269
  48.5 0.9 %collective-permute-start.21 = (f32[200,256]{1,0:T(8,128)S(1)}, f32[200,256]{1,0:T(8,128)S(1)}, u32[]{:S(2)}, u32[]{:S(2)}) collective-permute-start(f32[200,256]{1,0:T(8,128)S(1)} %collective-permute-done.15.near3), channel_id=1, source_target_pairs={{0,1},{1,0},{2,3},{3,2},{4,5},{5,4},{6,7},{7,6},{8,9},{9,8},{10,11... | collective-permute-start | bytes 614408 | tf_op jit(solution)/shard_map/ppermute | solution.py:21
  49.3 1.0 %collective-permute-done.20.near2 = f32[200,256]{1,0:T(8,128)S(1)} collective-permute-done((f32[200,256]{1,0:T(8,128)S(1)}, f32[200,256]{1,0:T(8,128)S(1)}, u32[]{:S(2)}, u32[]{:S(2)}) %collective-permute-start.20) | collective-permute-done | bytes 204832 | tf_op jit(solution)/shard_map/ppermute | solution.py:29
  50.4 1.3 %collective-permute-start.22 = (f32[200,256]{1,0:T(8,128)S(1)}, f32[200,256]{1,0:T(8,128)S(1)}, u32[]{:S(2)}, u32[]{:S(2)}) collective-permute-start(f32[200,256]{1,0:T(8,128)S(1)} %collective-permute-done.20.near2), channel_id=1, source_target_pairs={{0,1},{1,0},{2,3},{3,2},{4,5},{5,4},{6,7},{7,6},{8,9},{9,8},{10,11... | collective-permute-start | bytes 614408 | tf_op jit(solution)/shard_map/ppermute | solution.py:21
  51.7 1.1 %collective-permute-done.22.far2 = f32[200,256]{1,0:T(8,128)S(1)} collective-permute-done((f32[200,256]{1,0:T(8,128)S(1)}, f32[200,256]{1,0:T(8,128)S(1)}, u32[]{:S(2)}, u32[]{:S(2)}) %collective-permute-start.22) | collective-permute-done | bytes 204832 | tf_op jit(solution)/shard_map/ppermute | solution.py:21
  52.8 1.4 %shard_map.69 = (f32[1,256,256]{2,1,0:T(8,128)}, f32[1,256,256]{2,1,0:T(8,128)}, f32[1,256,256]{2,1,0:T(8,128)}) custom-call(f32[3,256,256]{2,1,0:T(8,128)S(1)} %get-tuple-element.62.half_ref, f32[200,256]{1,0:T(8,128)S(1)} %collective-permute-done.20.near2, ...), custom_call_target="tpu_custom_call", output_to_operand_aliasing={{0}: (5, {}), {1}: (6, {}), {2}: (7, {})} | custom-call | flops 301989888 | bytes 1310720 | tf_op jit(solution)/shard_map/pallas_call | solution.py:269
  (27 shorter events, 6.0 us)
Async XLA Ops:
  0.6 2.4 %collective-permute-start = (f32[1,256,256]{2,1,0:T(8,128)}, f32[1,256,256]{2,1,0:T(8,128)S(1)}, u32[]{:S(2)}, u32[]{:S(2)}) collective-permute-start(f32[1,256,256]{2,1,0:T(8,128)} %param.3), channel_id=1, source_target_pairs={{0,1},{1,0},{2,3},{3,2},{4,5},{5,4},{6,7},{7,6},{8,9},{9,8},{10,11... | collective-permute-start | bytes 786440 | tf_op jit(solution)/shard_map/ppermute | solution.py:21
  1.4 1.7 %collective-permute-start.1 = (f32[1,256,256]{2,1,0:T(8,128)}, f32[1,256,256]{2,1,0:T(8,128)S(1)}, u32[]{:S(2)}, u32[]{:S(2)}) collective-permute-start(f32[1,256,256]{2,1,0:T(8,128)} %param.4), channel_id=1, source_target_pairs={{0,1},{1,0},{2,3},{3,2},{4,5},{5,4},{6,7},{7,6},{8,9},{9,8},{10,11... | collective-permute-start | bytes 786440 | tf_op jit(solution)/shard_map/ppermute | solution.py:21
  1.4 2.0 %collective-permute-start.2 = (f32[1,256,256]{2,1,0:T(8,128)}, f32[1,256,256]{2,1,0:T(8,128)S(1)}, u32[]{:S(2)}, u32[]{:S(2)}) collective-permute-start(f32[1,256,256]{2,1,0:T(8,128)} %param.5), channel_id=1, source_target_pairs={{0,1},{1,0},{2,3},{3,2},{4,5},{5,4},{6,7},{7,6},{8,9},{9,8},{10,11... | collective-permute-start | bytes 786440 | tf_op jit(solution)/shard_map/ppermute | solution.py:21
  6.1 3.3 %collective-permute-start.4 = (f32[72,256]{1,0:T(8,128)S(1)}, f32[72,256]{1,0:T(8,128)S(1)}, u32[]{:S(2)}, u32[]{:S(2)}) collective-permute-start(f32[72,256]{1,0:T(8,128)S(1)} %get-tuple-element.38), channel_id=1, source_target_pairs={{0,2},{1,3},{2,0},{3,1},{4,6},{5,7},{6,4},{7,5},{8,10},{9,11},{10,... | collective-permute-start | bytes 221192 | tf_op jit(solution)/shard_map/ppermute | solution.py:21
  7.4 7.0 %collective-permute-start.3 = (f32[192,256]{1,0:T(8,128)S(1)}, f32[192,256]{1,0:T(8,128)S(1)}, u32[]{:S(2)}, u32[]{:S(2)}) collective-permute-start(f32[192,256]{1,0:T(8,128)S(1)} %get-tuple-element.36), channel_id=1, source_target_pairs={{0,2},{1,3},{2,0},{3,1},{4,6},{5,7},{6,4},{7,5},{8,10},{9,11},{10,... | collective-permute-start | bytes 589832 | tf_op jit(solution)/shard_map/ppermute | solution.py:21
  9.4 2.9 %collective-permute-start.5 = (f32[72,256]{1,0:T(8,128)S(1)}, f32[72,256]{1,0:T(8,128)S(1)}, u32[]{:S(2)}, u32[]{:S(2)}) collective-permute-start(f32[72,256]{1,0:T(8,128)S(1)} %collective-permute-done.4.near_ref.near1), channel_id=1, source_target_pairs={{0,1},{1,0},{2,3},{3,2},{4,5},{5,4},{6,7},{7,6},{8,9},{9,8},{10,11... | collective-permute-start | bytes 221192 | tf_op jit(solution)/shard_map/ppermute | solution.py:21
  14.4 1.8 %collective-permute-start.6 = (f32[192,256]{1,0:T(8,128)S(1)}, f32[192,256]{1,0:T(8,128)S(1)}, u32[]{:S(2)}, u32[]{:S(2)}) collective-permute-start(f32[192,256]{1,0:T(8,128)S(1)} %collective-permute-done.3.near_ref.near2), channel_id=1, source_target_pairs={{0,1},{1,0},{2,3},{3,2},{4,5},{5,4},{6,7},{7,6},{8,9},{9,8},{10,11... | collective-permute-start | bytes 589832 | tf_op jit(solution)/shard_map/ppermute | solution.py:21
  16.9 4.1 %collective-permute-start.8 = (f32[72,256]{1,0:T(8,128)S(1)}, f32[72,256]{1,0:T(8,128)S(1)}, u32[]{:S(2)}, u32[]{:S(2)}) collective-permute-start(f32[72,256]{1,0:T(8,128)S(1)} %get-tuple-element.43), channel_id=1, source_target_pairs={{0,4},{1,5},{2,6},{3,7},{4,0},{5,1},{6,2},{7,3},{8,12},{9,13},{10,... | collective-permute-start | bytes 221192 | tf_op jit(solution)/shard_map/ppermute | solution.py:21
  18.2 7.0 %collective-permute-start.7 = (f32[192,256]{1,0:T(8,128)S(1)}, f32[192,256]{1,0:T(8,128)S(1)}, u32[]{:S(2)}, u32[]{:S(2)}) collective-permute-start(f32[192,256]{1,0:T(8,128)S(1)} %get-tuple-element.41), channel_id=1, source_target_pairs={{0,4},{1,5},{2,6},{3,7},{4,0},{5,1},{6,2},{7,3},{8,12},{9,13},{10,... | collective-permute-start | bytes 589832 | tf_op jit(solution)/shard_map/ppermute | solution.py:21
  21.0 2.0 %collective-permute-start.9 = (f32[72,256]{1,0:T(8,128)S(1)}, f32[72,256]{1,0:T(8,128)S(1)}, u32[]{:S(2)}, u32[]{:S(2)}) collective-permute-start(f32[72,256]{1,0:T(8,128)S(1)} %collective-permute-done.8.near_ref.near1), channel_id=1, source_target_pairs={{0,1},{1,0},{2,3},{3,2},{4,5},{5,4},{6,7},{7,6},{8,9},{9,8},{10,11... | collective-permute-start | bytes 221192 | tf_op jit(solution)/shard_map/ppermute | solution.py:21
  25.2 1.8 %collective-permute-start.10 = (f32[192,256]{1,0:T(8,128)S(1)}, f32[192,256]{1,0:T(8,128)S(1)}, u32[]{:S(2)}, u32[]{:S(2)}) collective-permute-start(f32[192,256]{1,0:T(8,128)S(1)} %collective-permute-done.7.near_ref.near2), channel_id=1, source_target_pairs={{0,1},{1,0},{2,3},{3,2},{4,5},{5,4},{6,7},{7,6},{8,9},{9,8},{10,11... | collective-permute-start | bytes 589832 | tf_op jit(solution)/shard_map/ppermute | solution.py:21
  27.7 4.1 %collective-permute-start.12 = (f32[72,256]{1,0:T(8,128)S(1)}, f32[72,256]{1,0:T(8,128)S(1)}, u32[]{:S(2)}, u32[]{:S(2)}) collective-permute-start(f32[72,256]{1,0:T(8,128)S(1)} %get-tuple-element.50), channel_id=1, source_target_pairs={{0,8},{1,9},{2,10},{3,11},{4,12},{5,13},{6,14},{7,15},{8,0},{9,1},... | collective-permute-start | bytes 221192 | tf_op jit(solution)/shard_map/ppermute | solution.py:21
  29.0 6.8 %collective-permute-start.11 = (f32[192,256]{1,0:T(8,128)S(1)}, f32[192,256]{1,0:T(8,128)S(1)}, u32[]{:S(2)}, u32[]{:S(2)}) collective-permute-start(f32[192,256]{1,0:T(8,128)S(1)} %get-tuple-element.48), channel_id=1, source_target_pairs={{0,8},{1,9},{2,10},{3,11},{4,12},{5,13},{6,14},{7,15},{8,0},{9,1},... | collective-permute-start | bytes 589832 | tf_op jit(solution)/shard_map/ppermute | solution.py:21
  31.8 2.0 %collective-permute-start.13 = (f32[72,256]{1,0:T(8,128)S(1)}, f32[72,256]{1,0:T(8,128)S(1)}, u32[]{:S(2)}, u32[]{:S(2)}) collective-permute-start(f32[72,256]{1,0:T(8,128)S(1)} %collective-permute-done.12.near_ref.near1), channel_id=1, source_target_pairs={{0,1},{1,0},{2,3},{3,2},{4,5},{5,4},{6,7},{7,6},{8,9},{9,8},{10,11... | collective-permute-start | bytes 221192 | tf_op jit(solution)/shard_map/ppermute | solution.py:21
  35.9 1.9 %collective-permute-start.14 = (f32[192,256]{1,0:T(8,128)S(1)}, f32[192,256]{1,0:T(8,128)S(1)}, u32[]{:S(2)}, u32[]{:S(2)}) collective-permute-start(f32[192,256]{1,0:T(8,128)S(1)} %collective-permute-done.11.near_ref.near2), channel_id=1, source_target_pairs={{0,1},{1,0},{2,3},{3,2},{4,5},{5,4},{6,7},{7,6},{8,9},{9,8},{10,11... | collective-permute-start | bytes 589832 | tf_op jit(solution)/shard_map/ppermute | solution.py:21
  36.7 3.9 %collective-permute-start.17 = (f32[72,256]{1,0:T(8,128)S(1)}, f32[72,256]{1,0:T(8,128)S(1)}, u32[]{:S(2)}, u32[]{:S(2)}) collective-permute-start(f32[72,256]{1,0:T(8,128)S(1)} %get-tuple-element.56), channel_id=1, source_target_pairs={{0,1},{1,0},{2,3},{3,2},{4,5},{5,4},{6,7},{7,6},{8,16},{9,17},{10,... | collective-permute-start | bytes 221192 | tf_op jit(solution)/shard_map/ppermute | solution.py:29
  36.8 3.7 %collective-permute-start.16 = (f32[72,256]{1,0:T(8,128)S(1)}, f32[72,256]{1,0:T(8,128)S(1)}, u32[]{:S(2)}, u32[]{:S(2)}) collective-permute-start(f32[72,256]{1,0:T(8,128)S(1)} %get-tuple-element.56), channel_id=1, source_target_pairs={{0,1},{1,0},{2,3},{3,2},{4,5},{5,4},{6,7},{7,6},{8,24},{9,25},{10,... | collective-permute-start | bytes 221192 | tf_op jit(solution)/shard_map/ppermute | solution.py:29
  38.4 10.0 %collective-permute-start.15 = (f32[200,256]{1,0:T(8,128)S(1)}, f32[200,256]{1,0:T(8,128)S(1)}, u32[]{:S(2)}, u32[]{:S(2)}) collective-permute-start(f32[200,256]{1,0:T(8,128)S(1)} %shard_map.66), channel_id=1, source_target_pairs={{0,1},{1,0},{2,3},{3,2},{4,5},{5,4},{6,7},{7,6},{8,24},{9,25},{10,... | collective-permute-start | bytes 614408 | tf_op jit(solution)/shard_map/ppermute | solution.py:29
  40.6 5.7 %collective-permute-start.18 = (f32[72,256]{1,0:T(8,128)S(1)}, f32[72,256]{1,0:T(8,128)S(1)}, u32[]{:S(2)}, u32[]{:S(2)}) collective-permute-start(f32[72,256]{1,0:T(8,128)S(1)} %collective-permute-done.17.near2), channel_id=1, source_target_pairs={{0,1},{1,0},{2,3},{3,2},{4,5},{5,4},{6,7},{7,6},{8,9},{9,8},{10,11... | collective-permute-start | bytes 221192 | tf_op jit(solution)/shard_map/ppermute | solution.py:21
  41.8 4.6 %collective-permute-start.19 = (f32[72,256]{1,0:T(8,128)S(1)}, f32[72,256]{1,0:T(8,128)S(1)}, u32[]{:S(2)}, u32[]{:S(2)}) collective-permute-start(f32[72,256]{1,0:T(8,128)S(1)} %collective-permute-done.16.near3), channel_id=1, source_target_pairs={{0,1},{1,0},{2,3},{3,2},{4,5},{5,4},{6,7},{7,6},{8,9},{9,8},{10,11... | collective-permute-start | bytes 221192 | tf_op jit(solution)/shard_map/ppermute | solution.py:21
  41.8 8.6 %collective-permute-start.20 = (f32[200,256]{1,0:T(8,128)S(1)}, f32[200,256]{1,0:T(8,128)S(1)}, u32[]{:S(2)}, u32[]{:S(2)}) collective-permute-start(f32[200,256]{1,0:T(8,128)S(1)} %shard_map.66), channel_id=1, source_target_pairs={{0,1},{1,0},{2,3},{3,2},{4,5},{5,4},{6,7},{7,6},{8,16},{9,17},{10,... | collective-permute-start | bytes 614408 | tf_op jit(solution)/shard_map/ppermute | solution.py:29
  48.5 1.9 %collective-permute-start.21 = (f32[200,256]{1,0:T(8,128)S(1)}, f32[200,256]{1,0:T(8,128)S(1)}, u32[]{:S(2)}, u32[]{:S(2)}) collective-permute-start(f32[200,256]{1,0:T(8,128)S(1)} %collective-permute-done.15.near3), channel_id=1, source_target_pairs={{0,1},{1,0},{2,3},{3,2},{4,5},{5,4},{6,7},{7,6},{8,9},{9,8},{10,11... | collective-permute-start | bytes 614408 | tf_op jit(solution)/shard_map/ppermute | solution.py:21
  50.4 2.4 %collective-permute-start.22 = (f32[200,256]{1,0:T(8,128)S(1)}, f32[200,256]{1,0:T(8,128)S(1)}, u32[]{:S(2)}, u32[]{:S(2)}) collective-permute-start(f32[200,256]{1,0:T(8,128)S(1)} %collective-permute-done.20.near2), channel_id=1, source_target_pairs={{0,1},{1,0},{2,3},{3,2},{4,5},{5,4},{6,7},{7,6},{8,9},{9,8},{10,11... | collective-permute-start | bytes 614408 | tf_op jit(solution)/shard_map/ppermute | solution.py:21

commit v9 on v8

--- a/solution.py
+++ b/solution.py
@@ -184,11 +184,12 @@
         half_ref[i] = x
 
 
-def final_kernel(half_ref, near1, near_ref, far_ref, second_ref):
+def final_kernel(half_ref, near1, near_ref, far_ref, second_ref, trans_ref):
     core = bit(place(), 1)
     into, away = unpack_second(near_ref, far_ref, core, near1)
     trans, other_side = after_trans(half_ref[0], half_ref[1], away, into)
     pack_second(trans, other_side, core, second_ref)
+    store_half(trans, core, trans_ref, 0)
 
 
 def pack_second(back, away, core, ref):
@@ -242,7 +243,7 @@
             copy.wait()
 
 
-def last_kernel(distance, half_ref, near2, far2, near3, far3, _l, _r, _t, left_out, right_out, trans_out, new_ref, sems):
+def last_kernel(distance, half_ref, near2, far2, near3, far3, near_left, far_left, _l, _r, _t, left_out, right_out, trans_out, new_ref, sems):
     me = place()
 
     @pl.when(bit(me, distance))
@@ -251,7 +252,13 @@
         trans_copy = pltpu.make_async_copy(new_ref.at[0:1], trans_out, sems.at[1])
         left_copy = pltpu.make_async_copy(new_ref.at[1:2], left_out, sems.at[2])
         right_copy.start()
-        into, away = unpack_second(*by_third(distance, me, near2, far2, near3, far3), bit(me, 1))
+        core, third, h = bit(me, 1), bit(me, distance // 2), near2.shape[0]
+        near = jnp.where(third, near3[:h, :], near2[...])
+        far = jnp.where(third, far3[:h, :], far2[...])
+        into = joined(near, far, core, 0, h)
+        near = jnp.where(third, near3[h:, :], near_left[...])
+        far = jnp.where(third, far3[h:, :], far_left[...])
+        away = unpack_symmetric(near, far, core, 0)
         q = split(into)
         new_ref[0] = dot3(split(half_ref[0]), q)
         trans_copy.start()
@@ -306,19 +313,19 @@
 
     distance *= 2
     (send1,) = sends
-    first3, first2 = pair(send1, 1, 3), pair(send1, 1, 2)
-    (send2,) = call(final_kernel, 9, [padded], halfway, near1, near2, far2)
-    near3, near2 = pair(send2, 1, 3), pair(send2, 1, 2)
-    first3, first2, prefix = lax.optimization_barrier((first3, first2, prefix))
+    first3, first2, left = pair(send1, 1, 3), pair(send1, 1, 2), pair(send1, 0, 2)
+    send2, send3 = call(final_kernel, 9, [padded, (m // 2, m)], halfway, near1, near2, far2)
+    near3, near2 = pair(send2, 1, 3), pair(send3, 1, 2)
+    first3, first2, left, prefix = lax.optimization_barrier((first3, first2, left, prefix))
     (prefix,) = pending(prefix)
     args = prefix, first2, swap(first2, 1), first3, swap(first3, 1)
+    far_left, prefix = lax.optimization_barrier((swap(left, 1), prefix))
+    args = prefix, *args[1:]
     one, sems = (1, m, m), pltpu.SemaphoreType.DMA((3,))
     kernel = functools.partial(last_early_kernel, distance)
     halfway, *given = call(kernel, 27, [stack, one, one, one], *args, copied=3, scratch=[sems])
-    near3, halfway = lax.optimization_barrier((near3, halfway))
-    far3 = swap(near3, 1)
-    near2, far3 = lax.optimization_barrier((near2, far3))
-    args = halfway, near2, swap(near2, 1), near3, far3
+    near2, near3, halfway = lax.optimization_barrier((near2, near3, halfway))
+    args = halfway, near2, swap(near2, 1), near3, swap(near3, 1), left, far_left
     scratch = [pltpu.VMEM((2, m, m), F32), sems]
     return tuple(call(functools.partial(last_kernel, distance), 9, [one] * 3, *args, given=given, copied=3, scratch=scratch))
 

time: 54.6 us -> 57.7 us (1.057)
  starting transfers between devices: 18.6 us -> 21.7 us
    ppermute x4 -> x5, starting transfers between devices: 3.01 us -> 6.8 us  [pair(): lax.ppermute(block, AXES, [(i, step.get(i // quarter, lambda i: i ^ 1)(i)...]
    ppermute x19 -> x20, starting transfers between devices: 15.6 us -> 14.9 us  [swap(): return lax.ppermute(block, AXES, [(i, i ^ distance) for i in range(count)])]
    ppermute x4 -> x5, waiting for transfers between devices: 2.75 us -> 3.13 us  [pair(): lax.ppermute(block, AXES, [(i, step.get(i // quarter, lambda i: i ^ 1)(i)...]
    ppermute x19 -> x20, waiting for transfers between devices: 8.68 us -> 8.34 us  [swap(): return lax.ppermute(block, AXES, [(i, i ^ distance) for i in range(count)])]
  transfers between devices with their start and end apart: 23 -> 25, of which waited for: 12 -> 12; matrix products, arithmetic and copies ran while one was open for 2% -> 2% of each run, Pallas kernels for 31% -> 29%
where the time goes in v9:
time: 57.7 us; the launch traced here: 57.5 us
  Pallas kernels  22.2 us (38%)
  starting transfers between devices  21.7 us (38%)
  waiting for transfers between devices  11.5 us (20%)
  other arithmetic  1.16 us (2%)
  between operations  0.98 us (2%)
    pallas_call x12, Pallas kernels, call(): pl.pallas_call(kernel, out_shape=[jax.ShapeDtypeStruct(s, F32) for s in o...  22.2 us
    ppermute x20, starting transfers between devices, swap(): return lax.ppermute(block, AXES, [(i, i ^ distance) for i in range(count)])  14.9 us
    ppermute x20, waiting for transfers between devices, swap(): return lax.ppermute(block, AXES, [(i, i ^ distance) for i in range(count)])  8.34 us
    ppermute x5, starting transfers between devices, pair(): lax.ppermute(block, AXES, [(i, step.get(i // quarter, lambda i: i ^ 1)(i)...  6.8 us
    ppermute x5, waiting for transfers between devices, pair(): lax.ppermute(block, AXES, [(i, step.get(i // quarter, lambda i: i ^ 1)(i)...  3.13 us
    concatenate x1, other arithmetic, shards(): section = jnp.concatenate(sections, 0)  1.16 us
  transfers between devices with their start and end apart: 25, of which 12 were waited for; matrix products, arithmetic and copies ran while one was open for 2% of the time, Pallas kernels for 29%

profile of v9, /device:TPU:17, one launch (start us, length us, event | category | flops | bytes accessed | tf_op | source)
XLA Modules:
  0.0 57.5 jit_solution(8089931459021586006)
XLA Ops:
  0.6 0.7 %collective-permute-start = (f32[1,256,256]{2,1,0:T(8,128)}, f32[1,256,256]{2,1,0:T(8,128)S(1)}, u32[]{:S(2)}, u32[]{:S(2)}) collective-permute-start(f32[1,256,256]{2,1,0:T(8,128)} %param.3), channel_id=1, source_target_pairs={{0,1},{1,0},{2,3},{3,2},{4,5},{5,4},{6,7},{7,6},{8,9},{9,8},{10,11... | collective-permute-start | bytes 786440 | tf_op jit(solution)/shard_map/ppermute | solution.py:21
  1.9 1.2 %pad_maximum_fusion.section_ref = f32[3,256,256]{2,1,0:T(8,128)S(1)} fusion(f32[1,256,256]{2,1,0:T(8,128)} %param.5, f32[1,256,256]{2,1,0:T(8,128)} %param.4, f32[1,256,256]{2,1,0:T(8,128)} %param.3), kind=kLoop, calls=%fused_computation | loop fusion | flops 393216 | bytes 1572864 | tf_op jit(solution)/shard_map/concatenate | solution.py:295
  3.5 2.6 %shard_map.58 = (f32[3,256,256]{2,1,0:T(8,128)S(1)}, f32[72,256]{1,0:T(8,128)S(1)}, f32[192,256]{1,0:T(8,128)S(1)}, f32[3,256,256]{2,1,0:T(8,128)S(1)}) custom-call(f32[3,256,256]{2,1,0:T(8,128)S(1)} %pad_maximum_fusion.section_ref, f32[1,256,256]{2,1,0:T(8,128)S(1)} %collective-permute-done.got1, f32[1,256,256]{2,1,0:T(8,128)S(1)} %collective-permute-done.1.got2, ...), custom_call_target="tpu_custom_call" | custom-call | flops 1207959552 | bytes 1048576 | tf_op jit(solution)/shard_map/pallas_call | solution.py:276
  6.1 1.3 %collective-permute-start.4 = (f32[72,256]{1,0:T(8,128)S(1)}, f32[72,256]{1,0:T(8,128)S(1)}, u32[]{:S(2)}, u32[]{:S(2)}) collective-permute-start(f32[72,256]{1,0:T(8,128)S(1)} %get-tuple-element.42), channel_id=1, source_target_pairs={{0,2},{1,3},{2,0},{3,1},{4,6},{5,7},{6,4},{7,5},{8,10},{9,11},{10,... | collective-permute-start | bytes 221192 | tf_op jit(solution)/shard_map/ppermute | solution.py:21
  7.6 1.7 %collective-permute-done.4.near_ref.near1 = f32[72,256]{1,0:T(8,128)S(1)} collective-permute-done((f32[72,256]{1,0:T(8,128)S(1)}, f32[72,256]{1,0:T(8,128)S(1)}, u32[]{:S(2)}, u32[]{:S(2)}) %collective-permute-start.4) | collective-permute-done | bytes 73760 | tf_op jit(solution)/shard_map/ppermute | solution.py:21
  9.4 2.0 %collective-permute-start.5 = (f32[72,256]{1,0:T(8,128)S(1)}, f32[72,256]{1,0:T(8,128)S(1)}, u32[]{:S(2)}, u32[]{:S(2)}) collective-permute-start(f32[72,256]{1,0:T(8,128)S(1)} %collective-permute-done.4.near_ref.near1), channel_id=1, source_target_pairs={{0,1},{1,0},{2,3},{3,2},{4,5},{5,4},{6,7},{7,6},{8,9},{9,8},{10,11... | collective-permute-start | bytes 221192 | tf_op jit(solution)/shard_map/ppermute | solution.py:21
  11.4 0.9 %collective-permute-done.5.far_ref.far1 = f32[72,256]{1,0:T(8,128)S(1)} collective-permute-done((f32[72,256]{1,0:T(8,128)S(1)}, f32[72,256]{1,0:T(8,128)S(1)}, u32[]{:S(2)}, u32[]{:S(2)}) %collective-permute-start.5) | collective-permute-done | bytes 73760 | tf_op jit(solution)/shard_map/ppermute | solution.py:21
  12.3 2.1 %shard_map.59.half_ref = f32[3,256,256]{2,1,0:T(8,128)S(1)} custom-call(f32[3,256,256]{2,1,0:T(8,128)S(1)} %get-tuple-element.41.own_ref, f32[72,256]{1,0:T(8,128)S(1)} %collective-permute-done.4.near_ref.near1, f32[72,256]{1,0:T(8,128)S(1)} %collective-permute-done.5.far_ref.far1), custom_call_target="tpu_custom_call" | custom-call | flops 905969664 | bytes 786432 | tf_op jit(solution)/shard_map/pallas_call | solution.py:276
  14.4 0.7 %collective-permute-start.6 = (f32[192,256]{1,0:T(8,128)S(1)}, f32[192,256]{1,0:T(8,128)S(1)}, u32[]{:S(2)}, u32[]{:S(2)}) collective-permute-start(f32[192,256]{1,0:T(8,128)S(1)} %collective-permute-done.3.near_ref.near2), channel_id=1, source_target_pairs={{0,1},{1,0},{2,3},{3,2},{4,5},{5,4},{6,7},{7,6},{8,9},{9,8},{10,11... | collective-permute-start | bytes 589832 | tf_op jit(solution)/shard_map/ppermute | solution.py:21
  15.1 1.1 %collective-permute-done.6.far_ref.far2 = f32[192,256]{1,0:T(8,128)S(1)} collective-permute-done((f32[192,256]{1,0:T(8,128)S(1)}, f32[192,256]{1,0:T(8,128)S(1)}, u32[]{:S(2)}, u32[]{:S(2)}) %collective-permute-start.6) | collective-permute-done | bytes 196640 | tf_op jit(solution)/shard_map/ppermute | solution.py:21
  16.2 0.7 %shard_map.60 = (f32[72,256]{1,0:T(8,128)S(1)}, f32[192,256]{1,0:T(8,128)S(1)}, f32[3,256,256]{2,1,0:T(8,128)S(1)}) custom-call(f32[3,256,256]{2,1,0:T(8,128)S(1)} %shard_map.59.half_ref, f32[72,256]{1,0:T(8,128)S(1)} %collective-permute-done.4.near_ref.near1, f32[192,256]{1,0:T(8,128)S(1)} %collective-permute-done.3.near_ref.near2, ...), custom_call_target="tpu_custom_call" | custom-call | flops 301989888 | bytes 1048576 | tf_op jit(solution)/shard_map/pallas_call | solution.py:276
  16.9 1.3 %collective-permute-start.8 = (f32[72,256]{1,0:T(8,128)S(1)}, f32[72,256]{1,0:T(8,128)S(1)}, u32[]{:S(2)}, u32[]{:S(2)}) collective-permute-start(f32[72,256]{1,0:T(8,128)S(1)} %get-tuple-element.47), channel_id=1, source_target_pairs={{0,4},{1,5},{2,6},{3,7},{4,0},{5,1},{6,2},{7,3},{8,12},{9,13},{10,... | collective-permute-start | bytes 221192 | tf_op jit(solution)/shard_map/ppermute | solution.py:21
  18.4 2.6 %shard_map.61.old_ref = f32[3,256,256]{2,1,0:T(8,128)S(1)} custom-call(f32[3,256,256]{2,1,0:T(8,128)S(1)} %get-tuple-element.48.old_ref, f32[72,256]{1,0:T(8,128)S(1)} %collective-permute-done.4.near_ref.near1, f32[72,256]{1,0:T(8,128)S(1)} %collective-permute-done.5.far_ref.far1, f32[192,256]{1,0:T(8,128)S(1)} %collective-permute-done.3.near_ref.near2, ...), custom_call_target="tpu_custom_call" | custom-call | flops 1207959552 | bytes 1310720 | tf_op jit(solution)/shard_map/pallas_call | solution.py:276
  21.0 1.1 %collective-permute-start.9 = (f32[72,256]{1,0:T(8,128)S(1)}, f32[72,256]{1,0:T(8,128)S(1)}, u32[]{:S(2)}, u32[]{:S(2)}) collective-permute-start(f32[72,256]{1,0:T(8,128)S(1)} %collective-permute-done.8.near_ref.near1), channel_id=1, source_target_pairs={{0,1},{1,0},{2,3},{3,2},{4,5},{5,4},{6,7},{7,6},{8,9},{9,8},{10,11... | collective-permute-start | bytes 221192 | tf_op jit(solution)/shard_map/ppermute | solution.py:21
  22.2 0.9 %collective-permute-done.9.far_ref.far1 = f32[72,256]{1,0:T(8,128)S(1)} collective-permute-done((f32[72,256]{1,0:T(8,128)S(1)}, f32[72,256]{1,0:T(8,128)S(1)}, u32[]{:S(2)}, u32[]{:S(2)}) %collective-permute-start.9) | collective-permute-done | bytes 73760 | tf_op jit(solution)/shard_map/ppermute | solution.py:21
  23.1 2.1 %shard_map.62.half_ref = f32[3,256,256]{2,1,0:T(8,128)S(1)} custom-call(f32[3,256,256]{2,1,0:T(8,128)S(1)} %get-tuple-element.46.own_ref, f32[72,256]{1,0:T(8,128)S(1)} %collective-permute-done.8.near_ref.near1, f32[72,256]{1,0:T(8,128)S(1)} %collective-permute-done.9.far_ref.far1), custom_call_target="tpu_custom_call" | custom-call | flops 905969664 | bytes 786432 | tf_op jit(solution)/shard_map/pallas_call | solution.py:276
  25.2 0.7 %collective-permute-start.10 = (f32[192,256]{1,0:T(8,128)S(1)}, f32[192,256]{1,0:T(8,128)S(1)}, u32[]{:S(2)}, u32[]{:S(2)}) collective-permute-start(f32[192,256]{1,0:T(8,128)S(1)} %collective-permute-done.7.near_ref.near2), channel_id=1, source_target_pairs={{0,1},{1,0},{2,3},{3,2},{4,5},{5,4},{6,7},{7,6},{8,9},{9,8},{10,11... | collective-permute-start | bytes 589832 | tf_op jit(solution)/shard_map/ppermute | solution.py:21
  25.9 1.1 %collective-permute-done.10.far_ref.far2 = f32[192,256]{1,0:T(8,128)S(1)} collective-permute-done((f32[192,256]{1,0:T(8,128)S(1)}, f32[192,256]{1,0:T(8,128)S(1)}, u32[]{:S(2)}, u32[]{:S(2)}) %collective-permute-start.10) | collective-permute-done | bytes 196640 | tf_op jit(solution)/shard_map/ppermute | solution.py:21
  27.0 0.7 %shard_map.63 = (f32[72,256]{1,0:T(8,128)S(1)}, f32[192,256]{1,0:T(8,128)S(1)}, f32[3,256,256]{2,1,0:T(8,128)S(1)}) custom-call(f32[3,256,256]{2,1,0:T(8,128)S(1)} %shard_map.62.half_ref, f32[72,256]{1,0:T(8,128)S(1)} %collective-permute-done.8.near_ref.near1, f32[192,256]{1,0:T(8,128)S(1)} %collective-permute-done.7.near_ref.near2, ...), custom_call_target="tpu_custom_call" | custom-call | flops 301989888 | bytes 1048576 | tf_op jit(solution)/shard_map/pallas_call | solution.py:276
  27.7 1.4 %collective-permute-start.12 = (f32[72,256]{1,0:T(8,128)S(1)}, f32[72,256]{1,0:T(8,128)S(1)}, u32[]{:S(2)}, u32[]{:S(2)}) collective-permute-start(f32[72,256]{1,0:T(8,128)S(1)} %get-tuple-element.54), channel_id=1, source_target_pairs={{0,8},{1,9},{2,10},{3,11},{4,12},{5,13},{6,14},{7,15},{8,0},{9,1},... | collective-permute-start | bytes 221192 | tf_op jit(solution)/shard_map/ppermute | solution.py:21
  29.2 2.6 %shard_map.64.old_ref = f32[3,256,256]{2,1,0:T(8,128)S(1)} custom-call(f32[3,256,256]{2,1,0:T(8,128)S(1)} %shard_map.61.old_ref, f32[72,256]{1,0:T(8,128)S(1)} %collective-permute-done.8.near_ref.near1, f32[72,256]{1,0:T(8,128)S(1)} %collective-permute-done.9.far_ref.far1, f32[192,256]{1,0:T(8,128)S(1)} %collective-permute-done.7.near_ref.near2, ...), custom_call_target="tpu_custom_call" | custom-call | flops 1207959552 | bytes 1310720 | tf_op jit(solution)/shard_map/pallas_call | solution.py:276
  31.8 1.1 %collective-permute-start.13 = (f32[72,256]{1,0:T(8,128)S(1)}, f32[72,256]{1,0:T(8,128)S(1)}, u32[]{:S(2)}, u32[]{:S(2)}) collective-permute-start(f32[72,256]{1,0:T(8,128)S(1)} %collective-permute-done.12.near_ref.near1), channel_id=1, source_target_pairs={{0,1},{1,0},{2,3},{3,2},{4,5},{5,4},{6,7},{7,6},{8,9},{9,8},{10,11... | collective-permute-start | bytes 221192 | tf_op jit(solution)/shard_map/ppermute | solution.py:21
  32.9 0.9 %collective-permute-done.13.far_ref.far1 = f32[72,256]{1,0:T(8,128)S(1)} collective-permute-done((f32[72,256]{1,0:T(8,128)S(1)}, f32[72,256]{1,0:T(8,128)S(1)}, u32[]{:S(2)}, u32[]{:S(2)}) %collective-permute-start.13) | collective-permute-done | bytes 73760 | tf_op jit(solution)/shard_map/ppermute | solution.py:21
  33.8 2.1 %shard_map.65 = (f32[3,256,256]{2,1,0:T(8,128)S(1)}, f32[72,256]{1,0:T(8,128)S(1)}) custom-call(f32[3,256,256]{2,1,0:T(8,128)S(1)} %get-tuple-element.53.own_ref, f32[72,256]{1,0:T(8,128)S(1)} %collective-permute-done.12.near_ref.near1, f32[72,256]{1,0:T(8,128)S(1)} %collective-permute-done.13.far_ref.far1), custom_call_target="tpu_custom_call" | custom-call | flops 905969664 | bytes 786432 | tf_op jit(solution)/shard_map/pallas_call | solution.py:276
  35.9 0.8 %collective-permute-start.14 = (f32[192,256]{1,0:T(8,128)S(1)}, f32[192,256]{1,0:T(8,128)S(1)}, u32[]{:S(2)}, u32[]{:S(2)}) collective-permute-start(f32[192,256]{1,0:T(8,128)S(1)} %collective-permute-done.11.near_ref.near2), channel_id=1, source_target_pairs={{0,1},{1,0},{2,3},{3,2},{4,5},{5,4},{6,7},{7,6},{8,9},{9,8},{10,11... | collective-permute-start | bytes 589832 | tf_op jit(solution)/shard_map/ppermute | solution.py:21
  38.9 2.6 %collective-permute-done.19.near_left = f32[72,256]{1,0:T(8,128)S(1)} collective-permute-done((f32[72,256]{1,0:T(8,128)S(1)}, f32[72,256]{1,0:T(8,128)S(1)}, u32[]{:S(2)}, u32[]{:S(2)}) %collective-permute-start.19) | collective-permute-done | bytes 73760 | tf_op jit(solution)/shard_map/ppermute | solution.py:29
  42.0 1.5 %collective-permute-start.20 = (f32[72,256]{1,0:T(8,128)S(1)}, f32[72,256]{1,0:T(8,128)S(1)}, u32[]{:S(2)}, u32[]{:S(2)}) collective-permute-start(f32[72,256]{1,0:T(8,128)S(1)} %collective-permute-done.19.near_left), channel_id=1, source_target_pairs={{0,1},{1,0},{2,3},{3,2},{4,5},{5,4},{6,7},{7,6},{8,9},{9,8},{10,11... | collective-permute-start | bytes 221192 | tf_op jit(solution)/shard_map/ppermute | solution.py:21
  44.0 5.4 %collective-permute-start.15 = (f32[128,256]{1,0:T(8,128)S(1)}, f32[128,256]{1,0:T(8,128)S(1)}, u32[]{:S(2)}, u32[]{:S(2)}) collective-permute-start(f32[128,256]{1,0:T(8,128)S(1)} %get-tuple-element.60), channel_id=1, source_target_pairs={{0,1},{1,0},{2,3},{3,2},{4,5},{5,4},{6,7},{7,6},{8,16},{9,17},{10,... | collective-permute-start | bytes 393224 | tf_op jit(solution)/shard_map/ppermute | solution.py:29
  49.4 2.6 %shard_map.67.old_ref = f32[3,256,256]{2,1,0:T(8,128)S(1)} custom-call(f32[3,256,256]{2,1,0:T(8,128)S(1)} %shard_map.64.old_ref, f32[72,256]{1,0:T(8,128)S(1)} %collective-permute-done.12.near_ref.near1, f32[72,256]{1,0:T(8,128)S(1)} %collective-permute-done.13.far_ref.far1, f32[192,256]{1,0:T(8,128)S(1)} %collective-permute-done.11.near_ref.near2, ...), custom_call_target="tpu_custom_call" | custom-call | flops 1207959552 | bytes 1310720 | tf_op jit(solution)/shard_map/pallas_call | solution.py:276
  52.0 2.1 %shard_map.68 = (f32[3,256,256]{2,1,0:T(8,128)S(1)}, f32[1,256,256]{2,1,0:T(8,128)}, f32[1,256,256]{2,1,0:T(8,128)}, f32[1,256,256]{2,1,0:T(8,128)}) custom-call(f32[3,256,256]{2,1,0:T(8,128)S(1)} %shard_map.67.old_ref, f32[72,256]{1,0:T(8,128)S(1)} %collective-permute-done.18.near2, f32[72,256]{1,0:T(8,128)S(1)} %collective-permute-done.21.far2, ...), custom_call_target="tpu_custom_call" | custom-call | flops 905969664 | bytes 1310720 | tf_op jit(solution)/shard_map/pallas_call | solution.py:276
  54.8 1.1 %collective-permute-done.23.far2 = f32[128,256]{1,0:T(8,128)S(1)} collective-permute-done((f32[128,256]{1,0:T(8,128)S(1)}, f32[128,256]{1,0:T(8,128)S(1)}, u32[]{:S(2)}, u32[]{:S(2)}) %collective-permute-start.23) | collective-permute-done | bytes 131104 | tf_op jit(solution)/shard_map/ppermute | solution.py:21
  55.9 1.4 %shard_map.69 = (f32[1,256,256]{2,1,0:T(8,128)}, f32[1,256,256]{2,1,0:T(8,128)}, f32[1,256,256]{2,1,0:T(8,128)}) custom-call(f32[3,256,256]{2,1,0:T(8,128)S(1)} %get-tuple-element.70.half_ref, f32[128,256]{1,0:T(8,128)S(1)} %collective-permute-done.15.near2, ...), custom_call_target="tpu_custom_call", output_to_operand_aliasing={{0}: (7, {}), {1}: (8, {}), {2}: (9, {})} | custom-call | flops 301989888 | bytes 1835008 | tf_op jit(solution)/shard_map/pallas_call | solution.py:276
  (31 shorter events, 5.4 us)
Async XLA Ops:
  0.6 2.4 %collective-permute-start = (f32[1,256,256]{2,1,0:T(8,128)}, f32[1,256,256]{2,1,0:T(8,128)S(1)}, u32[]{:S(2)}, u32[]{:S(2)}) collective-permute-start(f32[1,256,256]{2,1,0:T(8,128)} %param.3), channel_id=1, source_target_pairs={{0,1},{1,0},{2,3},{3,2},{4,5},{5,4},{6,7},{7,6},{8,9},{9,8},{10,11... | collective-permute-start | bytes 786440 | tf_op jit(solution)/shard_map/ppermute | solution.py:21
  1.4 1.7 %collective-permute-start.1 = (f32[1,256,256]{2,1,0:T(8,128)}, f32[1,256,256]{2,1,0:T(8,128)S(1)}, u32[]{:S(2)}, u32[]{:S(2)}) collective-permute-start(f32[1,256,256]{2,1,0:T(8,128)} %param.4), channel_id=1, source_target_pairs={{0,1},{1,0},{2,3},{3,2},{4,5},{5,4},{6,7},{7,6},{8,9},{9,8},{10,11... | collective-permute-start | bytes 786440 | tf_op jit(solution)/shard_map/ppermute | solution.py:21
  1.4 2.0 %collective-permute-start.2 = (f32[1,256,256]{2,1,0:T(8,128)}, f32[1,256,256]{2,1,0:T(8,128)S(1)}, u32[]{:S(2)}, u32[]{:S(2)}) collective-permute-start(f32[1,256,256]{2,1,0:T(8,128)} %param.5), channel_id=1, source_target_pairs={{0,1},{1,0},{2,3},{3,2},{4,5},{5,4},{6,7},{7,6},{8,9},{9,8},{10,11... | collective-permute-start | bytes 786440 | tf_op jit(solution)/shard_map/ppermute | solution.py:21
  6.1 3.3 %collective-permute-start.4 = (f32[72,256]{1,0:T(8,128)S(1)}, f32[72,256]{1,0:T(8,128)S(1)}, u32[]{:S(2)}, u32[]{:S(2)}) collective-permute-start(f32[72,256]{1,0:T(8,128)S(1)} %get-tuple-element.42), channel_id=1, source_target_pairs={{0,2},{1,3},{2,0},{3,1},{4,6},{5,7},{6,4},{7,5},{8,10},{9,11},{10,... | collective-permute-start | bytes 221192 | tf_op jit(solution)/shard_map/ppermute | solution.py:21
  7.4 7.0 %collective-permute-start.3 = (f32[192,256]{1,0:T(8,128)S(1)}, f32[192,256]{1,0:T(8,128)S(1)}, u32[]{:S(2)}, u32[]{:S(2)}) collective-permute-start(f32[192,256]{1,0:T(8,128)S(1)} %get-tuple-element.40), channel_id=1, source_target_pairs={{0,2},{1,3},{2,0},{3,1},{4,6},{5,7},{6,4},{7,5},{8,10},{9,11},{10,... | collective-permute-start | bytes 589832 | tf_op jit(solution)/shard_map/ppermute | solution.py:21
  9.4 2.9 %collective-permute-start.5 = (f32[72,256]{1,0:T(8,128)S(1)}, f32[72,256]{1,0:T(8,128)S(1)}, u32[]{:S(2)}, u32[]{:S(2)}) collective-permute-start(f32[72,256]{1,0:T(8,128)S(1)} %collective-permute-done.4.near_ref.near1), channel_id=1, source_target_pairs={{0,1},{1,0},{2,3},{3,2},{4,5},{5,4},{6,7},{7,6},{8,9},{9,8},{10,11... | collective-permute-start | bytes 221192 | tf_op jit(solution)/shard_map/ppermute | solution.py:21
  14.4 1.8 %collective-permute-start.6 = (f32[192,256]{1,0:T(8,128)S(1)}, f32[192,256]{1,0:T(8,128)S(1)}, u32[]{:S(2)}, u32[]{:S(2)}) collective-permute-start(f32[192,256]{1,0:T(8,128)S(1)} %collective-permute-done.3.near_ref.near2), channel_id=1, source_target_pairs={{0,1},{1,0},{2,3},{3,2},{4,5},{5,4},{6,7},{7,6},{8,9},{9,8},{10,11... | collective-permute-start | bytes 589832 | tf_op jit(solution)/shard_map/ppermute | solution.py:21
  16.9 4.1 %collective-permute-start.8 = (f32[72,256]{1,0:T(8,128)S(1)}, f32[72,256]{1,0:T(8,128)S(1)}, u32[]{:S(2)}, u32[]{:S(2)}) collective-permute-start(f32[72,256]{1,0:T(8,128)S(1)} %get-tuple-element.47), channel_id=1, source_target_pairs={{0,4},{1,5},{2,6},{3,7},{4,0},{5,1},{6,2},{7,3},{8,12},{9,13},{10,... | collective-permute-start | bytes 221192 | tf_op jit(solution)/shard_map/ppermute | solution.py:21
  18.2 7.0 %collective-permute-start.7 = (f32[192,256]{1,0:T(8,128)S(1)}, f32[192,256]{1,0:T(8,128)S(1)}, u32[]{:S(2)}, u32[]{:S(2)}) collective-permute-start(f32[192,256]{1,0:T(8,128)S(1)} %get-tuple-element.45), channel_id=1, source_target_pairs={{0,4},{1,5},{2,6},{3,7},{4,0},{5,1},{6,2},{7,3},{8,12},{9,13},{10,... | collective-permute-start | bytes 589832 | tf_op jit(solution)/shard_map/ppermute | solution.py:21
  21.0 2.0 %collective-permute-start.9 = (f32[72,256]{1,0:T(8,128)S(1)}, f32[72,256]{1,0:T(8,128)S(1)}, u32[]{:S(2)}, u32[]{:S(2)}) collective-permute-start(f32[72,256]{1,0:T(8,128)S(1)} %collective-permute-done.8.near_ref.near1), channel_id=1, source_target_pairs={{0,1},{1,0},{2,3},{3,2},{4,5},{5,4},{6,7},{7,6},{8,9},{9,8},{10,11... | collective-permute-start | bytes 221192 | tf_op jit(solution)/shard_map/ppermute | solution.py:21
  25.2 1.8 %collective-permute-start.10 = (f32[192,256]{1,0:T(8,128)S(1)}, f32[192,256]{1,0:T(8,128)S(1)}, u32[]{:S(2)}, u32[]{:S(2)}) collective-permute-start(f32[192,256]{1,0:T(8,128)S(1)} %collective-permute-done.7.near_ref.near2), channel_id=1, source_target_pairs={{0,1},{1,0},{2,3},{3,2},{4,5},{5,4},{6,7},{7,6},{8,9},{9,8},{10,11... | collective-permute-start | bytes 589832 | tf_op jit(solution)/shard_map/ppermute | solution.py:21
  27.7 4.1 %collective-permute-start.12 = (f32[72,256]{1,0:T(8,128)S(1)}, f32[72,256]{1,0:T(8,128)S(1)}, u32[]{:S(2)}, u32[]{:S(2)}) collective-permute-start(f32[72,256]{1,0:T(8,128)S(1)} %get-tuple-element.54), channel_id=1, source_target_pairs={{0,8},{1,9},{2,10},{3,11},{4,12},{5,13},{6,14},{7,15},{8,0},{9,1},... | collective-permute-start | bytes 221192 | tf_op jit(solution)/shard_map/ppermute | solution.py:21
  29.0 6.8 %collective-permute-start.11 = (f32[192,256]{1,0:T(8,128)S(1)}, f32[192,256]{1,0:T(8,128)S(1)}, u32[]{:S(2)}, u32[]{:S(2)}) collective-permute-start(f32[192,256]{1,0:T(8,128)S(1)} %get-tuple-element.52), channel_id=1, source_target_pairs={{0,8},{1,9},{2,10},{3,11},{4,12},{5,13},{6,14},{7,15},{8,0},{9,1},... | collective-permute-start | bytes 589832 | tf_op jit(solution)/shard_map/ppermute | solution.py:21
  31.8 2.0 %collective-permute-start.13 = (f32[72,256]{1,0:T(8,128)S(1)}, f32[72,256]{1,0:T(8,128)S(1)}, u32[]{:S(2)}, u32[]{:S(2)}) collective-permute-start(f32[72,256]{1,0:T(8,128)S(1)} %collective-permute-done.12.near_ref.near1), channel_id=1, source_target_pairs={{0,1},{1,0},{2,3},{3,2},{4,5},{5,4},{6,7},{7,6},{8,9},{9,8},{10,11... | collective-permute-start | bytes 221192 | tf_op jit(solution)/shard_map/ppermute | solution.py:21
  35.9 1.9 %collective-permute-start.14 = (f32[192,256]{1,0:T(8,128)S(1)}, f32[192,256]{1,0:T(8,128)S(1)}, u32[]{:S(2)}, u32[]{:S(2)}) collective-permute-start(f32[192,256]{1,0:T(8,128)S(1)} %collective-permute-done.11.near_ref.near2), channel_id=1, source_target_pairs={{0,1},{1,0},{2,3},{3,2},{4,5},{5,4},{6,7},{7,6},{8,9},{9,8},{10,11... | collective-permute-start | bytes 589832 | tf_op jit(solution)/shard_map/ppermute | solution.py:21
  36.7 4.8 %collective-permute-start.19 = (f32[72,256]{1,0:T(8,128)S(1)}, f32[72,256]{1,0:T(8,128)S(1)}, u32[]{:S(2)}, u32[]{:S(2)}) collective-permute-start(f32[72,256]{1,0:T(8,128)S(1)} %get-tuple-element.62), channel_id=1, source_target_pairs={{0,16},{1,17},{2,18},{3,19},{4,20},{5,21},{6,22},{7,23},{8,9},{9,8... | collective-permute-start | bytes 221192 | tf_op jit(solution)/shard_map/ppermute | solution.py:29
  36.7 5.3 %collective-permute-start.18 = (f32[72,256]{1,0:T(8,128)S(1)}, f32[72,256]{1,0:T(8,128)S(1)}, u32[]{:S(2)}, u32[]{:S(2)}) collective-permute-start(f32[72,256]{1,0:T(8,128)S(1)} %get-tuple-element.62), channel_id=1, source_target_pairs={{0,1},{1,0},{2,3},{3,2},{4,5},{5,4},{6,7},{7,6},{8,16},{9,17},{10,... | collective-permute-start | bytes 221192 | tf_op jit(solution)/shard_map/ppermute | solution.py:29
  37.0 5.0 %collective-permute-start.17 = (f32[72,256]{1,0:T(8,128)S(1)}, f32[72,256]{1,0:T(8,128)S(1)}, u32[]{:S(2)}, u32[]{:S(2)}) collective-permute-start(f32[72,256]{1,0:T(8,128)S(1)} %get-tuple-element.62), channel_id=1, source_target_pairs={{0,1},{1,0},{2,3},{3,2},{4,5},{5,4},{6,7},{7,6},{8,24},{9,25},{10,... | collective-permute-start | bytes 221192 | tf_op jit(solution)/shard_map/ppermute | solution.py:29
  38.4 15.7 %collective-permute-start.16 = (f32[200,256]{1,0:T(8,128)S(1)}, f32[200,256]{1,0:T(8,128)S(1)}, u32[]{:S(2)}, u32[]{:S(2)}) collective-permute-start(f32[200,256]{1,0:T(8,128)S(1)} %get-tuple-element.61), channel_id=1, source_target_pairs={{0,1},{1,0},{2,3},{3,2},{4,5},{5,4},{6,7},{7,6},{8,24},{9,25},{10,... | collective-permute-start | bytes 614408 | tf_op jit(solution)/shard_map/ppermute | solution.py:29
  42.0 10.0 %collective-permute-start.20 = (f32[72,256]{1,0:T(8,128)S(1)}, f32[72,256]{1,0:T(8,128)S(1)}, u32[]{:S(2)}, u32[]{:S(2)}) collective-permute-start(f32[72,256]{1,0:T(8,128)S(1)} %collective-permute-done.19.near_left), channel_id=1, source_target_pairs={{0,1},{1,0},{2,3},{3,2},{4,5},{5,4},{6,7},{7,6},{8,9},{9,8},{10,11... | collective-permute-start | bytes 221192 | tf_op jit(solution)/shard_map/ppermute | solution.py:21
  43.5 8.5 %collective-permute-start.21 = (f32[72,256]{1,0:T(8,128)S(1)}, f32[72,256]{1,0:T(8,128)S(1)}, u32[]{:S(2)}, u32[]{:S(2)}) collective-permute-start(f32[72,256]{1,0:T(8,128)S(1)} %collective-permute-done.18.near2), channel_id=1, source_target_pairs={{0,1},{1,0},{2,3},{3,2},{4,5},{5,4},{6,7},{7,6},{8,9},{9,8},{10,11... | collective-permute-start | bytes 221192 | tf_op jit(solution)/shard_map/ppermute | solution.py:21
  43.5 8.5 %collective-permute-start.22 = (f32[72,256]{1,0:T(8,128)S(1)}, f32[72,256]{1,0:T(8,128)S(1)}, u32[]{:S(2)}, u32[]{:S(2)}) collective-permute-start(f32[72,256]{1,0:T(8,128)S(1)} %collective-permute-done.17.near3), channel_id=1, source_target_pairs={{0,1},{1,0},{2,3},{3,2},{4,5},{5,4},{6,7},{7,6},{8,9},{9,8},{10,11... | collective-permute-start | bytes 221192 | tf_op jit(solution)/shard_map/ppermute | solution.py:21
  44.0 10.1 %collective-permute-start.15 = (f32[128,256]{1,0:T(8,128)S(1)}, f32[128,256]{1,0:T(8,128)S(1)}, u32[]{:S(2)}, u32[]{:S(2)}) collective-permute-start(f32[128,256]{1,0:T(8,128)S(1)} %get-tuple-element.60), channel_id=1, source_target_pairs={{0,1},{1,0},{2,3},{3,2},{4,5},{5,4},{6,7},{7,6},{8,16},{9,17},{10,... | collective-permute-start | bytes 393224 | tf_op jit(solution)/shard_map/ppermute | solution.py:29
  54.2 1.7 %collective-permute-start.24 = (f32[200,256]{1,0:T(8,128)S(1)}, f32[200,256]{1,0:T(8,128)S(1)}, u32[]{:S(2)}, u32[]{:S(2)}) collective-permute-start(f32[200,256]{1,0:T(8,128)S(1)} %collective-permute-done.16.near3), channel_id=1, source_target_pairs={{0,1},{1,0},{2,3},{3,2},{4,5},{5,4},{6,7},{7,6},{8,9},{9,8},{10,11... | collective-permute-start | bytes 614408 | tf_op jit(solution)/shard_map/ppermute | solution.py:21
  54.5 1.4 %collective-permute-start.23 = (f32[128,256]{1,0:T(8,128)S(1)}, f32[128,256]{1,0:T(8,128)S(1)}, u32[]{:S(2)}, u32[]{:S(2)}) collective-permute-start(f32[128,256]{1,0:T(8,128)S(1)} %collective-permute-done.15.near2), channel_id=1, source_target_pairs={{0,1},{1,0},{2,3},{3,2},{4,5},{5,4},{6,7},{7,6},{8,9},{9,8},{10,11... | collective-permute-start | bytes 393224 | tf_op jit(solution)/shard_map/ppermute | solution.py:21

commit v10 on v8

--- a/solution.py
+++ b/solution.py
@@ -174,21 +174,38 @@
     prefix_ref[2] = pick(through, trans)
 
 
-def early_kernel(own_ref, near_ref, far_ref, half_ref, *first_ref):
-    core = bit(place(), 1)
-    facing = unpack_symmetric(near_ref, far_ref, core, 0)
-    half = before_trans((own_ref[0], own_ref[1], own_ref[2]), facing)
-    for ref in first_ref:
-        pack_symmetric(half[2], core, ref, 0)
-    for i, x in enumerate(half):
+def early_kernel(own_ref, near_ref, far_ref, half_ref):
+    facing = unpack_symmetric(near_ref, far_ref, bit(place(), 1), 0)
+    for i, x in enumerate(before_trans((own_ref[0], own_ref[1], own_ref[2]), facing)):
         half_ref[i] = x
 
 
-def final_kernel(half_ref, near1, near_ref, far_ref, second_ref):
-    core = bit(place(), 1)
-    into, away = unpack_second(near_ref, far_ref, core, near1)
-    trans, other_side = after_trans(half_ref[0], half_ref[1], away, into)
-    pack_second(trans, other_side, core, second_ref)
+def only_quarter_1(distance, body, *out_refs):
+    mine = place() // distance == 1
+    pl.when(mine)(body)
+
+    @pl.when(jnp.logical_not(mine))
+    def _():
+        for ref in out_refs:
+            ref[...] = jnp.zeros_like(ref)
+
+
+def final_early_kernel(distance, own_ref, near_ref, far_ref, half_ref, first_ref):
+    def body():
+        early_kernel(own_ref, near_ref, far_ref, half_ref)
+        pack_symmetric(half_ref[2], bit(place(), 1), first_ref, 0)
+
+    only_quarter_1(distance, body, half_ref, first_ref)
+
+
+def final_kernel(distance, half_ref, near1, near_ref, far_ref, second_ref):
+    def body():
+        core = bit(place(), 1)
+        into, away = unpack_second(near_ref, far_ref, core, near1)
+        trans, other_side = after_trans(half_ref[0], half_ref[1], away, into)
+        pack_second(trans, other_side, core, second_ref)
+
+    only_quarter_1(distance, body, second_ref)
 
 
 def pack_second(back, away, core, ref):
@@ -296,18 +313,19 @@
             (prefix,) = pending(prefix)
             near1, prefix = lax.optimization_barrier((near1, prefix))
         far1 = swap(near1, 1)
-        outs = [stack] + [first] * (level == levels - 2)
-        halfway, *sends = call(early_kernel, 27, outs, own, near1, far1)
+        if level < levels - 2:
+            (halfway,) = call(early_kernel, 27, [stack], own, near1, far1)
+        else:
+            halfway, send1 = call(bind(final_early_kernel), 27, [stack, first], own, near1, far1)
         near2, halfway = lax.optimization_barrier((near2, halfway))
         far2 = swap(near2, 1)
         pending = lambda old, kernel=bind(prefix_kernel), got=(near1, far1, near2, far2): call(kernel, 36, [stack], old, *got)
         if level < levels - 2:
             send1, send2, own = call(bind(late_kernel), 9, [first, second, stack], halfway, near1, near2, far2)
 
+    first3, first2 = pair(send1, 1, 3), pair(send1, 1, 2)
+    (send2,) = call(bind(final_kernel), 9, [padded], halfway, near1, near2, far2)
     distance *= 2
-    (send1,) = sends
-    first3, first2 = pair(send1, 1, 3), pair(send1, 1, 2)
-    (send2,) = call(final_kernel, 9, [padded], halfway, near1, near2, far2)
     near3, near2 = pair(send2, 1, 3), pair(send2, 1, 2)
     first3, first2, prefix = lax.optimization_barrier((first3, first2, prefix))
     (prefix,) = pending(prefix)

time: 54.6 us -> 54.6 us (level)
  waiting for transfers between devices: 11.4 us -> 14.3 us
  Pallas kernels: 22.2 us -> 19.5 us
    pallas_call x12, Pallas kernels: 22.2 us -> 19.5 us  [call(): pl.pallas_call(kernel, out_shape=[jax.ShapeDtypeStruct(s, F32) for s in o...]
    ppermute x19, waiting for transfers between devices: 8.68 us -> 10.3 us  [swap(): return lax.ppermute(block, AXES, [(i, i ^ distance) for i in range(count)])]
    ppermute x4, waiting for transfers between devices: 2.75 us -> 4.01 us  [pair(): lax.ppermute(block, AXES, [(i, step.get(i // quarter, lambda i: i ^ 1)(i)...]
  transfers between devices with their start and end apart: 23 -> 23, of which waited for: 12 -> 13; matrix products, arithmetic and copies ran while one was open for 2% -> 2% of each run, Pallas kernels for 31% -> 26%
where the time goes in v10:
time: 54.6 us; the launch traced here: 54.4 us
  Pallas kernels  19.5 us (36%)
  starting transfers between devices  18.5 us (34%)
  waiting for transfers between devices  14.3 us (26%)
  other arithmetic  1.16 us (2%)
  between operations  0.96 us (2%)
    pallas_call x12, Pallas kernels, call(): pl.pallas_call(kernel, out_shape=[jax.ShapeDtypeStruct(s, F32) for s in o...  19.5 us
    ppermute x19, starting transfers between devices, swap(): return lax.ppermute(block, AXES, [(i, i ^ distance) for i in range(count)])  15.5 us
    ppermute x19, waiting for transfers between devices, swap(): return lax.ppermute(block, AXES, [(i, i ^ distance) for i in range(count)])  10.3 us
    ppermute x4, waiting for transfers between devices, pair(): lax.ppermute(block, AXES, [(i, step.get(i // quarter, lambda i: i ^ 1)(i)...  4.01 us
    ppermute x4, starting transfers between devices, pair(): lax.ppermute(block, AXES, [(i, step.get(i // quarter, lambda i: i ^ 1)(i)...  2.98 us
    concatenate x1, other arithmetic, shards(): section = jnp.concatenate(sections, 0)  1.16 us
  transfers between devices with their start and end apart: 23, of which 13 were waited for; matrix products, arithmetic and copies ran while one was open for 2% of the time, Pallas kernels for 26%

profile of v10, /device:TPU:17, one launch (start us, length us, event | category | flops | bytes accessed | tf_op | source)
XLA Modules:
  0.0 54.4 jit_solution(4209078221939622516)
XLA Ops:
  0.6 0.7 %collective-permute-start = (f32[1,256,256]{2,1,0:T(8,128)}, f32[1,256,256]{2,1,0:T(8,128)S(1)}, u32[]{:S(2)}, u32[]{:S(2)}) collective-permute-start(f32[1,256,256]{2,1,0:T(8,128)} %param.3), channel_id=1, source_target_pairs={{0,1},{1,0},{2,3},{3,2},{4,5},{5,4},{6,7},{7,6},{8,9},{9,8},{10,11... | collective-permute-start | bytes 786440 | tf_op jit(solution)/shard_map/ppermute | solution.py:21
  1.9 1.2 %pad_maximum_fusion.section_ref = f32[3,256,256]{2,1,0:T(8,128)S(1)} fusion(f32[1,256,256]{2,1,0:T(8,128)} %param.5, f32[1,256,256]{2,1,0:T(8,128)} %param.4, f32[1,256,256]{2,1,0:T(8,128)} %param.3), kind=kLoop, calls=%fused_computation | loop fusion | flops 393216 | bytes 1572864 | tf_op jit(solution)/shard_map/concatenate | solution.py:305
  3.5 2.6 %shard_map.58 = (f32[3,256,256]{2,1,0:T(8,128)S(1)}, f32[72,256]{1,0:T(8,128)S(1)}, f32[192,256]{1,0:T(8,128)S(1)}, f32[3,256,256]{2,1,0:T(8,128)S(1)}) custom-call(f32[3,256,256]{2,1,0:T(8,128)S(1)} %pad_maximum_fusion.section_ref, f32[1,256,256]{2,1,0:T(8,128)S(1)} %collective-permute-done.got1, f32[1,256,256]{2,1,0:T(8,128)S(1)} %collective-permute-done.1.got2, ...), custom_call_target="tpu_custom_call" | custom-call | flops 1207959552 | bytes 1048576 | tf_op jit(solution)/shard_map/pallas_call | solution.py:286
  6.1 1.3 %collective-permute-start.4 = (f32[72,256]{1,0:T(8,128)S(1)}, f32[72,256]{1,0:T(8,128)S(1)}, u32[]{:S(2)}, u32[]{:S(2)}) collective-permute-start(f32[72,256]{1,0:T(8,128)S(1)} %get-tuple-element.38), channel_id=1, source_target_pairs={{0,2},{1,3},{2,0},{3,1},{4,6},{5,7},{6,4},{7,5},{8,10},{9,11},{10,... | collective-permute-start | bytes 221192 | tf_op jit(solution)/shard_map/ppermute | solution.py:21
  7.6 1.7 %collective-permute-done.4.near_ref.near1 = f32[72,256]{1,0:T(8,128)S(1)} collective-permute-done((f32[72,256]{1,0:T(8,128)S(1)}, f32[72,256]{1,0:T(8,128)S(1)}, u32[]{:S(2)}, u32[]{:S(2)}) %collective-permute-start.4) | collective-permute-done | bytes 73760 | tf_op jit(solution)/shard_map/ppermute | solution.py:21
  9.4 2.0 %collective-permute-start.5 = (f32[72,256]{1,0:T(8,128)S(1)}, f32[72,256]{1,0:T(8,128)S(1)}, u32[]{:S(2)}, u32[]{:S(2)}) collective-permute-start(f32[72,256]{1,0:T(8,128)S(1)} %collective-permute-done.4.near_ref.near1), channel_id=1, source_target_pairs={{0,1},{1,0},{2,3},{3,2},{4,5},{5,4},{6,7},{7,6},{8,9},{9,8},{10,11... | collective-permute-start | bytes 221192 | tf_op jit(solution)/shard_map/ppermute | solution.py:21
  11.4 0.9 %collective-permute-done.5.far_ref.far1 = f32[72,256]{1,0:T(8,128)S(1)} collective-permute-done((f32[72,256]{1,0:T(8,128)S(1)}, f32[72,256]{1,0:T(8,128)S(1)}, u32[]{:S(2)}, u32[]{:S(2)}) %collective-permute-start.5) | collective-permute-done | bytes 73760 | tf_op jit(solution)/shard_map/ppermute | solution.py:21
  12.3 2.1 %shard_map.59.half_ref = f32[3,256,256]{2,1,0:T(8,128)S(1)} custom-call(f32[3,256,256]{2,1,0:T(8,128)S(1)} %get-tuple-element.37.own_ref, f32[72,256]{1,0:T(8,128)S(1)} %collective-permute-done.4.near_ref.near1, f32[72,256]{1,0:T(8,128)S(1)} %collective-permute-done.5.far_ref.far1), custom_call_target="tpu_custom_call" | custom-call | flops 905969664 | bytes 786432 | tf_op jit(solution)/shard_map/pallas_call | solution.py:286
  15.1 1.1 %collective-permute-done.6.far_ref.far2 = f32[192,256]{1,0:T(8,128)S(1)} collective-permute-done((f32[192,256]{1,0:T(8,128)S(1)}, f32[192,256]{1,0:T(8,128)S(1)}, u32[]{:S(2)}, u32[]{:S(2)}) %collective-permute-start.6) | collective-permute-done | bytes 196640 | tf_op jit(solution)/shard_map/ppermute | solution.py:21
  16.9 1.3 %collective-permute-start.8 = (f32[72,256]{1,0:T(8,128)S(1)}, f32[72,256]{1,0:T(8,128)S(1)}, u32[]{:S(2)}, u32[]{:S(2)}) collective-permute-start(f32[72,256]{1,0:T(8,128)S(1)} %get-tuple-element.43), channel_id=1, source_target_pairs={{0,4},{1,5},{2,6},{3,7},{4,0},{5,1},{6,2},{7,3},{8,12},{9,13},{10,... | collective-permute-start | bytes 221192 | tf_op jit(solution)/shard_map/ppermute | solution.py:21
  18.4 2.6 %shard_map.61.old_ref = f32[3,256,256]{2,1,0:T(8,128)S(1)} custom-call(f32[3,256,256]{2,1,0:T(8,128)S(1)} %get-tuple-element.44.old_ref, f32[72,256]{1,0:T(8,128)S(1)} %collective-permute-done.4.near_ref.near1, f32[72,256]{1,0:T(8,128)S(1)} %collective-permute-done.5.far_ref.far1, f32[192,256]{1,0:T(8,128)S(1)} %collective-permute-done.3.near_ref.near2, ...), custom_call_target="tpu_custom_call" | custom-call | flops 1207959552 | bytes 1310720 | tf_op jit(solution)/shard_map/pallas_call | solution.py:286
  21.0 1.1 %collective-permute-start.9 = (f32[72,256]{1,0:T(8,128)S(1)}, f32[72,256]{1,0:T(8,128)S(1)}, u32[]{:S(2)}, u32[]{:S(2)}) collective-permute-start(f32[72,256]{1,0:T(8,128)S(1)} %collective-permute-done.8.near_ref.near1), channel_id=1, source_target_pairs={{0,1},{1,0},{2,3},{3,2},{4,5},{5,4},{6,7},{7,6},{8,9},{9,8},{10,11... | collective-permute-start | bytes 221192 | tf_op jit(solution)/shard_map/ppermute | solution.py:21
  22.2 0.9 %collective-permute-done.9.far_ref.far1 = f32[72,256]{1,0:T(8,128)S(1)} collective-permute-done((f32[72,256]{1,0:T(8,128)S(1)}, f32[72,256]{1,0:T(8,128)S(1)}, u32[]{:S(2)}, u32[]{:S(2)}) %collective-permute-start.9) | collective-permute-done | bytes 73760 | tf_op jit(solution)/shard_map/ppermute | solution.py:21
  23.1 2.1 %shard_map.62.half_ref = f32[3,256,256]{2,1,0:T(8,128)S(1)} custom-call(f32[3,256,256]{2,1,0:T(8,128)S(1)} %get-tuple-element.42.own_ref, f32[72,256]{1,0:T(8,128)S(1)} %collective-permute-done.8.near_ref.near1, f32[72,256]{1,0:T(8,128)S(1)} %collective-permute-done.9.far_ref.far1), custom_call_target="tpu_custom_call" | custom-call | flops 905969664 | bytes 786432 | tf_op jit(solution)/shard_map/pallas_call | solution.py:286
  25.2 0.7 %collective-permute-start.10 = (f32[192,256]{1,0:T(8,128)S(1)}, f32[192,256]{1,0:T(8,128)S(1)}, u32[]{:S(2)}, u32[]{:S(2)}) collective-permute-start(f32[192,256]{1,0:T(8,128)S(1)} %collective-permute-done.7.near_ref.near2), channel_id=1, source_target_pairs={{0,1},{1,0},{2,3},{3,2},{4,5},{5,4},{6,7},{7,6},{8,9},{9,8},{10,11... | collective-permute-start | bytes 589832 | tf_op jit(solution)/shard_map/ppermute | solution.py:21
  25.9 1.1 %collective-permute-done.10.far_ref.far2 = f32[192,256]{1,0:T(8,128)S(1)} collective-permute-done((f32[192,256]{1,0:T(8,128)S(1)}, f32[192,256]{1,0:T(8,128)S(1)}, u32[]{:S(2)}, u32[]{:S(2)}) %collective-permute-start.10) | collective-permute-done | bytes 196640 | tf_op jit(solution)/shard_map/ppermute | solution.py:21
  27.7 1.4 %collective-permute-start.12 = (f32[72,256]{1,0:T(8,128)S(1)}, f32[72,256]{1,0:T(8,128)S(1)}, u32[]{:S(2)}, u32[]{:S(2)}) collective-permute-start(f32[72,256]{1,0:T(8,128)S(1)} %get-tuple-element.50), channel_id=1, source_target_pairs={{0,8},{1,9},{2,10},{3,11},{4,12},{5,13},{6,14},{7,15},{8,0},{9,1},... | collective-permute-start | bytes 221192 | tf_op jit(solution)/shard_map/ppermute | solution.py:21
  29.2 2.6 %shard_map.64.old_ref = f32[3,256,256]{2,1,0:T(8,128)S(1)} custom-call(f32[3,256,256]{2,1,0:T(8,128)S(1)} %shard_map.61.old_ref, f32[72,256]{1,0:T(8,128)S(1)} %collective-permute-done.8.near_ref.near1, f32[72,256]{1,0:T(8,128)S(1)} %collective-permute-done.9.far_ref.far1, f32[192,256]{1,0:T(8,128)S(1)} %collective-permute-done.7.near_ref.near2, ...), custom_call_target="tpu_custom_call" | custom-call | flops 1207959552 | bytes 1310720 | tf_op jit(solution)/shard_map/pallas_call | solution.py:286
  31.8 1.1 %collective-permute-start.13 = (f32[72,256]{1,0:T(8,128)S(1)}, f32[72,256]{1,0:T(8,128)S(1)}, u32[]{:S(2)}, u32[]{:S(2)}) collective-permute-start(f32[72,256]{1,0:T(8,128)S(1)} %collective-permute-done.12.near_ref.near1), channel_id=1, source_target_pairs={{0,1},{1,0},{2,3},{3,2},{4,5},{5,4},{6,7},{7,6},{8,9},{9,8},{10,11... | collective-permute-start | bytes 221192 | tf_op jit(solution)/shard_map/ppermute | solution.py:21
  32.9 0.9 %collective-permute-done.13.far_ref.far1 = f32[72,256]{1,0:T(8,128)S(1)} collective-permute-done((f32[72,256]{1,0:T(8,128)S(1)}, f32[72,256]{1,0:T(8,128)S(1)}, u32[]{:S(2)}, u32[]{:S(2)}) %collective-permute-start.13) | collective-permute-done | bytes 73760 | tf_op jit(solution)/shard_map/ppermute | solution.py:21
  33.8 1.6 %collective-permute-done.11.near_ref.near2 = f32[192,256]{1,0:T(8,128)S(1)} collective-permute-done((f32[192,256]{1,0:T(8,128)S(1)}, f32[192,256]{1,0:T(8,128)S(1)}, u32[]{:S(2)}, u32[]{:S(2)}) %collective-permute-start.11) | collective-permute-done | bytes 196640 | tf_op jit(solution)/shard_map/ppermute | solution.py:21
  35.5 1.2 %collective-permute-start.14 = (f32[192,256]{1,0:T(8,128)S(1)}, f32[192,256]{1,0:T(8,128)S(1)}, u32[]{:S(2)}, u32[]{:S(2)}) collective-permute-start(f32[192,256]{1,0:T(8,128)S(1)} %collective-permute-done.11.near_ref.near2), channel_id=1, source_target_pairs={{0,1},{1,0},{2,3},{3,2},{4,5},{5,4},{6,7},{7,6},{8,9},{9,8},{10,11... | collective-permute-start | bytes 589832 | tf_op jit(solution)/shard_map/ppermute | solution.py:21
  38.2 2.4 %collective-permute-done.17.near2 = f32[72,256]{1,0:T(8,128)S(1)} collective-permute-done((f32[72,256]{1,0:T(8,128)S(1)}, f32[72,256]{1,0:T(8,128)S(1)}, u32[]{:S(2)}, u32[]{:S(2)}) %collective-permute-start.17) | collective-permute-done | bytes 73760 | tf_op jit(solution)/shard_map/ppermute | solution.py:29
  40.6 1.2 %collective-permute-start.18 = (f32[72,256]{1,0:T(8,128)S(1)}, f32[72,256]{1,0:T(8,128)S(1)}, u32[]{:S(2)}, u32[]{:S(2)}) collective-permute-start(f32[72,256]{1,0:T(8,128)S(1)} %collective-permute-done.17.near2), channel_id=1, source_target_pairs={{0,1},{1,0},{2,3},{3,2},{4,5},{5,4},{6,7},{7,6},{8,9},{9,8},{10,11... | collective-permute-start | bytes 221192 | tf_op jit(solution)/shard_map/ppermute | solution.py:21
  41.8 2.0 %collective-permute-start.20 = (f32[200,256]{1,0:T(8,128)S(1)}, f32[200,256]{1,0:T(8,128)S(1)}, u32[]{:S(2)}, u32[]{:S(2)}) collective-permute-start(f32[200,256]{1,0:T(8,128)S(1)} %shard_map.66), channel_id=1, source_target_pairs={{0,1},{1,0},{2,3},{3,2},{4,5},{5,4},{6,7},{7,6},{8,16},{9,17},{10,... | collective-permute-start | bytes 614408 | tf_op jit(solution)/shard_map/ppermute | solution.py:29
  43.7 2.6 %shard_map.67.old_ref = f32[3,256,256]{2,1,0:T(8,128)S(1)} custom-call(f32[3,256,256]{2,1,0:T(8,128)S(1)} %shard_map.64.old_ref, f32[72,256]{1,0:T(8,128)S(1)} %collective-permute-done.12.near_ref.near1, f32[72,256]{1,0:T(8,128)S(1)} %collective-permute-done.13.far_ref.far1, f32[192,256]{1,0:T(8,128)S(1)} %collective-permute-done.11.near_ref.near2, ...), custom_call_target="tpu_custom_call" | custom-call | flops 1207959552 | bytes 1310720 | tf_op jit(solution)/shard_map/pallas_call | solution.py:286
  46.3 2.1 %shard_map.68 = (f32[3,256,256]{2,1,0:T(8,128)S(1)}, f32[1,256,256]{2,1,0:T(8,128)}, f32[1,256,256]{2,1,0:T(8,128)}, f32[1,256,256]{2,1,0:T(8,128)}) custom-call(f32[3,256,256]{2,1,0:T(8,128)S(1)} %shard_map.67.old_ref, f32[72,256]{1,0:T(8,128)S(1)} %collective-permute-done.17.near2, f32[72,256]{1,0:T(8,128)S(1)} %collective-permute-done.18.far2, ...), custom_call_target="tpu_custom_call" | custom-call | flops 905969664 | bytes 1310720 | tf_op jit(solution)/shard_map/pallas_call | solution.py:286
  48.5 0.9 %collective-permute-start.21 = (f32[200,256]{1,0:T(8,128)S(1)}, f32[200,256]{1,0:T(8,128)S(1)}, u32[]{:S(2)}, u32[]{:S(2)}) collective-permute-start(f32[200,256]{1,0:T(8,128)S(1)} %collective-permute-done.15.near3), channel_id=1, source_target_pairs={{0,1},{1,0},{2,3},{3,2},{4,5},{5,4},{6,7},{7,6},{8,9},{9,8},{10,11... | collective-permute-start | bytes 614408 | tf_op jit(solution)/shard_map/ppermute | solution.py:21
  49.3 1.6 %collective-permute-done.20.near2 = f32[200,256]{1,0:T(8,128)S(1)} collective-permute-done((f32[200,256]{1,0:T(8,128)S(1)}, f32[200,256]{1,0:T(8,128)S(1)}, u32[]{:S(2)}, u32[]{:S(2)}) %collective-permute-start.20) | collective-permute-done | bytes 204832 | tf_op jit(solution)/shard_map/ppermute | solution.py:29
  50.9 0.8 %collective-permute-start.22 = (f32[200,256]{1,0:T(8,128)S(1)}, f32[200,256]{1,0:T(8,128)S(1)}, u32[]{:S(2)}, u32[]{:S(2)}) collective-permute-start(f32[200,256]{1,0:T(8,128)S(1)} %collective-permute-done.20.near2), channel_id=1, source_target_pairs={{0,1},{1,0},{2,3},{3,2},{4,5},{5,4},{6,7},{7,6},{8,9},{9,8},{10,11... | collective-permute-start | bytes 614408 | tf_op jit(solution)/shard_map/ppermute | solution.py:21
  51.7 1.1 %collective-permute-done.22.far2 = f32[200,256]{1,0:T(8,128)S(1)} collective-permute-done((f32[200,256]{1,0:T(8,128)S(1)}, f32[200,256]{1,0:T(8,128)S(1)}, u32[]{:S(2)}, u32[]{:S(2)}) %collective-permute-start.22) | collective-permute-done | bytes 204832 | tf_op jit(solution)/shard_map/ppermute | solution.py:21
  52.8 1.4 %shard_map.69 = (f32[1,256,256]{2,1,0:T(8,128)}, f32[1,256,256]{2,1,0:T(8,128)}, f32[1,256,256]{2,1,0:T(8,128)}) custom-call(f32[3,256,256]{2,1,0:T(8,128)S(1)} %get-tuple-element.62.half_ref, f32[200,256]{1,0:T(8,128)S(1)} %collective-permute-done.20.near2, ...), custom_call_target="tpu_custom_call", output_to_operand_aliasing={{0}: (5, {}), {1}: (6, {}), {2}: (7, {})} | custom-call | flops 301989888 | bytes 1310720 | tf_op jit(solution)/shard_map/pallas_call | solution.py:286
  (27 shorter events, 5.3 us)
Async XLA Ops:
  0.6 2.4 %collective-permute-start = (f32[1,256,256]{2,1,0:T(8,128)}, f32[1,256,256]{2,1,0:T(8,128)S(1)}, u32[]{:S(2)}, u32[]{:S(2)}) collective-permute-start(f32[1,256,256]{2,1,0:T(8,128)} %param.3), channel_id=1, source_target_pairs={{0,1},{1,0},{2,3},{3,2},{4,5},{5,4},{6,7},{7,6},{8,9},{9,8},{10,11... | collective-permute-start | bytes 786440 | tf_op jit(solution)/shard_map/ppermute | solution.py:21
  1.4 1.7 %collective-permute-start.1 = (f32[1,256,256]{2,1,0:T(8,128)}, f32[1,256,256]{2,1,0:T(8,128)S(1)}, u32[]{:S(2)}, u32[]{:S(2)}) collective-permute-start(f32[1,256,256]{2,1,0:T(8,128)} %param.4), channel_id=1, source_target_pairs={{0,1},{1,0},{2,3},{3,2},{4,5},{5,4},{6,7},{7,6},{8,9},{9,8},{10,11... | collective-permute-start | bytes 786440 | tf_op jit(solution)/shard_map/ppermute | solution.py:21
  1.4 2.0 %collective-permute-start.2 = (f32[1,256,256]{2,1,0:T(8,128)}, f32[1,256,256]{2,1,0:T(8,128)S(1)}, u32[]{:S(2)}, u32[]{:S(2)}) collective-permute-start(f32[1,256,256]{2,1,0:T(8,128)} %param.5), channel_id=1, source_target_pairs={{0,1},{1,0},{2,3},{3,2},{4,5},{5,4},{6,7},{7,6},{8,9},{9,8},{10,11... | collective-permute-start | bytes 786440 | tf_op jit(solution)/shard_map/ppermute | solution.py:21
  6.1 3.3 %collective-permute-start.4 = (f32[72,256]{1,0:T(8,128)S(1)}, f32[72,256]{1,0:T(8,128)S(1)}, u32[]{:S(2)}, u32[]{:S(2)}) collective-permute-start(f32[72,256]{1,0:T(8,128)S(1)} %get-tuple-element.38), channel_id=1, source_target_pairs={{0,2},{1,3},{2,0},{3,1},{4,6},{5,7},{6,4},{7,5},{8,10},{9,11},{10,... | collective-permute-start | bytes 221192 | tf_op jit(solution)/shard_map/ppermute | solution.py:21
  7.4 7.0 %collective-permute-start.3 = (f32[192,256]{1,0:T(8,128)S(1)}, f32[192,256]{1,0:T(8,128)S(1)}, u32[]{:S(2)}, u32[]{:S(2)}) collective-permute-start(f32[192,256]{1,0:T(8,128)S(1)} %get-tuple-element.36), channel_id=1, source_target_pairs={{0,2},{1,3},{2,0},{3,1},{4,6},{5,7},{6,4},{7,5},{8,10},{9,11},{10,... | collective-permute-start | bytes 589832 | tf_op jit(solution)/shard_map/ppermute | solution.py:21
  9.4 2.9 %collective-permute-start.5 = (f32[72,256]{1,0:T(8,128)S(1)}, f32[72,256]{1,0:T(8,128)S(1)}, u32[]{:S(2)}, u32[]{:S(2)}) collective-permute-start(f32[72,256]{1,0:T(8,128)S(1)} %collective-permute-done.4.near_ref.near1), channel_id=1, source_target_pairs={{0,1},{1,0},{2,3},{3,2},{4,5},{5,4},{6,7},{7,6},{8,9},{9,8},{10,11... | collective-permute-start | bytes 221192 | tf_op jit(solution)/shard_map/ppermute | solution.py:21
  14.4 1.8 %collective-permute-start.6 = (f32[192,256]{1,0:T(8,128)S(1)}, f32[192,256]{1,0:T(8,128)S(1)}, u32[]{:S(2)}, u32[]{:S(2)}) collective-permute-start(f32[192,256]{1,0:T(8,128)S(1)} %collective-permute-done.3.near_ref.near2), channel_id=1, source_target_pairs={{0,1},{1,0},{2,3},{3,2},{4,5},{5,4},{6,7},{7,6},{8,9},{9,8},{10,11... | collective-permute-start | bytes 589832 | tf_op jit(solution)/shard_map/ppermute | solution.py:21
  16.9 4.1 %collective-permute-start.8 = (f32[72,256]{1,0:T(8,128)S(1)}, f32[72,256]{1,0:T(8,128)S(1)}, u32[]{:S(2)}, u32[]{:S(2)}) collective-permute-start(f32[72,256]{1,0:T(8,128)S(1)} %get-tuple-element.43), channel_id=1, source_target_pairs={{0,4},{1,5},{2,6},{3,7},{4,0},{5,1},{6,2},{7,3},{8,12},{9,13},{10,... | collective-permute-start | bytes 221192 | tf_op jit(solution)/shard_map/ppermute | solution.py:21
  18.2 7.0 %collective-permute-start.7 = (f32[192,256]{1,0:T(8,128)S(1)}, f32[192,256]{1,0:T(8,128)S(1)}, u32[]{:S(2)}, u32[]{:S(2)}) collective-permute-start(f32[192,256]{1,0:T(8,128)S(1)} %get-tuple-element.41), channel_id=1, source_target_pairs={{0,4},{1,5},{2,6},{3,7},{4,0},{5,1},{6,2},{7,3},{8,12},{9,13},{10,... | collective-permute-start | bytes 589832 | tf_op jit(solution)/shard_map/ppermute | solution.py:21
  21.0 2.0 %collective-permute-start.9 = (f32[72,256]{1,0:T(8,128)S(1)}, f32[72,256]{1,0:T(8,128)S(1)}, u32[]{:S(2)}, u32[]{:S(2)}) collective-permute-start(f32[72,256]{1,0:T(8,128)S(1)} %collective-permute-done.8.near_ref.near1), channel_id=1, source_target_pairs={{0,1},{1,0},{2,3},{3,2},{4,5},{5,4},{6,7},{7,6},{8,9},{9,8},{10,11... | collective-permute-start | bytes 221192 | tf_op jit(solution)/shard_map/ppermute | solution.py:21
  25.2 1.8 %collective-permute-start.10 = (f32[192,256]{1,0:T(8,128)S(1)}, f32[192,256]{1,0:T(8,128)S(1)}, u32[]{:S(2)}, u32[]{:S(2)}) collective-permute-start(f32[192,256]{1,0:T(8,128)S(1)} %collective-permute-done.7.near_ref.near2), channel_id=1, source_target_pairs={{0,1},{1,0},{2,3},{3,2},{4,5},{5,4},{6,7},{7,6},{8,9},{9,8},{10,11... | collective-permute-start | bytes 589832 | tf_op jit(solution)/shard_map/ppermute | solution.py:21
  27.7 4.1 %collective-permute-start.12 = (f32[72,256]{1,0:T(8,128)S(1)}, f32[72,256]{1,0:T(8,128)S(1)}, u32[]{:S(2)}, u32[]{:S(2)}) collective-permute-start(f32[72,256]{1,0:T(8,128)S(1)} %get-tuple-element.50), channel_id=1, source_target_pairs={{0,8},{1,9},{2,10},{3,11},{4,12},{5,13},{6,14},{7,15},{8,0},{9,1},... | collective-permute-start | bytes 221192 | tf_op jit(solution)/shard_map/ppermute | solution.py:21
  29.0 6.4 %collective-permute-start.11 = (f32[192,256]{1,0:T(8,128)S(1)}, f32[192,256]{1,0:T(8,128)S(1)}, u32[]{:S(2)}, u32[]{:S(2)}) collective-permute-start(f32[192,256]{1,0:T(8,128)S(1)} %get-tuple-element.48), channel_id=1, source_target_pairs={{0,8},{1,9},{2,10},{3,11},{4,12},{5,13},{6,14},{7,15},{8,0},{9,1},... | collective-permute-start | bytes 589832 | tf_op jit(solution)/shard_map/ppermute | solution.py:21
  31.8 2.0 %collective-permute-start.13 = (f32[72,256]{1,0:T(8,128)S(1)}, f32[72,256]{1,0:T(8,128)S(1)}, u32[]{:S(2)}, u32[]{:S(2)}) collective-permute-start(f32[72,256]{1,0:T(8,128)S(1)} %collective-permute-done.12.near_ref.near1), channel_id=1, source_target_pairs={{0,1},{1,0},{2,3},{3,2},{4,5},{5,4},{6,7},{7,6},{8,9},{9,8},{10,11... | collective-permute-start | bytes 221192 | tf_op jit(solution)/shard_map/ppermute | solution.py:21
  35.5 2.3 %collective-permute-start.14 = (f32[192,256]{1,0:T(8,128)S(1)}, f32[192,256]{1,0:T(8,128)S(1)}, u32[]{:S(2)}, u32[]{:S(2)}) collective-permute-start(f32[192,256]{1,0:T(8,128)S(1)} %collective-permute-done.11.near_ref.near2), channel_id=1, source_target_pairs={{0,1},{1,0},{2,3},{3,2},{4,5},{5,4},{6,7},{7,6},{8,9},{9,8},{10,11... | collective-permute-start | bytes 589832 | tf_op jit(solution)/shard_map/ppermute | solution.py:21
  36.7 3.9 %collective-permute-start.17 = (f32[72,256]{1,0:T(8,128)S(1)}, f32[72,256]{1,0:T(8,128)S(1)}, u32[]{:S(2)}, u32[]{:S(2)}) collective-permute-start(f32[72,256]{1,0:T(8,128)S(1)} %get-tuple-element.56), channel_id=1, source_target_pairs={{0,1},{1,0},{2,3},{3,2},{4,5},{5,4},{6,7},{7,6},{8,16},{9,17},{10,... | collective-permute-start | bytes 221192 | tf_op jit(solution)/shard_map/ppermute | solution.py:29
  36.8 3.8 %collective-permute-start.16 = (f32[72,256]{1,0:T(8,128)S(1)}, f32[72,256]{1,0:T(8,128)S(1)}, u32[]{:S(2)}, u32[]{:S(2)}) collective-permute-start(f32[72,256]{1,0:T(8,128)S(1)} %get-tuple-element.56), channel_id=1, source_target_pairs={{0,1},{1,0},{2,3},{3,2},{4,5},{5,4},{6,7},{7,6},{8,24},{9,25},{10,... | collective-permute-start | bytes 221192 | tf_op jit(solution)/shard_map/ppermute | solution.py:29
  37.8 10.7 %collective-permute-start.15 = (f32[200,256]{1,0:T(8,128)S(1)}, f32[200,256]{1,0:T(8,128)S(1)}, u32[]{:S(2)}, u32[]{:S(2)}) collective-permute-start(f32[200,256]{1,0:T(8,128)S(1)} %shard_map.66), channel_id=1, source_target_pairs={{0,1},{1,0},{2,3},{3,2},{4,5},{5,4},{6,7},{7,6},{8,24},{9,25},{10,... | collective-permute-start | bytes 614408 | tf_op jit(solution)/shard_map/ppermute | solution.py:29
  40.6 5.7 %collective-permute-start.18 = (f32[72,256]{1,0:T(8,128)S(1)}, f32[72,256]{1,0:T(8,128)S(1)}, u32[]{:S(2)}, u32[]{:S(2)}) collective-permute-start(f32[72,256]{1,0:T(8,128)S(1)} %collective-permute-done.17.near2), channel_id=1, source_target_pairs={{0,1},{1,0},{2,3},{3,2},{4,5},{5,4},{6,7},{7,6},{8,9},{9,8},{10,11... | collective-permute-start | bytes 221192 | tf_op jit(solution)/shard_map/ppermute | solution.py:21
  41.8 4.6 %collective-permute-start.19 = (f32[72,256]{1,0:T(8,128)S(1)}, f32[72,256]{1,0:T(8,128)S(1)}, u32[]{:S(2)}, u32[]{:S(2)}) collective-permute-start(f32[72,256]{1,0:T(8,128)S(1)} %collective-permute-done.16.near3), channel_id=1, source_target_pairs={{0,1},{1,0},{2,3},{3,2},{4,5},{5,4},{6,7},{7,6},{8,9},{9,8},{10,11... | collective-permute-start | bytes 221192 | tf_op jit(solution)/shard_map/ppermute | solution.py:21
  41.8 9.2 %collective-permute-start.20 = (f32[200,256]{1,0:T(8,128)S(1)}, f32[200,256]{1,0:T(8,128)S(1)}, u32[]{:S(2)}, u32[]{:S(2)}) collective-permute-start(f32[200,256]{1,0:T(8,128)S(1)} %shard_map.66), channel_id=1, source_target_pairs={{0,1},{1,0},{2,3},{3,2},{4,5},{5,4},{6,7},{7,6},{8,16},{9,17},{10,... | collective-permute-start | bytes 614408 | tf_op jit(solution)/shard_map/ppermute | solution.py:29
  48.5 2.5 %collective-permute-start.21 = (f32[200,256]{1,0:T(8,128)S(1)}, f32[200,256]{1,0:T(8,128)S(1)}, u32[]{:S(2)}, u32[]{:S(2)}) collective-permute-start(f32[200,256]{1,0:T(8,128)S(1)} %collective-permute-done.15.near3), channel_id=1, source_target_pairs={{0,1},{1,0},{2,3},{3,2},{4,5},{5,4},{6,7},{7,6},{8,9},{9,8},{10,11... | collective-permute-start | bytes 614408 | tf_op jit(solution)/shard_map/ppermute | solution.py:21
  50.9 1.9 %collective-permute-start.22 = (f32[200,256]{1,0:T(8,128)S(1)}, f32[200,256]{1,0:T(8,128)S(1)}, u32[]{:S(2)}, u32[]{:S(2)}) collective-permute-start(f32[200,256]{1,0:T(8,128)S(1)} %collective-permute-done.20.near2), channel_id=1, source_target_pairs={{0,1},{1,0},{2,3},{3,2},{4,5},{5,4},{6,7},{7,6},{8,9},{9,8},{10,11... | collective-permute-start | bytes 614408 | tf_op jit(solution)/shard_map/ppermute | solution.py:21

commit v11 on v10

--- a/solution.py
+++ b/solution.py
@@ -34,14 +34,17 @@
     return high, (x - high.astype(F32)).astype(BF16)
 
 
+def dot(a, b, dims=NN):
+    return lax.dot_general(a, b, dims, preferred_element_type=F32)
+
+
 def dot1(a, b, dims=NN):
     h = a.shape[0] // 2
-    parts = [lax.dot_general(x, b, dims, preferred_element_type=F32) for x in (a[:h], a[h:])]
-    return jnp.concatenate(parts, 0)
-
-
-def dot3(a, b, dims=NN):
-    return dot1(a[0], b[0], dims) + (dot1(a[0], b[1], dims) + dot1(a[1], b[0], dims))
+    return jnp.concatenate([dot(a[:h], b, dims), dot(a[h:], b, dims)], 0)
+
+
+def dot3(a, b, dims=NN, one=dot1):
+    return one(a[0], b[0], dims) + (one(a[0], b[1], dims) + one(a[1], b[0], dims))
 
 
 def half(x):
@@ -49,11 +52,13 @@
 
 
 def four_steps(power):
-    rest, power = power, half(power)
-    for _ in range(NS_STEPS - 1):
-        squared = dot1(power, power)
-        power = half(squared)
-        rest = rest + squared + dot1(half(rest), power)
+    rest, high = power, half(power)
+    squared = dot1(high, high)
+    for step in range(1, NS_STEPS):
+        high = half(squared)
+        following = dot1(high, high) if step < NS_STEPS - 1 else None
+        rest = rest + squared + dot1(half(rest), high)
+        squared = following
     return half(rest)
 
 
@@ -61,16 +66,16 @@
     near, away, out = own
     f, o, s = split(facing), split(near), split(out)
     rough = dot1(f[0], o[0])
+    coupling = rough + (dot1(f[0], o[1]) + dot1(f[1], o[0]))
+    inner = split(dot3(f, s, NT, dot))
     rest = four_steps(rough)
-    coupling = rough + (dot1(f[0], o[1]) + dot1(f[1], o[0]))
-    inner = split(dot3(f, s, NT))
     high, low = split(coupling)
     error = half((coupling - rest.astype(F32)) + (dot1(high, rest) + dot1(low, rest)))
     leading = out + (dot1(s[0], rest) + dot1(s[1], rest))
     mirror = near + (dot1(o[0], rest) + dot1(o[1], rest))
     leading = leading + dot1(half(leading), error)
     mirror = mirror + dot1(half(mirror), error)
-    return leading, mirror, away + dot3(split(leading), inner)
+    return leading, mirror, away + dot3(split(leading), inner, NN, dot)
 
 
 def after_trans(leading, mirror, away, into):

time: 54.6 us -> 54.3 us (level)
  Pallas kernels: 19.5 us -> 18.1 us
  starting transfers between devices: 18.5 us -> 19.4 us
    pallas_call x12, Pallas kernels: 19.5 us -> 18.1 us  [call(): pl.pallas_call(kernel, out_shape=[jax.ShapeDtypeStruct(s, F32) for s in o...]
    ppermute x19, starting transfers between devices: 15.5 us -> 16.4 us  [swap(): return lax.ppermute(block, AXES, [(i, i ^ distance) for i in range(count)])]
  transfers between devices with their start and end apart: 23 -> 23, of which waited for: 13 -> 13; matrix products, arithmetic and copies ran while one was open for 2% -> 2% of each run, Pallas kernels for 26% -> 24%
where the time goes in v11:
time: 54.3 us; the launch traced here: 54.2 us
  starting transfers between devices  19.4 us (36%)
  Pallas kernels  18.1 us (33%)
  waiting for transfers between devices  14.6 us (27%)
  other arithmetic  1.16 us (2%)
  between operations  0.96 us (2%)
    pallas_call x12, Pallas kernels, call(): pl.pallas_call(kernel, out_shape=[jax.ShapeDtypeStruct(s, F32) for s in o...  18.1 us
    ppermute x19, starting transfers between devices, swap(): return lax.ppermute(block, AXES, [(i, i ^ distance) for i in range(count)])  16.4 us
    ppermute x19, waiting for transfers between devices, swap(): return lax.ppermute(block, AXES, [(i, i ^ distance) for i in range(count)])  10.1 us
    ppermute x4, waiting for transfers between devices, pair(): lax.ppermute(block, AXES, [(i, step.get(i // quarter, lambda i: i ^ 1)(i)...  4.44 us
    ppermute x4, starting transfers between devices, pair(): lax.ppermute(block, AXES, [(i, step.get(i // quarter, lambda i: i ^ 1)(i)...  2.98 us
    concatenate x1, other arithmetic, shards(): section = jnp.concatenate(sections, 0)  1.16 us
  transfers between devices with their start and end apart: 23, of which 13 were waited for; matrix products, arithmetic and copies ran while one was open for 2% of the time, Pallas kernels for 24%

profile of v11, /device:TPU:17, one launch (start us, length us, event | category | flops | bytes accessed | tf_op | source)
XLA Modules:
  0.0 54.2 jit_solution(7914386473479963334)
XLA Ops:
  1.9 1.2 %pad_maximum_fusion.section_ref = f32[3,256,256]{2,1,0:T(8,128)S(1)} fusion(f32[1,256,256]{2,1,0:T(8,128)} %param.5, f32[1,256,256]{2,1,0:T(8,128)} %param.4, f32[1,256,256]{2,1,0:T(8,128)} %param.3), kind=kLoop, calls=%fused_computation | loop fusion | flops 393216 | bytes 1572864 | tf_op jit(solution)/shard_map/concatenate | solution.py:310
  3.5 2.4 %shard_map.58 = (f32[3,256,256]{2,1,0:T(8,128)S(1)}, f32[72,256]{1,0:T(8,128)S(1)}, f32[192,256]{1,0:T(8,128)S(1)}, f32[3,256,256]{2,1,0:T(8,128)S(1)}) custom-call(f32[3,256,256]{2,1,0:T(8,128)S(1)} %pad_maximum_fusion.section_ref, f32[1,256,256]{2,1,0:T(8,128)S(1)} %collective-permute-done.got1, f32[1,256,256]{2,1,0:T(8,128)S(1)} %collective-permute-done.1.got2, ...), custom_call_target="tpu_custom_call" | custom-call | flops 1207959552 | bytes 1048576 | tf_op jit(solution)/shard_map/pallas_call | solution.py:291
  5.9 1.3 %collective-permute-start.4 = (f32[72,256]{1,0:T(8,128)S(1)}, f32[72,256]{1,0:T(8,128)S(1)}, u32[]{:S(2)}, u32[]{:S(2)}) collective-permute-start(f32[72,256]{1,0:T(8,128)S(1)} %get-tuple-element.38), channel_id=1, source_target_pairs={{0,2},{1,3},{2,0},{3,1},{4,6},{5,7},{6,4},{7,5},{8,10},{9,11},{10,... | collective-permute-start | bytes 221192 | tf_op jit(solution)/shard_map/ppermute | solution.py:21
  7.4 1.7 %collective-permute-done.4.near_ref.near1 = f32[72,256]{1,0:T(8,128)S(1)} collective-permute-done((f32[72,256]{1,0:T(8,128)S(1)}, f32[72,256]{1,0:T(8,128)S(1)}, u32[]{:S(2)}, u32[]{:S(2)}) %collective-permute-start.4) | collective-permute-done | bytes 73760 | tf_op jit(solution)/shard_map/ppermute | solution.py:21
  9.2 2.0 %collective-permute-start.5 = (f32[72,256]{1,0:T(8,128)S(1)}, f32[72,256]{1,0:T(8,128)S(1)}, u32[]{:S(2)}, u32[]{:S(2)}) collective-permute-start(f32[72,256]{1,0:T(8,128)S(1)} %collective-permute-done.4.near_ref.near1), channel_id=1, source_target_pairs={{0,1},{1,0},{2,3},{3,2},{4,5},{5,4},{6,7},{7,6},{8,9},{9,8},{10,11... | collective-permute-start | bytes 221192 | tf_op jit(solution)/shard_map/ppermute | solution.py:21
  11.2 0.9 %collective-permute-done.5.far_ref.far1 = f32[72,256]{1,0:T(8,128)S(1)} collective-permute-done((f32[72,256]{1,0:T(8,128)S(1)}, f32[72,256]{1,0:T(8,128)S(1)}, u32[]{:S(2)}, u32[]{:S(2)}) %collective-permute-start.5) | collective-permute-done | bytes 73760 | tf_op jit(solution)/shard_map/ppermute | solution.py:21
  12.1 1.9 %shard_map.59.half_ref = f32[3,256,256]{2,1,0:T(8,128)S(1)} custom-call(f32[3,256,256]{2,1,0:T(8,128)S(1)} %get-tuple-element.37.own_ref, f32[72,256]{1,0:T(8,128)S(1)} %collective-permute-done.4.near_ref.near1, f32[72,256]{1,0:T(8,128)S(1)} %collective-permute-done.5.far_ref.far1), custom_call_target="tpu_custom_call" | custom-call | flops 905969664 | bytes 786432 | tf_op jit(solution)/shard_map/pallas_call | solution.py:291
  14.0 0.9 %collective-permute-start.6 = (f32[192,256]{1,0:T(8,128)S(1)}, f32[192,256]{1,0:T(8,128)S(1)}, u32[]{:S(2)}, u32[]{:S(2)}) collective-permute-start(f32[192,256]{1,0:T(8,128)S(1)} %collective-permute-done.3.near_ref.near2), channel_id=1, source_target_pairs={{0,1},{1,0},{2,3},{3,2},{4,5},{5,4},{6,7},{7,6},{8,9},{9,8},{10,11... | collective-permute-start | bytes 589832 | tf_op jit(solution)/shard_map/ppermute | solution.py:21
  14.9 1.1 %collective-permute-done.6.far_ref.far2 = f32[192,256]{1,0:T(8,128)S(1)} collective-permute-done((f32[192,256]{1,0:T(8,128)S(1)}, f32[192,256]{1,0:T(8,128)S(1)}, u32[]{:S(2)}, u32[]{:S(2)}) %collective-permute-start.6) | collective-permute-done | bytes 196640 | tf_op jit(solution)/shard_map/ppermute | solution.py:21
  16.7 1.3 %collective-permute-start.8 = (f32[72,256]{1,0:T(8,128)S(1)}, f32[72,256]{1,0:T(8,128)S(1)}, u32[]{:S(2)}, u32[]{:S(2)}) collective-permute-start(f32[72,256]{1,0:T(8,128)S(1)} %get-tuple-element.43), channel_id=1, source_target_pairs={{0,4},{1,5},{2,6},{3,7},{4,0},{5,1},{6,2},{7,3},{8,12},{9,13},{10,... | collective-permute-start | bytes 221192 | tf_op jit(solution)/shard_map/ppermute | solution.py:21
  18.2 2.4 %shard_map.61.old_ref = f32[3,256,256]{2,1,0:T(8,128)S(1)} custom-call(f32[3,256,256]{2,1,0:T(8,128)S(1)} %get-tuple-element.44.old_ref, f32[72,256]{1,0:T(8,128)S(1)} %collective-permute-done.4.near_ref.near1, f32[72,256]{1,0:T(8,128)S(1)} %collective-permute-done.5.far_ref.far1, f32[192,256]{1,0:T(8,128)S(1)} %collective-permute-done.3.near_ref.near2, ...), custom_call_target="tpu_custom_call" | custom-call | flops 1207959552 | bytes 1310720 | tf_op jit(solution)/shard_map/pallas_call | solution.py:291
  20.6 1.3 %collective-permute-start.9 = (f32[72,256]{1,0:T(8,128)S(1)}, f32[72,256]{1,0:T(8,128)S(1)}, u32[]{:S(2)}, u32[]{:S(2)}) collective-permute-start(f32[72,256]{1,0:T(8,128)S(1)} %collective-permute-done.8.near_ref.near1), channel_id=1, source_target_pairs={{0,1},{1,0},{2,3},{3,2},{4,5},{5,4},{6,7},{7,6},{8,9},{9,8},{10,11... | collective-permute-start | bytes 221192 | tf_op jit(solution)/shard_map/ppermute | solution.py:21
  21.9 0.9 %collective-permute-done.9.far_ref.far1 = f32[72,256]{1,0:T(8,128)S(1)} collective-permute-done((f32[72,256]{1,0:T(8,128)S(1)}, f32[72,256]{1,0:T(8,128)S(1)}, u32[]{:S(2)}, u32[]{:S(2)}) %collective-permute-start.9) | collective-permute-done | bytes 73760 | tf_op jit(solution)/shard_map/ppermute | solution.py:21
  22.9 1.9 %shard_map.62.half_ref = f32[3,256,256]{2,1,0:T(8,128)S(1)} custom-call(f32[3,256,256]{2,1,0:T(8,128)S(1)} %get-tuple-element.42.own_ref, f32[72,256]{1,0:T(8,128)S(1)} %collective-permute-done.8.near_ref.near1, f32[72,256]{1,0:T(8,128)S(1)} %collective-permute-done.9.far_ref.far1), custom_call_target="tpu_custom_call" | custom-call | flops 905969664 | bytes 786432 | tf_op jit(solution)/shard_map/pallas_call | solution.py:291
  24.7 0.9 %collective-permute-start.10 = (f32[192,256]{1,0:T(8,128)S(1)}, f32[192,256]{1,0:T(8,128)S(1)}, u32[]{:S(2)}, u32[]{:S(2)}) collective-permute-start(f32[192,256]{1,0:T(8,128)S(1)} %collective-permute-done.7.near_ref.near2), channel_id=1, source_target_pairs={{0,1},{1,0},{2,3},{3,2},{4,5},{5,4},{6,7},{7,6},{8,9},{9,8},{10,11... | collective-permute-start | bytes 589832 | tf_op jit(solution)/shard_map/ppermute | solution.py:21
  25.7 1.1 %collective-permute-done.10.far_ref.far2 = f32[192,256]{1,0:T(8,128)S(1)} collective-permute-done((f32[192,256]{1,0:T(8,128)S(1)}, f32[192,256]{1,0:T(8,128)S(1)}, u32[]{:S(2)}, u32[]{:S(2)}) %collective-permute-start.10) | collective-permute-done | bytes 196640 | tf_op jit(solution)/shard_map/ppermute | solution.py:21
  27.5 1.4 %collective-permute-start.12 = (f32[72,256]{1,0:T(8,128)S(1)}, f32[72,256]{1,0:T(8,128)S(1)}, u32[]{:S(2)}, u32[]{:S(2)}) collective-permute-start(f32[72,256]{1,0:T(8,128)S(1)} %get-tuple-element.50), channel_id=1, source_target_pairs={{0,8},{1,9},{2,10},{3,11},{4,12},{5,13},{6,14},{7,15},{8,0},{9,1},... | collective-permute-start | bytes 221192 | tf_op jit(solution)/shard_map/ppermute | solution.py:21
  29.0 2.3 %shard_map.64.old_ref = f32[3,256,256]{2,1,0:T(8,128)S(1)} custom-call(f32[3,256,256]{2,1,0:T(8,128)S(1)} %shard_map.61.old_ref, f32[72,256]{1,0:T(8,128)S(1)} %collective-permute-done.8.near_ref.near1, f32[72,256]{1,0:T(8,128)S(1)} %collective-permute-done.9.far_ref.far1, f32[192,256]{1,0:T(8,128)S(1)} %collective-permute-done.7.near_ref.near2, ...), custom_call_target="tpu_custom_call" | custom-call | flops 1207959552 | bytes 1310720 | tf_op jit(solution)/shard_map/pallas_call | solution.py:291
  31.4 1.3 %collective-permute-start.13 = (f32[72,256]{1,0:T(8,128)S(1)}, f32[72,256]{1,0:T(8,128)S(1)}, u32[]{:S(2)}, u32[]{:S(2)}) collective-permute-start(f32[72,256]{1,0:T(8,128)S(1)} %collective-permute-done.12.near_ref.near1), channel_id=1, source_target_pairs={{0,1},{1,0},{2,3},{3,2},{4,5},{5,4},{6,7},{7,6},{8,9},{9,8},{10,11... | collective-permute-start | bytes 221192 | tf_op jit(solution)/shard_map/ppermute | solution.py:21
  32.7 0.9 %collective-permute-done.13.far_ref.far1 = f32[72,256]{1,0:T(8,128)S(1)} collective-permute-done((f32[72,256]{1,0:T(8,128)S(1)}, f32[72,256]{1,0:T(8,128)S(1)}, u32[]{:S(2)}, u32[]{:S(2)}) %collective-permute-start.13) | collective-permute-done | bytes 73760 | tf_op jit(solution)/shard_map/ppermute | solution.py:21
  33.8 1.5 %collective-permute-done.11.near_ref.near2 = f32[192,256]{1,0:T(8,128)S(1)} collective-permute-done((f32[192,256]{1,0:T(8,128)S(1)}, f32[192,256]{1,0:T(8,128)S(1)}, u32[]{:S(2)}, u32[]{:S(2)}) %collective-permute-start.11) | collective-permute-done | bytes 196640 | tf_op jit(solution)/shard_map/ppermute | solution.py:21
  35.3 1.2 %collective-permute-start.14 = (f32[192,256]{1,0:T(8,128)S(1)}, f32[192,256]{1,0:T(8,128)S(1)}, u32[]{:S(2)}, u32[]{:S(2)}) collective-permute-start(f32[192,256]{1,0:T(8,128)S(1)} %collective-permute-done.11.near_ref.near2), channel_id=1, source_target_pairs={{0,1},{1,0},{2,3},{3,2},{4,5},{5,4},{6,7},{7,6},{8,9},{9,8},{10,11... | collective-permute-start | bytes 589832 | tf_op jit(solution)/shard_map/ppermute | solution.py:21
  38.0 2.4 %collective-permute-done.17.near2 = f32[72,256]{1,0:T(8,128)S(1)} collective-permute-done((f32[72,256]{1,0:T(8,128)S(1)}, f32[72,256]{1,0:T(8,128)S(1)}, u32[]{:S(2)}, u32[]{:S(2)}) %collective-permute-start.17) | collective-permute-done | bytes 73760 | tf_op jit(solution)/shard_map/ppermute | solution.py:29
  40.4 1.2 %collective-permute-start.18 = (f32[72,256]{1,0:T(8,128)S(1)}, f32[72,256]{1,0:T(8,128)S(1)}, u32[]{:S(2)}, u32[]{:S(2)}) collective-permute-start(f32[72,256]{1,0:T(8,128)S(1)} %collective-permute-done.17.near2), channel_id=1, source_target_pairs={{0,1},{1,0},{2,3},{3,2},{4,5},{5,4},{6,7},{7,6},{8,9},{9,8},{10,11... | collective-permute-start | bytes 221192 | tf_op jit(solution)/shard_map/ppermute | solution.py:21
  41.6 2.0 %collective-permute-start.20 = (f32[200,256]{1,0:T(8,128)S(1)}, f32[200,256]{1,0:T(8,128)S(1)}, u32[]{:S(2)}, u32[]{:S(2)}) collective-permute-start(f32[200,256]{1,0:T(8,128)S(1)} %shard_map.66), channel_id=1, source_target_pairs={{0,1},{1,0},{2,3},{3,2},{4,5},{5,4},{6,7},{7,6},{8,16},{9,17},{10,... | collective-permute-start | bytes 614408 | tf_op jit(solution)/shard_map/ppermute | solution.py:29
  43.5 2.4 %shard_map.67.old_ref = f32[3,256,256]{2,1,0:T(8,128)S(1)} custom-call(f32[3,256,256]{2,1,0:T(8,128)S(1)} %shard_map.64.old_ref, f32[72,256]{1,0:T(8,128)S(1)} %collective-permute-done.12.near_ref.near1, f32[72,256]{1,0:T(8,128)S(1)} %collective-permute-done.13.far_ref.far1, f32[192,256]{1,0:T(8,128)S(1)} %collective-permute-done.11.near_ref.near2, ...), custom_call_target="tpu_custom_call" | custom-call | flops 1207959552 | bytes 1310720 | tf_op jit(solution)/shard_map/pallas_call | solution.py:291
  45.9 1.9 %shard_map.68 = (f32[3,256,256]{2,1,0:T(8,128)S(1)}, f32[1,256,256]{2,1,0:T(8,128)}, f32[1,256,256]{2,1,0:T(8,128)}, f32[1,256,256]{2,1,0:T(8,128)}) custom-call(f32[3,256,256]{2,1,0:T(8,128)S(1)} %shard_map.67.old_ref, f32[72,256]{1,0:T(8,128)S(1)} %collective-permute-done.17.near2, f32[72,256]{1,0:T(8,128)S(1)} %collective-permute-done.18.far2, ...), custom_call_target="tpu_custom_call" | custom-call | flops 905969664 | bytes 1310720 | tf_op jit(solution)/shard_map/pallas_call | solution.py:291
  47.8 0.8 %collective-permute-start.21 = (f32[200,256]{1,0:T(8,128)S(1)}, f32[200,256]{1,0:T(8,128)S(1)}, u32[]{:S(2)}, u32[]{:S(2)}) collective-permute-start(f32[200,256]{1,0:T(8,128)S(1)} %collective-permute-done.15.near3), channel_id=1, source_target_pairs={{0,1},{1,0},{2,3},{3,2},{4,5},{5,4},{6,7},{7,6},{8,9},{9,8},{10,11... | collective-permute-start | bytes 614408 | tf_op jit(solution)/shard_map/ppermute | solution.py:21
  48.7 2.1 %collective-permute-done.20.near2 = f32[200,256]{1,0:T(8,128)S(1)} collective-permute-done((f32[200,256]{1,0:T(8,128)S(1)}, f32[200,256]{1,0:T(8,128)S(1)}, u32[]{:S(2)}, u32[]{:S(2)}) %collective-permute-start.20) | collective-permute-done | bytes 204832 | tf_op jit(solution)/shard_map/ppermute | solution.py:29
  50.7 0.8 %collective-permute-start.22 = (f32[200,256]{1,0:T(8,128)S(1)}, f32[200,256]{1,0:T(8,128)S(1)}, u32[]{:S(2)}, u32[]{:S(2)}) collective-permute-start(f32[200,256]{1,0:T(8,128)S(1)} %collective-permute-done.20.near2), channel_id=1, source_target_pairs={{0,1},{1,0},{2,3},{3,2},{4,5},{5,4},{6,7},{7,6},{8,9},{9,8},{10,11... | collective-permute-start | bytes 614408 | tf_op jit(solution)/shard_map/ppermute | solution.py:21
  51.5 1.1 %collective-permute-done.22.far2 = f32[200,256]{1,0:T(8,128)S(1)} collective-permute-done((f32[200,256]{1,0:T(8,128)S(1)}, f32[200,256]{1,0:T(8,128)S(1)}, u32[]{:S(2)}, u32[]{:S(2)}) %collective-permute-start.22) | collective-permute-done | bytes 204832 | tf_op jit(solution)/shard_map/ppermute | solution.py:21
  52.6 1.4 %shard_map.69 = (f32[1,256,256]{2,1,0:T(8,128)}, f32[1,256,256]{2,1,0:T(8,128)}, f32[1,256,256]{2,1,0:T(8,128)}) custom-call(f32[3,256,256]{2,1,0:T(8,128)S(1)} %get-tuple-element.62.half_ref, f32[200,256]{1,0:T(8,128)S(1)} %collective-permute-done.20.near2, ...), custom_call_target="tpu_custom_call", output_to_operand_aliasing={{0}: (5, {}), {1}: (6, {}), {2}: (7, {})} | custom-call | flops 301989888 | bytes 1310720 | tf_op jit(solution)/shard_map/pallas_call | solution.py:291
  (27 shorter events, 5.5 us)
Async XLA Ops:
  0.6 2.4 %collective-permute-start = (f32[1,256,256]{2,1,0:T(8,128)}, f32[1,256,256]{2,1,0:T(8,128)S(1)}, u32[]{:S(2)}, u32[]{:S(2)}) collective-permute-start(f32[1,256,256]{2,1,0:T(8,128)} %param.3), channel_id=1, source_target_pairs={{0,1},{1,0},{2,3},{3,2},{4,5},{5,4},{6,7},{7,6},{8,9},{9,8},{10,11... | collective-permute-start | bytes 786440 | tf_op jit(solution)/shard_map/ppermute | solution.py:21
  1.4 1.7 %collective-permute-start.1 = (f32[1,256,256]{2,1,0:T(8,128)}, f32[1,256,256]{2,1,0:T(8,128)S(1)}, u32[]{:S(2)}, u32[]{:S(2)}) collective-permute-start(f32[1,256,256]{2,1,0:T(8,128)} %param.4), channel_id=1, source_target_pairs={{0,1},{1,0},{2,3},{3,2},{4,5},{5,4},{6,7},{7,6},{8,9},{9,8},{10,11... | collective-permute-start | bytes 786440 | tf_op jit(solution)/shard_map/ppermute | solution.py:21
  1.4 2.0 %collective-permute-start.2 = (f32[1,256,256]{2,1,0:T(8,128)}, f32[1,256,256]{2,1,0:T(8,128)S(1)}, u32[]{:S(2)}, u32[]{:S(2)}) collective-permute-start(f32[1,256,256]{2,1,0:T(8,128)} %param.5), channel_id=1, source_target_pairs={{0,1},{1,0},{2,3},{3,2},{4,5},{5,4},{6,7},{7,6},{8,9},{9,8},{10,11... | collective-permute-start | bytes 786440 | tf_op jit(solution)/shard_map/ppermute | solution.py:21
  5.9 3.3 %collective-permute-start.4 = (f32[72,256]{1,0:T(8,128)S(1)}, f32[72,256]{1,0:T(8,128)S(1)}, u32[]{:S(2)}, u32[]{:S(2)}) collective-permute-start(f32[72,256]{1,0:T(8,128)S(1)} %get-tuple-element.38), channel_id=1, source_target_pairs={{0,2},{1,3},{2,0},{3,1},{4,6},{5,7},{6,4},{7,5},{8,10},{9,11},{10,... | collective-permute-start | bytes 221192 | tf_op jit(solution)/shard_map/ppermute | solution.py:21
  7.2 6.8 %collective-permute-start.3 = (f32[192,256]{1,0:T(8,128)S(1)}, f32[192,256]{1,0:T(8,128)S(1)}, u32[]{:S(2)}, u32[]{:S(2)}) collective-permute-start(f32[192,256]{1,0:T(8,128)S(1)} %get-tuple-element.36), channel_id=1, source_target_pairs={{0,2},{1,3},{2,0},{3,1},{4,6},{5,7},{6,4},{7,5},{8,10},{9,11},{10,... | collective-permute-start | bytes 589832 | tf_op jit(solution)/shard_map/ppermute | solution.py:21
  9.2 2.9 %collective-permute-start.5 = (f32[72,256]{1,0:T(8,128)S(1)}, f32[72,256]{1,0:T(8,128)S(1)}, u32[]{:S(2)}, u32[]{:S(2)}) collective-permute-start(f32[72,256]{1,0:T(8,128)S(1)} %collective-permute-done.4.near_ref.near1), channel_id=1, source_target_pairs={{0,1},{1,0},{2,3},{3,2},{4,5},{5,4},{6,7},{7,6},{8,9},{9,8},{10,11... | collective-permute-start | bytes 221192 | tf_op jit(solution)/shard_map/ppermute | solution.py:21
  14.0 2.0 %collective-permute-start.6 = (f32[192,256]{1,0:T(8,128)S(1)}, f32[192,256]{1,0:T(8,128)S(1)}, u32[]{:S(2)}, u32[]{:S(2)}) collective-permute-start(f32[192,256]{1,0:T(8,128)S(1)} %collective-permute-done.3.near_ref.near2), channel_id=1, source_target_pairs={{0,1},{1,0},{2,3},{3,2},{4,5},{5,4},{6,7},{7,6},{8,9},{9,8},{10,11... | collective-permute-start | bytes 589832 | tf_op jit(solution)/shard_map/ppermute | solution.py:21
  16.7 3.9 %collective-permute-start.8 = (f32[72,256]{1,0:T(8,128)S(1)}, f32[72,256]{1,0:T(8,128)S(1)}, u32[]{:S(2)}, u32[]{:S(2)}) collective-permute-start(f32[72,256]{1,0:T(8,128)S(1)} %get-tuple-element.43), channel_id=1, source_target_pairs={{0,4},{1,5},{2,6},{3,7},{4,0},{5,1},{6,2},{7,3},{8,12},{9,13},{10,... | collective-permute-start | bytes 221192 | tf_op jit(solution)/shard_map/ppermute | solution.py:21
  18.0 6.7 %collective-permute-start.7 = (f32[192,256]{1,0:T(8,128)S(1)}, f32[192,256]{1,0:T(8,128)S(1)}, u32[]{:S(2)}, u32[]{:S(2)}) collective-permute-start(f32[192,256]{1,0:T(8,128)S(1)} %get-tuple-element.41), channel_id=1, source_target_pairs={{0,4},{1,5},{2,6},{3,7},{4,0},{5,1},{6,2},{7,3},{8,12},{9,13},{10,... | collective-permute-start | bytes 589832 | tf_op jit(solution)/shard_map/ppermute | solution.py:21
  20.6 2.3 %collective-permute-start.9 = (f32[72,256]{1,0:T(8,128)S(1)}, f32[72,256]{1,0:T(8,128)S(1)}, u32[]{:S(2)}, u32[]{:S(2)}) collective-permute-start(f32[72,256]{1,0:T(8,128)S(1)} %collective-permute-done.8.near_ref.near1), channel_id=1, source_target_pairs={{0,1},{1,0},{2,3},{3,2},{4,5},{5,4},{6,7},{7,6},{8,9},{9,8},{10,11... | collective-permute-start | bytes 221192 | tf_op jit(solution)/shard_map/ppermute | solution.py:21
  24.7 2.0 %collective-permute-start.10 = (f32[192,256]{1,0:T(8,128)S(1)}, f32[192,256]{1,0:T(8,128)S(1)}, u32[]{:S(2)}, u32[]{:S(2)}) collective-permute-start(f32[192,256]{1,0:T(8,128)S(1)} %collective-permute-done.7.near_ref.near2), channel_id=1, source_target_pairs={{0,1},{1,0},{2,3},{3,2},{4,5},{5,4},{6,7},{7,6},{8,9},{9,8},{10,11... | collective-permute-start | bytes 589832 | tf_op jit(solution)/shard_map/ppermute | solution.py:21
  27.5 3.9 %collective-permute-start.12 = (f32[72,256]{1,0:T(8,128)S(1)}, f32[72,256]{1,0:T(8,128)S(1)}, u32[]{:S(2)}, u32[]{:S(2)}) collective-permute-start(f32[72,256]{1,0:T(8,128)S(1)} %get-tuple-element.50), channel_id=1, source_target_pairs={{0,8},{1,9},{2,10},{3,11},{4,12},{5,13},{6,14},{7,15},{8,0},{9,1},... | collective-permute-start | bytes 221192 | tf_op jit(solution)/shard_map/ppermute | solution.py:21
  28.8 6.5 %collective-permute-start.11 = (f32[192,256]{1,0:T(8,128)S(1)}, f32[192,256]{1,0:T(8,128)S(1)}, u32[]{:S(2)}, u32[]{:S(2)}) collective-permute-start(f32[192,256]{1,0:T(8,128)S(1)} %get-tuple-element.48), channel_id=1, source_target_pairs={{0,8},{1,9},{2,10},{3,11},{4,12},{5,13},{6,14},{7,15},{8,0},{9,1},... | collective-permute-start | bytes 589832 | tf_op jit(solution)/shard_map/ppermute | solution.py:21
  31.4 2.2 %collective-permute-start.13 = (f32[72,256]{1,0:T(8,128)S(1)}, f32[72,256]{1,0:T(8,128)S(1)}, u32[]{:S(2)}, u32[]{:S(2)}) collective-permute-start(f32[72,256]{1,0:T(8,128)S(1)} %collective-permute-done.12.near_ref.near1), channel_id=1, source_target_pairs={{0,1},{1,0},{2,3},{3,2},{4,5},{5,4},{6,7},{7,6},{8,9},{9,8},{10,11... | collective-permute-start | bytes 221192 | tf_op jit(solution)/shard_map/ppermute | solution.py:21
  35.3 2.3 %collective-permute-start.14 = (f32[192,256]{1,0:T(8,128)S(1)}, f32[192,256]{1,0:T(8,128)S(1)}, u32[]{:S(2)}, u32[]{:S(2)}) collective-permute-start(f32[192,256]{1,0:T(8,128)S(1)} %collective-permute-done.11.near_ref.near2), channel_id=1, source_target_pairs={{0,1},{1,0},{2,3},{3,2},{4,5},{5,4},{6,7},{7,6},{8,9},{9,8},{10,11... | collective-permute-start | bytes 589832 | tf_op jit(solution)/shard_map/ppermute | solution.py:21
  36.5 3.9 %collective-permute-start.17 = (f32[72,256]{1,0:T(8,128)S(1)}, f32[72,256]{1,0:T(8,128)S(1)}, u32[]{:S(2)}, u32[]{:S(2)}) collective-permute-start(f32[72,256]{1,0:T(8,128)S(1)} %get-tuple-element.56), channel_id=1, source_target_pairs={{0,1},{1,0},{2,3},{3,2},{4,5},{5,4},{6,7},{7,6},{8,16},{9,17},{10,... | collective-permute-start | bytes 221192 | tf_op jit(solution)/shard_map/ppermute | solution.py:29
  36.6 3.8 %collective-permute-start.16 = (f32[72,256]{1,0:T(8,128)S(1)}, f32[72,256]{1,0:T(8,128)S(1)}, u32[]{:S(2)}, u32[]{:S(2)}) collective-permute-start(f32[72,256]{1,0:T(8,128)S(1)} %get-tuple-element.56), channel_id=1, source_target_pairs={{0,1},{1,0},{2,3},{3,2},{4,5},{5,4},{6,7},{7,6},{8,24},{9,25},{10,... | collective-permute-start | bytes 221192 | tf_op jit(solution)/shard_map/ppermute | solution.py:29
  37.6 10.3 %collective-permute-start.15 = (f32[200,256]{1,0:T(8,128)S(1)}, f32[200,256]{1,0:T(8,128)S(1)}, u32[]{:S(2)}, u32[]{:S(2)}) collective-permute-start(f32[200,256]{1,0:T(8,128)S(1)} %shard_map.66), channel_id=1, source_target_pairs={{0,1},{1,0},{2,3},{3,2},{4,5},{5,4},{6,7},{7,6},{8,24},{9,25},{10,... | collective-permute-start | bytes 614408 | tf_op jit(solution)/shard_map/ppermute | solution.py:29
  40.4 5.5 %collective-permute-start.18 = (f32[72,256]{1,0:T(8,128)S(1)}, f32[72,256]{1,0:T(8,128)S(1)}, u32[]{:S(2)}, u32[]{:S(2)}) collective-permute-start(f32[72,256]{1,0:T(8,128)S(1)} %collective-permute-done.17.near2), channel_id=1, source_target_pairs={{0,1},{1,0},{2,3},{3,2},{4,5},{5,4},{6,7},{7,6},{8,9},{9,8},{10,11... | collective-permute-start | bytes 221192 | tf_op jit(solution)/shard_map/ppermute | solution.py:21
  41.6 4.4 %collective-permute-start.19 = (f32[72,256]{1,0:T(8,128)S(1)}, f32[72,256]{1,0:T(8,128)S(1)}, u32[]{:S(2)}, u32[]{:S(2)}) collective-permute-start(f32[72,256]{1,0:T(8,128)S(1)} %collective-permute-done.16.near3), channel_id=1, source_target_pairs={{0,1},{1,0},{2,3},{3,2},{4,5},{5,4},{6,7},{7,6},{8,9},{9,8},{10,11... | collective-permute-start | bytes 221192 | tf_op jit(solution)/shard_map/ppermute | solution.py:21
  41.6 9.2 %collective-permute-start.20 = (f32[200,256]{1,0:T(8,128)S(1)}, f32[200,256]{1,0:T(8,128)S(1)}, u32[]{:S(2)}, u32[]{:S(2)}) collective-permute-start(f32[200,256]{1,0:T(8,128)S(1)} %shard_map.66), channel_id=1, source_target_pairs={{0,1},{1,0},{2,3},{3,2},{4,5},{5,4},{6,7},{7,6},{8,16},{9,17},{10,... | collective-permute-start | bytes 614408 | tf_op jit(solution)/shard_map/ppermute | solution.py:29
  47.8 2.9 %collective-permute-start.21 = (f32[200,256]{1,0:T(8,128)S(1)}, f32[200,256]{1,0:T(8,128)S(1)}, u32[]{:S(2)}, u32[]{:S(2)}) collective-permute-start(f32[200,256]{1,0:T(8,128)S(1)} %collective-permute-done.15.near3), channel_id=1, source_target_pairs={{0,1},{1,0},{2,3},{3,2},{4,5},{5,4},{6,7},{7,6},{8,9},{9,8},{10,11... | collective-permute-start | bytes 614408 | tf_op jit(solution)/shard_map/ppermute | solution.py:21
  50.7 1.9 %collective-permute-start.22 = (f32[200,256]{1,0:T(8,128)S(1)}, f32[200,256]{1,0:T(8,128)S(1)}, u32[]{:S(2)}, u32[]{:S(2)}) collective-permute-start(f32[200,256]{1,0:T(8,128)S(1)} %collective-permute-done.20.near2), channel_id=1, source_target_pairs={{0,1},{1,0},{2,3},{3,2},{4,5},{5,4},{6,7},{7,6},{8,9},{9,8},{10,11... | collective-permute-start | bytes 614408 | tf_op jit(solution)/shard_map/ppermute | solution.py:21

commit v12 on v11

--- a/solution.py
+++ b/solution.py
@@ -80,8 +80,8 @@
 
 def after_trans(leading, mirror, away, into):
     q = split(into)
+    bounced = split(dot3(split(mirror), q))
     trans = dot3(split(leading), q)
-    bounced = split(dot3(split(mirror), q))
     return trans, away + dot3(split(into.T), bounced)
 
 
@@ -164,19 +164,25 @@
     store_half(away_rows, core, second_ref, h)
 
 
-def first_kernel(section_ref, got1, got2, got3, prefix_ref, *send_refs):
-    me = place()
-    upper = bit(me, 1)
+def first_early_kernel(section_ref, got1, got2, half_ref):
+    upper = bit(place(), 1)
     left, right, trans = section_ref[0], section_ref[1], section_ref[2]
     pick = lambda a, b: jnp.where(upper, a, b)
     own = pick(left, right), pick(right, left), pick(trans, trans.T)
-    leading, mirror, own_side = before_trans(own, pick(got2[0], got1[0]))
-    into = pick(got3[0], got3[0].T)
-    through, other_side = after_trans(leading, mirror, pick(got1[0], got2[0]), into)
+    for i, x in enumerate(before_trans(own, pick(got2[0], got1[0]))):
+        half_ref[i] = x
+
+
+def first_late_kernel(section_ref, half_ref, got1, got2, got3, prefix_ref, *send_refs):
+    me = place()
+    upper = bit(me, 1)
+    pick = lambda a, b: jnp.where(upper, a, b)
+    own_side, into = half_ref[2], pick(got3[0], got3[0].T)
+    through, other_side = after_trans(half_ref[0], half_ref[1], pick(got1[0], got2[0]), into)
     send_total(own_side, other_side, through, upper == bit(me, 2), upper, *send_refs)
-    prefix_ref[0] = pick(other_side, left)
-    prefix_ref[1] = pick(own_side, right)
-    prefix_ref[2] = pick(through, trans)
+    prefix_ref[0] = pick(other_side, section_ref[0])
+    prefix_ref[1] = pick(own_side, section_ref[1])
+    prefix_ref[2] = pick(through, section_ref[2])
 
 
 def early_kernel(own_ref, near_ref, far_ref, half_ref):
@@ -275,9 +281,9 @@
         right_copy.start()
         into, away = unpack_second(*by_third(distance, me, near2, far2, near3, far3), bit(me, 1))
         q = split(into)
+        bounced = split(dot3(split(half_ref[1]), q))
         new_ref[0] = dot3(split(half_ref[0]), q)
         trans_copy.start()
-        bounced = split(dot3(split(half_ref[1]), q))
         new_ref[1] = away + dot3(split(into.T), bounced)
         left_copy.start()
         right_copy.wait()
@@ -308,7 +314,8 @@
     sections = refl_left, refl_right, trans
     got = [swap(x, 1) for x in sections]
     section = jnp.concatenate(sections, 0)
-    prefix, send1, send2, own = call(first_kernel, 36, [stack, first, second, stack], section, *got)
+    (halfway,) = call(first_early_kernel, 27, [stack], section, *got[:2])
+    prefix, send1, send2, own = call(first_late_kernel, 9, [stack, first, second, stack], section, halfway, *got)
     pending = None
     for level in range(1, levels - 1):
         distance = 1 << level

time: 54.3 us -> 54.6 us (level)
  local copies, waits for them, and re-layouts: 0 us -> 1.93 us
  other arithmetic: 1.16 us -> 0 us
  starting transfers between devices: 19.4 us -> 18.6 us
    unnamed x0 -> x6, local copies, waits for them, and re-layouts: none -> 1.91 us
    concatenate x1 -> x0, other arithmetic: 1.16 us -> none  [shards(): section = jnp.concatenate(sections, 0)]
    ppermute x19, starting transfers between devices: 16.4 us -> 15.7 us  [swap(): return lax.ppermute(block, AXES, [(i, i ^ distance) for i in range(count)])]
    pallas_call x12 -> x13, Pallas kernels: 18.1 us -> 17.8 us  [call(): pl.pallas_call(kernel, out_shape=[jax.ShapeDtypeStruct(s, F32) for s in o...]
  transfers between devices with their start and end apart: 23 -> 23, of which waited for: 13 -> 12; matrix products, arithmetic and copies ran while one was open for 2% -> 2% of each run, Pallas kernels for 24% -> 27%
where the time goes in v12:
time: 54.6 us; the launch traced here: 54.4 us
  starting transfers between devices  18.6 us (34%)
  Pallas kernels  17.8 us (33%)
  waiting for transfers between devices  15 us (27%)
  local copies, waits for them, and re-layouts  1.93 us (4%)
  between operations  1.01 us (2%)
    pallas_call x13, Pallas kernels, call(): pl.pallas_call(kernel, out_shape=[jax.ShapeDtypeStruct(s, F32) for s in o...  17.8 us
    ppermute x19, starting transfers between devices, swap(): return lax.ppermute(block, AXES, [(i, i ^ distance) for i in range(count)])  15.7 us
    ppermute x19, waiting for transfers between devices, swap(): return lax.ppermute(block, AXES, [(i, i ^ distance) for i in range(count)])  10.5 us
    ppermute x4, waiting for transfers between devices, pair(): lax.ppermute(block, AXES, [(i, step.get(i // quarter, lambda i: i ^ 1)(i)...  4.5 us
    ppermute x4, starting transfers between devices, pair(): lax.ppermute(block, AXES, [(i, step.get(i // quarter, lambda i: i ^ 1)(i)...  2.96 us
    unnamed x6, local copies, waits for them, and re-layouts  1.91 us
  transfers between devices with their start and end apart: 23, of which 12 were waited for; matrix products, arithmetic and copies ran while one was open for 2% of the time, Pallas kernels for 27%

profile of v12, /device:TPU:17, one launch (start us, length us, event | category | flops | bytes accessed | tf_op | source)
XLA Modules:
  0.0 54.4 jit_solution(16123811785937774175)
XLA Ops:
  1.9 1.0 %constant_dynamic-update-slice_fusion.2 = f32[3,256,256]{2,1,0:T(8,128)S(1)} fusion(f32[1,256,256]{2,1,0:T(8,128)} %param.3), kind=kLoop, calls=%fused_computation.2 | loop fusion | bytes 524288
  2.9 0.9 %copy-done.1 = f32[1,256,256]{2,1,0:T(8,128)S(1)} copy-done((f32[1,256,256]{2,1,0:T(8,128)S(1)}, f32[1,256,256]{2,1,0:T(8,128)}, u32[]{:S(2)}) %copy-start.1) | copy-done | bytes 262168
  3.9 1.8 %shard_map.58.half_ref = f32[3,256,256]{2,1,0:T(8,128)S(1)} custom-call(f32[3,256,256]{2,1,0:T(8,128)S(1)} %constant_dynamic-update-slice_fusion.section_ref, f32[1,256,256]{2,1,0:T(8,128)S(1)} %collective-permute-done.got1, f32[1,256,256]{2,1,0:T(8,128)S(1)} %collective-permute-done.1.got2), custom_call_target="tpu_custom_call" | custom-call | flops 905969664 | bytes 786432 | tf_op jit(solution)/shard_map/pallas_call | solution.py:297
  6.5 1.3 %collective-permute-start.4 = (f32[72,256]{1,0:T(8,128)S(1)}, f32[72,256]{1,0:T(8,128)S(1)}, u32[]{:S(2)}, u32[]{:S(2)}) collective-permute-start(f32[72,256]{1,0:T(8,128)S(1)} %get-tuple-element.38), channel_id=1, source_target_pairs={{0,2},{1,3},{2,0},{3,1},{4,6},{5,7},{6,4},{7,5},{8,10},{9,11},{10,... | collective-permute-start | bytes 221192 | tf_op jit(solution)/shard_map/ppermute | solution.py:21
  8.0 2.4 %collective-permute-done.4.near_ref.near1 = f32[72,256]{1,0:T(8,128)S(1)} collective-permute-done((f32[72,256]{1,0:T(8,128)S(1)}, f32[72,256]{1,0:T(8,128)S(1)}, u32[]{:S(2)}, u32[]{:S(2)}) %collective-permute-start.4) | collective-permute-done | bytes 73760 | tf_op jit(solution)/shard_map/ppermute | solution.py:21
  10.4 1.3 %collective-permute-start.5 = (f32[72,256]{1,0:T(8,128)S(1)}, f32[72,256]{1,0:T(8,128)S(1)}, u32[]{:S(2)}, u32[]{:S(2)}) collective-permute-start(f32[72,256]{1,0:T(8,128)S(1)} %collective-permute-done.4.near_ref.near1), channel_id=1, source_target_pairs={{0,1},{1,0},{2,3},{3,2},{4,5},{5,4},{6,7},{7,6},{8,9},{9,8},{10,11... | collective-permute-start | bytes 221192 | tf_op jit(solution)/shard_map/ppermute | solution.py:21
  11.7 0.9 %collective-permute-done.5.far_ref.far1 = f32[72,256]{1,0:T(8,128)S(1)} collective-permute-done((f32[72,256]{1,0:T(8,128)S(1)}, f32[72,256]{1,0:T(8,128)S(1)}, u32[]{:S(2)}, u32[]{:S(2)}) %collective-permute-start.5) | collective-permute-done | bytes 73760 | tf_op jit(solution)/shard_map/ppermute | solution.py:21
  12.6 1.9 %shard_map.60.half_ref = f32[3,256,256]{2,1,0:T(8,128)S(1)} custom-call(f32[3,256,256]{2,1,0:T(8,128)S(1)} %get-tuple-element.37.own_ref, f32[72,256]{1,0:T(8,128)S(1)} %collective-permute-done.4.near_ref.near1, f32[72,256]{1,0:T(8,128)S(1)} %collective-permute-done.5.far_ref.far1), custom_call_target="tpu_custom_call" | custom-call | flops 905969664 | bytes 786432 | tf_op jit(solution)/shard_map/pallas_call | solution.py:297
  14.7 0.8 %collective-permute-start.6 = (f32[192,256]{1,0:T(8,128)S(1)}, f32[192,256]{1,0:T(8,128)S(1)}, u32[]{:S(2)}, u32[]{:S(2)}) collective-permute-start(f32[192,256]{1,0:T(8,128)S(1)} %collective-permute-done.3.near_ref.near2), channel_id=1, source_target_pairs={{0,1},{1,0},{2,3},{3,2},{4,5},{5,4},{6,7},{7,6},{8,9},{9,8},{10,11... | collective-permute-start | bytes 589832 | tf_op jit(solution)/shard_map/ppermute | solution.py:21
  15.5 1.1 %collective-permute-done.6.far_ref.far2 = f32[192,256]{1,0:T(8,128)S(1)} collective-permute-done((f32[192,256]{1,0:T(8,128)S(1)}, f32[192,256]{1,0:T(8,128)S(1)}, u32[]{:S(2)}, u32[]{:S(2)}) %collective-permute-start.6) | collective-permute-done | bytes 196640 | tf_op jit(solution)/shard_map/ppermute | solution.py:21
  17.1 1.3 %collective-permute-start.8 = (f32[72,256]{1,0:T(8,128)S(1)}, f32[72,256]{1,0:T(8,128)S(1)}, u32[]{:S(2)}, u32[]{:S(2)}) collective-permute-start(f32[72,256]{1,0:T(8,128)S(1)} %get-tuple-element.43), channel_id=1, source_target_pairs={{0,4},{1,5},{2,6},{3,7},{4,0},{5,1},{6,2},{7,3},{8,12},{9,13},{10,... | collective-permute-start | bytes 221192 | tf_op jit(solution)/shard_map/ppermute | solution.py:21
  18.7 2.3 %shard_map.62.old_ref = f32[3,256,256]{2,1,0:T(8,128)S(1)} custom-call(f32[3,256,256]{2,1,0:T(8,128)S(1)} %get-tuple-element.44.old_ref, f32[72,256]{1,0:T(8,128)S(1)} %collective-permute-done.4.near_ref.near1, f32[72,256]{1,0:T(8,128)S(1)} %collective-permute-done.5.far_ref.far1, f32[192,256]{1,0:T(8,128)S(1)} %collective-permute-done.3.near_ref.near2, ...), custom_call_target="tpu_custom_call" | custom-call | flops 1207959552 | bytes 1310720 | tf_op jit(solution)/shard_map/pallas_call | solution.py:297
  21.0 1.4 %collective-permute-start.9 = (f32[72,256]{1,0:T(8,128)S(1)}, f32[72,256]{1,0:T(8,128)S(1)}, u32[]{:S(2)}, u32[]{:S(2)}) collective-permute-start(f32[72,256]{1,0:T(8,128)S(1)} %collective-permute-done.8.near_ref.near1), channel_id=1, source_target_pairs={{0,1},{1,0},{2,3},{3,2},{4,5},{5,4},{6,7},{7,6},{8,9},{9,8},{10,11... | collective-permute-start | bytes 221192 | tf_op jit(solution)/shard_map/ppermute | solution.py:21
  22.4 0.9 %collective-permute-done.9.far_ref.far1 = f32[72,256]{1,0:T(8,128)S(1)} collective-permute-done((f32[72,256]{1,0:T(8,128)S(1)}, f32[72,256]{1,0:T(8,128)S(1)}, u32[]{:S(2)}, u32[]{:S(2)}) %collective-permute-start.9) | collective-permute-done | bytes 73760 | tf_op jit(solution)/shard_map/ppermute | solution.py:21
  23.3 1.9 %shard_map.63.half_ref = f32[3,256,256]{2,1,0:T(8,128)S(1)} custom-call(f32[3,256,256]{2,1,0:T(8,128)S(1)} %get-tuple-element.42.own_ref, f32[72,256]{1,0:T(8,128)S(1)} %collective-permute-done.8.near_ref.near1, f32[72,256]{1,0:T(8,128)S(1)} %collective-permute-done.9.far_ref.far1), custom_call_target="tpu_custom_call" | custom-call | flops 905969664 | bytes 786432 | tf_op jit(solution)/shard_map/pallas_call | solution.py:297
  25.2 1.0 %collective-permute-start.10 = (f32[192,256]{1,0:T(8,128)S(1)}, f32[192,256]{1,0:T(8,128)S(1)}, u32[]{:S(2)}, u32[]{:S(2)}) collective-permute-start(f32[192,256]{1,0:T(8,128)S(1)} %collective-permute-done.7.near_ref.near2), channel_id=1, source_target_pairs={{0,1},{1,0},{2,3},{3,2},{4,5},{5,4},{6,7},{7,6},{8,9},{9,8},{10,11... | collective-permute-start | bytes 589832 | tf_op jit(solution)/shard_map/ppermute | solution.py:21
  26.2 1.1 %collective-permute-done.10.far_ref.far2 = f32[192,256]{1,0:T(8,128)S(1)} collective-permute-done((f32[192,256]{1,0:T(8,128)S(1)}, f32[192,256]{1,0:T(8,128)S(1)}, u32[]{:S(2)}, u32[]{:S(2)}) %collective-permute-start.10) | collective-permute-done | bytes 196640 | tf_op jit(solution)/shard_map/ppermute | solution.py:21
  27.8 1.4 %collective-permute-start.12 = (f32[72,256]{1,0:T(8,128)S(1)}, f32[72,256]{1,0:T(8,128)S(1)}, u32[]{:S(2)}, u32[]{:S(2)}) collective-permute-start(f32[72,256]{1,0:T(8,128)S(1)} %get-tuple-element.50), channel_id=1, source_target_pairs={{0,8},{1,9},{2,10},{3,11},{4,12},{5,13},{6,14},{7,15},{8,0},{9,1},... | collective-permute-start | bytes 221192 | tf_op jit(solution)/shard_map/ppermute | solution.py:21
  29.4 2.3 %shard_map.65.old_ref = f32[3,256,256]{2,1,0:T(8,128)S(1)} custom-call(f32[3,256,256]{2,1,0:T(8,128)S(1)} %shard_map.62.old_ref, f32[72,256]{1,0:T(8,128)S(1)} %collective-permute-done.8.near_ref.near1, f32[72,256]{1,0:T(8,128)S(1)} %collective-permute-done.9.far_ref.far1, f32[192,256]{1,0:T(8,128)S(1)} %collective-permute-done.7.near_ref.near2, ...), custom_call_target="tpu_custom_call" | custom-call | flops 1207959552 | bytes 1310720 | tf_op jit(solution)/shard_map/pallas_call | solution.py:297
  31.7 1.4 %collective-permute-start.13 = (f32[72,256]{1,0:T(8,128)S(1)}, f32[72,256]{1,0:T(8,128)S(1)}, u32[]{:S(2)}, u32[]{:S(2)}) collective-permute-start(f32[72,256]{1,0:T(8,128)S(1)} %collective-permute-done.12.near_ref.near1), channel_id=1, source_target_pairs={{0,1},{1,0},{2,3},{3,2},{4,5},{5,4},{6,7},{7,6},{8,9},{9,8},{10,11... | collective-permute-start | bytes 221192 | tf_op jit(solution)/shard_map/ppermute | solution.py:21
  33.0 0.9 %collective-permute-done.13.far_ref.far1 = f32[72,256]{1,0:T(8,128)S(1)} collective-permute-done((f32[72,256]{1,0:T(8,128)S(1)}, f32[72,256]{1,0:T(8,128)S(1)}, u32[]{:S(2)}, u32[]{:S(2)}) %collective-permute-start.13) | collective-permute-done | bytes 73760 | tf_op jit(solution)/shard_map/ppermute | solution.py:21
  34.2 1.5 %collective-permute-done.11.near_ref.near2 = f32[192,256]{1,0:T(8,128)S(1)} collective-permute-done((f32[192,256]{1,0:T(8,128)S(1)}, f32[192,256]{1,0:T(8,128)S(1)}, u32[]{:S(2)}, u32[]{:S(2)}) %collective-permute-start.11) | collective-permute-done | bytes 196640 | tf_op jit(solution)/shard_map/ppermute | solution.py:21
  35.7 1.2 %collective-permute-start.14 = (f32[192,256]{1,0:T(8,128)S(1)}, f32[192,256]{1,0:T(8,128)S(1)}, u32[]{:S(2)}, u32[]{:S(2)}) collective-permute-start(f32[192,256]{1,0:T(8,128)S(1)} %collective-permute-done.11.near_ref.near2), channel_id=1, source_target_pairs={{0,1},{1,0},{2,3},{3,2},{4,5},{5,4},{6,7},{7,6},{8,9},{9,8},{10,11... | collective-permute-start | bytes 589832 | tf_op jit(solution)/shard_map/ppermute | solution.py:21
  38.4 2.4 %collective-permute-done.17.near2 = f32[72,256]{1,0:T(8,128)S(1)} collective-permute-done((f32[72,256]{1,0:T(8,128)S(1)}, f32[72,256]{1,0:T(8,128)S(1)}, u32[]{:S(2)}, u32[]{:S(2)}) %collective-permute-start.17) | collective-permute-done | bytes 73760 | tf_op jit(solution)/shard_map/ppermute | solution.py:29
  40.8 1.2 %collective-permute-start.18 = (f32[72,256]{1,0:T(8,128)S(1)}, f32[72,256]{1,0:T(8,128)S(1)}, u32[]{:S(2)}, u32[]{:S(2)}) collective-permute-start(f32[72,256]{1,0:T(8,128)S(1)} %collective-permute-done.17.near2), channel_id=1, source_target_pairs={{0,1},{1,0},{2,3},{3,2},{4,5},{5,4},{6,7},{7,6},{8,9},{9,8},{10,11... | collective-permute-start | bytes 221192 | tf_op jit(solution)/shard_map/ppermute | solution.py:21
  41.9 2.0 %collective-permute-start.20 = (f32[200,256]{1,0:T(8,128)S(1)}, f32[200,256]{1,0:T(8,128)S(1)}, u32[]{:S(2)}, u32[]{:S(2)}) collective-permute-start(f32[200,256]{1,0:T(8,128)S(1)} %shard_map.67), channel_id=1, source_target_pairs={{0,1},{1,0},{2,3},{3,2},{4,5},{5,4},{6,7},{7,6},{8,16},{9,17},{10,... | collective-permute-start | bytes 614408 | tf_op jit(solution)/shard_map/ppermute | solution.py:29
  43.9 2.3 %shard_map.68.old_ref = f32[3,256,256]{2,1,0:T(8,128)S(1)} custom-call(f32[3,256,256]{2,1,0:T(8,128)S(1)} %shard_map.65.old_ref, f32[72,256]{1,0:T(8,128)S(1)} %collective-permute-done.12.near_ref.near1, f32[72,256]{1,0:T(8,128)S(1)} %collective-permute-done.13.far_ref.far1, f32[192,256]{1,0:T(8,128)S(1)} %collective-permute-done.11.near_ref.near2, ...), custom_call_target="tpu_custom_call" | custom-call | flops 1207959552 | bytes 1310720 | tf_op jit(solution)/shard_map/pallas_call | solution.py:297
  46.2 1.9 %shard_map.69 = (f32[3,256,256]{2,1,0:T(8,128)S(1)}, f32[1,256,256]{2,1,0:T(8,128)}, f32[1,256,256]{2,1,0:T(8,128)}, f32[1,256,256]{2,1,0:T(8,128)}) custom-call(f32[3,256,256]{2,1,0:T(8,128)S(1)} %shard_map.68.old_ref, f32[72,256]{1,0:T(8,128)S(1)} %collective-permute-done.17.near2, f32[72,256]{1,0:T(8,128)S(1)} %collective-permute-done.18.far2, ...), custom_call_target="tpu_custom_call" | custom-call | flops 905969664 | bytes 1310720 | tf_op jit(solution)/shard_map/pallas_call | solution.py:297
  48.1 0.9 %collective-permute-start.21 = (f32[200,256]{1,0:T(8,128)S(1)}, f32[200,256]{1,0:T(8,128)S(1)}, u32[]{:S(2)}, u32[]{:S(2)}) collective-permute-start(f32[200,256]{1,0:T(8,128)S(1)} %collective-permute-done.15.near3), channel_id=1, source_target_pairs={{0,1},{1,0},{2,3},{3,2},{4,5},{5,4},{6,7},{7,6},{8,9},{9,8},{10,11... | collective-permute-start | bytes 614408 | tf_op jit(solution)/shard_map/ppermute | solution.py:21
  49.0 2.1 %collective-permute-done.20.near2 = f32[200,256]{1,0:T(8,128)S(1)} collective-permute-done((f32[200,256]{1,0:T(8,128)S(1)}, f32[200,256]{1,0:T(8,128)S(1)}, u32[]{:S(2)}, u32[]{:S(2)}) %collective-permute-start.20) | collective-permute-done | bytes 204832 | tf_op jit(solution)/shard_map/ppermute | solution.py:29
  51.9 1.1 %collective-permute-done.22.far2 = f32[200,256]{1,0:T(8,128)S(1)} collective-permute-done((f32[200,256]{1,0:T(8,128)S(1)}, f32[200,256]{1,0:T(8,128)S(1)}, u32[]{:S(2)}, u32[]{:S(2)}) %collective-permute-start.22) | collective-permute-done | bytes 204832 | tf_op jit(solution)/shard_map/ppermute | solution.py:21
  53.0 1.3 %shard_map.70 = (f32[1,256,256]{2,1,0:T(8,128)}, f32[1,256,256]{2,1,0:T(8,128)}, f32[1,256,256]{2,1,0:T(8,128)}) custom-call(f32[3,256,256]{2,1,0:T(8,128)S(1)} %get-tuple-element.62.half_ref, f32[200,256]{1,0:T(8,128)S(1)} %collective-permute-done.20.near2, ...), custom_call_target="tpu_custom_call", output_to_operand_aliasing={{0}: (5, {}), {1}: (6, {}), {2}: (7, {})} | custom-call | flops 301989888 | bytes 1310720 | tf_op jit(solution)/shard_map/pallas_call | solution.py:297
  (34 shorter events, 6.7 us)
Async XLA Ops:
  0.6 2.2 %copy-start = (f32[1,256,256]{2,1,0:T(8,128)S(1)}, f32[1,256,256]{2,1,0:T(8,128)}, u32[]{:S(2)}) copy-start(f32[1,256,256]{2,1,0:T(8,128)} %param.4) | copy-start | bytes 786436
  0.6 3.2 %collective-permute-start = (f32[1,256,256]{2,1,0:T(8,128)}, f32[1,256,256]{2,1,0:T(8,128)S(1)}, u32[]{:S(2)}, u32[]{:S(2)}) collective-permute-start(f32[1,256,256]{2,1,0:T(8,128)} %param.3), channel_id=1, source_target_pairs={{0,1},{1,0},{2,3},{3,2},{4,5},{5,4},{6,7},{7,6},{8,9},{9,8},{10,11... | collective-permute-start | bytes 786440 | tf_op jit(solution)/shard_map/ppermute | solution.py:21
  1.4 2.5 %collective-permute-start.1 = (f32[1,256,256]{2,1,0:T(8,128)}, f32[1,256,256]{2,1,0:T(8,128)S(1)}, u32[]{:S(2)}, u32[]{:S(2)}) collective-permute-start(f32[1,256,256]{2,1,0:T(8,128)} %param.4), channel_id=1, source_target_pairs={{0,1},{1,0},{2,3},{3,2},{4,5},{5,4},{6,7},{7,6},{8,9},{9,8},{10,11... | collective-permute-start | bytes 786440 | tf_op jit(solution)/shard_map/ppermute | solution.py:21
  1.5 4.3 %collective-permute-start.2 = (f32[1,256,256]{2,1,0:T(8,128)}, f32[1,256,256]{2,1,0:T(8,128)S(1)}, u32[]{:S(2)}, u32[]{:S(2)}) collective-permute-start(f32[1,256,256]{2,1,0:T(8,128)} %param.5), channel_id=1, source_target_pairs={{0,1},{1,0},{2,3},{3,2},{4,5},{5,4},{6,7},{7,6},{8,9},{9,8},{10,11... | collective-permute-start | bytes 786440 | tf_op jit(solution)/shard_map/ppermute | solution.py:21
  2.9 1.0 %copy-start.1 = (f32[1,256,256]{2,1,0:T(8,128)S(1)}, f32[1,256,256]{2,1,0:T(8,128)}, u32[]{:S(2)}) copy-start(f32[1,256,256]{2,1,0:T(8,128)} %param.5) | copy-start | bytes 786436
  6.5 3.9 %collective-permute-start.4 = (f32[72,256]{1,0:T(8,128)S(1)}, f32[72,256]{1,0:T(8,128)S(1)}, u32[]{:S(2)}, u32[]{:S(2)}) collective-permute-start(f32[72,256]{1,0:T(8,128)S(1)} %get-tuple-element.38), channel_id=1, source_target_pairs={{0,2},{1,3},{2,0},{3,1},{4,6},{5,7},{6,4},{7,5},{8,10},{9,11},{10,... | collective-permute-start | bytes 221192 | tf_op jit(solution)/shard_map/ppermute | solution.py:21
  7.8 6.9 %collective-permute-start.3 = (f32[192,256]{1,0:T(8,128)S(1)}, f32[192,256]{1,0:T(8,128)S(1)}, u32[]{:S(2)}, u32[]{:S(2)}) collective-permute-start(f32[192,256]{1,0:T(8,128)S(1)} %get-tuple-element.36), channel_id=1, source_target_pairs={{0,2},{1,3},{2,0},{3,1},{4,6},{5,7},{6,4},{7,5},{8,10},{9,11},{10,... | collective-permute-start | bytes 589832 | tf_op jit(solution)/shard_map/ppermute | solution.py:21
  10.4 2.2 %collective-permute-start.5 = (f32[72,256]{1,0:T(8,128)S(1)}, f32[72,256]{1,0:T(8,128)S(1)}, u32[]{:S(2)}, u32[]{:S(2)}) collective-permute-start(f32[72,256]{1,0:T(8,128)S(1)} %collective-permute-done.4.near_ref.near1), channel_id=1, source_target_pairs={{0,1},{1,0},{2,3},{3,2},{4,5},{5,4},{6,7},{7,6},{8,9},{9,8},{10,11... | collective-permute-start | bytes 221192 | tf_op jit(solution)/shard_map/ppermute | solution.py:21
  14.7 1.9 %collective-permute-start.6 = (f32[192,256]{1,0:T(8,128)S(1)}, f32[192,256]{1,0:T(8,128)S(1)}, u32[]{:S(2)}, u32[]{:S(2)}) collective-permute-start(f32[192,256]{1,0:T(8,128)S(1)} %collective-permute-done.3.near_ref.near2), channel_id=1, source_target_pairs={{0,1},{1,0},{2,3},{3,2},{4,5},{5,4},{6,7},{7,6},{8,9},{9,8},{10,11... | collective-permute-start | bytes 589832 | tf_op jit(solution)/shard_map/ppermute | solution.py:21
  17.1 3.8 %collective-permute-start.8 = (f32[72,256]{1,0:T(8,128)S(1)}, f32[72,256]{1,0:T(8,128)S(1)}, u32[]{:S(2)}, u32[]{:S(2)}) collective-permute-start(f32[72,256]{1,0:T(8,128)S(1)} %get-tuple-element.43), channel_id=1, source_target_pairs={{0,4},{1,5},{2,6},{3,7},{4,0},{5,1},{6,2},{7,3},{8,12},{9,13},{10,... | collective-permute-start | bytes 221192 | tf_op jit(solution)/shard_map/ppermute | solution.py:21
  18.4 6.7 %collective-permute-start.7 = (f32[192,256]{1,0:T(8,128)S(1)}, f32[192,256]{1,0:T(8,128)S(1)}, u32[]{:S(2)}, u32[]{:S(2)}) collective-permute-start(f32[192,256]{1,0:T(8,128)S(1)} %get-tuple-element.41), channel_id=1, source_target_pairs={{0,4},{1,5},{2,6},{3,7},{4,0},{5,1},{6,2},{7,3},{8,12},{9,13},{10,... | collective-permute-start | bytes 589832 | tf_op jit(solution)/shard_map/ppermute | solution.py:21
  21.0 2.3 %collective-permute-start.9 = (f32[72,256]{1,0:T(8,128)S(1)}, f32[72,256]{1,0:T(8,128)S(1)}, u32[]{:S(2)}, u32[]{:S(2)}) collective-permute-start(f32[72,256]{1,0:T(8,128)S(1)} %collective-permute-done.8.near_ref.near1), channel_id=1, source_target_pairs={{0,1},{1,0},{2,3},{3,2},{4,5},{5,4},{6,7},{7,6},{8,9},{9,8},{10,11... | collective-permute-start | bytes 221192 | tf_op jit(solution)/shard_map/ppermute | solution.py:21
  25.2 2.0 %collective-permute-start.10 = (f32[192,256]{1,0:T(8,128)S(1)}, f32[192,256]{1,0:T(8,128)S(1)}, u32[]{:S(2)}, u32[]{:S(2)}) collective-permute-start(f32[192,256]{1,0:T(8,128)S(1)} %collective-permute-done.7.near_ref.near2), channel_id=1, source_target_pairs={{0,1},{1,0},{2,3},{3,2},{4,5},{5,4},{6,7},{7,6},{8,9},{9,8},{10,11... | collective-permute-start | bytes 589832 | tf_op jit(solution)/shard_map/ppermute | solution.py:21
  27.8 3.8 %collective-permute-start.12 = (f32[72,256]{1,0:T(8,128)S(1)}, f32[72,256]{1,0:T(8,128)S(1)}, u32[]{:S(2)}, u32[]{:S(2)}) collective-permute-start(f32[72,256]{1,0:T(8,128)S(1)} %get-tuple-element.50), channel_id=1, source_target_pairs={{0,8},{1,9},{2,10},{3,11},{4,12},{5,13},{6,14},{7,15},{8,0},{9,1},... | collective-permute-start | bytes 221192 | tf_op jit(solution)/shard_map/ppermute | solution.py:21
  29.2 6.5 %collective-permute-start.11 = (f32[192,256]{1,0:T(8,128)S(1)}, f32[192,256]{1,0:T(8,128)S(1)}, u32[]{:S(2)}, u32[]{:S(2)}) collective-permute-start(f32[192,256]{1,0:T(8,128)S(1)} %get-tuple-element.48), channel_id=1, source_target_pairs={{0,8},{1,9},{2,10},{3,11},{4,12},{5,13},{6,14},{7,15},{8,0},{9,1},... | collective-permute-start | bytes 589832 | tf_op jit(solution)/shard_map/ppermute | solution.py:21
  31.7 2.3 %collective-permute-start.13 = (f32[72,256]{1,0:T(8,128)S(1)}, f32[72,256]{1,0:T(8,128)S(1)}, u32[]{:S(2)}, u32[]{:S(2)}) collective-permute-start(f32[72,256]{1,0:T(8,128)S(1)} %collective-permute-done.12.near_ref.near1), channel_id=1, source_target_pairs={{0,1},{1,0},{2,3},{3,2},{4,5},{5,4},{6,7},{7,6},{8,9},{9,8},{10,11... | collective-permute-start | bytes 221192 | tf_op jit(solution)/shard_map/ppermute | solution.py:21
  35.7 2.3 %collective-permute-start.14 = (f32[192,256]{1,0:T(8,128)S(1)}, f32[192,256]{1,0:T(8,128)S(1)}, u32[]{:S(2)}, u32[]{:S(2)}) collective-permute-start(f32[192,256]{1,0:T(8,128)S(1)} %collective-permute-done.11.near_ref.near2), channel_id=1, source_target_pairs={{0,1},{1,0},{2,3},{3,2},{4,5},{5,4},{6,7},{7,6},{8,9},{9,8},{10,11... | collective-permute-start | bytes 589832 | tf_op jit(solution)/shard_map/ppermute | solution.py:21
  36.8 3.9 %collective-permute-start.17 = (f32[72,256]{1,0:T(8,128)S(1)}, f32[72,256]{1,0:T(8,128)S(1)}, u32[]{:S(2)}, u32[]{:S(2)}) collective-permute-start(f32[72,256]{1,0:T(8,128)S(1)} %get-tuple-element.56), channel_id=1, source_target_pairs={{0,1},{1,0},{2,3},{3,2},{4,5},{5,4},{6,7},{7,6},{8,16},{9,17},{10,... | collective-permute-start | bytes 221192 | tf_op jit(solution)/shard_map/ppermute | solution.py:29
  37.0 3.8 %collective-permute-start.16 = (f32[72,256]{1,0:T(8,128)S(1)}, f32[72,256]{1,0:T(8,128)S(1)}, u32[]{:S(2)}, u32[]{:S(2)}) collective-permute-start(f32[72,256]{1,0:T(8,128)S(1)} %get-tuple-element.56), channel_id=1, source_target_pairs={{0,1},{1,0},{2,3},{3,2},{4,5},{5,4},{6,7},{7,6},{8,24},{9,25},{10,... | collective-permute-start | bytes 221192 | tf_op jit(solution)/shard_map/ppermute | solution.py:29
  37.9 10.2 %collective-permute-start.15 = (f32[200,256]{1,0:T(8,128)S(1)}, f32[200,256]{1,0:T(8,128)S(1)}, u32[]{:S(2)}, u32[]{:S(2)}) collective-permute-start(f32[200,256]{1,0:T(8,128)S(1)} %shard_map.67), channel_id=1, source_target_pairs={{0,1},{1,0},{2,3},{3,2},{4,5},{5,4},{6,7},{7,6},{8,24},{9,25},{10,... | collective-permute-start | bytes 614408 | tf_op jit(solution)/shard_map/ppermute | solution.py:29
  40.8 5.4 %collective-permute-start.18 = (f32[72,256]{1,0:T(8,128)S(1)}, f32[72,256]{1,0:T(8,128)S(1)}, u32[]{:S(2)}, u32[]{:S(2)}) collective-permute-start(f32[72,256]{1,0:T(8,128)S(1)} %collective-permute-done.17.near2), channel_id=1, source_target_pairs={{0,1},{1,0},{2,3},{3,2},{4,5},{5,4},{6,7},{7,6},{8,9},{9,8},{10,11... | collective-permute-start | bytes 221192 | tf_op jit(solution)/shard_map/ppermute | solution.py:21
  41.9 4.3 %collective-permute-start.19 = (f32[72,256]{1,0:T(8,128)S(1)}, f32[72,256]{1,0:T(8,128)S(1)}, u32[]{:S(2)}, u32[]{:S(2)}) collective-permute-start(f32[72,256]{1,0:T(8,128)S(1)} %collective-permute-done.16.near3), channel_id=1, source_target_pairs={{0,1},{1,0},{2,3},{3,2},{4,5},{5,4},{6,7},{7,6},{8,9},{9,8},{10,11... | collective-permute-start | bytes 221192 | tf_op jit(solution)/shard_map/ppermute | solution.py:21
  41.9 9.2 %collective-permute-start.20 = (f32[200,256]{1,0:T(8,128)S(1)}, f32[200,256]{1,0:T(8,128)S(1)}, u32[]{:S(2)}, u32[]{:S(2)}) collective-permute-start(f32[200,256]{1,0:T(8,128)S(1)} %shard_map.67), channel_id=1, source_target_pairs={{0,1},{1,0},{2,3},{3,2},{4,5},{5,4},{6,7},{7,6},{8,16},{9,17},{10,... | collective-permute-start | bytes 614408 | tf_op jit(solution)/shard_map/ppermute | solution.py:29
  48.1 3.0 %collective-permute-start.21 = (f32[200,256]{1,0:T(8,128)S(1)}, f32[200,256]{1,0:T(8,128)S(1)}, u32[]{:S(2)}, u32[]{:S(2)}) collective-permute-start(f32[200,256]{1,0:T(8,128)S(1)} %collective-permute-done.15.near3), channel_id=1, source_target_pairs={{0,1},{1,0},{2,3},{3,2},{4,5},{5,4},{6,7},{7,6},{8,9},{9,8},{10,11... | collective-permute-start | bytes 614408 | tf_op jit(solution)/shard_map/ppermute | solution.py:21
  51.1 1.9 %collective-permute-start.22 = (f32[200,256]{1,0:T(8,128)S(1)}, f32[200,256]{1,0:T(8,128)S(1)}, u32[]{:S(2)}, u32[]{:S(2)}) collective-permute-start(f32[200,256]{1,0:T(8,128)S(1)} %collective-permute-done.20.near2), channel_id=1, source_target_pairs={{0,1},{1,0},{2,3},{3,2},{4,5},{5,4},{6,7},{7,6},{8,9},{9,8},{10,11... | collective-permute-start | bytes 614408 | tf_op jit(solution)/shard_map/ppermute | solution.py:21

commit v13 on v11

--- a/solution.py
+++ b/solution.py
@@ -80,8 +80,8 @@
 
 def after_trans(leading, mirror, away, into):
     q = split(into)
+    bounced = split(dot3(split(mirror), q))
     trans = dot3(split(leading), q)
-    bounced = split(dot3(split(mirror), q))
     return trans, away + dot3(split(into.T), bounced)
 
 
@@ -275,9 +275,9 @@
         right_copy.start()
         into, away = unpack_second(*by_third(distance, me, near2, far2, near3, far3), bit(me, 1))
         q = split(into)
+        bounced = split(dot3(split(half_ref[1]), q))
         new_ref[0] = dot3(split(half_ref[0]), q)
         trans_copy.start()
-        bounced = split(dot3(split(half_ref[1]), q))
         new_ref[1] = away + dot3(split(into.T), bounced)
         left_copy.start()
         right_copy.wait()

time: 54.3 us -> 53.9 us (level)
  Pallas kernels: 18.1 us -> 17.3 us
    pallas_call x12, Pallas kernels: 18.1 us -> 17.3 us  [call(): pl.pallas_call(kernel, out_shape=[jax.ShapeDtypeStruct(s, F32) for s in o...]
  transfers between devices with their start and end apart: 23 -> 23, of which waited for: 13 -> 13; matrix products, arithmetic and copies ran while one was open for 2% -> 2% of each run, Pallas kernels for 24% -> 23%
where the time goes in v13:
time: 53.9 us; the launch traced here: 53.8 us
  starting transfers between devices  19.4 us (36%)
  Pallas kernels  17.3 us (32%)
  waiting for transfers between devices  15 us (28%)
  other arithmetic  1.16 us (2%)
  between operations  0.96 us (2%)
    pallas_call x12, Pallas kernels, call(): pl.pallas_call(kernel, out_shape=[jax.ShapeDtypeStruct(s, F32) for s in o...  17.3 us
    ppermute x19, starting transfers between devices, swap(): return lax.ppermute(block, AXES, [(i, i ^ distance) for i in range(count)])  16.6 us
    ppermute x19, waiting for transfers between devices, swap(): return lax.ppermute(block, AXES, [(i, i ^ distance) for i in range(count)])  10.4 us
    ppermute x4, waiting for transfers between devices, pair(): lax.ppermute(block, AXES, [(i, step.get(i // quarter, lambda i: i ^ 1)(i)...  4.51 us
    ppermute x4, starting transfers between devices, pair(): lax.ppermute(block, AXES, [(i, step.get(i // quarter, lambda i: i ^ 1)(i)...  2.83 us
    concatenate x1, other arithmetic, shards(): section = jnp.concatenate(sections, 0)  1.16 us
  transfers between devices with their start and end apart: 23, of which 13 were waited for; matrix products, arithmetic and copies ran while one was open for 2% of the time, Pallas kernels for 23%

profile of v13, /device:TPU:17, one launch (start us, length us, event | category | flops | bytes accessed | tf_op | source)
XLA Modules:
  0.0 53.8 jit_solution(15778163427887937320)
XLA Ops:
  1.9 1.2 %pad_maximum_fusion.section_ref = f32[3,256,256]{2,1,0:T(8,128)S(1)} fusion(f32[1,256,256]{2,1,0:T(8,128)} %param.5, f32[1,256,256]{2,1,0:T(8,128)} %param.4, f32[1,256,256]{2,1,0:T(8,128)} %param.3), kind=kLoop, calls=%fused_computation | loop fusion | flops 393216 | bytes 1572864 | tf_op jit(solution)/shard_map/concatenate | solution.py:310
  3.5 2.3 %shard_map.58 = (f32[3,256,256]{2,1,0:T(8,128)S(1)}, f32[72,256]{1,0:T(8,128)S(1)}, f32[192,256]{1,0:T(8,128)S(1)}, f32[3,256,256]{2,1,0:T(8,128)S(1)}) custom-call(f32[3,256,256]{2,1,0:T(8,128)S(1)} %pad_maximum_fusion.section_ref, f32[1,256,256]{2,1,0:T(8,128)S(1)} %collective-permute-done.got1, f32[1,256,256]{2,1,0:T(8,128)S(1)} %collective-permute-done.1.got2, ...), custom_call_target="tpu_custom_call" | custom-call | flops 1207959552 | bytes 1048576 | tf_op jit(solution)/shard_map/pallas_call | solution.py:291
  5.8 1.3 %collective-permute-start.4 = (f32[72,256]{1,0:T(8,128)S(1)}, f32[72,256]{1,0:T(8,128)S(1)}, u32[]{:S(2)}, u32[]{:S(2)}) collective-permute-start(f32[72,256]{1,0:T(8,128)S(1)} %get-tuple-element.38), channel_id=1, source_target_pairs={{0,2},{1,3},{2,0},{3,1},{4,6},{5,7},{6,4},{7,5},{8,10},{9,11},{10,... | collective-permute-start | bytes 221192 | tf_op jit(solution)/shard_map/ppermute | solution.py:21
  7.3 1.7 %collective-permute-done.4.near_ref.near1 = f32[72,256]{1,0:T(8,128)S(1)} collective-permute-done((f32[72,256]{1,0:T(8,128)S(1)}, f32[72,256]{1,0:T(8,128)S(1)}, u32[]{:S(2)}, u32[]{:S(2)}) %collective-permute-start.4) | collective-permute-done | bytes 73760 | tf_op jit(solution)/shard_map/ppermute | solution.py:21
  9.1 2.0 %collective-permute-start.5 = (f32[72,256]{1,0:T(8,128)S(1)}, f32[72,256]{1,0:T(8,128)S(1)}, u32[]{:S(2)}, u32[]{:S(2)}) collective-permute-start(f32[72,256]{1,0:T(8,128)S(1)} %collective-permute-done.4.near_ref.near1), channel_id=1, source_target_pairs={{0,1},{1,0},{2,3},{3,2},{4,5},{5,4},{6,7},{7,6},{8,9},{9,8},{10,11... | collective-permute-start | bytes 221192 | tf_op jit(solution)/shard_map/ppermute | solution.py:21
  11.1 0.9 %collective-permute-done.5.far_ref.far1 = f32[72,256]{1,0:T(8,128)S(1)} collective-permute-done((f32[72,256]{1,0:T(8,128)S(1)}, f32[72,256]{1,0:T(8,128)S(1)}, u32[]{:S(2)}, u32[]{:S(2)}) %collective-permute-start.5) | collective-permute-done | bytes 73760 | tf_op jit(solution)/shard_map/ppermute | solution.py:21
  12.0 1.9 %shard_map.59.half_ref = f32[3,256,256]{2,1,0:T(8,128)S(1)} custom-call(f32[3,256,256]{2,1,0:T(8,128)S(1)} %get-tuple-element.37.own_ref, f32[72,256]{1,0:T(8,128)S(1)} %collective-permute-done.4.near_ref.near1, f32[72,256]{1,0:T(8,128)S(1)} %collective-permute-done.5.far_ref.far1), custom_call_target="tpu_custom_call" | custom-call | flops 905969664 | bytes 786432 | tf_op jit(solution)/shard_map/pallas_call | solution.py:291
  13.9 0.9 %collective-permute-start.6 = (f32[192,256]{1,0:T(8,128)S(1)}, f32[192,256]{1,0:T(8,128)S(1)}, u32[]{:S(2)}, u32[]{:S(2)}) collective-permute-start(f32[192,256]{1,0:T(8,128)S(1)} %collective-permute-done.3.near_ref.near2), channel_id=1, source_target_pairs={{0,1},{1,0},{2,3},{3,2},{4,5},{5,4},{6,7},{7,6},{8,9},{9,8},{10,11... | collective-permute-start | bytes 589832 | tf_op jit(solution)/shard_map/ppermute | solution.py:21
  14.8 1.1 %collective-permute-done.6.far_ref.far2 = f32[192,256]{1,0:T(8,128)S(1)} collective-permute-done((f32[192,256]{1,0:T(8,128)S(1)}, f32[192,256]{1,0:T(8,128)S(1)}, u32[]{:S(2)}, u32[]{:S(2)}) %collective-permute-start.6) | collective-permute-done | bytes 196640 | tf_op jit(solution)/shard_map/ppermute | solution.py:21
  16.5 1.3 %collective-permute-start.8 = (f32[72,256]{1,0:T(8,128)S(1)}, f32[72,256]{1,0:T(8,128)S(1)}, u32[]{:S(2)}, u32[]{:S(2)}) collective-permute-start(f32[72,256]{1,0:T(8,128)S(1)} %get-tuple-element.43), channel_id=1, source_target_pairs={{0,4},{1,5},{2,6},{3,7},{4,0},{5,1},{6,2},{7,3},{8,12},{9,13},{10,... | collective-permute-start | bytes 221192 | tf_op jit(solution)/shard_map/ppermute | solution.py:21
  18.1 2.3 %shard_map.61.old_ref = f32[3,256,256]{2,1,0:T(8,128)S(1)} custom-call(f32[3,256,256]{2,1,0:T(8,128)S(1)} %get-tuple-element.44.old_ref, f32[72,256]{1,0:T(8,128)S(1)} %collective-permute-done.4.near_ref.near1, f32[72,256]{1,0:T(8,128)S(1)} %collective-permute-done.5.far_ref.far1, f32[192,256]{1,0:T(8,128)S(1)} %collective-permute-done.3.near_ref.near2, ...), custom_call_target="tpu_custom_call" | custom-call | flops 1207959552 | bytes 1310720 | tf_op jit(solution)/shard_map/pallas_call | solution.py:291
  20.4 1.4 %collective-permute-start.9 = (f32[72,256]{1,0:T(8,128)S(1)}, f32[72,256]{1,0:T(8,128)S(1)}, u32[]{:S(2)}, u32[]{:S(2)}) collective-permute-start(f32[72,256]{1,0:T(8,128)S(1)} %collective-permute-done.8.near_ref.near1), channel_id=1, source_target_pairs={{0,1},{1,0},{2,3},{3,2},{4,5},{5,4},{6,7},{7,6},{8,9},{9,8},{10,11... | collective-permute-start | bytes 221192 | tf_op jit(solution)/shard_map/ppermute | solution.py:21
  21.8 0.9 %collective-permute-done.9.far_ref.far1 = f32[72,256]{1,0:T(8,128)S(1)} collective-permute-done((f32[72,256]{1,0:T(8,128)S(1)}, f32[72,256]{1,0:T(8,128)S(1)}, u32[]{:S(2)}, u32[]{:S(2)}) %collective-permute-start.9) | collective-permute-done | bytes 73760 | tf_op jit(solution)/shard_map/ppermute | solution.py:21
  22.7 1.9 %shard_map.62.half_ref = f32[3,256,256]{2,1,0:T(8,128)S(1)} custom-call(f32[3,256,256]{2,1,0:T(8,128)S(1)} %get-tuple-element.42.own_ref, f32[72,256]{1,0:T(8,128)S(1)} %collective-permute-done.8.near_ref.near1, f32[72,256]{1,0:T(8,128)S(1)} %collective-permute-done.9.far_ref.far1), custom_call_target="tpu_custom_call" | custom-call | flops 905969664 | bytes 786432 | tf_op jit(solution)/shard_map/pallas_call | solution.py:291
  24.6 1.0 %collective-permute-start.10 = (f32[192,256]{1,0:T(8,128)S(1)}, f32[192,256]{1,0:T(8,128)S(1)}, u32[]{:S(2)}, u32[]{:S(2)}) collective-permute-start(f32[192,256]{1,0:T(8,128)S(1)} %collective-permute-done.7.near_ref.near2), channel_id=1, source_target_pairs={{0,1},{1,0},{2,3},{3,2},{4,5},{5,4},{6,7},{7,6},{8,9},{9,8},{10,11... | collective-permute-start | bytes 589832 | tf_op jit(solution)/shard_map/ppermute | solution.py:21
  25.5 1.1 %collective-permute-done.10.far_ref.far2 = f32[192,256]{1,0:T(8,128)S(1)} collective-permute-done((f32[192,256]{1,0:T(8,128)S(1)}, f32[192,256]{1,0:T(8,128)S(1)}, u32[]{:S(2)}, u32[]{:S(2)}) %collective-permute-start.10) | collective-permute-done | bytes 196640 | tf_op jit(solution)/shard_map/ppermute | solution.py:21
  27.2 1.4 %collective-permute-start.12 = (f32[72,256]{1,0:T(8,128)S(1)}, f32[72,256]{1,0:T(8,128)S(1)}, u32[]{:S(2)}, u32[]{:S(2)}) collective-permute-start(f32[72,256]{1,0:T(8,128)S(1)} %get-tuple-element.50), channel_id=1, source_target_pairs={{0,8},{1,9},{2,10},{3,11},{4,12},{5,13},{6,14},{7,15},{8,0},{9,1},... | collective-permute-start | bytes 221192 | tf_op jit(solution)/shard_map/ppermute | solution.py:21
  28.7 2.3 %shard_map.64.old_ref = f32[3,256,256]{2,1,0:T(8,128)S(1)} custom-call(f32[3,256,256]{2,1,0:T(8,128)S(1)} %shard_map.61.old_ref, f32[72,256]{1,0:T(8,128)S(1)} %collective-permute-done.8.near_ref.near1, f32[72,256]{1,0:T(8,128)S(1)} %collective-permute-done.9.far_ref.far1, f32[192,256]{1,0:T(8,128)S(1)} %collective-permute-done.7.near_ref.near2, ...), custom_call_target="tpu_custom_call" | custom-call | flops 1207959552 | bytes 1310720 | tf_op jit(solution)/shard_map/pallas_call | solution.py:291
  31.0 1.4 %collective-permute-start.13 = (f32[72,256]{1,0:T(8,128)S(1)}, f32[72,256]{1,0:T(8,128)S(1)}, u32[]{:S(2)}, u32[]{:S(2)}) collective-permute-start(f32[72,256]{1,0:T(8,128)S(1)} %collective-permute-done.12.near_ref.near1), channel_id=1, source_target_pairs={{0,1},{1,0},{2,3},{3,2},{4,5},{5,4},{6,7},{7,6},{8,9},{9,8},{10,11... | collective-permute-start | bytes 221192 | tf_op jit(solution)/shard_map/ppermute | solution.py:21
  32.4 0.9 %collective-permute-done.13.far_ref.far1 = f32[72,256]{1,0:T(8,128)S(1)} collective-permute-done((f32[72,256]{1,0:T(8,128)S(1)}, f32[72,256]{1,0:T(8,128)S(1)}, u32[]{:S(2)}, u32[]{:S(2)}) %collective-permute-start.13) | collective-permute-done | bytes 73760 | tf_op jit(solution)/shard_map/ppermute | solution.py:21
  33.4 1.6 %collective-permute-done.11.near_ref.near2 = f32[192,256]{1,0:T(8,128)S(1)} collective-permute-done((f32[192,256]{1,0:T(8,128)S(1)}, f32[192,256]{1,0:T(8,128)S(1)}, u32[]{:S(2)}, u32[]{:S(2)}) %collective-permute-start.11) | collective-permute-done | bytes 196640 | tf_op jit(solution)/shard_map/ppermute | solution.py:21
  35.0 1.2 %collective-permute-start.14 = (f32[192,256]{1,0:T(8,128)S(1)}, f32[192,256]{1,0:T(8,128)S(1)}, u32[]{:S(2)}, u32[]{:S(2)}) collective-permute-start(f32[192,256]{1,0:T(8,128)S(1)} %collective-permute-done.11.near_ref.near2), channel_id=1, source_target_pairs={{0,1},{1,0},{2,3},{3,2},{4,5},{5,4},{6,7},{7,6},{8,9},{9,8},{10,11... | collective-permute-start | bytes 589832 | tf_op jit(solution)/shard_map/ppermute | solution.py:21
  37.7 2.4 %collective-permute-done.17.near2 = f32[72,256]{1,0:T(8,128)S(1)} collective-permute-done((f32[72,256]{1,0:T(8,128)S(1)}, f32[72,256]{1,0:T(8,128)S(1)}, u32[]{:S(2)}, u32[]{:S(2)}) %collective-permute-start.17) | collective-permute-done | bytes 73760 | tf_op jit(solution)/shard_map/ppermute | solution.py:29
  40.1 1.2 %collective-permute-start.18 = (f32[72,256]{1,0:T(8,128)S(1)}, f32[72,256]{1,0:T(8,128)S(1)}, u32[]{:S(2)}, u32[]{:S(2)}) collective-permute-start(f32[72,256]{1,0:T(8,128)S(1)} %collective-permute-done.17.near2), channel_id=1, source_target_pairs={{0,1},{1,0},{2,3},{3,2},{4,5},{5,4},{6,7},{7,6},{8,9},{9,8},{10,11... | collective-permute-start | bytes 221192 | tf_op jit(solution)/shard_map/ppermute | solution.py:21
  41.3 2.0 %collective-permute-start.20 = (f32[200,256]{1,0:T(8,128)S(1)}, f32[200,256]{1,0:T(8,128)S(1)}, u32[]{:S(2)}, u32[]{:S(2)}) collective-permute-start(f32[200,256]{1,0:T(8,128)S(1)} %shard_map.66), channel_id=1, source_target_pairs={{0,1},{1,0},{2,3},{3,2},{4,5},{5,4},{6,7},{7,6},{8,16},{9,17},{10,... | collective-permute-start | bytes 614408 | tf_op jit(solution)/shard_map/ppermute | solution.py:29
  43.3 2.3 %shard_map.67.old_ref = f32[3,256,256]{2,1,0:T(8,128)S(1)} custom-call(f32[3,256,256]{2,1,0:T(8,128)S(1)} %shard_map.64.old_ref, f32[72,256]{1,0:T(8,128)S(1)} %collective-permute-done.12.near_ref.near1, f32[72,256]{1,0:T(8,128)S(1)} %collective-permute-done.13.far_ref.far1, f32[192,256]{1,0:T(8,128)S(1)} %collective-permute-done.11.near_ref.near2, ...), custom_call_target="tpu_custom_call" | custom-call | flops 1207959552 | bytes 1310720 | tf_op jit(solution)/shard_map/pallas_call | solution.py:291
  45.6 1.9 %shard_map.68 = (f32[3,256,256]{2,1,0:T(8,128)S(1)}, f32[1,256,256]{2,1,0:T(8,128)}, f32[1,256,256]{2,1,0:T(8,128)}, f32[1,256,256]{2,1,0:T(8,128)}) custom-call(f32[3,256,256]{2,1,0:T(8,128)S(1)} %shard_map.67.old_ref, f32[72,256]{1,0:T(8,128)S(1)} %collective-permute-done.17.near2, f32[72,256]{1,0:T(8,128)S(1)} %collective-permute-done.18.far2, ...), custom_call_target="tpu_custom_call" | custom-call | flops 905969664 | bytes 1310720 | tf_op jit(solution)/shard_map/pallas_call | solution.py:291
  47.5 0.9 %collective-permute-start.21 = (f32[200,256]{1,0:T(8,128)S(1)}, f32[200,256]{1,0:T(8,128)S(1)}, u32[]{:S(2)}, u32[]{:S(2)}) collective-permute-start(f32[200,256]{1,0:T(8,128)S(1)} %collective-permute-done.15.near3), channel_id=1, source_target_pairs={{0,1},{1,0},{2,3},{3,2},{4,5},{5,4},{6,7},{7,6},{8,9},{9,8},{10,11... | collective-permute-start | bytes 614408 | tf_op jit(solution)/shard_map/ppermute | solution.py:21
  48.3 2.1 %collective-permute-done.20.near2 = f32[200,256]{1,0:T(8,128)S(1)} collective-permute-done((f32[200,256]{1,0:T(8,128)S(1)}, f32[200,256]{1,0:T(8,128)S(1)}, u32[]{:S(2)}, u32[]{:S(2)}) %collective-permute-start.20) | collective-permute-done | bytes 204832 | tf_op jit(solution)/shard_map/ppermute | solution.py:29
  50.5 0.8 %collective-permute-start.22 = (f32[200,256]{1,0:T(8,128)S(1)}, f32[200,256]{1,0:T(8,128)S(1)}, u32[]{:S(2)}, u32[]{:S(2)}) collective-permute-start(f32[200,256]{1,0:T(8,128)S(1)} %collective-permute-done.20.near2), channel_id=1, source_target_pairs={{0,1},{1,0},{2,3},{3,2},{4,5},{5,4},{6,7},{7,6},{8,9},{9,8},{10,11... | collective-permute-start | bytes 614408 | tf_op jit(solution)/shard_map/ppermute | solution.py:21
  51.3 1.1 %collective-permute-done.22.far2 = f32[200,256]{1,0:T(8,128)S(1)} collective-permute-done((f32[200,256]{1,0:T(8,128)S(1)}, f32[200,256]{1,0:T(8,128)S(1)}, u32[]{:S(2)}, u32[]{:S(2)}) %collective-permute-start.22) | collective-permute-done | bytes 204832 | tf_op jit(solution)/shard_map/ppermute | solution.py:21
  52.3 1.3 %shard_map.69 = (f32[1,256,256]{2,1,0:T(8,128)}, f32[1,256,256]{2,1,0:T(8,128)}, f32[1,256,256]{2,1,0:T(8,128)}) custom-call(f32[3,256,256]{2,1,0:T(8,128)S(1)} %get-tuple-element.62.half_ref, f32[200,256]{1,0:T(8,128)S(1)} %collective-permute-done.20.near2, ...), custom_call_target="tpu_custom_call", output_to_operand_aliasing={{0}: (5, {}), {1}: (6, {}), {2}: (7, {})} | custom-call | flops 301989888 | bytes 1310720 | tf_op jit(solution)/shard_map/pallas_call | solution.py:291
  (27 shorter events, 5.2 us)
Async XLA Ops:
  0.6 2.4 %collective-permute-start = (f32[1,256,256]{2,1,0:T(8,128)}, f32[1,256,256]{2,1,0:T(8,128)S(1)}, u32[]{:S(2)}, u32[]{:S(2)}) collective-permute-start(f32[1,256,256]{2,1,0:T(8,128)} %param.3), channel_id=1, source_target_pairs={{0,1},{1,0},{2,3},{3,2},{4,5},{5,4},{6,7},{7,6},{8,9},{9,8},{10,11... | collective-permute-start | bytes 786440 | tf_op jit(solution)/shard_map/ppermute | solution.py:21
  1.4 1.7 %collective-permute-start.1 = (f32[1,256,256]{2,1,0:T(8,128)}, f32[1,256,256]{2,1,0:T(8,128)S(1)}, u32[]{:S(2)}, u32[]{:S(2)}) collective-permute-start(f32[1,256,256]{2,1,0:T(8,128)} %param.4), channel_id=1, source_target_pairs={{0,1},{1,0},{2,3},{3,2},{4,5},{5,4},{6,7},{7,6},{8,9},{9,8},{10,11... | collective-permute-start | bytes 786440 | tf_op jit(solution)/shard_map/ppermute | solution.py:21
  1.4 2.0 %collective-permute-start.2 = (f32[1,256,256]{2,1,0:T(8,128)}, f32[1,256,256]{2,1,0:T(8,128)S(1)}, u32[]{:S(2)}, u32[]{:S(2)}) collective-permute-start(f32[1,256,256]{2,1,0:T(8,128)} %param.5), channel_id=1, source_target_pairs={{0,1},{1,0},{2,3},{3,2},{4,5},{5,4},{6,7},{7,6},{8,9},{9,8},{10,11... | collective-permute-start | bytes 786440 | tf_op jit(solution)/shard_map/ppermute | solution.py:21
  5.8 3.3 %collective-permute-start.4 = (f32[72,256]{1,0:T(8,128)S(1)}, f32[72,256]{1,0:T(8,128)S(1)}, u32[]{:S(2)}, u32[]{:S(2)}) collective-permute-start(f32[72,256]{1,0:T(8,128)S(1)} %get-tuple-element.38), channel_id=1, source_target_pairs={{0,2},{1,3},{2,0},{3,1},{4,6},{5,7},{6,4},{7,5},{8,10},{9,11},{10,... | collective-permute-start | bytes 221192 | tf_op jit(solution)/shard_map/ppermute | solution.py:21
  7.1 6.8 %collective-permute-start.3 = (f32[192,256]{1,0:T(8,128)S(1)}, f32[192,256]{1,0:T(8,128)S(1)}, u32[]{:S(2)}, u32[]{:S(2)}) collective-permute-start(f32[192,256]{1,0:T(8,128)S(1)} %get-tuple-element.36), channel_id=1, source_target_pairs={{0,2},{1,3},{2,0},{3,1},{4,6},{5,7},{6,4},{7,5},{8,10},{9,11},{10,... | collective-permute-start | bytes 589832 | tf_op jit(solution)/shard_map/ppermute | solution.py:21
  9.1 3.0 %collective-permute-start.5 = (f32[72,256]{1,0:T(8,128)S(1)}, f32[72,256]{1,0:T(8,128)S(1)}, u32[]{:S(2)}, u32[]{:S(2)}) collective-permute-start(f32[72,256]{1,0:T(8,128)S(1)} %collective-permute-done.4.near_ref.near1), channel_id=1, source_target_pairs={{0,1},{1,0},{2,3},{3,2},{4,5},{5,4},{6,7},{7,6},{8,9},{9,8},{10,11... | collective-permute-start | bytes 221192 | tf_op jit(solution)/shard_map/ppermute | solution.py:21
  13.9 2.0 %collective-permute-start.6 = (f32[192,256]{1,0:T(8,128)S(1)}, f32[192,256]{1,0:T(8,128)S(1)}, u32[]{:S(2)}, u32[]{:S(2)}) collective-permute-start(f32[192,256]{1,0:T(8,128)S(1)} %collective-permute-done.3.near_ref.near2), channel_id=1, source_target_pairs={{0,1},{1,0},{2,3},{3,2},{4,5},{5,4},{6,7},{7,6},{8,9},{9,8},{10,11... | collective-permute-start | bytes 589832 | tf_op jit(solution)/shard_map/ppermute | solution.py:21
  16.5 3.8 %collective-permute-start.8 = (f32[72,256]{1,0:T(8,128)S(1)}, f32[72,256]{1,0:T(8,128)S(1)}, u32[]{:S(2)}, u32[]{:S(2)}) collective-permute-start(f32[72,256]{1,0:T(8,128)S(1)} %get-tuple-element.43), channel_id=1, source_target_pairs={{0,4},{1,5},{2,6},{3,7},{4,0},{5,1},{6,2},{7,3},{8,12},{9,13},{10,... | collective-permute-start | bytes 221192 | tf_op jit(solution)/shard_map/ppermute | solution.py:21
  17.8 6.7 %collective-permute-start.7 = (f32[192,256]{1,0:T(8,128)S(1)}, f32[192,256]{1,0:T(8,128)S(1)}, u32[]{:S(2)}, u32[]{:S(2)}) collective-permute-start(f32[192,256]{1,0:T(8,128)S(1)} %get-tuple-element.41), channel_id=1, source_target_pairs={{0,4},{1,5},{2,6},{3,7},{4,0},{5,1},{6,2},{7,3},{8,12},{9,13},{10,... | collective-permute-start | bytes 589832 | tf_op jit(solution)/shard_map/ppermute | solution.py:21
  20.4 2.3 %collective-permute-start.9 = (f32[72,256]{1,0:T(8,128)S(1)}, f32[72,256]{1,0:T(8,128)S(1)}, u32[]{:S(2)}, u32[]{:S(2)}) collective-permute-start(f32[72,256]{1,0:T(8,128)S(1)} %collective-permute-done.8.near_ref.near1), channel_id=1, source_target_pairs={{0,1},{1,0},{2,3},{3,2},{4,5},{5,4},{6,7},{7,6},{8,9},{9,8},{10,11... | collective-permute-start | bytes 221192 | tf_op jit(solution)/shard_map/ppermute | solution.py:21
  24.6 2.0 %collective-permute-start.10 = (f32[192,256]{1,0:T(8,128)S(1)}, f32[192,256]{1,0:T(8,128)S(1)}, u32[]{:S(2)}, u32[]{:S(2)}) collective-permute-start(f32[192,256]{1,0:T(8,128)S(1)} %collective-permute-done.7.near_ref.near2), channel_id=1, source_target_pairs={{0,1},{1,0},{2,3},{3,2},{4,5},{5,4},{6,7},{7,6},{8,9},{9,8},{10,11... | collective-permute-start | bytes 589832 | tf_op jit(solution)/shard_map/ppermute | solution.py:21
  27.2 3.8 %collective-permute-start.12 = (f32[72,256]{1,0:T(8,128)S(1)}, f32[72,256]{1,0:T(8,128)S(1)}, u32[]{:S(2)}, u32[]{:S(2)}) collective-permute-start(f32[72,256]{1,0:T(8,128)S(1)} %get-tuple-element.50), channel_id=1, source_target_pairs={{0,8},{1,9},{2,10},{3,11},{4,12},{5,13},{6,14},{7,15},{8,0},{9,1},... | collective-permute-start | bytes 221192 | tf_op jit(solution)/shard_map/ppermute | solution.py:21
  28.6 6.5 %collective-permute-start.11 = (f32[192,256]{1,0:T(8,128)S(1)}, f32[192,256]{1,0:T(8,128)S(1)}, u32[]{:S(2)}, u32[]{:S(2)}) collective-permute-start(f32[192,256]{1,0:T(8,128)S(1)} %get-tuple-element.48), channel_id=1, source_target_pairs={{0,8},{1,9},{2,10},{3,11},{4,12},{5,13},{6,14},{7,15},{8,0},{9,1},... | collective-permute-start | bytes 589832 | tf_op jit(solution)/shard_map/ppermute | solution.py:21
  31.0 2.3 %collective-permute-start.13 = (f32[72,256]{1,0:T(8,128)S(1)}, f32[72,256]{1,0:T(8,128)S(1)}, u32[]{:S(2)}, u32[]{:S(2)}) collective-permute-start(f32[72,256]{1,0:T(8,128)S(1)} %collective-permute-done.12.near_ref.near1), channel_id=1, source_target_pairs={{0,1},{1,0},{2,3},{3,2},{4,5},{5,4},{6,7},{7,6},{8,9},{9,8},{10,11... | collective-permute-start | bytes 221192 | tf_op jit(solution)/shard_map/ppermute | solution.py:21
  35.0 2.3 %collective-permute-start.14 = (f32[192,256]{1,0:T(8,128)S(1)}, f32[192,256]{1,0:T(8,128)S(1)}, u32[]{:S(2)}, u32[]{:S(2)}) collective-permute-start(f32[192,256]{1,0:T(8,128)S(1)} %collective-permute-done.11.near_ref.near2), channel_id=1, source_target_pairs={{0,1},{1,0},{2,3},{3,2},{4,5},{5,4},{6,7},{7,6},{8,9},{9,8},{10,11... | collective-permute-start | bytes 589832 | tf_op jit(solution)/shard_map/ppermute | solution.py:21
  36.2 3.9 %collective-permute-start.17 = (f32[72,256]{1,0:T(8,128)S(1)}, f32[72,256]{1,0:T(8,128)S(1)}, u32[]{:S(2)}, u32[]{:S(2)}) collective-permute-start(f32[72,256]{1,0:T(8,128)S(1)} %get-tuple-element.56), channel_id=1, source_target_pairs={{0,1},{1,0},{2,3},{3,2},{4,5},{5,4},{6,7},{7,6},{8,16},{9,17},{10,... | collective-permute-start | bytes 221192 | tf_op jit(solution)/shard_map/ppermute | solution.py:29
  36.3 3.8 %collective-permute-start.16 = (f32[72,256]{1,0:T(8,128)S(1)}, f32[72,256]{1,0:T(8,128)S(1)}, u32[]{:S(2)}, u32[]{:S(2)}) collective-permute-start(f32[72,256]{1,0:T(8,128)S(1)} %get-tuple-element.56), channel_id=1, source_target_pairs={{0,1},{1,0},{2,3},{3,2},{4,5},{5,4},{6,7},{7,6},{8,24},{9,25},{10,... | collective-permute-start | bytes 221192 | tf_op jit(solution)/shard_map/ppermute | solution.py:29
  37.3 10.2 %collective-permute-start.15 = (f32[200,256]{1,0:T(8,128)S(1)}, f32[200,256]{1,0:T(8,128)S(1)}, u32[]{:S(2)}, u32[]{:S(2)}) collective-permute-start(f32[200,256]{1,0:T(8,128)S(1)} %shard_map.66), channel_id=1, source_target_pairs={{0,1},{1,0},{2,3},{3,2},{4,5},{5,4},{6,7},{7,6},{8,24},{9,25},{10,... | collective-permute-start | bytes 614408 | tf_op jit(solution)/shard_map/ppermute | solution.py:29
  40.1 5.4 %collective-permute-start.18 = (f32[72,256]{1,0:T(8,128)S(1)}, f32[72,256]{1,0:T(8,128)S(1)}, u32[]{:S(2)}, u32[]{:S(2)}) collective-permute-start(f32[72,256]{1,0:T(8,128)S(1)} %collective-permute-done.17.near2), channel_id=1, source_target_pairs={{0,1},{1,0},{2,3},{3,2},{4,5},{5,4},{6,7},{7,6},{8,9},{9,8},{10,11... | collective-permute-start | bytes 221192 | tf_op jit(solution)/shard_map/ppermute | solution.py:21
  41.3 4.3 %collective-permute-start.19 = (f32[72,256]{1,0:T(8,128)S(1)}, f32[72,256]{1,0:T(8,128)S(1)}, u32[]{:S(2)}, u32[]{:S(2)}) collective-permute-start(f32[72,256]{1,0:T(8,128)S(1)} %collective-permute-done.16.near3), channel_id=1, source_target_pairs={{0,1},{1,0},{2,3},{3,2},{4,5},{5,4},{6,7},{7,6},{8,9},{9,8},{10,11... | collective-permute-start | bytes 221192 | tf_op jit(solution)/shard_map/ppermute | solution.py:21
  41.3 9.2 %collective-permute-start.20 = (f32[200,256]{1,0:T(8,128)S(1)}, f32[200,256]{1,0:T(8,128)S(1)}, u32[]{:S(2)}, u32[]{:S(2)}) collective-permute-start(f32[200,256]{1,0:T(8,128)S(1)} %shard_map.66), channel_id=1, source_target_pairs={{0,1},{1,0},{2,3},{3,2},{4,5},{5,4},{6,7},{7,6},{8,16},{9,17},{10,... | collective-permute-start | bytes 614408 | tf_op jit(solution)/shard_map/ppermute | solution.py:29
  47.5 3.0 %collective-permute-start.21 = (f32[200,256]{1,0:T(8,128)S(1)}, f32[200,256]{1,0:T(8,128)S(1)}, u32[]{:S(2)}, u32[]{:S(2)}) collective-permute-start(f32[200,256]{1,0:T(8,128)S(1)} %collective-permute-done.15.near3), channel_id=1, source_target_pairs={{0,1},{1,0},{2,3},{3,2},{4,5},{5,4},{6,7},{7,6},{8,9},{9,8},{10,11... | collective-permute-start | bytes 614408 | tf_op jit(solution)/shard_map/ppermute | solution.py:21
  50.5 1.9 %collective-permute-start.22 = (f32[200,256]{1,0:T(8,128)S(1)}, f32[200,256]{1,0:T(8,128)S(1)}, u32[]{:S(2)}, u32[]{:S(2)}) collective-permute-start(f32[200,256]{1,0:T(8,128)S(1)} %collective-permute-done.20.near2), channel_id=1, source_target_pairs={{0,1},{1,0},{2,3},{3,2},{4,5},{5,4},{6,7},{7,6},{8,9},{9,8},{10,11... | collective-permute-start | bytes 614408 | tf_op jit(solution)/shard_map/ppermute | solution.py:21

commit v14 on v13

--- a/solution.py
+++ b/solution.py
@@ -338,10 +338,8 @@
     one, sems = (1, m, m), pltpu.SemaphoreType.DMA((3,))
     kernel = functools.partial(last_early_kernel, distance)
     halfway, *given = call(kernel, 27, [stack, one, one, one], *args, copied=3, scratch=[sems])
-    near3, halfway = lax.optimization_barrier((near3, halfway))
-    far3 = swap(near3, 1)
-    near2, far3 = lax.optimization_barrier((near2, far3))
-    args = halfway, near2, swap(near2, 1), near3, far3
+    near2, near3, halfway = lax.optimization_barrier((near2, near3, halfway))
+    args = halfway, near2, swap(near2, 1), near3, swap(near3, 1)
     scratch = [pltpu.VMEM((2, m, m), F32), sems]
     return tuple(call(functools.partial(last_kernel, distance), 9, [one] * 3, *args, given=given, copied=3, scratch=scratch))
 

time: 53.9 us -> 54.3 us (level)
  waiting for transfers between devices: 15 us -> 15.7 us
    ppermute x19, starting transfers between devices: 16.6 us -> 15.7 us  [swap(): return lax.ppermute(block, AXES, [(i, i ^ distance) for i in range(count)])]
where the time goes in v14:
time: 54.3 us; the launch traced here: 54.2 us
  starting transfers between devices  19 us (35%)
  Pallas kernels  17.3 us (32%)
  waiting for transfers between devices  15.7 us (29%)
  other arithmetic  1.16 us (2%)
  between operations  0.96 us (2%)
    pallas_call x12, Pallas kernels, call(): pl.pallas_call(kernel, out_shape=[jax.ShapeDtypeStruct(s, F32) for s in o...  17.3 us
    ppermute x19, starting transfers between devices, swap(): return lax.ppermute(block, AXES, [(i, i ^ distance) for i in range(count)])  15.7 us
    ppermute x19, waiting for transfers between devices, swap(): return lax.ppermute(block, AXES, [(i, i ^ distance) for i in range(count)])  10.8 us
    ppermute x4, waiting for transfers between devices, pair(): lax.ppermute(block, AXES, [(i, step.get(i // quarter, lambda i: i ^ 1)(i)...  4.92 us
    ppermute x4, starting transfers between devices, pair(): lax.ppermute(block, AXES, [(i, step.get(i // quarter, lambda i: i ^ 1)(i)...  3.24 us
    concatenate x1, other arithmetic, shards(): section = jnp.concatenate(sections, 0)  1.16 us
  transfers between devices with their start and end apart: 23, of which 13 were waited for; matrix products, arithmetic and copies ran while one was open for 2% of the time, Pallas kernels for 23%

profile of v14, /device:TPU:17, one launch (start us, length us, event | category | flops | bytes accessed | tf_op | source)
XLA Modules:
  0.0 54.2 jit_solution(13340476103576851404)
XLA Ops:
  0.6 0.7 %collective-permute-start = (f32[1,256,256]{2,1,0:T(8,128)}, f32[1,256,256]{2,1,0:T(8,128)S(1)}, u32[]{:S(2)}, u32[]{:S(2)}) collective-permute-start(f32[1,256,256]{2,1,0:T(8,128)} %param.3), channel_id=1, source_target_pairs={{0,1},{1,0},{2,3},{3,2},{4,5},{5,4},{6,7},{7,6},{8,9},{9,8},{10,11... | collective-permute-start | bytes 786440 | tf_op jit(solution)/shard_map/ppermute | solution.py:21
  1.9 1.2 %pad_maximum_fusion.section_ref = f32[3,256,256]{2,1,0:T(8,128)S(1)} fusion(f32[1,256,256]{2,1,0:T(8,128)} %param.5, f32[1,256,256]{2,1,0:T(8,128)} %param.4, f32[1,256,256]{2,1,0:T(8,128)} %param.3), kind=kLoop, calls=%fused_computation | loop fusion | flops 393216 | bytes 1572864 | tf_op jit(solution)/shard_map/concatenate | solution.py:310
  3.5 2.3 %shard_map.58 = (f32[3,256,256]{2,1,0:T(8,128)S(1)}, f32[72,256]{1,0:T(8,128)S(1)}, f32[192,256]{1,0:T(8,128)S(1)}, f32[3,256,256]{2,1,0:T(8,128)S(1)}) custom-call(f32[3,256,256]{2,1,0:T(8,128)S(1)} %pad_maximum_fusion.section_ref, f32[1,256,256]{2,1,0:T(8,128)S(1)} %collective-permute-done.got1, f32[1,256,256]{2,1,0:T(8,128)S(1)} %collective-permute-done.1.got2, ...), custom_call_target="tpu_custom_call" | custom-call | flops 1207959552 | bytes 1048576 | tf_op jit(solution)/shard_map/pallas_call | solution.py:291
  5.8 1.3 %collective-permute-start.4 = (f32[72,256]{1,0:T(8,128)S(1)}, f32[72,256]{1,0:T(8,128)S(1)}, u32[]{:S(2)}, u32[]{:S(2)}) collective-permute-start(f32[72,256]{1,0:T(8,128)S(1)} %get-tuple-element.37), channel_id=1, source_target_pairs={{0,2},{1,3},{2,0},{3,1},{4,6},{5,7},{6,4},{7,5},{8,10},{9,11},{10,... | collective-permute-start | bytes 221192 | tf_op jit(solution)/shard_map/ppermute | solution.py:21
  7.3 1.7 %collective-permute-done.4.near_ref.near1 = f32[72,256]{1,0:T(8,128)S(1)} collective-permute-done((f32[72,256]{1,0:T(8,128)S(1)}, f32[72,256]{1,0:T(8,128)S(1)}, u32[]{:S(2)}, u32[]{:S(2)}) %collective-permute-start.4) | collective-permute-done | bytes 73760 | tf_op jit(solution)/shard_map/ppermute | solution.py:21
  9.1 2.0 %collective-permute-start.5 = (f32[72,256]{1,0:T(8,128)S(1)}, f32[72,256]{1,0:T(8,128)S(1)}, u32[]{:S(2)}, u32[]{:S(2)}) collective-permute-start(f32[72,256]{1,0:T(8,128)S(1)} %collective-permute-done.4.near_ref.near1), channel_id=1, source_target_pairs={{0,1},{1,0},{2,3},{3,2},{4,5},{5,4},{6,7},{7,6},{8,9},{9,8},{10,11... | collective-permute-start | bytes 221192 | tf_op jit(solution)/shard_map/ppermute | solution.py:21
  11.1 0.9 %collective-permute-done.5.far_ref.far1 = f32[72,256]{1,0:T(8,128)S(1)} collective-permute-done((f32[72,256]{1,0:T(8,128)S(1)}, f32[72,256]{1,0:T(8,128)S(1)}, u32[]{:S(2)}, u32[]{:S(2)}) %collective-permute-start.5) | collective-permute-done | bytes 73760 | tf_op jit(solution)/shard_map/ppermute | solution.py:21
  12.0 1.9 %shard_map.59.half_ref = f32[3,256,256]{2,1,0:T(8,128)S(1)} custom-call(f32[3,256,256]{2,1,0:T(8,128)S(1)} %get-tuple-element.36.own_ref, f32[72,256]{1,0:T(8,128)S(1)} %collective-permute-done.4.near_ref.near1, f32[72,256]{1,0:T(8,128)S(1)} %collective-permute-done.5.far_ref.far1), custom_call_target="tpu_custom_call" | custom-call | flops 905969664 | bytes 786432 | tf_op jit(solution)/shard_map/pallas_call | solution.py:291
  13.9 0.9 %collective-permute-start.6 = (f32[192,256]{1,0:T(8,128)S(1)}, f32[192,256]{1,0:T(8,128)S(1)}, u32[]{:S(2)}, u32[]{:S(2)}) collective-permute-start(f32[192,256]{1,0:T(8,128)S(1)} %collective-permute-done.3.near_ref.near2), channel_id=1, source_target_pairs={{0,1},{1,0},{2,3},{3,2},{4,5},{5,4},{6,7},{7,6},{8,9},{9,8},{10,11... | collective-permute-start | bytes 589832 | tf_op jit(solution)/shard_map/ppermute | solution.py:21
  14.8 1.1 %collective-permute-done.6.far_ref.far2 = f32[192,256]{1,0:T(8,128)S(1)} collective-permute-done((f32[192,256]{1,0:T(8,128)S(1)}, f32[192,256]{1,0:T(8,128)S(1)}, u32[]{:S(2)}, u32[]{:S(2)}) %collective-permute-start.6) | collective-permute-done | bytes 196640 | tf_op jit(solution)/shard_map/ppermute | solution.py:21
  16.5 1.3 %collective-permute-start.8 = (f32[72,256]{1,0:T(8,128)S(1)}, f32[72,256]{1,0:T(8,128)S(1)}, u32[]{:S(2)}, u32[]{:S(2)}) collective-permute-start(f32[72,256]{1,0:T(8,128)S(1)} %get-tuple-element.42), channel_id=1, source_target_pairs={{0,4},{1,5},{2,6},{3,7},{4,0},{5,1},{6,2},{7,3},{8,12},{9,13},{10,... | collective-permute-start | bytes 221192 | tf_op jit(solution)/shard_map/ppermute | solution.py:21
  18.1 2.3 %shard_map.61.old_ref = f32[3,256,256]{2,1,0:T(8,128)S(1)} custom-call(f32[3,256,256]{2,1,0:T(8,128)S(1)} %get-tuple-element.43.old_ref, f32[72,256]{1,0:T(8,128)S(1)} %collective-permute-done.4.near_ref.near1, f32[72,256]{1,0:T(8,128)S(1)} %collective-permute-done.5.far_ref.far1, f32[192,256]{1,0:T(8,128)S(1)} %collective-permute-done.3.near_ref.near2, ...), custom_call_target="tpu_custom_call" | custom-call | flops 1207959552 | bytes 1310720 | tf_op jit(solution)/shard_map/pallas_call | solution.py:291
  20.4 1.4 %collective-permute-start.9 = (f32[72,256]{1,0:T(8,128)S(1)}, f32[72,256]{1,0:T(8,128)S(1)}, u32[]{:S(2)}, u32[]{:S(2)}) collective-permute-start(f32[72,256]{1,0:T(8,128)S(1)} %collective-permute-done.8.near_ref.near1), channel_id=1, source_target_pairs={{0,1},{1,0},{2,3},{3,2},{4,5},{5,4},{6,7},{7,6},{8,9},{9,8},{10,11... | collective-permute-start | bytes 221192 | tf_op jit(solution)/shard_map/ppermute | solution.py:21
  21.8 0.9 %collective-permute-done.9.far_ref.far1 = f32[72,256]{1,0:T(8,128)S(1)} collective-permute-done((f32[72,256]{1,0:T(8,128)S(1)}, f32[72,256]{1,0:T(8,128)S(1)}, u32[]{:S(2)}, u32[]{:S(2)}) %collective-permute-start.9) | collective-permute-done | bytes 73760 | tf_op jit(solution)/shard_map/ppermute | solution.py:21
  22.7 1.9 %shard_map.62.half_ref = f32[3,256,256]{2,1,0:T(8,128)S(1)} custom-call(f32[3,256,256]{2,1,0:T(8,128)S(1)} %get-tuple-element.41.own_ref, f32[72,256]{1,0:T(8,128)S(1)} %collective-permute-done.8.near_ref.near1, f32[72,256]{1,0:T(8,128)S(1)} %collective-permute-done.9.far_ref.far1), custom_call_target="tpu_custom_call" | custom-call | flops 905969664 | bytes 786432 | tf_op jit(solution)/shard_map/pallas_call | solution.py:291
  24.6 1.0 %collective-permute-start.10 = (f32[192,256]{1,0:T(8,128)S(1)}, f32[192,256]{1,0:T(8,128)S(1)}, u32[]{:S(2)}, u32[]{:S(2)}) collective-permute-start(f32[192,256]{1,0:T(8,128)S(1)} %collective-permute-done.7.near_ref.near2), channel_id=1, source_target_pairs={{0,1},{1,0},{2,3},{3,2},{4,5},{5,4},{6,7},{7,6},{8,9},{9,8},{10,11... | collective-permute-start | bytes 589832 | tf_op jit(solution)/shard_map/ppermute | solution.py:21
  25.5 1.1 %collective-permute-done.10.far_ref.far2 = f32[192,256]{1,0:T(8,128)S(1)} collective-permute-done((f32[192,256]{1,0:T(8,128)S(1)}, f32[192,256]{1,0:T(8,128)S(1)}, u32[]{:S(2)}, u32[]{:S(2)}) %collective-permute-start.10) | collective-permute-done | bytes 196640 | tf_op jit(solution)/shard_map/ppermute | solution.py:21
  27.2 1.4 %collective-permute-start.12 = (f32[72,256]{1,0:T(8,128)S(1)}, f32[72,256]{1,0:T(8,128)S(1)}, u32[]{:S(2)}, u32[]{:S(2)}) collective-permute-start(f32[72,256]{1,0:T(8,128)S(1)} %get-tuple-element.49), channel_id=1, source_target_pairs={{0,8},{1,9},{2,10},{3,11},{4,12},{5,13},{6,14},{7,15},{8,0},{9,1},... | collective-permute-start | bytes 221192 | tf_op jit(solution)/shard_map/ppermute | solution.py:21
  28.7 2.3 %shard_map.64.old_ref = f32[3,256,256]{2,1,0:T(8,128)S(1)} custom-call(f32[3,256,256]{2,1,0:T(8,128)S(1)} %shard_map.61.old_ref, f32[72,256]{1,0:T(8,128)S(1)} %collective-permute-done.8.near_ref.near1, f32[72,256]{1,0:T(8,128)S(1)} %collective-permute-done.9.far_ref.far1, f32[192,256]{1,0:T(8,128)S(1)} %collective-permute-done.7.near_ref.near2, ...), custom_call_target="tpu_custom_call" | custom-call | flops 1207959552 | bytes 1310720 | tf_op jit(solution)/shard_map/pallas_call | solution.py:291
  31.0 1.4 %collective-permute-start.13 = (f32[72,256]{1,0:T(8,128)S(1)}, f32[72,256]{1,0:T(8,128)S(1)}, u32[]{:S(2)}, u32[]{:S(2)}) collective-permute-start(f32[72,256]{1,0:T(8,128)S(1)} %collective-permute-done.12.near_ref.near1), channel_id=1, source_target_pairs={{0,1},{1,0},{2,3},{3,2},{4,5},{5,4},{6,7},{7,6},{8,9},{9,8},{10,11... | collective-permute-start | bytes 221192 | tf_op jit(solution)/shard_map/ppermute | solution.py:21
  32.4 0.9 %collective-permute-done.13.far_ref.far1 = f32[72,256]{1,0:T(8,128)S(1)} collective-permute-done((f32[72,256]{1,0:T(8,128)S(1)}, f32[72,256]{1,0:T(8,128)S(1)}, u32[]{:S(2)}, u32[]{:S(2)}) %collective-permute-start.13) | collective-permute-done | bytes 73760 | tf_op jit(solution)/shard_map/ppermute | solution.py:21
  33.4 1.6 %collective-permute-done.11.near_ref.near2 = f32[192,256]{1,0:T(8,128)S(1)} collective-permute-done((f32[192,256]{1,0:T(8,128)S(1)}, f32[192,256]{1,0:T(8,128)S(1)}, u32[]{:S(2)}, u32[]{:S(2)}) %collective-permute-start.11) | collective-permute-done | bytes 196640 | tf_op jit(solution)/shard_map/ppermute | solution.py:21
  35.0 1.2 %collective-permute-start.14 = (f32[192,256]{1,0:T(8,128)S(1)}, f32[192,256]{1,0:T(8,128)S(1)}, u32[]{:S(2)}, u32[]{:S(2)}) collective-permute-start(f32[192,256]{1,0:T(8,128)S(1)} %collective-permute-done.11.near_ref.near2), channel_id=1, source_target_pairs={{0,1},{1,0},{2,3},{3,2},{4,5},{5,4},{6,7},{7,6},{8,9},{9,8},{10,11... | collective-permute-start | bytes 589832 | tf_op jit(solution)/shard_map/ppermute | solution.py:21
  36.6 0.7 %collective-permute-done.14.far_ref.far2 = f32[192,256]{1,0:T(8,128)S(1)} collective-permute-done((f32[192,256]{1,0:T(8,128)S(1)}, f32[192,256]{1,0:T(8,128)S(1)}, u32[]{:S(2)}, u32[]{:S(2)}) %collective-permute-start.14) | collective-permute-done | bytes 196640 | tf_op jit(solution)/shard_map/ppermute | solution.py:21
  37.7 2.4 %collective-permute-start.15 = (f32[200,256]{1,0:T(8,128)S(1)}, f32[200,256]{1,0:T(8,128)S(1)}, u32[]{:S(2)}, u32[]{:S(2)}) collective-permute-start(f32[200,256]{1,0:T(8,128)S(1)} %shard_map.66), channel_id=1, source_target_pairs={{0,1},{1,0},{2,3},{3,2},{4,5},{5,4},{6,7},{7,6},{8,16},{9,17},{10,... | collective-permute-start | bytes 614408 | tf_op jit(solution)/shard_map/ppermute | solution.py:29
  40.1 1.1 %collective-permute-start.19 = (f32[72,256]{1,0:T(8,128)S(1)}, f32[72,256]{1,0:T(8,128)S(1)}, u32[]{:S(2)}, u32[]{:S(2)}) collective-permute-start(f32[72,256]{1,0:T(8,128)S(1)} %collective-permute-done.18.near2), channel_id=1, source_target_pairs={{0,1},{1,0},{2,3},{3,2},{4,5},{5,4},{6,7},{7,6},{8,9},{9,8},{10,11... | collective-permute-start | bytes 221192 | tf_op jit(solution)/shard_map/ppermute | solution.py:21
  41.3 2.3 %shard_map.67.old_ref = f32[3,256,256]{2,1,0:T(8,128)S(1)} custom-call(f32[3,256,256]{2,1,0:T(8,128)S(1)} %shard_map.64.old_ref, f32[72,256]{1,0:T(8,128)S(1)} %collective-permute-done.12.near_ref.near1, f32[72,256]{1,0:T(8,128)S(1)} %collective-permute-done.13.far_ref.far1, f32[192,256]{1,0:T(8,128)S(1)} %collective-permute-done.11.near_ref.near2, ...), custom_call_target="tpu_custom_call" | custom-call | flops 1207959552 | bytes 1310720 | tf_op jit(solution)/shard_map/pallas_call | solution.py:291
  43.6 1.9 %shard_map.68 = (f32[3,256,256]{2,1,0:T(8,128)S(1)}, f32[1,256,256]{2,1,0:T(8,128)}, f32[1,256,256]{2,1,0:T(8,128)}, f32[1,256,256]{2,1,0:T(8,128)}) custom-call(f32[3,256,256]{2,1,0:T(8,128)S(1)} %shard_map.67.old_ref, f32[72,256]{1,0:T(8,128)S(1)} %collective-permute-done.18.near2, f32[72,256]{1,0:T(8,128)S(1)} %collective-permute-done.19.far2, ...), custom_call_target="tpu_custom_call" | custom-call | flops 905969664 | bytes 1310720 | tf_op jit(solution)/shard_map/pallas_call | solution.py:291
  45.6 4.9 %collective-permute-done.15.near2 = f32[200,256]{1,0:T(8,128)S(1)} collective-permute-done((f32[200,256]{1,0:T(8,128)S(1)}, f32[200,256]{1,0:T(8,128)S(1)}, u32[]{:S(2)}, u32[]{:S(2)}) %collective-permute-start.15) | collective-permute-done | bytes 204832 | tf_op jit(solution)/shard_map/ppermute | solution.py:29
  50.5 0.8 %collective-permute-start.21 = (f32[200,256]{1,0:T(8,128)S(1)}, f32[200,256]{1,0:T(8,128)S(1)}, u32[]{:S(2)}, u32[]{:S(2)}) collective-permute-start(f32[200,256]{1,0:T(8,128)S(1)} %collective-permute-done.15.near2), channel_id=1, source_target_pairs={{0,1},{1,0},{2,3},{3,2},{4,5},{5,4},{6,7},{7,6},{8,9},{9,8},{10,11... | collective-permute-start | bytes 614408 | tf_op jit(solution)/shard_map/ppermute | solution.py:21
  51.3 1.1 %collective-permute-done.21.far2 = f32[200,256]{1,0:T(8,128)S(1)} collective-permute-done((f32[200,256]{1,0:T(8,128)S(1)}, f32[200,256]{1,0:T(8,128)S(1)}, u32[]{:S(2)}, u32[]{:S(2)}) %collective-permute-start.21) | collective-permute-done | bytes 204832 | tf_op jit(solution)/shard_map/ppermute | solution.py:21
  52.7 1.3 %shard_map.69 = (f32[1,256,256]{2,1,0:T(8,128)}, f32[1,256,256]{2,1,0:T(8,128)}, f32[1,256,256]{2,1,0:T(8,128)}) custom-call(f32[3,256,256]{2,1,0:T(8,128)S(1)} %get-tuple-element.61.half_ref, f32[200,256]{1,0:T(8,128)S(1)} %collective-permute-done.15.near2, ...), custom_call_target="tpu_custom_call", output_to_operand_aliasing={{0}: (5, {}), {1}: (6, {}), {2}: (7, {})} | custom-call | flops 301989888 | bytes 1310720 | tf_op jit(solution)/shard_map/pallas_call | solution.py:291
  (27 shorter events, 4.2 us)
Async XLA Ops:
  0.6 2.4 %collective-permute-start = (f32[1,256,256]{2,1,0:T(8,128)}, f32[1,256,256]{2,1,0:T(8,128)S(1)}, u32[]{:S(2)}, u32[]{:S(2)}) collective-permute-start(f32[1,256,256]{2,1,0:T(8,128)} %param.3), channel_id=1, source_target_pairs={{0,1},{1,0},{2,3},{3,2},{4,5},{5,4},{6,7},{7,6},{8,9},{9,8},{10,11... | collective-permute-start | bytes 786440 | tf_op jit(solution)/shard_map/ppermute | solution.py:21
  1.4 1.7 %collective-permute-start.1 = (f32[1,256,256]{2,1,0:T(8,128)}, f32[1,256,256]{2,1,0:T(8,128)S(1)}, u32[]{:S(2)}, u32[]{:S(2)}) collective-permute-start(f32[1,256,256]{2,1,0:T(8,128)} %param.4), channel_id=1, source_target_pairs={{0,1},{1,0},{2,3},{3,2},{4,5},{5,4},{6,7},{7,6},{8,9},{9,8},{10,11... | collective-permute-start | bytes 786440 | tf_op jit(solution)/shard_map/ppermute | solution.py:21
  1.4 2.0 %collective-permute-start.2 = (f32[1,256,256]{2,1,0:T(8,128)}, f32[1,256,256]{2,1,0:T(8,128)S(1)}, u32[]{:S(2)}, u32[]{:S(2)}) collective-permute-start(f32[1,256,256]{2,1,0:T(8,128)} %param.5), channel_id=1, source_target_pairs={{0,1},{1,0},{2,3},{3,2},{4,5},{5,4},{6,7},{7,6},{8,9},{9,8},{10,11... | collective-permute-start | bytes 786440 | tf_op jit(solution)/shard_map/ppermute | solution.py:21
  5.8 3.3 %collective-permute-start.4 = (f32[72,256]{1,0:T(8,128)S(1)}, f32[72,256]{1,0:T(8,128)S(1)}, u32[]{:S(2)}, u32[]{:S(2)}) collective-permute-start(f32[72,256]{1,0:T(8,128)S(1)} %get-tuple-element.37), channel_id=1, source_target_pairs={{0,2},{1,3},{2,0},{3,1},{4,6},{5,7},{6,4},{7,5},{8,10},{9,11},{10,... | collective-permute-start | bytes 221192 | tf_op jit(solution)/shard_map/ppermute | solution.py:21
  7.1 6.8 %collective-permute-start.3 = (f32[192,256]{1,0:T(8,128)S(1)}, f32[192,256]{1,0:T(8,128)S(1)}, u32[]{:S(2)}, u32[]{:S(2)}) collective-permute-start(f32[192,256]{1,0:T(8,128)S(1)} %get-tuple-element.35), channel_id=1, source_target_pairs={{0,2},{1,3},{2,0},{3,1},{4,6},{5,7},{6,4},{7,5},{8,10},{9,11},{10,... | collective-permute-start | bytes 589832 | tf_op jit(solution)/shard_map/ppermute | solution.py:21
  9.1 3.0 %collective-permute-start.5 = (f32[72,256]{1,0:T(8,128)S(1)}, f32[72,256]{1,0:T(8,128)S(1)}, u32[]{:S(2)}, u32[]{:S(2)}) collective-permute-start(f32[72,256]{1,0:T(8,128)S(1)} %collective-permute-done.4.near_ref.near1), channel_id=1, source_target_pairs={{0,1},{1,0},{2,3},{3,2},{4,5},{5,4},{6,7},{7,6},{8,9},{9,8},{10,11... | collective-permute-start | bytes 221192 | tf_op jit(solution)/shard_map/ppermute | solution.py:21
  13.9 2.0 %collective-permute-start.6 = (f32[192,256]{1,0:T(8,128)S(1)}, f32[192,256]{1,0:T(8,128)S(1)}, u32[]{:S(2)}, u32[]{:S(2)}) collective-permute-start(f32[192,256]{1,0:T(8,128)S(1)} %collective-permute-done.3.near_ref.near2), channel_id=1, source_target_pairs={{0,1},{1,0},{2,3},{3,2},{4,5},{5,4},{6,7},{7,6},{8,9},{9,8},{10,11... | collective-permute-start | bytes 589832 | tf_op jit(solution)/shard_map/ppermute | solution.py:21
  16.5 3.8 %collective-permute-start.8 = (f32[72,256]{1,0:T(8,128)S(1)}, f32[72,256]{1,0:T(8,128)S(1)}, u32[]{:S(2)}, u32[]{:S(2)}) collective-permute-start(f32[72,256]{1,0:T(8,128)S(1)} %get-tuple-element.42), channel_id=1, source_target_pairs={{0,4},{1,5},{2,6},{3,7},{4,0},{5,1},{6,2},{7,3},{8,12},{9,13},{10,... | collective-permute-start | bytes 221192 | tf_op jit(solution)/shard_map/ppermute | solution.py:21
  17.8 6.7 %collective-permute-start.7 = (f32[192,256]{1,0:T(8,128)S(1)}, f32[192,256]{1,0:T(8,128)S(1)}, u32[]{:S(2)}, u32[]{:S(2)}) collective-permute-start(f32[192,256]{1,0:T(8,128)S(1)} %get-tuple-element.40), channel_id=1, source_target_pairs={{0,4},{1,5},{2,6},{3,7},{4,0},{5,1},{6,2},{7,3},{8,12},{9,13},{10,... | collective-permute-start | bytes 589832 | tf_op jit(solution)/shard_map/ppermute | solution.py:21
  20.4 2.3 %collective-permute-start.9 = (f32[72,256]{1,0:T(8,128)S(1)}, f32[72,256]{1,0:T(8,128)S(1)}, u32[]{:S(2)}, u32[]{:S(2)}) collective-permute-start(f32[72,256]{1,0:T(8,128)S(1)} %collective-permute-done.8.near_ref.near1), channel_id=1, source_target_pairs={{0,1},{1,0},{2,3},{3,2},{4,5},{5,4},{6,7},{7,6},{8,9},{9,8},{10,11... | collective-permute-start | bytes 221192 | tf_op jit(solution)/shard_map/ppermute | solution.py:21
  24.6 2.0 %collective-permute-start.10 = (f32[192,256]{1,0:T(8,128)S(1)}, f32[192,256]{1,0:T(8,128)S(1)}, u32[]{:S(2)}, u32[]{:S(2)}) collective-permute-start(f32[192,256]{1,0:T(8,128)S(1)} %collective-permute-done.7.near_ref.near2), channel_id=1, source_target_pairs={{0,1},{1,0},{2,3},{3,2},{4,5},{5,4},{6,7},{7,6},{8,9},{9,8},{10,11... | collective-permute-start | bytes 589832 | tf_op jit(solution)/shard_map/ppermute | solution.py:21
  27.2 3.8 %collective-permute-start.12 = (f32[72,256]{1,0:T(8,128)S(1)}, f32[72,256]{1,0:T(8,128)S(1)}, u32[]{:S(2)}, u32[]{:S(2)}) collective-permute-start(f32[72,256]{1,0:T(8,128)S(1)} %get-tuple-element.49), channel_id=1, source_target_pairs={{0,8},{1,9},{2,10},{3,11},{4,12},{5,13},{6,14},{7,15},{8,0},{9,1},... | collective-permute-start | bytes 221192 | tf_op jit(solution)/shard_map/ppermute | solution.py:21
  28.6 6.5 %collective-permute-start.11 = (f32[192,256]{1,0:T(8,128)S(1)}, f32[192,256]{1,0:T(8,128)S(1)}, u32[]{:S(2)}, u32[]{:S(2)}) collective-permute-start(f32[192,256]{1,0:T(8,128)S(1)} %get-tuple-element.47), channel_id=1, source_target_pairs={{0,8},{1,9},{2,10},{3,11},{4,12},{5,13},{6,14},{7,15},{8,0},{9,1},... | collective-permute-start | bytes 589832 | tf_op jit(solution)/shard_map/ppermute | solution.py:21
  31.0 2.3 %collective-permute-start.13 = (f32[72,256]{1,0:T(8,128)S(1)}, f32[72,256]{1,0:T(8,128)S(1)}, u32[]{:S(2)}, u32[]{:S(2)}) collective-permute-start(f32[72,256]{1,0:T(8,128)S(1)} %collective-permute-done.12.near_ref.near1), channel_id=1, source_target_pairs={{0,1},{1,0},{2,3},{3,2},{4,5},{5,4},{6,7},{7,6},{8,9},{9,8},{10,11... | collective-permute-start | bytes 221192 | tf_op jit(solution)/shard_map/ppermute | solution.py:21
  35.0 2.3 %collective-permute-start.14 = (f32[192,256]{1,0:T(8,128)S(1)}, f32[192,256]{1,0:T(8,128)S(1)}, u32[]{:S(2)}, u32[]{:S(2)}) collective-permute-start(f32[192,256]{1,0:T(8,128)S(1)} %collective-permute-done.11.near_ref.near2), channel_id=1, source_target_pairs={{0,1},{1,0},{2,3},{3,2},{4,5},{5,4},{6,7},{7,6},{8,9},{9,8},{10,11... | collective-permute-start | bytes 589832 | tf_op jit(solution)/shard_map/ppermute | solution.py:21
  36.2 3.9 %collective-permute-start.18 = (f32[72,256]{1,0:T(8,128)S(1)}, f32[72,256]{1,0:T(8,128)S(1)}, u32[]{:S(2)}, u32[]{:S(2)}) collective-permute-start(f32[72,256]{1,0:T(8,128)S(1)} %get-tuple-element.55), channel_id=1, source_target_pairs={{0,1},{1,0},{2,3},{3,2},{4,5},{5,4},{6,7},{7,6},{8,16},{9,17},{10,... | collective-permute-start | bytes 221192 | tf_op jit(solution)/shard_map/ppermute | solution.py:29
  36.3 3.8 %collective-permute-start.17 = (f32[72,256]{1,0:T(8,128)S(1)}, f32[72,256]{1,0:T(8,128)S(1)}, u32[]{:S(2)}, u32[]{:S(2)}) collective-permute-start(f32[72,256]{1,0:T(8,128)S(1)} %get-tuple-element.55), channel_id=1, source_target_pairs={{0,1},{1,0},{2,3},{3,2},{4,5},{5,4},{6,7},{7,6},{8,24},{9,25},{10,... | collective-permute-start | bytes 221192 | tf_op jit(solution)/shard_map/ppermute | solution.py:29
  37.3 8.2 %collective-permute-start.16 = (f32[200,256]{1,0:T(8,128)S(1)}, f32[200,256]{1,0:T(8,128)S(1)}, u32[]{:S(2)}, u32[]{:S(2)}) collective-permute-start(f32[200,256]{1,0:T(8,128)S(1)} %shard_map.66), channel_id=1, source_target_pairs={{0,1},{1,0},{2,3},{3,2},{4,5},{5,4},{6,7},{7,6},{8,24},{9,25},{10,... | collective-permute-start | bytes 614408 | tf_op jit(solution)/shard_map/ppermute | solution.py:29
  37.7 12.7 %collective-permute-start.15 = (f32[200,256]{1,0:T(8,128)S(1)}, f32[200,256]{1,0:T(8,128)S(1)}, u32[]{:S(2)}, u32[]{:S(2)}) collective-permute-start(f32[200,256]{1,0:T(8,128)S(1)} %shard_map.66), channel_id=1, source_target_pairs={{0,1},{1,0},{2,3},{3,2},{4,5},{5,4},{6,7},{7,6},{8,16},{9,17},{10,... | collective-permute-start | bytes 614408 | tf_op jit(solution)/shard_map/ppermute | solution.py:29
  40.1 3.5 %collective-permute-start.19 = (f32[72,256]{1,0:T(8,128)S(1)}, f32[72,256]{1,0:T(8,128)S(1)}, u32[]{:S(2)}, u32[]{:S(2)}) collective-permute-start(f32[72,256]{1,0:T(8,128)S(1)} %collective-permute-done.18.near2), channel_id=1, source_target_pairs={{0,1},{1,0},{2,3},{3,2},{4,5},{5,4},{6,7},{7,6},{8,9},{9,8},{10,11... | collective-permute-start | bytes 221192 | tf_op jit(solution)/shard_map/ppermute | solution.py:21
  41.3 2.3 %collective-permute-start.20 = (f32[72,256]{1,0:T(8,128)S(1)}, f32[72,256]{1,0:T(8,128)S(1)}, u32[]{:S(2)}, u32[]{:S(2)}) collective-permute-start(f32[72,256]{1,0:T(8,128)S(1)} %collective-permute-done.17.near3), channel_id=1, source_target_pairs={{0,1},{1,0},{2,3},{3,2},{4,5},{5,4},{6,7},{7,6},{8,9},{9,8},{10,11... | collective-permute-start | bytes 221192 | tf_op jit(solution)/shard_map/ppermute | solution.py:21
  50.5 1.9 %collective-permute-start.21 = (f32[200,256]{1,0:T(8,128)S(1)}, f32[200,256]{1,0:T(8,128)S(1)}, u32[]{:S(2)}, u32[]{:S(2)}) collective-permute-start(f32[200,256]{1,0:T(8,128)S(1)} %collective-permute-done.15.near2), channel_id=1, source_target_pairs={{0,1},{1,0},{2,3},{3,2},{4,5},{5,4},{6,7},{7,6},{8,9},{9,8},{10,11... | collective-permute-start | bytes 614408 | tf_op jit(solution)/shard_map/ppermute | solution.py:21
  51.3 1.5 %collective-permute-start.22 = (f32[200,256]{1,0:T(8,128)S(1)}, f32[200,256]{1,0:T(8,128)S(1)}, u32[]{:S(2)}, u32[]{:S(2)}) collective-permute-start(f32[200,256]{1,0:T(8,128)S(1)} %collective-permute-done.16.near3), channel_id=1, source_target_pairs={{0,1},{1,0},{2,3},{3,2},{4,5},{5,4},{6,7},{7,6},{8,9},{9,8},{10,11... | collective-permute-start | bytes 614408 | tf_op jit(solution)/shard_map/ppermute | solution.py:21

commit v15 on v13

--- a/solution.py
+++ b/solution.py
@@ -231,12 +231,19 @@
 def prefix_kernel(distance, old_ref, near1, far1, near2, far2, new_ref):
     me = place()
     core, upper = bit(me, 1), bit(me, distance)
-    facing = unpack_symmetric(near1, far1, core, 0)
-    leading, mirror, right = before_trans((old_ref[0], old_ref[1], old_ref[2]), facing)
-    into, away = unpack_second(near2, far2, core, near1)
-    trans, left = after_trans(leading, mirror, away, into)
-    for i, x in enumerate((left, right, trans)):
-        new_ref[i] = jnp.where(upper, x, old_ref[i])
+
+    @pl.when(upper)
+    def _():
+        facing = unpack_symmetric(near1, far1, core, 0)
+        leading, mirror, right = before_trans((old_ref[0], old_ref[1], old_ref[2]), facing)
+        into, away = unpack_second(near2, far2, core, near1)
+        trans, left = after_trans(leading, mirror, away, into)
+        for i, x in enumerate((left, right, trans)):
+            new_ref[i] = x
+
+    @pl.when(jnp.logical_not(upper))
+    def _():
+        new_ref[...] = old_ref[...]
 
 
 def by_third(distance, me, near2, far2, near3, far3):

time: 53.9 us -> 53.9 us (level)
  Pallas kernels: 17.3 us -> 10.9 us
  waiting for transfers between devices: 15 us -> 20.2 us
  starting transfers between devices: 19.4 us -> 20.6 us
    pallas_call x12, Pallas kernels: 17.3 us -> 10.9 us  [call(): pl.pallas_call(kernel, out_shape=[jax.ShapeDtypeStruct(s, F32) for s in o...]
    ppermute x19, waiting for transfers between devices: 10.4 us -> 13.5 us  [swap(): return lax.ppermute(block, AXES, [(i, i ^ distance) for i in range(count)])]
    ppermute x4, waiting for transfers between devices: 4.51 us -> 6.73 us  [pair(): lax.ppermute(block, AXES, [(i, step.get(i // quarter, lambda i: i ^ 1)(i)...]
    ppermute x19, starting transfers between devices: 16.6 us -> 17.7 us  [swap(): return lax.ppermute(block, AXES, [(i, i ^ distance) for i in range(count)])]
  transfers between devices with their start and end apart: 23 -> 23, of which waited for: 13 -> 15; matrix products, arithmetic and copies ran while one was open for 2% -> 2% of each run, Pallas kernels for 23% -> 11%
where the time goes in v15:
time: 53.9 us; the launch traced here: 53.8 us
  starting transfers between devices  20.6 us (38%)
  waiting for transfers between devices  20.2 us (37%)
  Pallas kernels  10.9 us (20%)
  other arithmetic  1.16 us (2%)
  between operations  0.93 us (2%)
    ppermute x19, starting transfers between devices, swap(): return lax.ppermute(block, AXES, [(i, i ^ distance) for i in range(count)])  17.7 us
    ppermute x19, waiting for transfers between devices, swap(): return lax.ppermute(block, AXES, [(i, i ^ distance) for i in range(count)])  13.5 us
    pallas_call x12, Pallas kernels, call(): pl.pallas_call(kernel, out_shape=[jax.ShapeDtypeStruct(s, F32) for s in o...  10.9 us
    ppermute x4, waiting for transfers between devices, pair(): lax.ppermute(block, AXES, [(i, step.get(i // quarter, lambda i: i ^ 1)(i)...  6.73 us
    ppermute x4, starting transfers between devices, pair(): lax.ppermute(block, AXES, [(i, step.get(i // quarter, lambda i: i ^ 1)(i)...  2.97 us
    concatenate x1, other arithmetic, shards(): section = jnp.concatenate(sections, 0)  1.16 us
  transfers between devices with their start and end apart: 23, of which 15 were waited for; matrix products, arithmetic and copies ran while one was open for 2% of the time, Pallas kernels for 11%

profile of v15, /device:TPU:17, one launch (start us, length us, event | category | flops | bytes accessed | tf_op | source)
XLA Modules:
  0.0 53.8 jit_solution(9792781404829205353)
XLA Ops:
  0.6 0.7 %collective-permute-start = (f32[1,256,256]{2,1,0:T(8,128)}, f32[1,256,256]{2,1,0:T(8,128)S(1)}, u32[]{:S(2)}, u32[]{:S(2)}) collective-permute-start(f32[1,256,256]{2,1,0:T(8,128)} %param.3), channel_id=1, source_target_pairs={{0,1},{1,0},{2,3},{3,2},{4,5},{5,4},{6,7},{7,6},{8,9},{9,8},{10,11... | collective-permute-start | bytes 786440 | tf_op jit(solution)/shard_map/ppermute | solution.py:21
  1.9 1.2 %pad_maximum_fusion.section_ref = f32[3,256,256]{2,1,0:T(8,128)S(1)} fusion(f32[1,256,256]{2,1,0:T(8,128)} %param.5, f32[1,256,256]{2,1,0:T(8,128)} %param.4, f32[1,256,256]{2,1,0:T(8,128)} %param.3), kind=kLoop, calls=%fused_computation | loop fusion | flops 393216 | bytes 1572864 | tf_op jit(solution)/shard_map/concatenate | solution.py:317
  3.5 2.3 %shard_map.58 = (f32[3,256,256]{2,1,0:T(8,128)S(1)}, f32[72,256]{1,0:T(8,128)S(1)}, f32[192,256]{1,0:T(8,128)S(1)}, f32[3,256,256]{2,1,0:T(8,128)S(1)}) custom-call(f32[3,256,256]{2,1,0:T(8,128)S(1)} %pad_maximum_fusion.section_ref, f32[1,256,256]{2,1,0:T(8,128)S(1)} %collective-permute-done.got1, f32[1,256,256]{2,1,0:T(8,128)S(1)} %collective-permute-done.1.got2, ...), custom_call_target="tpu_custom_call" | custom-call | flops 1207959552 | bytes 1048576 | tf_op jit(solution)/shard_map/pallas_call | solution.py:298
  5.8 1.3 %collective-permute-start.4 = (f32[72,256]{1,0:T(8,128)S(1)}, f32[72,256]{1,0:T(8,128)S(1)}, u32[]{:S(2)}, u32[]{:S(2)}) collective-permute-start(f32[72,256]{1,0:T(8,128)S(1)} %get-tuple-element.38), channel_id=1, source_target_pairs={{0,2},{1,3},{2,0},{3,1},{4,6},{5,7},{6,4},{7,5},{8,10},{9,11},{10,... | collective-permute-start | bytes 221192 | tf_op jit(solution)/shard_map/ppermute | solution.py:21
  7.3 1.7 %collective-permute-done.4.near_ref.near1 = f32[72,256]{1,0:T(8,128)S(1)} collective-permute-done((f32[72,256]{1,0:T(8,128)S(1)}, f32[72,256]{1,0:T(8,128)S(1)}, u32[]{:S(2)}, u32[]{:S(2)}) %collective-permute-start.4) | collective-permute-done | bytes 73760 | tf_op jit(solution)/shard_map/ppermute | solution.py:21
  9.1 2.0 %collective-permute-start.5 = (f32[72,256]{1,0:T(8,128)S(1)}, f32[72,256]{1,0:T(8,128)S(1)}, u32[]{:S(2)}, u32[]{:S(2)}) collective-permute-start(f32[72,256]{1,0:T(8,128)S(1)} %collective-permute-done.4.near_ref.near1), channel_id=1, source_target_pairs={{0,1},{1,0},{2,3},{3,2},{4,5},{5,4},{6,7},{7,6},{8,9},{9,8},{10,11... | collective-permute-start | bytes 221192 | tf_op jit(solution)/shard_map/ppermute | solution.py:21
  11.1 0.9 %collective-permute-done.5.far_ref.far1 = f32[72,256]{1,0:T(8,128)S(1)} collective-permute-done((f32[72,256]{1,0:T(8,128)S(1)}, f32[72,256]{1,0:T(8,128)S(1)}, u32[]{:S(2)}, u32[]{:S(2)}) %collective-permute-start.5) | collective-permute-done | bytes 73760 | tf_op jit(solution)/shard_map/ppermute | solution.py:21
  12.0 1.9 %shard_map.59.half_ref = f32[3,256,256]{2,1,0:T(8,128)S(1)} custom-call(f32[3,256,256]{2,1,0:T(8,128)S(1)} %get-tuple-element.37.own_ref, f32[72,256]{1,0:T(8,128)S(1)} %collective-permute-done.4.near_ref.near1, f32[72,256]{1,0:T(8,128)S(1)} %collective-permute-done.5.far_ref.far1), custom_call_target="tpu_custom_call" | custom-call | flops 905969664 | bytes 786432 | tf_op jit(solution)/shard_map/pallas_call | solution.py:298
  13.9 0.9 %collective-permute-start.6 = (f32[192,256]{1,0:T(8,128)S(1)}, f32[192,256]{1,0:T(8,128)S(1)}, u32[]{:S(2)}, u32[]{:S(2)}) collective-permute-start(f32[192,256]{1,0:T(8,128)S(1)} %collective-permute-done.3.near_ref.near2), channel_id=1, source_target_pairs={{0,1},{1,0},{2,3},{3,2},{4,5},{5,4},{6,7},{7,6},{8,9},{9,8},{10,11... | collective-permute-start | bytes 589832 | tf_op jit(solution)/shard_map/ppermute | solution.py:21
  14.8 1.1 %collective-permute-done.6.far_ref.far2 = f32[192,256]{1,0:T(8,128)S(1)} collective-permute-done((f32[192,256]{1,0:T(8,128)S(1)}, f32[192,256]{1,0:T(8,128)S(1)}, u32[]{:S(2)}, u32[]{:S(2)}) %collective-permute-start.6) | collective-permute-done | bytes 196640 | tf_op jit(solution)/shard_map/ppermute | solution.py:21
  16.5 1.3 %collective-permute-start.8 = (f32[72,256]{1,0:T(8,128)S(1)}, f32[72,256]{1,0:T(8,128)S(1)}, u32[]{:S(2)}, u32[]{:S(2)}) collective-permute-start(f32[72,256]{1,0:T(8,128)S(1)} %get-tuple-element.43), channel_id=1, source_target_pairs={{0,4},{1,5},{2,6},{3,7},{4,0},{5,1},{6,2},{7,3},{8,12},{9,13},{10,... | collective-permute-start | bytes 221192 | tf_op jit(solution)/shard_map/ppermute | solution.py:21
  18.1 1.7 %collective-permute-done.8.near_ref.near1 = f32[72,256]{1,0:T(8,128)S(1)} collective-permute-done((f32[72,256]{1,0:T(8,128)S(1)}, f32[72,256]{1,0:T(8,128)S(1)}, u32[]{:S(2)}, u32[]{:S(2)}) %collective-permute-start.8) | collective-permute-done | bytes 73760 | tf_op jit(solution)/shard_map/ppermute | solution.py:21
  19.8 2.0 %collective-permute-start.9 = (f32[72,256]{1,0:T(8,128)S(1)}, f32[72,256]{1,0:T(8,128)S(1)}, u32[]{:S(2)}, u32[]{:S(2)}) collective-permute-start(f32[72,256]{1,0:T(8,128)S(1)} %collective-permute-done.8.near_ref.near1), channel_id=1, source_target_pairs={{0,1},{1,0},{2,3},{3,2},{4,5},{5,4},{6,7},{7,6},{8,9},{9,8},{10,11... | collective-permute-start | bytes 221192 | tf_op jit(solution)/shard_map/ppermute | solution.py:21
  21.8 0.9 %collective-permute-done.9.far_ref.far1 = f32[72,256]{1,0:T(8,128)S(1)} collective-permute-done((f32[72,256]{1,0:T(8,128)S(1)}, f32[72,256]{1,0:T(8,128)S(1)}, u32[]{:S(2)}, u32[]{:S(2)}) %collective-permute-start.9) | collective-permute-done | bytes 73760 | tf_op jit(solution)/shard_map/ppermute | solution.py:21
  22.7 1.9 %shard_map.62.half_ref = f32[3,256,256]{2,1,0:T(8,128)S(1)} custom-call(f32[3,256,256]{2,1,0:T(8,128)S(1)} %get-tuple-element.42.own_ref, f32[72,256]{1,0:T(8,128)S(1)} %collective-permute-done.8.near_ref.near1, f32[72,256]{1,0:T(8,128)S(1)} %collective-permute-done.9.far_ref.far1), custom_call_target="tpu_custom_call" | custom-call | flops 905969664 | bytes 786432 | tf_op jit(solution)/shard_map/pallas_call | solution.py:298
  24.6 1.0 %collective-permute-start.10 = (f32[192,256]{1,0:T(8,128)S(1)}, f32[192,256]{1,0:T(8,128)S(1)}, u32[]{:S(2)}, u32[]{:S(2)}) collective-permute-start(f32[192,256]{1,0:T(8,128)S(1)} %collective-permute-done.7.near_ref.near2), channel_id=1, source_target_pairs={{0,1},{1,0},{2,3},{3,2},{4,5},{5,4},{6,7},{7,6},{8,9},{9,8},{10,11... | collective-permute-start | bytes 589832 | tf_op jit(solution)/shard_map/ppermute | solution.py:21
  25.5 1.1 %collective-permute-done.10.far_ref.far2 = f32[192,256]{1,0:T(8,128)S(1)} collective-permute-done((f32[192,256]{1,0:T(8,128)S(1)}, f32[192,256]{1,0:T(8,128)S(1)}, u32[]{:S(2)}, u32[]{:S(2)}) %collective-permute-start.10) | collective-permute-done | bytes 196640 | tf_op jit(solution)/shard_map/ppermute | solution.py:21
  27.2 1.4 %collective-permute-start.12 = (f32[72,256]{1,0:T(8,128)S(1)}, f32[72,256]{1,0:T(8,128)S(1)}, u32[]{:S(2)}, u32[]{:S(2)}) collective-permute-start(f32[72,256]{1,0:T(8,128)S(1)} %get-tuple-element.50), channel_id=1, source_target_pairs={{0,8},{1,9},{2,10},{3,11},{4,12},{5,13},{6,14},{7,15},{8,0},{9,1},... | collective-permute-start | bytes 221192 | tf_op jit(solution)/shard_map/ppermute | solution.py:21
  28.8 1.7 %collective-permute-done.12.near_ref.near1 = f32[72,256]{1,0:T(8,128)S(1)} collective-permute-done((f32[72,256]{1,0:T(8,128)S(1)}, f32[72,256]{1,0:T(8,128)S(1)}, u32[]{:S(2)}, u32[]{:S(2)}) %collective-permute-start.12) | collective-permute-done | bytes 73760 | tf_op jit(solution)/shard_map/ppermute | solution.py:21
  30.5 1.9 %collective-permute-start.13 = (f32[72,256]{1,0:T(8,128)S(1)}, f32[72,256]{1,0:T(8,128)S(1)}, u32[]{:S(2)}, u32[]{:S(2)}) collective-permute-start(f32[72,256]{1,0:T(8,128)S(1)} %collective-permute-done.12.near_ref.near1), channel_id=1, source_target_pairs={{0,1},{1,0},{2,3},{3,2},{4,5},{5,4},{6,7},{7,6},{8,9},{9,8},{10,11... | collective-permute-start | bytes 221192 | tf_op jit(solution)/shard_map/ppermute | solution.py:21
  32.4 0.9 %collective-permute-done.13.far_ref.far1 = f32[72,256]{1,0:T(8,128)S(1)} collective-permute-done((f32[72,256]{1,0:T(8,128)S(1)}, f32[72,256]{1,0:T(8,128)S(1)}, u32[]{:S(2)}, u32[]{:S(2)}) %collective-permute-start.13) | collective-permute-done | bytes 73760 | tf_op jit(solution)/shard_map/ppermute | solution.py:21
  33.6 1.5 %collective-permute-done.11.near_ref.near2 = f32[192,256]{1,0:T(8,128)S(1)} collective-permute-done((f32[192,256]{1,0:T(8,128)S(1)}, f32[192,256]{1,0:T(8,128)S(1)}, u32[]{:S(2)}, u32[]{:S(2)}) %collective-permute-start.11) | collective-permute-done | bytes 196640 | tf_op jit(solution)/shard_map/ppermute | solution.py:21
  35.0 1.2 %collective-permute-start.14 = (f32[192,256]{1,0:T(8,128)S(1)}, f32[192,256]{1,0:T(8,128)S(1)}, u32[]{:S(2)}, u32[]{:S(2)}) collective-permute-start(f32[192,256]{1,0:T(8,128)S(1)} %collective-permute-done.11.near_ref.near2), channel_id=1, source_target_pairs={{0,1},{1,0},{2,3},{3,2},{4,5},{5,4},{6,7},{7,6},{8,9},{9,8},{10,11... | collective-permute-start | bytes 589832 | tf_op jit(solution)/shard_map/ppermute | solution.py:21
  37.7 2.4 %collective-permute-done.17.near2 = f32[72,256]{1,0:T(8,128)S(1)} collective-permute-done((f32[72,256]{1,0:T(8,128)S(1)}, f32[72,256]{1,0:T(8,128)S(1)}, u32[]{:S(2)}, u32[]{:S(2)}) %collective-permute-start.17) | collective-permute-done | bytes 73760 | tf_op jit(solution)/shard_map/ppermute | solution.py:29
  40.1 1.2 %collective-permute-start.18 = (f32[72,256]{1,0:T(8,128)S(1)}, f32[72,256]{1,0:T(8,128)S(1)}, u32[]{:S(2)}, u32[]{:S(2)}) collective-permute-start(f32[72,256]{1,0:T(8,128)S(1)} %collective-permute-done.17.near2), channel_id=1, source_target_pairs={{0,1},{1,0},{2,3},{3,2},{4,5},{5,4},{6,7},{7,6},{8,9},{9,8},{10,11... | collective-permute-start | bytes 221192 | tf_op jit(solution)/shard_map/ppermute | solution.py:21
  41.3 2.0 %collective-permute-start.20 = (f32[200,256]{1,0:T(8,128)S(1)}, f32[200,256]{1,0:T(8,128)S(1)}, u32[]{:S(2)}, u32[]{:S(2)}) collective-permute-start(f32[200,256]{1,0:T(8,128)S(1)} %shard_map.66), channel_id=1, source_target_pairs={{0,1},{1,0},{2,3},{3,2},{4,5},{5,4},{6,7},{7,6},{8,16},{9,17},{10,... | collective-permute-start | bytes 614408 | tf_op jit(solution)/shard_map/ppermute | solution.py:29
  43.3 1.9 %shard_map.68 = (f32[3,256,256]{2,1,0:T(8,128)S(1)}, f32[1,256,256]{2,1,0:T(8,128)}, f32[1,256,256]{2,1,0:T(8,128)}, f32[1,256,256]{2,1,0:T(8,128)}) custom-call(f32[3,256,256]{2,1,0:T(8,128)S(1)} %shard_map.67.old_ref, f32[72,256]{1,0:T(8,128)S(1)} %collective-permute-done.17.near2, f32[72,256]{1,0:T(8,128)S(1)} %collective-permute-done.18.far2, ...), custom_call_target="tpu_custom_call" | custom-call | flops 905969664 | bytes 1310720 | tf_op jit(solution)/shard_map/pallas_call | solution.py:298
  45.3 0.9 %collective-permute-start.21 = (f32[200,256]{1,0:T(8,128)S(1)}, f32[200,256]{1,0:T(8,128)S(1)}, u32[]{:S(2)}, u32[]{:S(2)}) collective-permute-start(f32[200,256]{1,0:T(8,128)S(1)} %collective-permute-done.15.near3), channel_id=1, source_target_pairs={{0,1},{1,0},{2,3},{3,2},{4,5},{5,4},{6,7},{7,6},{8,9},{9,8},{10,11... | collective-permute-start | bytes 614408 | tf_op jit(solution)/shard_map/ppermute | solution.py:21
  46.1 4.3 %collective-permute-done.20.near2 = f32[200,256]{1,0:T(8,128)S(1)} collective-permute-done((f32[200,256]{1,0:T(8,128)S(1)}, f32[200,256]{1,0:T(8,128)S(1)}, u32[]{:S(2)}, u32[]{:S(2)}) %collective-permute-start.20) | collective-permute-done | bytes 204832 | tf_op jit(solution)/shard_map/ppermute | solution.py:29
  50.5 0.8 %collective-permute-start.22 = (f32[200,256]{1,0:T(8,128)S(1)}, f32[200,256]{1,0:T(8,128)S(1)}, u32[]{:S(2)}, u32[]{:S(2)}) collective-permute-start(f32[200,256]{1,0:T(8,128)S(1)} %collective-permute-done.20.near2), channel_id=1, source_target_pairs={{0,1},{1,0},{2,3},{3,2},{4,5},{5,4},{6,7},{7,6},{8,9},{9,8},{10,11... | collective-permute-start | bytes 614408 | tf_op jit(solution)/shard_map/ppermute | solution.py:21
  51.3 1.1 %collective-permute-done.22.far2 = f32[200,256]{1,0:T(8,128)S(1)} collective-permute-done((f32[200,256]{1,0:T(8,128)S(1)}, f32[200,256]{1,0:T(8,128)S(1)}, u32[]{:S(2)}, u32[]{:S(2)}) %collective-permute-start.22) | collective-permute-done | bytes 204832 | tf_op jit(solution)/shard_map/ppermute | solution.py:21
  52.3 1.3 %shard_map.69 = (f32[1,256,256]{2,1,0:T(8,128)}, f32[1,256,256]{2,1,0:T(8,128)}, f32[1,256,256]{2,1,0:T(8,128)}) custom-call(f32[3,256,256]{2,1,0:T(8,128)S(1)} %get-tuple-element.62.half_ref, f32[200,256]{1,0:T(8,128)S(1)} %collective-permute-done.20.near2, ...), custom_call_target="tpu_custom_call", output_to_operand_aliasing={{0}: (5, {}), {1}: (6, {}), {2}: (7, {})} | custom-call | flops 301989888 | bytes 1310720 | tf_op jit(solution)/shard_map/pallas_call | solution.py:298
  (27 shorter events, 4.8 us)
Async XLA Ops:
  0.6 2.4 %collective-permute-start = (f32[1,256,256]{2,1,0:T(8,128)}, f32[1,256,256]{2,1,0:T(8,128)S(1)}, u32[]{:S(2)}, u32[]{:S(2)}) collective-permute-start(f32[1,256,256]{2,1,0:T(8,128)} %param.3), channel_id=1, source_target_pairs={{0,1},{1,0},{2,3},{3,2},{4,5},{5,4},{6,7},{7,6},{8,9},{9,8},{10,11... | collective-permute-start | bytes 786440 | tf_op jit(solution)/shard_map/ppermute | solution.py:21
  1.4 1.7 %collective-permute-start.1 = (f32[1,256,256]{2,1,0:T(8,128)}, f32[1,256,256]{2,1,0:T(8,128)S(1)}, u32[]{:S(2)}, u32[]{:S(2)}) collective-permute-start(f32[1,256,256]{2,1,0:T(8,128)} %param.4), channel_id=1, source_target_pairs={{0,1},{1,0},{2,3},{3,2},{4,5},{5,4},{6,7},{7,6},{8,9},{9,8},{10,11... | collective-permute-start | bytes 786440 | tf_op jit(solution)/shard_map/ppermute | solution.py:21
  1.4 2.0 %collective-permute-start.2 = (f32[1,256,256]{2,1,0:T(8,128)}, f32[1,256,256]{2,1,0:T(8,128)S(1)}, u32[]{:S(2)}, u32[]{:S(2)}) collective-permute-start(f32[1,256,256]{2,1,0:T(8,128)} %param.5), channel_id=1, source_target_pairs={{0,1},{1,0},{2,3},{3,2},{4,5},{5,4},{6,7},{7,6},{8,9},{9,8},{10,11... | collective-permute-start | bytes 786440 | tf_op jit(solution)/shard_map/ppermute | solution.py:21
  5.8 3.3 %collective-permute-start.4 = (f32[72,256]{1,0:T(8,128)S(1)}, f32[72,256]{1,0:T(8,128)S(1)}, u32[]{:S(2)}, u32[]{:S(2)}) collective-permute-start(f32[72,256]{1,0:T(8,128)S(1)} %get-tuple-element.38), channel_id=1, source_target_pairs={{0,2},{1,3},{2,0},{3,1},{4,6},{5,7},{6,4},{7,5},{8,10},{9,11},{10,... | collective-permute-start | bytes 221192 | tf_op jit(solution)/shard_map/ppermute | solution.py:21
  7.1 6.8 %collective-permute-start.3 = (f32[192,256]{1,0:T(8,128)S(1)}, f32[192,256]{1,0:T(8,128)S(1)}, u32[]{:S(2)}, u32[]{:S(2)}) collective-permute-start(f32[192,256]{1,0:T(8,128)S(1)} %get-tuple-element.36), channel_id=1, source_target_pairs={{0,2},{1,3},{2,0},{3,1},{4,6},{5,7},{6,4},{7,5},{8,10},{9,11},{10,... | collective-permute-start | bytes 589832 | tf_op jit(solution)/shard_map/ppermute | solution.py:21
  9.1 3.0 %collective-permute-start.5 = (f32[72,256]{1,0:T(8,128)S(1)}, f32[72,256]{1,0:T(8,128)S(1)}, u32[]{:S(2)}, u32[]{:S(2)}) collective-permute-start(f32[72,256]{1,0:T(8,128)S(1)} %collective-permute-done.4.near_ref.near1), channel_id=1, source_target_pairs={{0,1},{1,0},{2,3},{3,2},{4,5},{5,4},{6,7},{7,6},{8,9},{9,8},{10,11... | collective-permute-start | bytes 221192 | tf_op jit(solution)/shard_map/ppermute | solution.py:21
  13.9 2.0 %collective-permute-start.6 = (f32[192,256]{1,0:T(8,128)S(1)}, f32[192,256]{1,0:T(8,128)S(1)}, u32[]{:S(2)}, u32[]{:S(2)}) collective-permute-start(f32[192,256]{1,0:T(8,128)S(1)} %collective-permute-done.3.near_ref.near2), channel_id=1, source_target_pairs={{0,1},{1,0},{2,3},{3,2},{4,5},{5,4},{6,7},{7,6},{8,9},{9,8},{10,11... | collective-permute-start | bytes 589832 | tf_op jit(solution)/shard_map/ppermute | solution.py:21
  16.5 3.3 %collective-permute-start.8 = (f32[72,256]{1,0:T(8,128)S(1)}, f32[72,256]{1,0:T(8,128)S(1)}, u32[]{:S(2)}, u32[]{:S(2)}) collective-permute-start(f32[72,256]{1,0:T(8,128)S(1)} %get-tuple-element.43), channel_id=1, source_target_pairs={{0,4},{1,5},{2,6},{3,7},{4,0},{5,1},{6,2},{7,3},{8,12},{9,13},{10,... | collective-permute-start | bytes 221192 | tf_op jit(solution)/shard_map/ppermute | solution.py:21
  17.8 6.7 %collective-permute-start.7 = (f32[192,256]{1,0:T(8,128)S(1)}, f32[192,256]{1,0:T(8,128)S(1)}, u32[]{:S(2)}, u32[]{:S(2)}) collective-permute-start(f32[192,256]{1,0:T(8,128)S(1)} %get-tuple-element.41), channel_id=1, source_target_pairs={{0,4},{1,5},{2,6},{3,7},{4,0},{5,1},{6,2},{7,3},{8,12},{9,13},{10,... | collective-permute-start | bytes 589832 | tf_op jit(solution)/shard_map/ppermute | solution.py:21
  19.8 2.9 %collective-permute-start.9 = (f32[72,256]{1,0:T(8,128)S(1)}, f32[72,256]{1,0:T(8,128)S(1)}, u32[]{:S(2)}, u32[]{:S(2)}) collective-permute-start(f32[72,256]{1,0:T(8,128)S(1)} %collective-permute-done.8.near_ref.near1), channel_id=1, source_target_pairs={{0,1},{1,0},{2,3},{3,2},{4,5},{5,4},{6,7},{7,6},{8,9},{9,8},{10,11... | collective-permute-start | bytes 221192 | tf_op jit(solution)/shard_map/ppermute | solution.py:21
  24.6 2.0 %collective-permute-start.10 = (f32[192,256]{1,0:T(8,128)S(1)}, f32[192,256]{1,0:T(8,128)S(1)}, u32[]{:S(2)}, u32[]{:S(2)}) collective-permute-start(f32[192,256]{1,0:T(8,128)S(1)} %collective-permute-done.7.near_ref.near2), channel_id=1, source_target_pairs={{0,1},{1,0},{2,3},{3,2},{4,5},{5,4},{6,7},{7,6},{8,9},{9,8},{10,11... | collective-permute-start | bytes 589832 | tf_op jit(solution)/shard_map/ppermute | solution.py:21
  27.2 3.3 %collective-permute-start.12 = (f32[72,256]{1,0:T(8,128)S(1)}, f32[72,256]{1,0:T(8,128)S(1)}, u32[]{:S(2)}, u32[]{:S(2)}) collective-permute-start(f32[72,256]{1,0:T(8,128)S(1)} %get-tuple-element.50), channel_id=1, source_target_pairs={{0,8},{1,9},{2,10},{3,11},{4,12},{5,13},{6,14},{7,15},{8,0},{9,1},... | collective-permute-start | bytes 221192 | tf_op jit(solution)/shard_map/ppermute | solution.py:21
  28.6 6.5 %collective-permute-start.11 = (f32[192,256]{1,0:T(8,128)S(1)}, f32[192,256]{1,0:T(8,128)S(1)}, u32[]{:S(2)}, u32[]{:S(2)}) collective-permute-start(f32[192,256]{1,0:T(8,128)S(1)} %get-tuple-element.48), channel_id=1, source_target_pairs={{0,8},{1,9},{2,10},{3,11},{4,12},{5,13},{6,14},{7,15},{8,0},{9,1},... | collective-permute-start | bytes 589832 | tf_op jit(solution)/shard_map/ppermute | solution.py:21
  30.5 2.8 %collective-permute-start.13 = (f32[72,256]{1,0:T(8,128)S(1)}, f32[72,256]{1,0:T(8,128)S(1)}, u32[]{:S(2)}, u32[]{:S(2)}) collective-permute-start(f32[72,256]{1,0:T(8,128)S(1)} %collective-permute-done.12.near_ref.near1), channel_id=1, source_target_pairs={{0,1},{1,0},{2,3},{3,2},{4,5},{5,4},{6,7},{7,6},{8,9},{9,8},{10,11... | collective-permute-start | bytes 221192 | tf_op jit(solution)/shard_map/ppermute | solution.py:21
  35.0 2.3 %collective-permute-start.14 = (f32[192,256]{1,0:T(8,128)S(1)}, f32[192,256]{1,0:T(8,128)S(1)}, u32[]{:S(2)}, u32[]{:S(2)}) collective-permute-start(f32[192,256]{1,0:T(8,128)S(1)} %collective-permute-done.11.near_ref.near2), channel_id=1, source_target_pairs={{0,1},{1,0},{2,3},{3,2},{4,5},{5,4},{6,7},{7,6},{8,9},{9,8},{10,11... | collective-permute-start | bytes 589832 | tf_op jit(solution)/shard_map/ppermute | solution.py:21
  36.2 3.9 %collective-permute-start.17 = (f32[72,256]{1,0:T(8,128)S(1)}, f32[72,256]{1,0:T(8,128)S(1)}, u32[]{:S(2)}, u32[]{:S(2)}) collective-permute-start(f32[72,256]{1,0:T(8,128)S(1)} %get-tuple-element.56), channel_id=1, source_target_pairs={{0,1},{1,0},{2,3},{3,2},{4,5},{5,4},{6,7},{7,6},{8,16},{9,17},{10,... | collective-permute-start | bytes 221192 | tf_op jit(solution)/shard_map/ppermute | solution.py:29
  36.3 3.8 %collective-permute-start.16 = (f32[72,256]{1,0:T(8,128)S(1)}, f32[72,256]{1,0:T(8,128)S(1)}, u32[]{:S(2)}, u32[]{:S(2)}) collective-permute-start(f32[72,256]{1,0:T(8,128)S(1)} %get-tuple-element.56), channel_id=1, source_target_pairs={{0,1},{1,0},{2,3},{3,2},{4,5},{5,4},{6,7},{7,6},{8,24},{9,25},{10,... | collective-permute-start | bytes 221192 | tf_op jit(solution)/shard_map/ppermute | solution.py:29
  37.3 8.0 %collective-permute-start.15 = (f32[200,256]{1,0:T(8,128)S(1)}, f32[200,256]{1,0:T(8,128)S(1)}, u32[]{:S(2)}, u32[]{:S(2)}) collective-permute-start(f32[200,256]{1,0:T(8,128)S(1)} %shard_map.66), channel_id=1, source_target_pairs={{0,1},{1,0},{2,3},{3,2},{4,5},{5,4},{6,7},{7,6},{8,24},{9,25},{10,... | collective-permute-start | bytes 614408 | tf_op jit(solution)/shard_map/ppermute | solution.py:29
  40.1 3.2 %collective-permute-start.18 = (f32[72,256]{1,0:T(8,128)S(1)}, f32[72,256]{1,0:T(8,128)S(1)}, u32[]{:S(2)}, u32[]{:S(2)}) collective-permute-start(f32[72,256]{1,0:T(8,128)S(1)} %collective-permute-done.17.near2), channel_id=1, source_target_pairs={{0,1},{1,0},{2,3},{3,2},{4,5},{5,4},{6,7},{7,6},{8,9},{9,8},{10,11... | collective-permute-start | bytes 221192 | tf_op jit(solution)/shard_map/ppermute | solution.py:21
  41.3 2.0 %collective-permute-start.19 = (f32[72,256]{1,0:T(8,128)S(1)}, f32[72,256]{1,0:T(8,128)S(1)}, u32[]{:S(2)}, u32[]{:S(2)}) collective-permute-start(f32[72,256]{1,0:T(8,128)S(1)} %collective-permute-done.16.near3), channel_id=1, source_target_pairs={{0,1},{1,0},{2,3},{3,2},{4,5},{5,4},{6,7},{7,6},{8,9},{9,8},{10,11... | collective-permute-start | bytes 221192 | tf_op jit(solution)/shard_map/ppermute | solution.py:21
  41.3 9.2 %collective-permute-start.20 = (f32[200,256]{1,0:T(8,128)S(1)}, f32[200,256]{1,0:T(8,128)S(1)}, u32[]{:S(2)}, u32[]{:S(2)}) collective-permute-start(f32[200,256]{1,0:T(8,128)S(1)} %shard_map.66), channel_id=1, source_target_pairs={{0,1},{1,0},{2,3},{3,2},{4,5},{5,4},{6,7},{7,6},{8,16},{9,17},{10,... | collective-permute-start | bytes 614408 | tf_op jit(solution)/shard_map/ppermute | solution.py:29
  45.3 5.2 %collective-permute-start.21 = (f32[200,256]{1,0:T(8,128)S(1)}, f32[200,256]{1,0:T(8,128)S(1)}, u32[]{:S(2)}, u32[]{:S(2)}) collective-permute-start(f32[200,256]{1,0:T(8,128)S(1)} %collective-permute-done.15.near3), channel_id=1, source_target_pairs={{0,1},{1,0},{2,3},{3,2},{4,5},{5,4},{6,7},{7,6},{8,9},{9,8},{10,11... | collective-permute-start | bytes 614408 | tf_op jit(solution)/shard_map/ppermute | solution.py:21
  50.5 1.9 %collective-permute-start.22 = (f32[200,256]{1,0:T(8,128)S(1)}, f32[200,256]{1,0:T(8,128)S(1)}, u32[]{:S(2)}, u32[]{:S(2)}) collective-permute-start(f32[200,256]{1,0:T(8,128)S(1)} %collective-permute-done.20.near2), channel_id=1, source_target_pairs={{0,1},{1,0},{2,3},{3,2},{4,5},{5,4},{6,7},{7,6},{8,9},{9,8},{10,11... | collective-permute-start | bytes 614408 | tf_op jit(solution)/shard_map/ppermute | solution.py:21

commit v16 on v13

--- a/solution.py
+++ b/solution.py
@@ -197,8 +197,12 @@
 
 def final_early_kernel(distance, own_ref, near_ref, far_ref, half_ref, first_ref):
     def body():
-        early_kernel(own_ref, near_ref, far_ref, half_ref)
-        pack_symmetric(half_ref[2], bit(place(), 1), first_ref, 0)
+        core = bit(place(), 1)
+        facing = unpack_symmetric(near_ref, far_ref, core, 0)
+        half = before_trans((own_ref[0], own_ref[1], own_ref[2]), facing)
+        pack_symmetric(half[2], core, first_ref, 0)
+        for i, x in enumerate(half):
+            half_ref[i] = x
 
     only_quarter_1(distance, body, half_ref, first_ref)
 

time: 53.9 us -> 53.9 us (level)
  no operation moved by 1% of the time
where the time goes in v16:
time: 53.9 us; the launch traced here: 53.8 us
  starting transfers between devices  19.4 us (36%)
  Pallas kernels  17.3 us (32%)
  waiting for transfers between devices  15 us (28%)
  other arithmetic  1.16 us (2%)
  between operations  0.96 us (2%)
    pallas_call x12, Pallas kernels, call(): pl.pallas_call(kernel, out_shape=[jax.ShapeDtypeStruct(s, F32) for s in o...  17.3 us
    ppermute x19, starting transfers between devices, swap(): return lax.ppermute(block, AXES, [(i, i ^ distance) for i in range(count)])  16.6 us
    ppermute x19, waiting for transfers between devices, swap(): return lax.ppermute(block, AXES, [(i, i ^ distance) for i in range(count)])  10.4 us
    ppermute x4, waiting for transfers between devices, pair(): lax.ppermute(block, AXES, [(i, step.get(i // quarter, lambda i: i ^ 1)(i)...  4.51 us
    ppermute x4, starting transfers between devices, pair(): lax.ppermute(block, AXES, [(i, step.get(i // quarter, lambda i: i ^ 1)(i)...  2.83 us
    concatenate x1, other arithmetic, shards(): section = jnp.concatenate(sections, 0)  1.16 us
  transfers between devices with their start and end apart: 23, of which 13 were waited for; matrix products, arithmetic and copies ran while one was open for 2% of the time, Pallas kernels for 23%

profile of v16, /device:TPU:17, one launch (start us, length us, event | category | flops | bytes accessed | tf_op | source)
XLA Modules:
  0.0 53.8 jit_solution(3310781531703572163)
XLA Ops:
  1.9 1.2 %pad_maximum_fusion.section_ref = f32[3,256,256]{2,1,0:T(8,128)S(1)} fusion(f32[1,256,256]{2,1,0:T(8,128)} %param.5, f32[1,256,256]{2,1,0:T(8,128)} %param.4, f32[1,256,256]{2,1,0:T(8,128)} %param.3), kind=kLoop, calls=%fused_computation | loop fusion | flops 393216 | bytes 1572864 | tf_op jit(solution)/shard_map/concatenate | solution.py:314
  3.5 2.3 %shard_map.58 = (f32[3,256,256]{2,1,0:T(8,128)S(1)}, f32[72,256]{1,0:T(8,128)S(1)}, f32[192,256]{1,0:T(8,128)S(1)}, f32[3,256,256]{2,1,0:T(8,128)S(1)}) custom-call(f32[3,256,256]{2,1,0:T(8,128)S(1)} %pad_maximum_fusion.section_ref, f32[1,256,256]{2,1,0:T(8,128)S(1)} %collective-permute-done.got1, f32[1,256,256]{2,1,0:T(8,128)S(1)} %collective-permute-done.1.got2, ...), custom_call_target="tpu_custom_call" | custom-call | flops 1207959552 | bytes 1048576 | tf_op jit(solution)/shard_map/pallas_call | solution.py:295
  5.8 1.3 %collective-permute-start.4 = (f32[72,256]{1,0:T(8,128)S(1)}, f32[72,256]{1,0:T(8,128)S(1)}, u32[]{:S(2)}, u32[]{:S(2)}) collective-permute-start(f32[72,256]{1,0:T(8,128)S(1)} %get-tuple-element.38), channel_id=1, source_target_pairs={{0,2},{1,3},{2,0},{3,1},{4,6},{5,7},{6,4},{7,5},{8,10},{9,11},{10,... | collective-permute-start | bytes 221192 | tf_op jit(solution)/shard_map/ppermute | solution.py:21
  7.3 1.7 %collective-permute-done.4.near_ref.near1 = f32[72,256]{1,0:T(8,128)S(1)} collective-permute-done((f32[72,256]{1,0:T(8,128)S(1)}, f32[72,256]{1,0:T(8,128)S(1)}, u32[]{:S(2)}, u32[]{:S(2)}) %collective-permute-start.4) | collective-permute-done | bytes 73760 | tf_op jit(solution)/shard_map/ppermute | solution.py:21
  9.1 2.0 %collective-permute-start.5 = (f32[72,256]{1,0:T(8,128)S(1)}, f32[72,256]{1,0:T(8,128)S(1)}, u32[]{:S(2)}, u32[]{:S(2)}) collective-permute-start(f32[72,256]{1,0:T(8,128)S(1)} %collective-permute-done.4.near_ref.near1), channel_id=1, source_target_pairs={{0,1},{1,0},{2,3},{3,2},{4,5},{5,4},{6,7},{7,6},{8,9},{9,8},{10,11... | collective-permute-start | bytes 221192 | tf_op jit(solution)/shard_map/ppermute | solution.py:21
  11.1 0.9 %collective-permute-done.5.far_ref.far1 = f32[72,256]{1,0:T(8,128)S(1)} collective-permute-done((f32[72,256]{1,0:T(8,128)S(1)}, f32[72,256]{1,0:T(8,128)S(1)}, u32[]{:S(2)}, u32[]{:S(2)}) %collective-permute-start.5) | collective-permute-done | bytes 73760 | tf_op jit(solution)/shard_map/ppermute | solution.py:21
  12.0 1.9 %shard_map.59.half_ref = f32[3,256,256]{2,1,0:T(8,128)S(1)} custom-call(f32[3,256,256]{2,1,0:T(8,128)S(1)} %get-tuple-element.37.own_ref, f32[72,256]{1,0:T(8,128)S(1)} %collective-permute-done.4.near_ref.near1, f32[72,256]{1,0:T(8,128)S(1)} %collective-permute-done.5.far_ref.far1), custom_call_target="tpu_custom_call" | custom-call | flops 905969664 | bytes 786432 | tf_op jit(solution)/shard_map/pallas_call | solution.py:295
  13.9 0.9 %collective-permute-start.6 = (f32[192,256]{1,0:T(8,128)S(1)}, f32[192,256]{1,0:T(8,128)S(1)}, u32[]{:S(2)}, u32[]{:S(2)}) collective-permute-start(f32[192,256]{1,0:T(8,128)S(1)} %collective-permute-done.3.near_ref.near2), channel_id=1, source_target_pairs={{0,1},{1,0},{2,3},{3,2},{4,5},{5,4},{6,7},{7,6},{8,9},{9,8},{10,11... | collective-permute-start | bytes 589832 | tf_op jit(solution)/shard_map/ppermute | solution.py:21
  14.8 1.1 %collective-permute-done.6.far_ref.far2 = f32[192,256]{1,0:T(8,128)S(1)} collective-permute-done((f32[192,256]{1,0:T(8,128)S(1)}, f32[192,256]{1,0:T(8,128)S(1)}, u32[]{:S(2)}, u32[]{:S(2)}) %collective-permute-start.6) | collective-permute-done | bytes 196640 | tf_op jit(solution)/shard_map/ppermute | solution.py:21
  16.5 1.3 %collective-permute-start.8 = (f32[72,256]{1,0:T(8,128)S(1)}, f32[72,256]{1,0:T(8,128)S(1)}, u32[]{:S(2)}, u32[]{:S(2)}) collective-permute-start(f32[72,256]{1,0:T(8,128)S(1)} %get-tuple-element.43), channel_id=1, source_target_pairs={{0,4},{1,5},{2,6},{3,7},{4,0},{5,1},{6,2},{7,3},{8,12},{9,13},{10,... | collective-permute-start | bytes 221192 | tf_op jit(solution)/shard_map/ppermute | solution.py:21
  18.1 2.3 %shard_map.61.old_ref = f32[3,256,256]{2,1,0:T(8,128)S(1)} custom-call(f32[3,256,256]{2,1,0:T(8,128)S(1)} %get-tuple-element.44.old_ref, f32[72,256]{1,0:T(8,128)S(1)} %collective-permute-done.4.near_ref.near1, f32[72,256]{1,0:T(8,128)S(1)} %collective-permute-done.5.far_ref.far1, f32[192,256]{1,0:T(8,128)S(1)} %collective-permute-done.3.near_ref.near2, ...), custom_call_target="tpu_custom_call" | custom-call | flops 1207959552 | bytes 1310720 | tf_op jit(solution)/shard_map/pallas_call | solution.py:295
  20.4 1.4 %collective-permute-start.9 = (f32[72,256]{1,0:T(8,128)S(1)}, f32[72,256]{1,0:T(8,128)S(1)}, u32[]{:S(2)}, u32[]{:S(2)}) collective-permute-start(f32[72,256]{1,0:T(8,128)S(1)} %collective-permute-done.8.near_ref.near1), channel_id=1, source_target_pairs={{0,1},{1,0},{2,3},{3,2},{4,5},{5,4},{6,7},{7,6},{8,9},{9,8},{10,11... | collective-permute-start | bytes 221192 | tf_op jit(solution)/shard_map/ppermute | solution.py:21
  21.8 0.9 %collective-permute-done.9.far_ref.far1 = f32[72,256]{1,0:T(8,128)S(1)} collective-permute-done((f32[72,256]{1,0:T(8,128)S(1)}, f32[72,256]{1,0:T(8,128)S(1)}, u32[]{:S(2)}, u32[]{:S(2)}) %collective-permute-start.9) | collective-permute-done | bytes 73760 | tf_op jit(solution)/shard_map/ppermute | solution.py:21
  22.7 1.9 %shard_map.62.half_ref = f32[3,256,256]{2,1,0:T(8,128)S(1)} custom-call(f32[3,256,256]{2,1,0:T(8,128)S(1)} %get-tuple-element.42.own_ref, f32[72,256]{1,0:T(8,128)S(1)} %collective-permute-done.8.near_ref.near1, f32[72,256]{1,0:T(8,128)S(1)} %collective-permute-done.9.far_ref.far1), custom_call_target="tpu_custom_call" | custom-call | flops 905969664 | bytes 786432 | tf_op jit(solution)/shard_map/pallas_call | solution.py:295
  24.6 1.0 %collective-permute-start.10 = (f32[192,256]{1,0:T(8,128)S(1)}, f32[192,256]{1,0:T(8,128)S(1)}, u32[]{:S(2)}, u32[]{:S(2)}) collective-permute-start(f32[192,256]{1,0:T(8,128)S(1)} %collective-permute-done.7.near_ref.near2), channel_id=1, source_target_pairs={{0,1},{1,0},{2,3},{3,2},{4,5},{5,4},{6,7},{7,6},{8,9},{9,8},{10,11... | collective-permute-start | bytes 589832 | tf_op jit(solution)/shard_map/ppermute | solution.py:21
  25.5 1.1 %collective-permute-done.10.far_ref.far2 = f32[192,256]{1,0:T(8,128)S(1)} collective-permute-done((f32[192,256]{1,0:T(8,128)S(1)}, f32[192,256]{1,0:T(8,128)S(1)}, u32[]{:S(2)}, u32[]{:S(2)}) %collective-permute-start.10) | collective-permute-done | bytes 196640 | tf_op jit(solution)/shard_map/ppermute | solution.py:21
  27.2 1.4 %collective-permute-start.12 = (f32[72,256]{1,0:T(8,128)S(1)}, f32[72,256]{1,0:T(8,128)S(1)}, u32[]{:S(2)}, u32[]{:S(2)}) collective-permute-start(f32[72,256]{1,0:T(8,128)S(1)} %get-tuple-element.50), channel_id=1, source_target_pairs={{0,8},{1,9},{2,10},{3,11},{4,12},{5,13},{6,14},{7,15},{8,0},{9,1},... | collective-permute-start | bytes 221192 | tf_op jit(solution)/shard_map/ppermute | solution.py:21
  28.7 2.3 %shard_map.64.old_ref = f32[3,256,256]{2,1,0:T(8,128)S(1)} custom-call(f32[3,256,256]{2,1,0:T(8,128)S(1)} %shard_map.61.old_ref, f32[72,256]{1,0:T(8,128)S(1)} %collective-permute-done.8.near_ref.near1, f32[72,256]{1,0:T(8,128)S(1)} %collective-permute-done.9.far_ref.far1, f32[192,256]{1,0:T(8,128)S(1)} %collective-permute-done.7.near_ref.near2, ...), custom_call_target="tpu_custom_call" | custom-call | flops 1207959552 | bytes 1310720 | tf_op jit(solution)/shard_map/pallas_call | solution.py:295
  31.0 1.4 %collective-permute-start.13 = (f32[72,256]{1,0:T(8,128)S(1)}, f32[72,256]{1,0:T(8,128)S(1)}, u32[]{:S(2)}, u32[]{:S(2)}) collective-permute-start(f32[72,256]{1,0:T(8,128)S(1)} %collective-permute-done.12.near_ref.near1), channel_id=1, source_target_pairs={{0,1},{1,0},{2,3},{3,2},{4,5},{5,4},{6,7},{7,6},{8,9},{9,8},{10,11... | collective-permute-start | bytes 221192 | tf_op jit(solution)/shard_map/ppermute | solution.py:21
  32.4 0.9 %collective-permute-done.13.far_ref.far1 = f32[72,256]{1,0:T(8,128)S(1)} collective-permute-done((f32[72,256]{1,0:T(8,128)S(1)}, f32[72,256]{1,0:T(8,128)S(1)}, u32[]{:S(2)}, u32[]{:S(2)}) %collective-permute-start.13) | collective-permute-done | bytes 73760 | tf_op jit(solution)/shard_map/ppermute | solution.py:21
  33.4 1.6 %collective-permute-done.11.near_ref.near2 = f32[192,256]{1,0:T(8,128)S(1)} collective-permute-done((f32[192,256]{1,0:T(8,128)S(1)}, f32[192,256]{1,0:T(8,128)S(1)}, u32[]{:S(2)}, u32[]{:S(2)}) %collective-permute-start.11) | collective-permute-done | bytes 196640 | tf_op jit(solution)/shard_map/ppermute | solution.py:21
  35.0 1.2 %collective-permute-start.14 = (f32[192,256]{1,0:T(8,128)S(1)}, f32[192,256]{1,0:T(8,128)S(1)}, u32[]{:S(2)}, u32[]{:S(2)}) collective-permute-start(f32[192,256]{1,0:T(8,128)S(1)} %collective-permute-done.11.near_ref.near2), channel_id=1, source_target_pairs={{0,1},{1,0},{2,3},{3,2},{4,5},{5,4},{6,7},{7,6},{8,9},{9,8},{10,11... | collective-permute-start | bytes 589832 | tf_op jit(solution)/shard_map/ppermute | solution.py:21
  37.7 2.4 %collective-permute-done.17.near2 = f32[72,256]{1,0:T(8,128)S(1)} collective-permute-done((f32[72,256]{1,0:T(8,128)S(1)}, f32[72,256]{1,0:T(8,128)S(1)}, u32[]{:S(2)}, u32[]{:S(2)}) %collective-permute-start.17) | collective-permute-done | bytes 73760 | tf_op jit(solution)/shard_map/ppermute | solution.py:29
  40.1 1.2 %collective-permute-start.18 = (f32[72,256]{1,0:T(8,128)S(1)}, f32[72,256]{1,0:T(8,128)S(1)}, u32[]{:S(2)}, u32[]{:S(2)}) collective-permute-start(f32[72,256]{1,0:T(8,128)S(1)} %collective-permute-done.17.near2), channel_id=1, source_target_pairs={{0,1},{1,0},{2,3},{3,2},{4,5},{5,4},{6,7},{7,6},{8,9},{9,8},{10,11... | collective-permute-start | bytes 221192 | tf_op jit(solution)/shard_map/ppermute | solution.py:21
  41.3 2.0 %collective-permute-start.20 = (f32[200,256]{1,0:T(8,128)S(1)}, f32[200,256]{1,0:T(8,128)S(1)}, u32[]{:S(2)}, u32[]{:S(2)}) collective-permute-start(f32[200,256]{1,0:T(8,128)S(1)} %shard_map.66), channel_id=1, source_target_pairs={{0,1},{1,0},{2,3},{3,2},{4,5},{5,4},{6,7},{7,6},{8,16},{9,17},{10,... | collective-permute-start | bytes 614408 | tf_op jit(solution)/shard_map/ppermute | solution.py:29
  43.3 2.3 %shard_map.67.old_ref = f32[3,256,256]{2,1,0:T(8,128)S(1)} custom-call(f32[3,256,256]{2,1,0:T(8,128)S(1)} %shard_map.64.old_ref, f32[72,256]{1,0:T(8,128)S(1)} %collective-permute-done.12.near_ref.near1, f32[72,256]{1,0:T(8,128)S(1)} %collective-permute-done.13.far_ref.far1, f32[192,256]{1,0:T(8,128)S(1)} %collective-permute-done.11.near_ref.near2, ...), custom_call_target="tpu_custom_call" | custom-call | flops 1207959552 | bytes 1310720 | tf_op jit(solution)/shard_map/pallas_call | solution.py:295
  45.6 1.9 %shard_map.68 = (f32[3,256,256]{2,1,0:T(8,128)S(1)}, f32[1,256,256]{2,1,0:T(8,128)}, f32[1,256,256]{2,1,0:T(8,128)}, f32[1,256,256]{2,1,0:T(8,128)}) custom-call(f32[3,256,256]{2,1,0:T(8,128)S(1)} %shard_map.67.old_ref, f32[72,256]{1,0:T(8,128)S(1)} %collective-permute-done.17.near2, f32[72,256]{1,0:T(8,128)S(1)} %collective-permute-done.18.far2, ...), custom_call_target="tpu_custom_call" | custom-call | flops 905969664 | bytes 1310720 | tf_op jit(solution)/shard_map/pallas_call | solution.py:295
  47.5 0.9 %collective-permute-start.21 = (f32[200,256]{1,0:T(8,128)S(1)}, f32[200,256]{1,0:T(8,128)S(1)}, u32[]{:S(2)}, u32[]{:S(2)}) collective-permute-start(f32[200,256]{1,0:T(8,128)S(1)} %collective-permute-done.15.near3), channel_id=1, source_target_pairs={{0,1},{1,0},{2,3},{3,2},{4,5},{5,4},{6,7},{7,6},{8,9},{9,8},{10,11... | collective-permute-start | bytes 614408 | tf_op jit(solution)/shard_map/ppermute | solution.py:21
  48.3 2.1 %collective-permute-done.20.near2 = f32[200,256]{1,0:T(8,128)S(1)} collective-permute-done((f32[200,256]{1,0:T(8,128)S(1)}, f32[200,256]{1,0:T(8,128)S(1)}, u32[]{:S(2)}, u32[]{:S(2)}) %collective-permute-start.20) | collective-permute-done | bytes 204832 | tf_op jit(solution)/shard_map/ppermute | solution.py:29
  50.5 0.8 %collective-permute-start.22 = (f32[200,256]{1,0:T(8,128)S(1)}, f32[200,256]{1,0:T(8,128)S(1)}, u32[]{:S(2)}, u32[]{:S(2)}) collective-permute-start(f32[200,256]{1,0:T(8,128)S(1)} %collective-permute-done.20.near2), channel_id=1, source_target_pairs={{0,1},{1,0},{2,3},{3,2},{4,5},{5,4},{6,7},{7,6},{8,9},{9,8},{10,11... | collective-permute-start | bytes 614408 | tf_op jit(solution)/shard_map/ppermute | solution.py:21
  51.3 1.1 %collective-permute-done.22.far2 = f32[200,256]{1,0:T(8,128)S(1)} collective-permute-done((f32[200,256]{1,0:T(8,128)S(1)}, f32[200,256]{1,0:T(8,128)S(1)}, u32[]{:S(2)}, u32[]{:S(2)}) %collective-permute-start.22) | collective-permute-done | bytes 204832 | tf_op jit(solution)/shard_map/ppermute | solution.py:21
  52.3 1.3 %shard_map.69 = (f32[1,256,256]{2,1,0:T(8,128)}, f32[1,256,256]{2,1,0:T(8,128)}, f32[1,256,256]{2,1,0:T(8,128)}) custom-call(f32[3,256,256]{2,1,0:T(8,128)S(1)} %get-tuple-element.62.half_ref, f32[200,256]{1,0:T(8,128)S(1)} %collective-permute-done.20.near2, ...), custom_call_target="tpu_custom_call", output_to_operand_aliasing={{0}: (5, {}), {1}: (6, {}), {2}: (7, {})} | custom-call | flops 301989888 | bytes 1310720 | tf_op jit(solution)/shard_map/pallas_call | solution.py:295
  (27 shorter events, 5.2 us)
Async XLA Ops:
  0.6 2.4 %collective-permute-start = (f32[1,256,256]{2,1,0:T(8,128)}, f32[1,256,256]{2,1,0:T(8,128)S(1)}, u32[]{:S(2)}, u32[]{:S(2)}) collective-permute-start(f32[1,256,256]{2,1,0:T(8,128)} %param.3), channel_id=1, source_target_pairs={{0,1},{1,0},{2,3},{3,2},{4,5},{5,4},{6,7},{7,6},{8,9},{9,8},{10,11... | collective-permute-start | bytes 786440 | tf_op jit(solution)/shard_map/ppermute | solution.py:21
  1.4 1.7 %collective-permute-start.1 = (f32[1,256,256]{2,1,0:T(8,128)}, f32[1,256,256]{2,1,0:T(8,128)S(1)}, u32[]{:S(2)}, u32[]{:S(2)}) collective-permute-start(f32[1,256,256]{2,1,0:T(8,128)} %param.4), channel_id=1, source_target_pairs={{0,1},{1,0},{2,3},{3,2},{4,5},{5,4},{6,7},{7,6},{8,9},{9,8},{10,11... | collective-permute-start | bytes 786440 | tf_op jit(solution)/shard_map/ppermute | solution.py:21
  1.4 2.0 %collective-permute-start.2 = (f32[1,256,256]{2,1,0:T(8,128)}, f32[1,256,256]{2,1,0:T(8,128)S(1)}, u32[]{:S(2)}, u32[]{:S(2)}) collective-permute-start(f32[1,256,256]{2,1,0:T(8,128)} %param.5), channel_id=1, source_target_pairs={{0,1},{1,0},{2,3},{3,2},{4,5},{5,4},{6,7},{7,6},{8,9},{9,8},{10,11... | collective-permute-start | bytes 786440 | tf_op jit(solution)/shard_map/ppermute | solution.py:21
  5.8 3.3 %collective-permute-start.4 = (f32[72,256]{1,0:T(8,128)S(1)}, f32[72,256]{1,0:T(8,128)S(1)}, u32[]{:S(2)}, u32[]{:S(2)}) collective-permute-start(f32[72,256]{1,0:T(8,128)S(1)} %get-tuple-element.38), channel_id=1, source_target_pairs={{0,2},{1,3},{2,0},{3,1},{4,6},{5,7},{6,4},{7,5},{8,10},{9,11},{10,... | collective-permute-start | bytes 221192 | tf_op jit(solution)/shard_map/ppermute | solution.py:21
  7.1 6.8 %collective-permute-start.3 = (f32[192,256]{1,0:T(8,128)S(1)}, f32[192,256]{1,0:T(8,128)S(1)}, u32[]{:S(2)}, u32[]{:S(2)}) collective-permute-start(f32[192,256]{1,0:T(8,128)S(1)} %get-tuple-element.36), channel_id=1, source_target_pairs={{0,2},{1,3},{2,0},{3,1},{4,6},{5,7},{6,4},{7,5},{8,10},{9,11},{10,... | collective-permute-start | bytes 589832 | tf_op jit(solution)/shard_map/ppermute | solution.py:21
  9.1 3.0 %collective-permute-start.5 = (f32[72,256]{1,0:T(8,128)S(1)}, f32[72,256]{1,0:T(8,128)S(1)}, u32[]{:S(2)}, u32[]{:S(2)}) collective-permute-start(f32[72,256]{1,0:T(8,128)S(1)} %collective-permute-done.4.near_ref.near1), channel_id=1, source_target_pairs={{0,1},{1,0},{2,3},{3,2},{4,5},{5,4},{6,7},{7,6},{8,9},{9,8},{10,11... | collective-permute-start | bytes 221192 | tf_op jit(solution)/shard_map/ppermute | solution.py:21
  13.9 2.0 %collective-permute-start.6 = (f32[192,256]{1,0:T(8,128)S(1)}, f32[192,256]{1,0:T(8,128)S(1)}, u32[]{:S(2)}, u32[]{:S(2)}) collective-permute-start(f32[192,256]{1,0:T(8,128)S(1)} %collective-permute-done.3.near_ref.near2), channel_id=1, source_target_pairs={{0,1},{1,0},{2,3},{3,2},{4,5},{5,4},{6,7},{7,6},{8,9},{9,8},{10,11... | collective-permute-start | bytes 589832 | tf_op jit(solution)/shard_map/ppermute | solution.py:21
  16.5 3.8 %collective-permute-start.8 = (f32[72,256]{1,0:T(8,128)S(1)}, f32[72,256]{1,0:T(8,128)S(1)}, u32[]{:S(2)}, u32[]{:S(2)}) collective-permute-start(f32[72,256]{1,0:T(8,128)S(1)} %get-tuple-element.43), channel_id=1, source_target_pairs={{0,4},{1,5},{2,6},{3,7},{4,0},{5,1},{6,2},{7,3},{8,12},{9,13},{10,... | collective-permute-start | bytes 221192 | tf_op jit(solution)/shard_map/ppermute | solution.py:21
  17.8 6.7 %collective-permute-start.7 = (f32[192,256]{1,0:T(8,128)S(1)}, f32[192,256]{1,0:T(8,128)S(1)}, u32[]{:S(2)}, u32[]{:S(2)}) collective-permute-start(f32[192,256]{1,0:T(8,128)S(1)} %get-tuple-element.41), channel_id=1, source_target_pairs={{0,4},{1,5},{2,6},{3,7},{4,0},{5,1},{6,2},{7,3},{8,12},{9,13},{10,... | collective-permute-start | bytes 589832 | tf_op jit(solution)/shard_map/ppermute | solution.py:21
  20.4 2.3 %collective-permute-start.9 = (f32[72,256]{1,0:T(8,128)S(1)}, f32[72,256]{1,0:T(8,128)S(1)}, u32[]{:S(2)}, u32[]{:S(2)}) collective-permute-start(f32[72,256]{1,0:T(8,128)S(1)} %collective-permute-done.8.near_ref.near1), channel_id=1, source_target_pairs={{0,1},{1,0},{2,3},{3,2},{4,5},{5,4},{6,7},{7,6},{8,9},{9,8},{10,11... | collective-permute-start | bytes 221192 | tf_op jit(solution)/shard_map/ppermute | solution.py:21
  24.6 2.0 %collective-permute-start.10 = (f32[192,256]{1,0:T(8,128)S(1)}, f32[192,256]{1,0:T(8,128)S(1)}, u32[]{:S(2)}, u32[]{:S(2)}) collective-permute-start(f32[192,256]{1,0:T(8,128)S(1)} %collective-permute-done.7.near_ref.near2), channel_id=1, source_target_pairs={{0,1},{1,0},{2,3},{3,2},{4,5},{5,4},{6,7},{7,6},{8,9},{9,8},{10,11... | collective-permute-start | bytes 589832 | tf_op jit(solution)/shard_map/ppermute | solution.py:21
  27.2 3.8 %collective-permute-start.12 = (f32[72,256]{1,0:T(8,128)S(1)}, f32[72,256]{1,0:T(8,128)S(1)}, u32[]{:S(2)}, u32[]{:S(2)}) collective-permute-start(f32[72,256]{1,0:T(8,128)S(1)} %get-tuple-element.50), channel_id=1, source_target_pairs={{0,8},{1,9},{2,10},{3,11},{4,12},{5,13},{6,14},{7,15},{8,0},{9,1},... | collective-permute-start | bytes 221192 | tf_op jit(solution)/shard_map/ppermute | solution.py:21
  28.6 6.5 %collective-permute-start.11 = (f32[192,256]{1,0:T(8,128)S(1)}, f32[192,256]{1,0:T(8,128)S(1)}, u32[]{:S(2)}, u32[]{:S(2)}) collective-permute-start(f32[192,256]{1,0:T(8,128)S(1)} %get-tuple-element.48), channel_id=1, source_target_pairs={{0,8},{1,9},{2,10},{3,11},{4,12},{5,13},{6,14},{7,15},{8,0},{9,1},... | collective-permute-start | bytes 589832 | tf_op jit(solution)/shard_map/ppermute | solution.py:21
  31.0 2.3 %collective-permute-start.13 = (f32[72,256]{1,0:T(8,128)S(1)}, f32[72,256]{1,0:T(8,128)S(1)}, u32[]{:S(2)}, u32[]{:S(2)}) collective-permute-start(f32[72,256]{1,0:T(8,128)S(1)} %collective-permute-done.12.near_ref.near1), channel_id=1, source_target_pairs={{0,1},{1,0},{2,3},{3,2},{4,5},{5,4},{6,7},{7,6},{8,9},{9,8},{10,11... | collective-permute-start | bytes 221192 | tf_op jit(solution)/shard_map/ppermute | solution.py:21
  35.0 2.3 %collective-permute-start.14 = (f32[192,256]{1,0:T(8,128)S(1)}, f32[192,256]{1,0:T(8,128)S(1)}, u32[]{:S(2)}, u32[]{:S(2)}) collective-permute-start(f32[192,256]{1,0:T(8,128)S(1)} %collective-permute-done.11.near_ref.near2), channel_id=1, source_target_pairs={{0,1},{1,0},{2,3},{3,2},{4,5},{5,4},{6,7},{7,6},{8,9},{9,8},{10,11... | collective-permute-start | bytes 589832 | tf_op jit(solution)/shard_map/ppermute | solution.py:21
  36.2 3.9 %collective-permute-start.17 = (f32[72,256]{1,0:T(8,128)S(1)}, f32[72,256]{1,0:T(8,128)S(1)}, u32[]{:S(2)}, u32[]{:S(2)}) collective-permute-start(f32[72,256]{1,0:T(8,128)S(1)} %get-tuple-element.56), channel_id=1, source_target_pairs={{0,1},{1,0},{2,3},{3,2},{4,5},{5,4},{6,7},{7,6},{8,16},{9,17},{10,... | collective-permute-start | bytes 221192 | tf_op jit(solution)/shard_map/ppermute | solution.py:29
  36.3 3.8 %collective-permute-start.16 = (f32[72,256]{1,0:T(8,128)S(1)}, f32[72,256]{1,0:T(8,128)S(1)}, u32[]{:S(2)}, u32[]{:S(2)}) collective-permute-start(f32[72,256]{1,0:T(8,128)S(1)} %get-tuple-element.56), channel_id=1, source_target_pairs={{0,1},{1,0},{2,3},{3,2},{4,5},{5,4},{6,7},{7,6},{8,24},{9,25},{10,... | collective-permute-start | bytes 221192 | tf_op jit(solution)/shard_map/ppermute | solution.py:29
  37.3 10.2 %collective-permute-start.15 = (f32[200,256]{1,0:T(8,128)S(1)}, f32[200,256]{1,0:T(8,128)S(1)}, u32[]{:S(2)}, u32[]{:S(2)}) collective-permute-start(f32[200,256]{1,0:T(8,128)S(1)} %shard_map.66), channel_id=1, source_target_pairs={{0,1},{1,0},{2,3},{3,2},{4,5},{5,4},{6,7},{7,6},{8,24},{9,25},{10,... | collective-permute-start | bytes 614408 | tf_op jit(solution)/shard_map/ppermute | solution.py:29
  40.1 5.4 %collective-permute-start.18 = (f32[72,256]{1,0:T(8,128)S(1)}, f32[72,256]{1,0:T(8,128)S(1)}, u32[]{:S(2)}, u32[]{:S(2)}) collective-permute-start(f32[72,256]{1,0:T(8,128)S(1)} %collective-permute-done.17.near2), channel_id=1, source_target_pairs={{0,1},{1,0},{2,3},{3,2},{4,5},{5,4},{6,7},{7,6},{8,9},{9,8},{10,11... | collective-permute-start | bytes 221192 | tf_op jit(solution)/shard_map/ppermute | solution.py:21
  41.3 4.3 %collective-permute-start.19 = (f32[72,256]{1,0:T(8,128)S(1)}, f32[72,256]{1,0:T(8,128)S(1)}, u32[]{:S(2)}, u32[]{:S(2)}) collective-permute-start(f32[72,256]{1,0:T(8,128)S(1)} %collective-permute-done.16.near3), channel_id=1, source_target_pairs={{0,1},{1,0},{2,3},{3,2},{4,5},{5,4},{6,7},{7,6},{8,9},{9,8},{10,11... | collective-permute-start | bytes 221192 | tf_op jit(solution)/shard_map/ppermute | solution.py:21
  41.3 9.2 %collective-permute-start.20 = (f32[200,256]{1,0:T(8,128)S(1)}, f32[200,256]{1,0:T(8,128)S(1)}, u32[]{:S(2)}, u32[]{:S(2)}) collective-permute-start(f32[200,256]{1,0:T(8,128)S(1)} %shard_map.66), channel_id=1, source_target_pairs={{0,1},{1,0},{2,3},{3,2},{4,5},{5,4},{6,7},{7,6},{8,16},{9,17},{10,... | collective-permute-start | bytes 614408 | tf_op jit(solution)/shard_map/ppermute | solution.py:29
  47.5 3.0 %collective-permute-start.21 = (f32[200,256]{1,0:T(8,128)S(1)}, f32[200,256]{1,0:T(8,128)S(1)}, u32[]{:S(2)}, u32[]{:S(2)}) collective-permute-start(f32[200,256]{1,0:T(8,128)S(1)} %collective-permute-done.15.near3), channel_id=1, source_target_pairs={{0,1},{1,0},{2,3},{3,2},{4,5},{5,4},{6,7},{7,6},{8,9},{9,8},{10,11... | collective-permute-start | bytes 614408 | tf_op jit(solution)/shard_map/ppermute | solution.py:21
  50.5 1.9 %collective-permute-start.22 = (f32[200,256]{1,0:T(8,128)S(1)}, f32[200,256]{1,0:T(8,128)S(1)}, u32[]{:S(2)}, u32[]{:S(2)}) collective-permute-start(f32[200,256]{1,0:T(8,128)S(1)} %collective-permute-done.20.near2), channel_id=1, source_target_pairs={{0,1},{1,0},{2,3},{3,2},{4,5},{5,4},{6,7},{7,6},{8,9},{9,8},{10,11... | collective-permute-start | bytes 614408 | tf_op jit(solution)/shard_map/ppermute | solution.py:21
